TPU v7x, 32 devices: a whole 2x2x4 slice. The times are simulated.
32 devices in a mesh: inst: 2 (over x), dom: 16 (over z, y, core).
Axes of the slice: x: 2, y: 2, z: 4, core: 2. Of those that a mesh axis runs over, the one named last changes fastest.
Arguments:
- initial_state: bfloat16 [8, 256, 320], P('inst', 'dom'), may hold values from -6 to 6
- forcing: bfloat16 [8, 256, 320], P('inst', 'dom'), may hold values from -6 to 6
- diagonal_blocks: bfloat16 [256, 320, 320], P('dom'), may hold values from -0.3125 to 0.3125
- flux_jacobian: bfloat16 [256, 2400], P('dom'), may hold values from -0.5 to 0.5
- send_list: int32 [16, 4, 8], P('dom'), may hold values from 0 to 96, as said below
- source_index: int32 [256, 6], P('dom'), may hold values from 0 to 128, as said below
- frequency: float32 [1], replicated, may hold values from 0.5 to 2
Outputs:
- final_state: bfloat16 [8, 256, 320], P('inst', 'dom')
- final_residual: float32 [8, 256, 320], P('inst', 'dom')
Inputs may be any that keep to these rules, and one draw needn't show every extreme that they name: `send_list`: entry [p, k, c] is a face-block 6 e + f of partition p (its element e, face f) that partition p sends to partition p + o_k; the value 6 * 16 marks an empty slot, and used slots come first in each row. Slots toward partitions outside the mesh are empty. No partition sends more than 8 face-blocks to one neighbour, and in every draw some partition sends exactly 8. `source_index`: values under 6 * 16 name a face-block of the element's own partition; 96 + k * 8 + c names slot c of what partition p + o_k sends toward offset -o_k; the largest value marks a boundary face without neighbour. Every used slot sent to a partition is named by exactly one face of that partition.
All inputs are finite; a program needn't handle non-finite values.
Results may differ from a plain program's by a relative error of at most 0.014.
Values may be sent and summed in bfloat16 or wider, within the bound.
No kernel may reach another device: no remote copies, remote signals or barrier semaphores. Data moves between devices by JAX's collectives and lax.ppermute only.
A program may use at most 64 MiB of HBM per device.

v0:
```python
import math

import jax
import jax.numpy as jnp
import numpy as np
from jax import lax
from jax.sharding import PartitionSpec as P

FIELDS = 5
ORDER = 3
NODES = 64
FPTS = 16
NI = 8
REACH = 2
ITERS = 2


pseudo_step = 0.5
dissipation = 0.25


def passed_along(block, axis, distance):
    devices = range(lax.axis_size(axis))
    route = [(i - distance, i) for i in devices if i - distance in devices]
    return lax.ppermute(block, axis, route)


def gauss_legendre(count):
    points = []
    weights = []
    for i in range(count):
        where = math.cos(math.pi * (i + 0.75) / (count + 0.5))
        for sweep in range(100):
            before = 1.0
            value = where
            for j in range(2, count + 1):
                after = ((2 * j - 1) * where * value - (j - 1) * before) / j
                before = value
                value = after
            slope = count * (where * value - before) / (where * where - 1.0)
            where = where - value / slope
        before = 1.0
        value = where
        for j in range(2, count + 1):
            after = ((2 * j - 1) * where * value - (j - 1) * before) / j
            before = value
            value = after
        slope = count * (where * value - before) / (where * where - 1.0)
        points.append(where)
        weights.append(2.0 / ((1.0 - where * where) * slope * slope))
    return (np.array(points[::-1]), np.array(weights[::-1]))


def lagrange_at(points, where):
    values = np.ones(points.shape[0])
    for i in range(points.shape[0]):
        for j in range(points.shape[0]):
            if j != i:
                values[i] = values[i] * (where - points[j]) / (points[i] - points[j])
    return values


def tables(order, count):
    points, weights = gauss_legendre(order + 1)
    at_minus = lagrange_at(points, -1.0)
    at_plus = lagrange_at(points, 1.0)
    per_side = order + 1
    node_count = per_side**3
    face_points = per_side**2
    trace_table = np.zeros((node_count, 6 * face_points))
    lift_table = np.zeros((node_count, 6 * face_points))
    for k in range(per_side):
        for j in range(per_side):
            for i in range(per_side):
                node = i + per_side * j + per_side * per_side * k
                entries = [
                    (0, at_minus[i], j + per_side * k, weights[i]),
                    (1, at_plus[i], j + per_side * k, weights[i]),
                    (2, at_minus[j], i + per_side * k, weights[j]),
                    (3, at_plus[j], i + per_side * k, weights[j]),
                    (4, at_minus[k], i + per_side * j, weights[k]),
                    (5, at_plus[k], i + per_side * j, weights[k]),
                ]
                for face_index, factor, point, weight in entries:
                    trace_table[node, face_index * face_points + point] = factor
                    lift_table[node, face_index * face_points + point] = factor / weight
    spectral = np.zeros((count, count))
    second = np.zeros((count, count))
    for t in range(count):
        for s in range(count):
            if t != s:
                spectral[t, s] = 0.5 * (-1.0) ** (t - s + 1) / math.tan(math.pi * (t - s) / count)
                second[t, s] = -0.5 * (-1.0) ** (t - s) / math.sin(math.pi * (t - s) / count) ** 2
            else:
                second[t, s] = -(count * count + 2.0) / 12.0
    return (trace_table, lift_table, spectral, second)


def on_device(
    initial_state, forcing, diagonal_blocks, flux_jacobian, send_list, source_index, frequency
):
    inst_dev, elem_count, row_width = initial_state.shape
    face_count = 6 * elem_count
    reach_slots = send_list.shape[1]
    capacity = send_list.shape[2]
    block_width = inst_dev * FIELDS * FPTS
    trace_np, lift_np, spectral_np, second_np = tables(ORDER, NI)
    trace_table = jnp.asarray(trace_np, jnp.float32)
    lift_table = jnp.asarray(lift_np, jnp.float32).reshape(NODES, 6, FPTS)
    coupler = frequency[0] * jnp.asarray(spectral_np, jnp.float32) - dissipation * jnp.asarray(
        second_np, jnp.float32
    )
    offsets = np.concatenate([np.arange(-REACH, 0), np.arange(1, REACH + 1)])
    flux_blocks = flux_jacobian.reshape(elem_count, 6, FIELDS, FIELDS, FPTS)
    source_rows = source_index.reshape(face_count)
    send_rows = send_list.reshape(reach_slots * capacity)
    forcing_wide = forcing.astype(jnp.float32)
    zero_block = jnp.zeros((1, block_width), jnp.bfloat16)
    current = initial_state
    residual = jnp.zeros(forcing.shape, jnp.float32)
    for iteration in range(ITERS):
        current_wide = current.astype(jnp.float32)
        traces = jnp.einsum(
            "iecn,nm->iecm",
            current_wide.reshape(inst_dev, elem_count, FIELDS, NODES),
            trace_table,
            precision=lax.Precision.HIGHEST,
        ).astype(jnp.bfloat16)
        face_rows = traces.reshape(inst_dev, elem_count, FIELDS, 6, FPTS).transpose(1, 3, 0, 2, 4)
        face_rows = face_rows.reshape(face_count, block_width)
        local_pool = jnp.concatenate([face_rows, zero_block], 0)
        outgoing = local_pool[send_rows].reshape(reach_slots, capacity, block_width)
        pieces = []
        for slot_index in range(reach_slots):
            shift_by = -int(offsets[slot_index])
            pieces.append(passed_along(outgoing[reach_slots - 1 - slot_index], "dom", shift_by))
        received = jnp.stack(pieces)
        face_pool = jnp.concatenate(
            [face_rows, received.reshape(reach_slots * capacity, block_width), zero_block], 0
        )
        picked = face_pool[source_rows].reshape(elem_count, 6, inst_dev, FIELDS, FPTS)
        normal_flux = jnp.einsum(
            "efcdq,efidq->eifcq", flux_blocks, picked, preferred_element_type=jnp.float32
        )
        lifted = jnp.einsum(
            "eifcq,nfq->iecn", normal_flux, lift_table, precision=lax.Precision.HIGHEST
        )
        lifted = lifted.reshape(inst_dev, elem_count, row_width)
        diagonal_term = jnp.einsum(
            "iem,emn->ien", current, diagonal_blocks, preferred_element_type=jnp.float32
        )
        my_inst = lax.axis_index("inst")
        coupler_rows = lax.dynamic_slice_in_dim(coupler, my_inst * inst_dev, inst_dev, 0)
        summed = jnp.einsum(
            "ts,sem->tem",
            coupler_rows,
            lax.all_gather(current, "inst", axis=0, tiled=True).astype(jnp.float32),
            precision=lax.Precision.HIGHEST,
        )
        coupling = summed.astype(jnp.bfloat16)
        residual = diagonal_term + lifted + coupling.astype(jnp.float32) - forcing_wide
        current = (current_wide - pseudo_step * residual).astype(jnp.bfloat16)
    return (current, residual)


def solution(mesh):
    return jax.shard_map(
        on_device,
        mesh=mesh,
        in_specs=(
            P("inst", "dom", None),
            P("inst", "dom", None),
            P("dom", None, None),
            P("dom", None),
            P("dom", None, None),
            P("dom", None),
            P(),
        ),
        out_specs=(P("inst", "dom", None), P("inst", "dom", None)),
        check_vma=False,
    )
```

profile of v0, /device:TPU:8, one launch (start us, length us, event | category | flops | bytes accessed | tf_op | source)
XLA Modules:
  0.0 98.7 jit_solution(4757446661141071899)
XLA Ops:
  0.7 0.9 reshape.126
  1.6 1.0 fusion.8
  4.8 3.4 %collective-permute-start = (bf16[8,320]{1,0:T(8,128)(2,1)S(1)}, bf16[8,320]{1,0:T(8,128)(2,1)S(1)}, u32[]{:S(2)}, u32[]{:S(2)}) collective-permute-start(bf16[8,320]{1,0:T(8,128)(2,1)S(1)} %get-tuple-element.12), channel_id=1, source_target_pairs={{0,2},{1,3},{2,4},{3,5},{4,6},{5,7},{6,8},{7,9},{8,10},{9,11},{10,... | collective-permute-start | bytes 15368 | tf_op jit(solution)/shard_map/ppermute | solution.py:25
  8.2 1.9 %collective-permute-start.1 = (bf16[8,320]{1,0:T(8,128)(2,1)S(1)}, bf16[8,320]{1,0:T(8,128)(2,1)S(1)}, u32[]{:S(2)}, u32[]{:S(2)}) collective-permute-start(bf16[8,320]{1,0:T(8,128)(2,1)S(1)} %get-tuple-element.14), channel_id=1, source_target_pairs={{0,1},{1,2},{2,3},{3,4},{4,5},{5,6},{6,7},{7,8},{8,9},{9,10},{10,1... | collective-permute-start | bytes 15368 | tf_op jit(solution)/shard_map/ppermute | solution.py:25
  10.1 4.5 %collective-permute-start.2 = (bf16[8,320]{1,0:T(8,128)(2,1)S(1)}, bf16[8,320]{1,0:T(8,128)(2,1)S(1)}, u32[]{:S(2)}, u32[]{:S(2)}) collective-permute-start(bf16[8,320]{1,0:T(8,128)(2,1)S(1)} %get-tuple-element.13), channel_id=1, source_target_pairs={{1,0},{2,1},{3,2},{4,3},{5,4},{6,5},{7,6},{8,7},{9,8},{10,9},{11,1... | collective-permute-start | bytes 15368 | tf_op jit(solution)/shard_map/ppermute | solution.py:25
  14.7 2.4 %collective-permute-start.3 = (bf16[8,320]{1,0:T(8,128)(2,1)S(1)}, bf16[8,320]{1,0:T(8,128)(2,1)S(1)}, u32[]{:S(2)}, u32[]{:S(2)}) collective-permute-start(bf16[8,320]{1,0:T(8,128)(2,1)S(1)} %get-tuple-element.15), channel_id=1, source_target_pairs={{2,0},{3,1},{4,2},{5,3},{6,4},{7,5},{8,6},{9,7},{10,8},{11,9},{12,... | collective-permute-start | bytes 15368 | tf_op jit(solution)/shard_map/ppermute | solution.py:25
  17.1 4.8 %all_gather.6 = bf16[8,16,320]{2,1,0:T(8,128)(2,1)S(1)} all-gather(bf16[4,16,320]{2,1,0:T(8,128)(2,1)S(1)} %copy-done), channel_id=1, replica_groups=mesh['inst'=2,'dom'=16] {'inst'}, dimensions={0}, use_global_device_ids=true | all-gather | bytes 122880 | tf_op jit(solution)/shard_map/all_gather | solution.py:157
  23.0 1.7 %reshape.133 = bf16[16,6,5,5,16]{4,3,2,1,0:T(8,128)(2,1)} reshape(bf16[16,2400]{1,0:T(8,128)(2,1)S(1)} %copy-done.4) | data formatting | bytes 153600 | tf_op jit(solution)/shard_map/reshape | solution.py:114
  24.7 4.2 %copy.48 = bf16[16,6,5,5,16]{3,2,4,1,0:T(8,128)(2,1)S(1)} copy(bf16[16,6,5,5,16]{4,3,2,1,0:T(8,128)(2,1)} %reshape.133) | data formatting | bytes 153600 | tf_op jit(solution)/shard_map/reshape | solution.py:114
  29.6 0.8 gather_fusion.1
  30.4 1.5 %reshape.132 = bf16[16,6,4,5,16]{4,3,2,1,0:T(8,128)(2,1)} reshape(bf16[96,320]{1,0:T(8,128)(2,1)S(1)} %gather_fusion.1) | data formatting | bytes 122880 | tf_op jit(solution)/shard_map/reshape | solution.py:141
  31.9 4.5 %copy.47 = bf16[16,6,4,5,16]{3,2,4,1,0:T(4,128)(2,1)} copy(bf16[16,6,4,5,16]{4,3,2,1,0:T(8,128)(2,1)} %reshape.132) | data formatting | bytes 122880 | tf_op jit(solution)/shard_map/reshape | solution.py:141
  36.4 4.8 %convolution_bitcast_fusion.1 = f32[16,4,6,5,16]{3,1,4,2,0:T(4,128)} fusion(bf16[16,6,4,5,16]{3,2,4,1,0:T(4,128)(2,1)} %copy.47, bf16[16,6,5,5,16]{3,2,4,1,0:T(8,128)(2,1)S(1)} %copy.48), kind=kOutput, calls=%fused_computation.5 | convolution fusion | flops 307200 | bytes 261120 | tf_op jit(solution)/shard_map/efcdq,efidq->eifcq/dot_general | solution.py:142
  41.2 5.3 %copy.49 = f32[16,4,6,5,16]{4,0,2,3,1:T(8,128)} copy(f32[16,4,6,5,16]{3,1,4,2,0:T(4,128)} %convolution_bitcast_fusion.1) | data formatting | bytes 245760 | tf_op jit(solution)/shard_map/efcdq,efidq->eifcq/transpose | solution.py:142
  46.5 2.2 %convolution_bitcast_fusion.3 = f32[4,16,5,64]{3,1,2,0:T(8,128)S(1)} fusion(f32[16,4,6,5,16]{4,0,2,3,1:T(8,128)} %copy.49, f32[64,6,16,1,1]{0,2,1,4,3:T(8,128)S(1)} %copy-done.2), kind=kOutput, calls=%fused_computation.7 | convolution fusion | flops 23592960 | bytes 229376 | tf_op jit(solution)/shard_map/eifcq,nfq->iecn/dot_general | solution.py:145
  49.5 2.8 %fusion.11 = bf16[4,16,320]{2,0,1:T(4,128)(2,1)S(1)} fusion(f32[4,16,320]{2,0,1:T(4,128)S(1)} %fusion.10, f32[4,16,320]{2,0,1:T(4,128)} %reshape.179, bf16[16,320,320]{2,1,0:T(8,128)(2,1)} %param.13, bf16[4,16,320]{2,1,0:T(8,128)(2,1)S(1)} %copy-done, bf16[4,16,320]{2,1,0:T(8,128)(2,1)} %param.12), kind=kOutput, calls=%fused_computation.25 | convolution fusion | flops 13271040 | bytes 3563520 | tf_op jit(solution)/shard_map/iem,emn->ien/dot_general | solution.py:149
  52.5 1.0 convolution_convert_fusion
  53.5 1.2 %reshape.137 = bf16[4,16,5,6,16]{4,3,1,2,0:T(8,128)(2,1)} reshape(bf16[4,16,5,96]{3,1,2,0:T(8,128)(2,1)S(1)} %convolution_convert_fusion) | data formatting | bytes 122880 | tf_op jit(solution)/shard_map/reshape | solution.py:129
  54.7 2.3 %copy.56 = bf16[16,6,4,5,16]{4,3,2,1,0:T(8,128)(2,1)} copy(bf16[16,6,4,5,16]{4,1,0,3,2:T(8,128)(2,1)} %bitcast.98) | data formatting | bytes 122880 | tf_op jit(solution)/shard_map/transpose | solution.py:129
  57.1 1.8 %reshape.138 = bf16[96,320]{1,0:T(8,128)(2,1)S(1)} reshape(bf16[16,6,4,5,16]{4,3,2,1,0:T(8,128)(2,1)} %copy.56) | data formatting | bytes 122880 | tf_op jit(solution)/shard_map/reshape | solution.py:130
  59.6 3.4 %collective-permute-start.4 = (bf16[8,320]{1,0:T(8,128)(2,1)S(1)}, bf16[8,320]{1,0:T(8,128)(2,1)S(1)}, u32[]{:S(2)}, u32[]{:S(2)}) collective-permute-start(bf16[8,320]{1,0:T(8,128)(2,1)S(1)} %get-tuple-element.8), channel_id=1, source_target_pairs={{0,2},{1,3},{2,4},{3,5},{4,6},{5,7},{6,8},{7,9},{8,10},{9,11},{10,... | collective-permute-start | bytes 15368 | tf_op jit(solution)/shard_map/ppermute | solution.py:25
  63.0 1.9 %collective-permute-start.5 = (bf16[8,320]{1,0:T(8,128)(2,1)S(1)}, bf16[8,320]{1,0:T(8,128)(2,1)S(1)}, u32[]{:S(2)}, u32[]{:S(2)}) collective-permute-start(bf16[8,320]{1,0:T(8,128)(2,1)S(1)} %get-tuple-element.10), channel_id=1, source_target_pairs={{0,1},{1,2},{2,3},{3,4},{4,5},{5,6},{6,7},{7,8},{8,9},{9,10},{10,1... | collective-permute-start | bytes 15368 | tf_op jit(solution)/shard_map/ppermute | solution.py:25
  65.0 4.5 %collective-permute-start.6 = (bf16[8,320]{1,0:T(8,128)(2,1)S(1)}, bf16[8,320]{1,0:T(8,128)(2,1)S(1)}, u32[]{:S(2)}, u32[]{:S(2)}) collective-permute-start(bf16[8,320]{1,0:T(8,128)(2,1)S(1)} %get-tuple-element.9), channel_id=1, source_target_pairs={{1,0},{2,1},{3,2},{4,3},{5,4},{6,5},{7,6},{8,7},{9,8},{10,9},{11,1... | collective-permute-start | bytes 15368 | tf_op jit(solution)/shard_map/ppermute | solution.py:25
  69.5 2.4 %collective-permute-start.7 = (bf16[8,320]{1,0:T(8,128)(2,1)S(1)}, bf16[8,320]{1,0:T(8,128)(2,1)S(1)}, u32[]{:S(2)}, u32[]{:S(2)}) collective-permute-start(bf16[8,320]{1,0:T(8,128)(2,1)S(1)} %get-tuple-element.11), channel_id=1, source_target_pairs={{2,0},{3,1},{4,2},{5,3},{6,4},{7,5},{8,6},{9,7},{10,8},{11,9},{12,... | collective-permute-start | bytes 15368 | tf_op jit(solution)/shard_map/ppermute | solution.py:25
  71.9 4.9 %all_gather.7 = bf16[8,16,320]{2,1,0:T(8,128)(2,1)S(1)} all-gather(bf16[4,16,320]{2,1,0:T(8,128)(2,1)S(1)} %copy.62), channel_id=1, replica_groups=mesh['inst'=2,'dom'=16] {'inst'}, dimensions={0}, use_global_device_ids=true | all-gather | bytes 122880 | tf_op jit(solution)/shard_map/all_gather | solution.py:157
  77.3 0.9 gather_fusion.3
  78.2 1.5 %reshape.140 = bf16[16,6,4,5,16]{4,3,2,1,0:T(8,128)(2,1)} reshape(bf16[96,320]{1,0:T(8,128)(2,1)S(1)} %gather_fusion.3) | data formatting | bytes 122880 | tf_op jit(solution)/shard_map/reshape | solution.py:141
  79.7 4.5 %copy.57 = bf16[16,6,4,5,16]{3,2,4,1,0:T(4,128)(2,1)} copy(bf16[16,6,4,5,16]{4,3,2,1,0:T(8,128)(2,1)} %reshape.140) | data formatting | bytes 122880 | tf_op jit(solution)/shard_map/reshape | solution.py:141
  84.2 4.8 %convolution_bitcast_fusion = f32[16,4,6,5,16]{3,1,4,2,0:T(4,128)} fusion(bf16[16,6,4,5,16]{3,2,4,1,0:T(4,128)(2,1)} %copy.57, bf16[16,6,5,5,16]{3,2,4,1,0:T(8,128)(2,1)S(1)} %copy.48), kind=kOutput, calls=%fused_computation.4 | convolution fusion | flops 307200 | bytes 261120 | tf_op jit(solution)/shard_map/efcdq,efidq->eifcq/dot_general | solution.py:142
  89.0 4.4 %copy.59 = f32[16,4,6,5,16]{4,0,2,3,1:T(8,128)S(1)} copy(f32[16,4,6,5,16]{3,1,4,2,0:T(4,128)} %convolution_bitcast_fusion) | data formatting | bytes 245760 | tf_op jit(solution)/shard_map/efcdq,efidq->eifcq/transpose | solution.py:142
  93.5 0.9 convolution_bitcast_fusion.2
  94.6 2.8 %subtract_convert_fusion = (bf16[4,16,320]{2,0,1:T(4,128)(2,1)S(1)}, f32[4,16,320]{2,0,1:T(4,128)S(1)}) fusion(bf16[4,16,320]{2,0,1:T(4,128)(2,1)S(1)} %fusion.11, bf16[4,16,320]{2,1,0:T(8,128)(2,1)S(1)} %copy-done.1, f32[4,16,320]{2,0,1:T(4,128)S(1)} %fusion.9, f32[4,16,320]{2,0,1:T(4,128)S(1)} %reshape.181, bf16[16,320,320]{2,1,0:T(8,128)(2,1)} %param.13), kind=kOutput, calls=%fused_computation.30 | convolution fusion | flops 13271040 | bytes 3645440 | tf_op jit(solution)/shard_map/iem,emn->ien/dot_general | solution.py:149
  (70 shorter events, 6.6 us)
Async XLA Ops:
  0.6 22.1 %copy-start.10 = (f32[8,8]{1,0:T(8,128)S(1)}, f32[8,8]{1,0:T(8,128)}, u32[]{:S(2)}) copy-start(f32[8,8]{1,0:T(8,128)} %constant.34.clone) | copy-start | bytes 772
  0.6 22.1 %copy-start.11 = (f32[8,8]{1,0:T(8,128)S(1)}, f32[8,8]{1,0:T(8,128)}, u32[]{:S(2)}) copy-start(f32[8,8]{1,0:T(8,128)} %constant.43) | copy-start | bytes 772
  0.7 16.5 %copy-start = (bf16[4,16,320]{2,1,0:T(8,128)(2,1)S(1)}, bf16[4,16,320]{2,1,0:T(8,128)(2,1)}, u32[]{:S(2)}) copy-start(bf16[4,16,320]{2,1,0:T(8,128)(2,1)} %param.11) | copy-start | bytes 122884
  0.7 3.3 %copy-start.14 = (s32[1,4,8]{2,1,0:T(4,128)S(1)}, s32[1,4,8]{2,1,0:T(4,128)}, u32[]{:S(2)}) copy-start(s32[1,4,8]{2,1,0:T(4,128)} %param.15) | copy-start | bytes 388
  0.7 21.2 %copy-start.9 = (s32[16,6]{0,1:T(8,128)S(1)}, s32[16,6]{0,1:T(8,128)}, u32[]{:S(2)}) copy-start(s32[16,6]{0,1:T(8,128)} %param.16) | copy-start | bytes 1156
  0.7 22.3 %copy-start.4 = (bf16[16,2400]{1,0:T(8,128)(2,1)S(1)}, bf16[16,2400]{1,0:T(8,128)(2,1)}, u32[]{:S(2)}) copy-start(bf16[16,2400]{1,0:T(8,128)(2,1)} %param.14) | copy-start | bytes 230404
  4.1 25.5 %copy-start.7 = (s32[1024]{0:T(1024)}, s32[1024]{0:T(1024)S(1)}, u32[]{:S(2)}) copy-start(s32[1024]{0:T(1024)S(1)} %pad_clamp_fusion.1) | copy-start | bytes 12292
  4.8 24.2 %collective-permute-start = (bf16[8,320]{1,0:T(8,128)(2,1)S(1)}, bf16[8,320]{1,0:T(8,128)(2,1)S(1)}, u32[]{:S(2)}, u32[]{:S(2)}) collective-permute-start(bf16[8,320]{1,0:T(8,128)(2,1)S(1)} %get-tuple-element.12), channel_id=1, source_target_pairs={{0,2},{1,3},{2,4},{3,5},{4,6},{5,7},{6,8},{7,9},{8,10},{9,11},{10,... | collective-permute-start | bytes 15368 | tf_op jit(solution)/shard_map/ppermute | solution.py:25
  8.2 20.8 %collective-permute-start.1 = (bf16[8,320]{1,0:T(8,128)(2,1)S(1)}, bf16[8,320]{1,0:T(8,128)(2,1)S(1)}, u32[]{:S(2)}, u32[]{:S(2)}) collective-permute-start(bf16[8,320]{1,0:T(8,128)(2,1)S(1)} %get-tuple-element.14), channel_id=1, source_target_pairs={{0,1},{1,2},{2,3},{3,4},{4,5},{5,6},{6,7},{7,8},{8,9},{9,10},{10,1... | collective-permute-start | bytes 15368 | tf_op jit(solution)/shard_map/ppermute | solution.py:25
  10.1 18.8 %collective-permute-start.2 = (bf16[8,320]{1,0:T(8,128)(2,1)S(1)}, bf16[8,320]{1,0:T(8,128)(2,1)S(1)}, u32[]{:S(2)}, u32[]{:S(2)}) collective-permute-start(bf16[8,320]{1,0:T(8,128)(2,1)S(1)} %get-tuple-element.13), channel_id=1, source_target_pairs={{1,0},{2,1},{3,2},{4,3},{5,4},{6,5},{7,6},{8,7},{9,8},{10,9},{11,1... | collective-permute-start | bytes 15368 | tf_op jit(solution)/shard_map/ppermute | solution.py:25
  14.7 14.3 %collective-permute-start.3 = (bf16[8,320]{1,0:T(8,128)(2,1)S(1)}, bf16[8,320]{1,0:T(8,128)(2,1)S(1)}, u32[]{:S(2)}, u32[]{:S(2)}) collective-permute-start(bf16[8,320]{1,0:T(8,128)(2,1)S(1)} %get-tuple-element.15), channel_id=1, source_target_pairs={{2,0},{3,1},{4,2},{5,3},{6,4},{7,5},{8,6},{9,7},{10,8},{11,9},{12,... | collective-permute-start | bytes 15368 | tf_op jit(solution)/shard_map/ppermute | solution.py:25
  22.8 6.2 %copy-start.5 = (f32[8,8]{1,0:T(8,128)}, f32[8,8]{1,0:T(8,128)S(1)}, u32[]{:S(2)}) copy-start(f32[8,8]{1,0:T(8,128)S(1)} %multiply_add_fusion) | copy-start | bytes 772
  23.0 8.8 %copy-start.8 = (s32[1024]{0:T(1024)}, s32[1024]{0:T(1024)S(1)}, u32[]{:S(2)}) copy-start(s32[1024]{0:T(1024)S(1)} %pad_clamp_fusion) | copy-start | bytes 12292
  28.9 0.5 copy-start.12
  41.2 5.3 %copy-start.2 = (f32[64,6,16,1,1]{0,2,1,4,3:T(8,128)S(1)}, f32[64,6,16,1,1]{0,2,1,4,3:T(8,128)}, u32[]{:S(2)}) copy-start(f32[64,6,16,1,1]{0,2,1,4,3:T(8,128)} %constant.45) | copy-start | bytes 73732
  52.4 24.5 %copy-start.6 = (f32[8,8]{1,0:T(8,128)S(1)}, f32[8,8]{1,0:T(8,128)}, u32[]{:S(2)}) copy-start(f32[8,8]{1,0:T(8,128)} %copy-done.5) | copy-start | bytes 772
  52.4 24.8 %copy-start.13 = (bf16[129]{0:T(256)(128)(2,1)S(1)}, bf16[129]{0:T(256)(128)(2,1)}, u32[]{:S(2)}) copy-start(bf16[129]{0:T(256)(128)(2,1)} %copy-done.12) | copy-start | bytes 778
  59.6 17.5 %collective-permute-start.4 = (bf16[8,320]{1,0:T(8,128)(2,1)S(1)}, bf16[8,320]{1,0:T(8,128)(2,1)S(1)}, u32[]{:S(2)}, u32[]{:S(2)}) collective-permute-start(bf16[8,320]{1,0:T(8,128)(2,1)S(1)} %get-tuple-element.8), channel_id=1, source_target_pairs={{0,2},{1,3},{2,4},{3,5},{4,6},{5,7},{6,8},{7,9},{8,10},{9,11},{10,... | collective-permute-start | bytes 15368 | tf_op jit(solution)/shard_map/ppermute | solution.py:25
  63.0 14.1 %collective-permute-start.5 = (bf16[8,320]{1,0:T(8,128)(2,1)S(1)}, bf16[8,320]{1,0:T(8,128)(2,1)S(1)}, u32[]{:S(2)}, u32[]{:S(2)}) collective-permute-start(bf16[8,320]{1,0:T(8,128)(2,1)S(1)} %get-tuple-element.10), channel_id=1, source_target_pairs={{0,1},{1,2},{2,3},{3,4},{4,5},{5,6},{6,7},{7,8},{8,9},{9,10},{10,1... | collective-permute-start | bytes 15368 | tf_op jit(solution)/shard_map/ppermute | solution.py:25
  65.0 12.2 %collective-permute-start.6 = (bf16[8,320]{1,0:T(8,128)(2,1)S(1)}, bf16[8,320]{1,0:T(8,128)(2,1)S(1)}, u32[]{:S(2)}, u32[]{:S(2)}) collective-permute-start(bf16[8,320]{1,0:T(8,128)(2,1)S(1)} %get-tuple-element.9), channel_id=1, source_target_pairs={{1,0},{2,1},{3,2},{4,3},{5,4},{6,5},{7,6},{8,7},{9,8},{10,9},{11,1... | collective-permute-start | bytes 15368 | tf_op jit(solution)/shard_map/ppermute | solution.py:25
  69.5 7.6 %collective-permute-start.7 = (bf16[8,320]{1,0:T(8,128)(2,1)S(1)}, bf16[8,320]{1,0:T(8,128)(2,1)S(1)}, u32[]{:S(2)}, u32[]{:S(2)}) collective-permute-start(bf16[8,320]{1,0:T(8,128)(2,1)S(1)} %get-tuple-element.11), channel_id=1, source_target_pairs={{2,0},{3,1},{4,2},{5,3},{6,4},{7,5},{8,6},{9,7},{10,8},{11,9},{12,... | collective-permute-start | bytes 15368 | tf_op jit(solution)/shard_map/ppermute | solution.py:25
  89.0 4.5 %copy-start.3 = (f32[64,6,16,1,1]{0,2,1,4,3:T(8,128)S(1)}, f32[64,6,16,1,1]{0,2,1,4,3:T(8,128)}, u32[]{:S(2)}) copy-start(f32[64,6,16,1,1]{0,2,1,4,3:T(8,128)} %constant.45) | copy-start | bytes 73732
  89.0 5.6 %copy-start.1 = (bf16[4,16,320]{2,1,0:T(8,128)(2,1)S(1)}, bf16[4,16,320]{2,1,0:T(8,128)(2,1)}, u32[]{:S(2)}) copy-start(bf16[4,16,320]{2,1,0:T(8,128)(2,1)} %param.12) | copy-start | bytes 122884
where the time goes:
time: 99.7 us; the launch traced here: 98.7 us
  local copies, waits for them, and re-layouts  41.6 us (42%)
  starting transfers between devices  24.6 us (25%)
  matrix products  20.7 us (21%)
  blocking collectives  9.71 us (10%)
  between operations  1.81 us (2%)
    ppermute x8, starting transfers between devices, passed_along(): return lax.ppermute(block, axis, route)  24.6 us
    reshape x4, local copies, waits for them, and re-layouts, on_device(): face_pool[source_rows].reshape(elem_count, 6, inst_dev, FIELDS, FPTS)  12.1 us
    transpose x2, local copies, waits for them, and re-layouts, on_device(): jnp.einsum('efcdq,efidq->eifcq', flux_blocks, picked, preferred_element_t...  9.76 us
    all_gather x2, blocking collectives, on_device(): lax.all_gather(current, 'inst', axis=0, tiled=True).astype(jnp.float32)  9.71 us
    dot_general x2, matrix products, on_device(): jnp.einsum('efcdq,efidq->eifcq', flux_blocks, picked, preferred_element_t...  9.62 us
    reshape x2, local copies, waits for them, and re-layouts, on_device(): flux_blocks = flux_jacobian.reshape(elem_count, 6, FIELDS, FIELDS, FPTS)  5.87 us
    dot_general x2, matrix products, on_device(): jnp.einsum('iem,emn->ien', current, diagonal_blocks, preferred_element_ty...  5.61 us
    dot_general x2, matrix products, on_device(): jnp.einsum('eifcq,nfq->iecn', normal_flux, lift_table, precision=lax.Prec...  3.11 us
  transfers between devices with their start and end apart: 8, of which 0 were waited for; matrix products, arithmetic and copies ran while one was open for 7% of the time, Pallas kernels for 0%

commit v1 on v0

v1 whole, which is shorter than its diff:
```python
import functools
import math

import jax
import jax.numpy as jnp
import numpy as np
from jax import lax
from jax.experimental import pallas as pl
from jax.experimental.pallas import tpu as pltpu
from jax.sharding import PartitionSpec as P

FIELDS = 5
ORDER = 3
NODES = 64
FPTS = 16
NI = 8
REACH = 2
ITERS = 2


pseudo_step = 0.5
dissipation = 0.25


def gauss_legendre(count):
    points = []
    weights = []
    for i in range(count):
        where = math.cos(math.pi * (i + 0.75) / (count + 0.5))
        for sweep in range(100):
            before = 1.0
            value = where
            for j in range(2, count + 1):
                after = ((2 * j - 1) * where * value - (j - 1) * before) / j
                before = value
                value = after
            slope = count * (where * value - before) / (where * where - 1.0)
            where = where - value / slope
        before = 1.0
        value = where
        for j in range(2, count + 1):
            after = ((2 * j - 1) * where * value - (j - 1) * before) / j
            before = value
            value = after
        slope = count * (where * value - before) / (where * where - 1.0)
        points.append(where)
        weights.append(2.0 / ((1.0 - where * where) * slope * slope))
    return (np.array(points[::-1]), np.array(weights[::-1]))


def lagrange_at(points, where):
    values = np.ones(points.shape[0])
    for i in range(points.shape[0]):
        for j in range(points.shape[0]):
            if j != i:
                values[i] = values[i] * (where - points[j]) / (points[i] - points[j])
    return values


def tables(order, count):
    points, weights = gauss_legendre(order + 1)
    at_minus = lagrange_at(points, -1.0)
    at_plus = lagrange_at(points, 1.0)
    per_side = order + 1
    node_count = per_side**3
    face_points = per_side**2
    trace_table = np.zeros((node_count, 6 * face_points))
    lift_table = np.zeros((node_count, 6 * face_points))
    for k in range(per_side):
        for j in range(per_side):
            for i in range(per_side):
                node = i + per_side * j + per_side * per_side * k
                entries = [
                    (0, at_minus[i], j + per_side * k, weights[i]),
                    (1, at_plus[i], j + per_side * k, weights[i]),
                    (2, at_minus[j], i + per_side * k, weights[j]),
                    (3, at_plus[j], i + per_side * k, weights[j]),
                    (4, at_minus[k], i + per_side * j, weights[k]),
                    (5, at_plus[k], i + per_side * j, weights[k]),
                ]
                for face_index, factor, point, weight in entries:
                    trace_table[node, face_index * face_points + point] = factor
                    lift_table[node, face_index * face_points + point] = factor / weight
    spectral = np.zeros((count, count))
    second = np.zeros((count, count))
    for t in range(count):
        for s in range(count):
            if t != s:
                spectral[t, s] = 0.5 * (-1.0) ** (t - s + 1) / math.tan(math.pi * (t - s) / count)
                second[t, s] = -0.5 * (-1.0) ** (t - s) / math.sin(math.pi * (t - s) / count) ** 2
            else:
                second[t, s] = -(count * count + 2.0) / 12.0
    return (trace_table, lift_table, spectral, second)


LANE = 128
WIDE = FIELDS * NODES
FACES = 6
VMEM_LIMIT = 16 * 1024 * 1024
BF16 = jnp.bfloat16
F32 = jnp.float32
OFFSETS = list(range(-REACH, 0)) + list(range(1, REACH + 1))
SWAP_ORDER = (3, 1, 2, 0)


def wide_tables():
    trace_np, lift_np, spectral_np, second_np = tables(ORDER, NI)
    trace_wide = np.zeros((WIDE, FACES * LANE))
    lift_wide = np.zeros((FACES * LANE, WIDE))
    for c in range(FIELDS):
        rows = slice(c * NODES, (c + 1) * NODES)
        for f in range(FACES):
            cols = slice(f * LANE + c * FPTS, f * LANE + (c + 1) * FPTS)
            face = slice(f * FPTS, (f + 1) * FPTS)
            trace_wide[rows, cols] = trace_np[:, face]
            lift_wide[cols, rows] = lift_np[:, face].T
    return trace_wide, lift_wide, spectral_np[:, 0], second_np[:, 0]


def iotas(shape):
    return [lax.broadcasted_iota(jnp.int32, shape, axis) for axis in range(2)]


def one_hot(mask):
    return jnp.where(mask, 1.0, 0.0).astype(BF16)


def spread_table():
    row, col = iotas((LANE, FIELDS * LANE))
    inside = col % LANE < FIELDS * FPTS
    return one_hot(inside & (row == col // LANE * FPTS + col % FPTS))


def order_table():
    row, col = iotas((FIELDS * FIELDS * FPTS, FIELDS * LANE))
    place = col % LANE
    source = place // FPTS * FIELDS * FPTS + col // LANE * FPTS + col % FPTS
    return one_hot((place < FIELDS * FPTS) & (row == source))


def trace_pool(state, trace_wide, insts, elems):
    wide = jnp.dot(state, trace_wide, preferred_element_type=F32).astype(BF16)
    by_inst = []
    for t in range(insts):
        rows = wide[t * elems : (t + 1) * elems]
        by_inst.append(
            jnp.concatenate([rows[:, f * LANE : (f + 1) * LANE] for f in range(FACES)], 0)
        )
    return jnp.concatenate(by_inst, 1)


def swap_routes(ranks, parts):
    near = [[(p, p + 1) for p in range(first, parts - 1, 2)] for first in range(2)]
    far = [
        [(p + i, p + i + 2) for p in range(first, parts - 3, 4) for i in range(2)]
        for first in (0, 2)
    ]
    routes = []
    for pairs in near + far:
        met = {p for pair in pairs for p in pair}
        alone = [p for p in range(parts) if p not in met]
        swaps = [(r * parts + p, r * parts + q) for r in range(ranks) for p, q in pairs]
        swaps += [(r * parts + p, (r ^ 1) * parts + p) for r in range(0, ranks, 2) for p in alone]
        routes.append(swaps + [(q, p) for p, q in swaps])
    return routes


def by_swap(place, by_offset):
    two_down, one_down, one_up, two_up = by_offset
    even = place % 2 == 0
    low = place // 2 % 2 == 0
    return [
        jnp.where(even, one_up, one_down),
        jnp.where(even, one_down, one_up),
        jnp.where(low, two_up, two_down),
        jnp.where(low, two_down, two_up),
    ]


def by_offset(place, blocks):
    even = place % 2 == 0
    low = place // 2 % 2 == 0
    return [
        jnp.where(low, blocks[3], blocks[2]),
        jnp.where(even, blocks[1], blocks[0]),
        jnp.where(even, blocks[0], blocks[1]),
        jnp.where(low, blocks[2], blocks[3]),
    ]


def fill_outgoing(pool, send, out_refs, place, elems):
    slots, capacity = send.shape
    rows, cols = iotas((FACES * elems, slots * capacity))
    ids = FACES * (rows % elems) + rows // elems
    wanted = jnp.concatenate([send[k : k + 1] for k in range(slots)], 1)
    out = lax.dot_general(
        one_hot(ids == wanted), pool, (((0,), (0,)), ((), ())), preferred_element_type=F32
    )
    blocks = by_swap(place, [out[k * capacity : (k + 1) * capacity] for k in range(slots)])
    for block, ref in zip(blocks, out_refs):
        ref[...] = block.astype(BF16)


def diagonal(states, diag, wide_ref, prod_ref, insts, elems):
    tall = insts * elems
    width = diag.shape[1]
    cuts = [(j, j * LANE, min((j + 1) * LANE, width)) for j in range(pl.cdiv(width, LANE))]
    for t in range(insts):
        rows = states[t].astype(F32)
        for j, low, high in cuts:
            first = j * tall + t * elems
            wide_ref[first : first + elems, 0 : high - low] = rows[:, low:high]
    for e in range(elems):
        rows = jnp.concatenate(
            [wide_ref[pl.ds(j * tall + e, insts, stride=elems), :] for j, low, high in cuts], 1
        )
        product = jnp.dot(rows[:, 0:width].astype(BF16), diag[e], preferred_element_type=F32)
        for j, low, high in cuts:
            chunk = product[:, low:high]
            if high - low < LANE:
                chunk = jnp.concatenate([chunk, jnp.zeros((insts, LANE - high + low), F32)], 1)
            prod_ref[pl.ds(j * tall + e, insts, stride=elems), :] = chunk
    return [
        jnp.concatenate(
            [
                prod_ref[j * tall + t * elems : j * tall + (t + 1) * elems, 0 : high - low]
                for j, low, high in cuts
            ],
            1,
        )
        for t in range(insts)
    ]


def flux_order(rows, order):
    per_face = FIELDS * FIELDS * FPTS
    by_face = jnp.concatenate(
        [rows[:, f * per_face : (f + 1) * per_face] for f in range(FACES)], 0
    )
    return jnp.dot(by_face, order, preferred_element_type=F32).astype(BF16)


def source_table(sources, elems, slots):
    faces = FACES * elems
    columns = lax.broadcasted_iota(jnp.int32, (elems, faces + slots), 1)
    ids = jnp.where(columns < faces, FACES * (columns % elems) + columns // elems, columns)
    hot = [jnp.where(sources[:, f : f + 1] == ids, 1.0, 0.0) for f in range(FACES)]
    return jnp.concatenate(hot, 0).astype(BF16)


def table_kernel(spread_ref, order_ref):
    spread_ref[...] = spread_table()
    order_ref[...] = order_table()


def first_kernel(place_ref, order_ref, state_ref, trace_ref, send_ref, flux_ref, source_ref,
                 flux_out_ref, hot_ref, pool_ref, *out_refs):
    insts, elems, width = state_ref.shape
    state = state_ref[...].reshape(insts * elems, width)
    pool = trace_pool(state, trace_ref[...], insts, elems)
    pool_ref[...] = pool
    fill_outgoing(pool, send_ref[0], out_refs, place_ref[0], elems)
    hot_ref[...] = source_table(source_ref[...].T, elems, send_ref.shape[1] * send_ref.shape[2])
    flux_out_ref[...] = flux_order(flux_ref[...], order_ref[...])


def base_kernel(state_ref, diag_ref, forcing_ref, base_ref, wide_ref, prod_ref):
    insts, elems, width = state_ref.shape
    states = [state_ref[t] for t in range(insts)]
    products = diagonal(states, diag_ref, wide_ref, prod_ref, insts, elems)
    for t in range(insts):
        base_ref[t] = products[t] - forcing_ref[t].astype(F32)


def step_kernel(parts, ranks, last, spectral, second, *refs):
    place_ref, freq_ref, spread_ref = refs[:3]
    got_refs = {swap: refs[3 + i] for i, swap in enumerate(SWAP_ORDER)}
    got_refs = [got_refs[swap] for swap in range(len(OFFSETS))]
    refs = refs[3 + len(OFFSETS) :]
    states = refs[:ranks]
    pool_ref, refs = refs[ranks], refs[ranks + 1 :]
    base_ref, hot_ref, flux_ref, lift_ref = refs[:4]
    if last:
        final_ref, residual_ref = refs[4:]
    else:
        trace_ref, send_ref, next_ref, next_pool_ref = refs[4:8]
        out_refs = refs[8:]
    insts, elems, width = states[0].shape
    place = place_ref[0]
    faces = FACES * elems

    freq = freq_ref[...]
    entries = [freq * float(spectral[d]) - dissipation * float(second[d]) for d in range(NI)]

    arrived = by_offset(place, [ref[...].astype(F32) for ref in got_refs])
    for k, offset in enumerate(OFFSETS):
        exists = (place + offset >= 0) & (place + offset < parts)
        arrived[k] = jnp.where(exists, arrived[k], jnp.zeros_like(arrived[k]))
    pool = jnp.concatenate([pool_ref[...], jnp.concatenate(arrived, 0).astype(BF16)], 0)
    picked = jnp.dot(hot_ref[...], pool, preferred_element_type=F32).astype(BF16)
    stacked = jnp.concatenate([picked[:, t * LANE : (t + 1) * LANE] for t in range(insts)], 0)
    wide = jnp.dot(stacked, spread_ref[...], preferred_element_type=F32)

    flux = flux_ref[...].astype(F32)
    normal = []
    for t in range(insts):
        rows = wide[t * faces : (t + 1) * faces]
        summed = flux[:, 0:LANE] * rows[:, 0:LANE]
        for d in range(1, FIELDS):
            summed += flux[:, d * LANE : (d + 1) * LANE] * rows[:, d * LANE : (d + 1) * LANE]
        summed = summed.astype(BF16)
        normal.append(
            jnp.concatenate([summed[f * elems : (f + 1) * elems] for f in range(FACES)], 1)
        )
    lifted = jnp.dot(jnp.concatenate(normal, 0), lift_ref[...], preferred_element_type=F32)

    fresh = []
    for t in range(insts):
        summed = jnp.zeros((elems, width), F32)
        for rank in range(ranks):
            for s in range(insts):
                summed += entries[(t - s - rank * insts) % NI] * states[rank][s].astype(F32)
        residual = (
            base_ref[t] + lifted[t * elems : (t + 1) * elems] + summed.astype(BF16).astype(F32)
        )
        moved = (states[0][t].astype(F32) - pseudo_step * residual).astype(BF16)
        if last:
            final_ref[t] = moved
            residual_ref[t] = residual
        else:
            next_ref[t] = moved
            fresh.append(moved)
    if not last:
        pool = trace_pool(jnp.concatenate(fresh, 0), trace_ref[...], insts, elems)
        next_pool_ref[...] = pool
        fill_outgoing(pool, send_ref[0], out_refs, place, elems)


def on_device(
    initial_state, forcing, diagonal_blocks, flux_jacobian, send_list, source_index, frequency
):
    insts, elems, width = initial_state.shape
    parts = lax.axis_size("dom")
    ranks = lax.axis_size("inst")
    slots, capacity = send_list.shape[1:]
    faces = FACES * elems
    trace_np, lift_np, spectral, second = wide_tables()
    trace_wide = jnp.asarray(trace_np, BF16)
    lift_wide = jnp.asarray(lift_np, BF16)
    place = lax.axis_index("dom").reshape(1)
    sources = source_index.T
    routes = swap_routes(ranks, parts)

    smem = pl.BlockSpec(memory_space=pltpu.SMEM)
    vmem = pl.BlockSpec(memory_space=pltpu.VMEM)
    params = pltpu.CompilerParams(vmem_limit_bytes=VMEM_LIMIT)

    def like(array):
        return jax.ShapeDtypeStruct(array.shape, array.dtype)

    wide_shape = jax.ShapeDtypeStruct(initial_state.shape, F32)
    pool_shape = jax.ShapeDtypeStruct((faces, insts * LANE), BF16)
    out_shapes = [jax.ShapeDtypeStruct((capacity, insts * LANE), BF16)] * slots
    flux_shape = jax.ShapeDtypeStruct((faces, FIELDS * LANE), BF16)
    hot_shape = jax.ShapeDtypeStruct((faces, faces + slots * capacity), BF16)

    def exchange(state, outgoing):
        got = [lax.ppermute(outgoing[swap], ("inst", "dom"), routes[swap]) for swap in SWAP_ORDER]
        states = [state]
        for rank in range(1, ranks):
            route = [((i + rank) % ranks, i) for i in range(ranks)]
            states.append(lax.ppermute(state, "inst", route))
        return states, got

    def own_terms(state, diag, force):
        return pl.pallas_call(
            base_kernel,
            out_shape=wide_shape,
            in_specs=[vmem] * 3,
            out_specs=vmem,
            scratch_shapes=[pltpu.VMEM((pl.cdiv(width, LANE) * insts * elems, LANE), F32)] * 2,
            compiler_params=params,
            cost_estimate=pl.CostEstimate(
                flops=2 * insts * diagonal_blocks.size,
                bytes_accessed=2 * diagonal_blocks.size,
                transcendentals=0,
            ),
            name="own_terms",
        )(state, diag, force)

    freq = frequency.reshape(1, 1)
    spread, order = pl.pallas_call(
        table_kernel,
        out_shape=[
            jax.ShapeDtypeStruct((LANE, FIELDS * LANE), BF16),
            jax.ShapeDtypeStruct((FIELDS * FIELDS * FPTS, FIELDS * LANE), BF16),
        ],
        out_specs=[vmem] * 2,
        compiler_params=params,
        cost_estimate=pl.CostEstimate(flops=10**10, bytes_accessed=10**6, transcendentals=0),
        name="tables",
    )()
    flux, hot, pool, *outgoing = pl.pallas_call(
        first_kernel,
        out_shape=[flux_shape, hot_shape, pool_shape] + out_shapes,
        in_specs=[smem] + [vmem] * 6,
        out_specs=[vmem] * (3 + len(out_shapes)),
        compiler_params=params,
        cost_estimate=pl.CostEstimate(flops=10**10, bytes_accessed=10**6, transcendentals=0),
        name="first_traces",
    )(place, order, initial_state, trace_wide, send_list, flux_jacobian, sources)
    state, trace, send = initial_state, trace_wide, send_list
    force, lift, diag = forcing, lift_wide, diagonal_blocks
    states, got = exchange(state, outgoing)
    base = own_terms(state, diag, force)
    state, pool, *outgoing = pl.pallas_call(
        functools.partial(step_kernel, parts, ranks, False, spectral, second),
        out_shape=[like(initial_state), pool_shape] + out_shapes,
        in_specs=[smem] + [vmem] * (ranks + slots + 9),
        out_specs=[vmem] * (2 + len(out_shapes)),
        compiler_params=params,
        name="first_step",
    )(place, freq, spread, *got, *states, pool, base, hot, flux, lift, trace, send)
    states, got = exchange(state, outgoing)
    base = own_terms(state, diag, force)
    return pl.pallas_call(
        functools.partial(step_kernel, parts, ranks, True, spectral, second),
        out_shape=[like(initial_state), wide_shape],
        in_specs=[smem] + [vmem] * (ranks + slots + 7),
        out_specs=[vmem] * 2,
        compiler_params=params,
        name="last_step",
    )(place, freq, spread, *got, *states, pool, base, hot, flux, lift)


def solution(mesh):
    return jax.shard_map(
        on_device,
        mesh=mesh,
        in_specs=(
            P("inst", "dom", None),
            P("inst", "dom", None),
            P("dom", None, None),
            P("dom", None),
            P("dom", None, None),
            P("dom", None),
            P(),
        ),
        out_specs=(P("inst", "dom", None), P("inst", "dom", None)),
        check_vma=False,
    )
```

time: 99.7 us -> 19.6 us (0.20)
  the two profiles are of different devices: /device:TPU:8 before, /device:TPU:0 now
where the time goes in v1:
time: 19.6 us; the launch traced here: 19.4 us
  starting transfers between devices  11.7 us (60%)
  Pallas kernels  4.17 us (21%)
  between operations  1.4 us (7%)
  waiting for transfers between devices  1.24 us (6%)
  local copies, waits for them, and re-layouts  0.88 us (4%)
    ppermute x8, starting transfers between devices, exchange(): lax.ppermute(outgoing[swap], ('inst', 'dom'), routes[swap])  8.15 us
    ppermute x2, starting transfers between devices, exchange(): states.append(lax.ppermute(state, 'inst', route))  3.6 us
    pallas_call x2, Pallas kernels, own_terms(): pl.pallas_call(base_kernel, out_shape=wide_shape, in_specs=[vmem] * 3, ou...  1.33 us
    pallas_call x1, Pallas kernels, on_device(): pl.pallas_call(functools.partial(step_kernel, parts, ranks, True, spectra...  1.27 us
    ppermute x8, waiting for transfers between devices, exchange(): lax.ppermute(outgoing[swap], ('inst', 'dom'), routes[swap])  1.23 us
    pallas_call x1, Pallas kernels, on_device(): pl.pallas_call(functools.partial(step_kernel, parts, ranks, False, spectr...  0.94 us
    unnamed x16, local copies, waits for them, and re-layouts  0.88 us
    pallas_call x1, Pallas kernels, on_device(): pl.pallas_call(first_kernel, out_shape=[flux_shape, hot_shape, pool_shape...  0.46 us
  transfers between devices with their start and end apart: 10, of which 2 were waited for; matrix products, arithmetic and copies ran while one was open for 0% of the time, Pallas kernels for 10%

profile of v1, /device:TPU:0, one launch (start us, length us, event | category | flops | bytes accessed | tf_op | source)
XLA Modules:
  0.0 19.4 jit_solution(14799546242269982320)
XLA Ops:
  0.6 3.0 %collective-permute-start.4 = (bf16[4,16,320]{2,1,0:T(8,128)(2,1)}, bf16[4,16,320]{2,1,0:T(8,128)(2,1)S(1)}, u32[]{:S(2)}, u32[]{:S(2)}) collective-permute-start(bf16[4,16,320]{2,1,0:T(8,128)(2,1)} %refs_7_.1), channel_id=1, source_target_pairs={{16,0},{0,16},{17,1},{1,17},{18,2},{2,18},{19,3},{3,19},{20,4},{4,... | collective-permute-start | bytes 122888 | tf_op jit(solution)/shard_map/ppermute | solution.py:372
  3.7 0.2 tables.1
  3.8 0.8 %copy-done.2 = bf16[320,768]{1,0:T(8,128)(2,1)S(1)} copy-done((bf16[320,768]{1,0:T(8,128)(2,1)S(1)}, bf16[320,768]{1,0:T(8,128)(2,1)}, u32[]{:S(2)}) %copy-start.2) | copy-done | bytes 491544
  4.7 0.0 copy-done.4
  4.7 0.0 copy-done.6
  4.7 0.5 %first_traces.1 = (bf16[96,640]{1,0:T(8,128)(2,1)S(1)}, bf16[96,128]{1,0:T(8,128)(2,1)S(1)}, bf16[96,512]{1,0:T(8,128)(2,1)S(1)}, bf16[8,512]{1,0:T(8,128)(2,1)S...) custom-call(s32[1]{0:T(128)} %bitcast.place_ref.refs_0_, ...), custom_call_target="tpu_custom_call" | custom-call | flops 10000000000 | bytes 1000000 | tf_op jit(solution)/shard_map/first_traces/pallas_call | solution.py:403
  5.2 0.0 copy-start.1
  5.2 0.1 collective-permute-start
  5.3 2.0 %collective-permute-start.1 = (bf16[8,512]{1,0:T(8,128)(2,1)S(1)}, bf16[8,512]{1,0:T(8,128)(2,1)S(1)}, u32[]{:S(2)}, u32[]{:S(2)}) collective-permute-start(bf16[8,512]{1,0:T(8,128)(2,1)S(1)} %get-tuple-element.20), channel_id=1, source_target_pairs={{1,2},{3,4},{5,6},{7,8},{9,10},{11,12},{13,14},{17,18},{19,20},{21... | collective-permute-start | bytes 24584 | tf_op jit(solution)/shard_map/ppermute | solution.py:368
  7.3 1.0 %collective-permute-start.2 = (bf16[8,512]{1,0:T(8,128)(2,1)S(1)}, bf16[8,512]{1,0:T(8,128)(2,1)S(1)}, u32[]{:S(2)}, u32[]{:S(2)}) collective-permute-start(bf16[8,512]{1,0:T(8,128)(2,1)S(1)} %get-tuple-element.21), channel_id=1, source_target_pairs={{0,2},{1,3},{4,6},{5,7},{8,10},{9,11},{12,14},{13,15},{16,18},{17,... | collective-permute-start | bytes 24584 | tf_op jit(solution)/shard_map/ppermute | solution.py:368
  8.3 1.2 %collective-permute-start.3 = (bf16[8,512]{1,0:T(8,128)(2,1)S(1)}, bf16[8,512]{1,0:T(8,128)(2,1)S(1)}, u32[]{:S(2)}, u32[]{:S(2)}) collective-permute-start(bf16[8,512]{1,0:T(8,128)(2,1)S(1)} %get-tuple-element.22), channel_id=1, source_target_pairs={{0,1},{2,3},{4,5},{6,7},{8,9},{10,11},{12,13},{14,15},{16,17},{18,... | collective-permute-start | bytes 24584 | tf_op jit(solution)/shard_map/ppermute | solution.py:368
  10.2 0.0 copy-done
  10.2 0.0 copy-done.3
  10.2 0.7 %own_terms.2.refs_10_ = f32[4,16,320]{2,1,0:T(8,128)S(1)} custom-call(bf16[4,16,320]{2,1,0:T(8,128)(2,1)S(1)} %copy-done.4, bf16[16,320,320]{2,1,0:T(8,128)(2,1)S(1)} %copy-done, bf16[4,16,320]{2,1,0:T(8,128)(2,1)S(1)} %copy-done.3), custom_call_target="tpu_custom_call" | custom-call | flops 13107200 | bytes 3276800 | tf_op jit(solution)/shard_map/own_terms/pallas_call | solution.py:376
  10.9 0.0 collective-permute-done.refs_3_
  10.9 0.0 collective-permute-done.1.refs_4_
  10.9 0.0 collective-permute-done.2.refs_5_
  10.9 0.0 collective-permute-done.3.refs_6_
  10.9 0.0 collective-permute-done.4.refs_8_
  10.9 0.9 %first_step.1 = (bf16[4,16,320]{2,1,0:T(8,128)(2,1)S(1)}, bf16[96,512]{1,0:T(8,128)(2,1)S(1)}, bf16[8,512]{1,0:T(8,128)(2,1)S(1)}, bf16[8,512]{1,0:T(8,128)(2,1)...) custom-call(s32[1]{0:T(128)} %bitcast.place_ref.refs_0_, f32[1,1]{1,0:T(1,128)} %bitcast.3.refs_1_, ...), custom_call_target="tpu_custom_call" | custom-call | tf_op jit(solution)/shard_map/first_step/pallas_call | solution.py:416
  11.9 0.6 %collective-permute-start.9 = (bf16[4,16,320]{2,1,0:T(8,128)(2,1)S(1)}, bf16[4,16,320]{2,1,0:T(8,128)(2,1)S(1)}, u32[]{:S(2)}, u32[]{:S(2)}) collective-permute-start(bf16[4,16,320]{2,1,0:T(8,128)(2,1)S(1)} %get-tuple-element.30.state_ref.refs_7_), channel_id=1, source_target_pairs={{16,0},{0,16},{17,1},{1,17},{18,2},{2,18},{19,3},{3,19},{20,4},{4,... | collective-permute-start | bytes 122888 | tf_op jit(solution)/shard_map/ppermute | solution.py:372
  12.5 1.5 %collective-permute-start.5 = (bf16[8,512]{1,0:T(8,128)(2,1)S(1)}, bf16[8,512]{1,0:T(8,128)(2,1)S(1)}, u32[]{:S(2)}, u32[]{:S(2)}) collective-permute-start(bf16[8,512]{1,0:T(8,128)(2,1)S(1)} %get-tuple-element.26), channel_id=1, source_target_pairs={{2,4},{3,5},{6,8},{7,9},{10,12},{11,13},{18,20},{19,21},{22,24},{2... | collective-permute-start | bytes 24584 | tf_op jit(solution)/shard_map/ppermute | solution.py:368
  14.0 0.5 %collective-permute-start.6 = (bf16[8,512]{1,0:T(8,128)(2,1)S(1)}, bf16[8,512]{1,0:T(8,128)(2,1)S(1)}, u32[]{:S(2)}, u32[]{:S(2)}) collective-permute-start(bf16[8,512]{1,0:T(8,128)(2,1)S(1)} %get-tuple-element.27), channel_id=1, source_target_pairs={{1,2},{3,4},{5,6},{7,8},{9,10},{11,12},{13,14},{17,18},{19,20},{21... | collective-permute-start | bytes 24584 | tf_op jit(solution)/shard_map/ppermute | solution.py:368
  14.5 1.0 %collective-permute-start.7 = (bf16[8,512]{1,0:T(8,128)(2,1)S(1)}, bf16[8,512]{1,0:T(8,128)(2,1)S(1)}, u32[]{:S(2)}, u32[]{:S(2)}) collective-permute-start(bf16[8,512]{1,0:T(8,128)(2,1)S(1)} %get-tuple-element.28), channel_id=1, source_target_pairs={{0,2},{1,3},{4,6},{5,7},{8,10},{9,11},{12,14},{13,15},{16,18},{17,... | collective-permute-start | bytes 24584 | tf_op jit(solution)/shard_map/ppermute | solution.py:368
  15.6 0.7 %collective-permute-start.8 = (bf16[8,512]{1,0:T(8,128)(2,1)S(1)}, bf16[8,512]{1,0:T(8,128)(2,1)S(1)}, u32[]{:S(2)}, u32[]{:S(2)}) collective-permute-start(bf16[8,512]{1,0:T(8,128)(2,1)S(1)} %get-tuple-element.29), channel_id=1, source_target_pairs={{0,1},{2,3},{4,5},{6,7},{8,9},{10,11},{12,13},{14,15},{16,17},{18,... | collective-permute-start | bytes 24584 | tf_op jit(solution)/shard_map/ppermute | solution.py:368
  16.3 0.7 %own_terms.3.refs_10_ = f32[4,16,320]{2,1,0:T(8,128)S(1)} custom-call(bf16[4,16,320]{2,1,0:T(8,128)(2,1)S(1)} %get-tuple-element.30.state_ref.refs_7_, bf16[16,320,320]{2,1,0:T(8,128)(2,1)S(1)} %copy-done, bf16[4,16,320]{2,1,0:T(8,128)(2,1)S(1)} %copy-done.3), custom_call_target="tpu_custom_call" | custom-call | flops 13107200 | bytes 3276800 | tf_op jit(solution)/shard_map/own_terms/pallas_call | solution.py:376
  17.0 0.0 collective-permute-done.5.refs_3_
  17.0 0.7 %collective-permute-done.6.refs_4_ = bf16[8,512]{1,0:T(8,128)(2,1)S(1)} collective-permute-done((bf16[8,512]{1,0:T(8,128)(2,1)S(1)}, bf16[8,512]{1,0:T(8,128)(2,1)S(1)}, u32[]{:S(2)}, u32[]{:S(2)}) %collective-permute-start.6) | collective-permute-done | bytes 8224 | tf_op jit(solution)/shard_map/ppermute | solution.py:368
  17.6 0.5 %collective-permute-done.7.refs_5_ = bf16[8,512]{1,0:T(8,128)(2,1)S(1)} collective-permute-done((bf16[8,512]{1,0:T(8,128)(2,1)S(1)}, bf16[8,512]{1,0:T(8,128)(2,1)S(1)}, u32[]{:S(2)}, u32[]{:S(2)}) %collective-permute-start.7) | collective-permute-done | bytes 8224 | tf_op jit(solution)/shard_map/ppermute | solution.py:368
  18.2 0.0 collective-permute-done.8.refs_6_
  18.2 0.0 collective-permute-done.9.refs_8_
  18.2 1.3 %last_step.1 = (bf16[4,16,320]{2,1,0:T(8,128)(2,1)}, f32[4,16,320]{2,1,0:T(8,128)}) custom-call(s32[1]{0:T(128)} %bitcast.place_ref.refs_0_, f32[1,1]{1,0:T(1,128)} %bitcast.4.refs_1_, bf16[128,640]{1,0:T(8,128)(2,1)S(1)} %get-tuple-element.17.refs_2_, bf16[8,512]{1,0:T(8,128)(2,1)S(1)} %collective-permute-done.5.refs_3_, ...), custom_call_target="tpu_custom_call" | custom-call | tf_op jit(solution)/shard_map/last_step/pallas_call | solution.py:426
  (10 shorter events, 0.0 us)
Async XLA Ops:
  0.6 10.3 %collective-permute-start.4 = (bf16[4,16,320]{2,1,0:T(8,128)(2,1)}, bf16[4,16,320]{2,1,0:T(8,128)(2,1)S(1)}, u32[]{:S(2)}, u32[]{:S(2)}) collective-permute-start(bf16[4,16,320]{2,1,0:T(8,128)(2,1)} %refs_7_.1), channel_id=1, source_target_pairs={{16,0},{0,16},{17,1},{1,17},{18,2},{2,18},{19,3},{3,19},{20,4},{4,... | collective-permute-start | bytes 122888 | tf_op jit(solution)/shard_map/ppermute | solution.py:372
  3.6 1.0 %copy-start.2 = (bf16[320,768]{1,0:T(8,128)(2,1)S(1)}, bf16[320,768]{1,0:T(8,128)(2,1)}, u32[]{:S(2)}) copy-start(bf16[320,768]{1,0:T(8,128)(2,1)} %constant.8.clone.trace_ref.refs_14_) | copy-start | bytes 1474564
  3.6 1.0 %copy-start.4 = (bf16[4,16,320]{2,1,0:T(8,128)(2,1)S(1)}, bf16[4,16,320]{2,1,0:T(8,128)(2,1)}, u32[]{:S(2)}) copy-start(bf16[4,16,320]{2,1,0:T(8,128)(2,1)} %refs_7_.1) | copy-start | bytes 122884
  3.6 1.0 %copy-start.5 = (s32[1,4,8]{2,1,0:T(4,128)S(1)}, s32[1,4,8]{2,1,0:T(4,128)}, u32[]{:S(2)}) copy-start(s32[1,4,8]{2,1,0:T(4,128)} %refs_15_.1) | copy-start | bytes 388
  3.6 1.1 %copy-start.6 = (bf16[16,2400]{1,0:T(8,128)(2,1)S(1)}, bf16[16,2400]{1,0:T(8,128)(2,1)}, u32[]{:S(2)}) copy-start(bf16[16,2400]{1,0:T(8,128)(2,1)} %flux_ref.1) | copy-start | bytes 230404
  3.6 1.1 %copy-start.7 = (s32[16,6]{0,1:T(8,128)S(1)}, s32[16,6]{0,1:T(8,128)}, u32[]{:S(2)}) copy-start(s32[16,6]{0,1:T(8,128)} %param.14) | copy-start | bytes 1156
  4.7 5.5 %copy-start = (bf16[16,320,320]{2,1,0:T(8,128)(2,1)S(1)}, bf16[16,320,320]{2,1,0:T(8,128)(2,1)}, u32[]{:S(2)}) copy-start(bf16[16,320,320]{2,1,0:T(8,128)(2,1)} %diag_ref.3) | copy-start | bytes 9830404
  4.7 5.5 %copy-start.3 = (bf16[4,16,320]{2,1,0:T(8,128)(2,1)S(1)}, bf16[4,16,320]{2,1,0:T(8,128)(2,1)}, u32[]{:S(2)}) copy-start(bf16[4,16,320]{2,1,0:T(8,128)(2,1)} %forcing_ref.3) | copy-start | bytes 122884
  5.2 5.8 %copy-start.1 = (bf16[768,320]{1,0:T(8,128)(2,1)S(1)}, bf16[768,320]{1,0:T(8,128)(2,1)}, u32[]{:S(2)}) copy-start(bf16[768,320]{1,0:T(8,128)(2,1)} %constant.9.clone.refs_13_) | copy-start | bytes 1474564
  5.2 5.7 %collective-permute-start = (bf16[8,512]{1,0:T(8,128)(2,1)S(1)}, bf16[8,512]{1,0:T(8,128)(2,1)S(1)}, u32[]{:S(2)}, u32[]{:S(2)}) collective-permute-start(bf16[8,512]{1,0:T(8,128)(2,1)S(1)} %get-tuple-element.19), channel_id=1, source_target_pairs={{2,4},{3,5},{6,8},{7,9},{10,12},{11,13},{18,20},{19,21},{22,24},{2... | collective-permute-start | bytes 24584 | tf_op jit(solution)/shard_map/ppermute | solution.py:368
  5.3 5.6 %collective-permute-start.1 = (bf16[8,512]{1,0:T(8,128)(2,1)S(1)}, bf16[8,512]{1,0:T(8,128)(2,1)S(1)}, u32[]{:S(2)}, u32[]{:S(2)}) collective-permute-start(bf16[8,512]{1,0:T(8,128)(2,1)S(1)} %get-tuple-element.20), channel_id=1, source_target_pairs={{1,2},{3,4},{5,6},{7,8},{9,10},{11,12},{13,14},{17,18},{19,20},{21... | collective-permute-start | bytes 24584 | tf_op jit(solution)/shard_map/ppermute | solution.py:368
  7.3 3.7 %collective-permute-start.2 = (bf16[8,512]{1,0:T(8,128)(2,1)S(1)}, bf16[8,512]{1,0:T(8,128)(2,1)S(1)}, u32[]{:S(2)}, u32[]{:S(2)}) collective-permute-start(bf16[8,512]{1,0:T(8,128)(2,1)S(1)} %get-tuple-element.21), channel_id=1, source_target_pairs={{0,2},{1,3},{4,6},{5,7},{8,10},{9,11},{12,14},{13,15},{16,18},{17,... | collective-permute-start | bytes 24584 | tf_op jit(solution)/shard_map/ppermute | solution.py:368
  8.3 2.6 %collective-permute-start.3 = (bf16[8,512]{1,0:T(8,128)(2,1)S(1)}, bf16[8,512]{1,0:T(8,128)(2,1)S(1)}, u32[]{:S(2)}, u32[]{:S(2)}) collective-permute-start(bf16[8,512]{1,0:T(8,128)(2,1)S(1)} %get-tuple-element.22), channel_id=1, source_target_pairs={{0,1},{2,3},{4,5},{6,7},{8,9},{10,11},{12,13},{14,15},{16,17},{18,... | collective-permute-start | bytes 24584 | tf_op jit(solution)/shard_map/ppermute | solution.py:368
  11.9 6.3 %collective-permute-start.9 = (bf16[4,16,320]{2,1,0:T(8,128)(2,1)S(1)}, bf16[4,16,320]{2,1,0:T(8,128)(2,1)S(1)}, u32[]{:S(2)}, u32[]{:S(2)}) collective-permute-start(bf16[4,16,320]{2,1,0:T(8,128)(2,1)S(1)} %get-tuple-element.30.state_ref.refs_7_), channel_id=1, source_target_pairs={{16,0},{0,16},{17,1},{1,17},{18,2},{2,18},{19,3},{3,19},{20,4},{4,... | collective-permute-start | bytes 122888 | tf_op jit(solution)/shard_map/ppermute | solution.py:372
  12.5 4.5 %collective-permute-start.5 = (bf16[8,512]{1,0:T(8,128)(2,1)S(1)}, bf16[8,512]{1,0:T(8,128)(2,1)S(1)}, u32[]{:S(2)}, u32[]{:S(2)}) collective-permute-start(bf16[8,512]{1,0:T(8,128)(2,1)S(1)} %get-tuple-element.26), channel_id=1, source_target_pairs={{2,4},{3,5},{6,8},{7,9},{10,12},{11,13},{18,20},{19,21},{22,24},{2... | collective-permute-start | bytes 24584 | tf_op jit(solution)/shard_map/ppermute | solution.py:368
  14.0 3.7 %collective-permute-start.6 = (bf16[8,512]{1,0:T(8,128)(2,1)S(1)}, bf16[8,512]{1,0:T(8,128)(2,1)S(1)}, u32[]{:S(2)}, u32[]{:S(2)}) collective-permute-start(bf16[8,512]{1,0:T(8,128)(2,1)S(1)} %get-tuple-element.27), channel_id=1, source_target_pairs={{1,2},{3,4},{5,6},{7,8},{9,10},{11,12},{13,14},{17,18},{19,20},{21... | collective-permute-start | bytes 24584 | tf_op jit(solution)/shard_map/ppermute | solution.py:368
  14.5 3.7 %collective-permute-start.7 = (bf16[8,512]{1,0:T(8,128)(2,1)S(1)}, bf16[8,512]{1,0:T(8,128)(2,1)S(1)}, u32[]{:S(2)}, u32[]{:S(2)}) collective-permute-start(bf16[8,512]{1,0:T(8,128)(2,1)S(1)} %get-tuple-element.28), channel_id=1, source_target_pairs={{0,2},{1,3},{4,6},{5,7},{8,10},{9,11},{12,14},{13,15},{16,18},{17,... | collective-permute-start | bytes 24584 | tf_op jit(solution)/shard_map/ppermute | solution.py:368
  15.6 2.6 %collective-permute-start.8 = (bf16[8,512]{1,0:T(8,128)(2,1)S(1)}, bf16[8,512]{1,0:T(8,128)(2,1)S(1)}, u32[]{:S(2)}, u32[]{:S(2)}) collective-permute-start(bf16[8,512]{1,0:T(8,128)(2,1)S(1)} %get-tuple-element.29), channel_id=1, source_target_pairs={{0,1},{2,3},{4,5},{6,7},{8,9},{10,11},{12,13},{14,15},{16,17},{18,... | collective-permute-start | bytes 24584 | tf_op jit(solution)/shard_map/ppermute | solution.py:368

commit v2 on v1

--- a/solution.py
+++ b/solution.py
@@ -253,8 +253,8 @@
     order_ref[...] = order_table()
 
 
-def first_kernel(place_ref, order_ref, state_ref, trace_ref, send_ref, flux_ref, source_ref,
-                 flux_out_ref, hot_ref, pool_ref, *out_refs):
+def first_kernel(spectral, second, place_ref, freq_ref, order_ref, state_ref, trace_ref, send_ref, flux_ref, source_ref,
+                 flux_out_ref, hot_ref, entry_ref, pool_ref, *out_refs):
     insts, elems, width = state_ref.shape
     state = state_ref[...].reshape(insts * elems, width)
     pool = trace_pool(state, trace_ref[...], insts, elems)
@@ -262,6 +262,10 @@
     fill_outgoing(pool, send_ref[0], out_refs, place_ref[0], elems)
     hot_ref[...] = source_table(source_ref[...].T, elems, send_ref.shape[1] * send_ref.shape[2])
     flux_out_ref[...] = flux_order(flux_ref[...], order_ref[...])
+    freq = freq_ref[0]
+    for d in range(NI):
+        entry = freq * float(spectral[d]) - dissipation * float(second[d])
+        entry_ref[d : d + 1, :] = jnp.full((1, width), entry, F32)
 
 
 def base_kernel(state_ref, diag_ref, forcing_ref, base_ref, wide_ref, prod_ref):
@@ -272,8 +276,8 @@
         base_ref[t] = products[t] - forcing_ref[t].astype(F32)
 
 
-def step_kernel(parts, ranks, last, spectral, second, *refs):
-    place_ref, freq_ref, spread_ref = refs[:3]
+def step_kernel(parts, ranks, last, *refs):
+    place_ref, entry_ref, spread_ref = refs[:3]
     got_refs = {swap: refs[3 + i] for i, swap in enumerate(SWAP_ORDER)}
     got_refs = [got_refs[swap] for swap in range(len(OFFSETS))]
     refs = refs[3 + len(OFFSETS) :]
@@ -289,8 +293,7 @@
     place = place_ref[0]
     faces = FACES * elems
 
-    freq = freq_ref[...]
-    entries = [freq * float(spectral[d]) - dissipation * float(second[d]) for d in range(NI)]
+    entries = [entry_ref[d : d + 1, :] for d in range(NI)]
 
     arrived = by_offset(place, [ref[...].astype(F32) for ref in got_refs])
     for k, offset in enumerate(OFFSETS):
@@ -362,6 +365,7 @@
     pool_shape = jax.ShapeDtypeStruct((faces, insts * LANE), BF16)
     out_shapes = [jax.ShapeDtypeStruct((capacity, insts * LANE), BF16)] * slots
     flux_shape = jax.ShapeDtypeStruct((faces, FIELDS * LANE), BF16)
+    entry_shape = jax.ShapeDtypeStruct((NI, width), F32)
     hot_shape = jax.ShapeDtypeStruct((faces, faces + slots * capacity), BF16)
 
     def exchange(state, outgoing):
@@ -388,7 +392,6 @@
             name="own_terms",
         )(state, diag, force)
 
-    freq = frequency.reshape(1, 1)
     spread, order = pl.pallas_call(
         table_kernel,
         out_shape=[
@@ -400,37 +403,37 @@
         cost_estimate=pl.CostEstimate(flops=10**10, bytes_accessed=10**6, transcendentals=0),
         name="tables",
     )()
-    flux, hot, pool, *outgoing = pl.pallas_call(
-        first_kernel,
-        out_shape=[flux_shape, hot_shape, pool_shape] + out_shapes,
-        in_specs=[smem] + [vmem] * 6,
-        out_specs=[vmem] * (3 + len(out_shapes)),
+    flux, hot, entries, pool, *outgoing = pl.pallas_call(
+        functools.partial(first_kernel, spectral, second),
+        out_shape=[flux_shape, hot_shape, entry_shape, pool_shape] + out_shapes,
+        in_specs=[smem] * 2 + [vmem] * 6,
+        out_specs=[vmem] * (4 + len(out_shapes)),
         compiler_params=params,
         cost_estimate=pl.CostEstimate(flops=10**10, bytes_accessed=10**6, transcendentals=0),
         name="first_traces",
-    )(place, order, initial_state, trace_wide, send_list, flux_jacobian, sources)
+    )(place, frequency, order, initial_state, trace_wide, send_list, flux_jacobian, sources)
     state, trace, send = initial_state, trace_wide, send_list
     force, lift, diag = forcing, lift_wide, diagonal_blocks
     states, got = exchange(state, outgoing)
     base = own_terms(state, diag, force)
     state, pool, *outgoing = pl.pallas_call(
-        functools.partial(step_kernel, parts, ranks, False, spectral, second),
+        functools.partial(step_kernel, parts, ranks, False),
         out_shape=[like(initial_state), pool_shape] + out_shapes,
         in_specs=[smem] + [vmem] * (ranks + slots + 9),
         out_specs=[vmem] * (2 + len(out_shapes)),
         compiler_params=params,
         name="first_step",
-    )(place, freq, spread, *got, *states, pool, base, hot, flux, lift, trace, send)
+    )(place, entries, spread, *got, *states, pool, base, hot, flux, lift, trace, send)
     states, got = exchange(state, outgoing)
     base = own_terms(state, diag, force)
     return pl.pallas_call(
-        functools.partial(step_kernel, parts, ranks, True, spectral, second),
+        functools.partial(step_kernel, parts, ranks, True),
         out_shape=[like(initial_state), wide_shape],
         in_specs=[smem] + [vmem] * (ranks + slots + 7),
         out_specs=[vmem] * 2,
         compiler_params=params,
         name="last_step",
-    )(place, freq, spread, *got, *states, pool, base, hot, flux, lift)
+    )(place, entries, spread, *got, *states, pool, base, hot, flux, lift)
 
 
 def solution(mesh):

time: 19.6 us -> 19.1 us (0.974)
  local copies, waits for them, and re-layouts: 0.88 us -> 0.21 us
  waiting for transfers between devices: 1.24 us -> 1.46 us
    unnamed x16, local copies, waits for them, and re-layouts: 0.88 us -> 0.21 us
    ppermute x8, starting transfers between devices: 8.15 us -> 8.6 us  [exchange(): lax.ppermute(outgoing[swap], ('inst', 'dom'), routes[swap])]
    ppermute x2, starting transfers between devices: 3.6 us -> 3.15 us  [exchange(): states.append(lax.ppermute(state, 'inst', route))]
    ppermute x8, waiting for transfers between devices: 1.23 us -> 1.45 us  [exchange(): lax.ppermute(outgoing[swap], ('inst', 'dom'), routes[swap])]
  transfers between devices with their start and end apart: 10 -> 10, of which waited for: 2 -> 3; matrix products, arithmetic and copies ran while one was open for 0% -> 0% of each run, Pallas kernels for 10% -> 10%
where the time goes in v2:
time: 19.1 us; the launch traced here: 19 us
  starting transfers between devices  11.7 us (61%)
  Pallas kernels  4.17 us (22%)
  waiting for transfers between devices  1.46 us (8%)
  between operations  1.41 us (7%)
  local copies, waits for them, and re-layouts  0.21 us (1%)
    ppermute x8, starting transfers between devices, exchange(): lax.ppermute(outgoing[swap], ('inst', 'dom'), routes[swap])  8.6 us
    ppermute x2, starting transfers between devices, exchange(): states.append(lax.ppermute(state, 'inst', route))  3.15 us
    ppermute x8, waiting for transfers between devices, exchange(): lax.ppermute(outgoing[swap], ('inst', 'dom'), routes[swap])  1.45 us
    pallas_call x2, Pallas kernels, own_terms(): pl.pallas_call(base_kernel, out_shape=wide_shape, in_specs=[vmem] * 3, ou...  1.33 us
    pallas_call x1, Pallas kernels, on_device(): pl.pallas_call(functools.partial(step_kernel, parts, ranks, True), out_sh...  1.27 us
    pallas_call x1, Pallas kernels, on_device(): pl.pallas_call(functools.partial(step_kernel, parts, ranks, False), out_s...  0.93 us
    pallas_call x1, Pallas kernels, on_device(): pl.pallas_call(functools.partial(first_kernel, spectral, second), out_sha...  0.46 us
  transfers between devices with their start and end apart: 10, of which 3 were waited for; matrix products, arithmetic and copies ran while one was open for 0% of the time, Pallas kernels for 10%

profile of v2, /device:TPU:0, one launch (start us, length us, event | category | flops | bytes accessed | tf_op | source)
XLA Modules:
  0.0 19.0 jit_solution(88628958961464992)
XLA Ops:
  0.6 3.0 %collective-permute-start.4 = (bf16[4,16,320]{2,1,0:T(8,128)(2,1)}, bf16[4,16,320]{2,1,0:T(8,128)(2,1)S(1)}, u32[]{:S(2)}, u32[]{:S(2)}) collective-permute-start(bf16[4,16,320]{2,1,0:T(8,128)(2,1)} %refs_7_.1), channel_id=1, source_target_pairs={{16,0},{0,16},{17,1},{1,17},{18,2},{2,18},{19,3},{3,19},{20,4},{4,... | collective-permute-start | bytes 122888 | tf_op jit(solution)/shard_map/ppermute | solution.py:376
  3.6 0.0 copy-start.7
  3.7 0.2 tables.1
  4.5 0.1 copy-done.2
  4.7 0.0 copy-done.5
  4.7 0.0 copy-done.6
  4.7 0.5 %first_traces.1 = (bf16[96,640]{1,0:T(8,128)(2,1)S(1)}, bf16[96,128]{1,0:T(8,128)(2,1)S(1)}, f32[8,320]{1,0:T(8,128)S(1)}, bf16[96,512]{1,0:T(8,128)(2,1)S(1)}, ...) custom-call(s32[1]{0:T(128)} %bitcast.place_ref.refs_0_, ...), custom_call_target="tpu_custom_call" | custom-call | flops 10000000000 | bytes 1000000 | tf_op jit(solution)/shard_map/first_traces/pallas_call | solution.py:406
  5.2 0.0 copy-start.1
  5.2 0.1 collective-permute-start
  5.3 2.0 %collective-permute-start.1 = (bf16[8,512]{1,0:T(8,128)(2,1)S(1)}, bf16[8,512]{1,0:T(8,128)(2,1)S(1)}, u32[]{:S(2)}, u32[]{:S(2)}) collective-permute-start(bf16[8,512]{1,0:T(8,128)(2,1)S(1)} %get-tuple-element.22), channel_id=1, source_target_pairs={{1,2},{3,4},{5,6},{7,8},{9,10},{11,12},{13,14},{17,18},{19,20},{21... | collective-permute-start | bytes 24584 | tf_op jit(solution)/shard_map/ppermute | solution.py:372
  7.3 1.0 %collective-permute-start.2 = (bf16[8,512]{1,0:T(8,128)(2,1)S(1)}, bf16[8,512]{1,0:T(8,128)(2,1)S(1)}, u32[]{:S(2)}, u32[]{:S(2)}) collective-permute-start(bf16[8,512]{1,0:T(8,128)(2,1)S(1)} %get-tuple-element.23), channel_id=1, source_target_pairs={{0,2},{1,3},{4,6},{5,7},{8,10},{9,11},{12,14},{13,15},{16,18},{17,... | collective-permute-start | bytes 24584 | tf_op jit(solution)/shard_map/ppermute | solution.py:372
  8.3 1.2 %collective-permute-start.3 = (bf16[8,512]{1,0:T(8,128)(2,1)S(1)}, bf16[8,512]{1,0:T(8,128)(2,1)S(1)}, u32[]{:S(2)}, u32[]{:S(2)}) collective-permute-start(bf16[8,512]{1,0:T(8,128)(2,1)S(1)} %get-tuple-element.24), channel_id=1, source_target_pairs={{0,1},{2,3},{4,5},{6,7},{8,9},{10,11},{12,13},{14,15},{16,17},{18,... | collective-permute-start | bytes 24584 | tf_op jit(solution)/shard_map/ppermute | solution.py:372
  9.5 0.7 %own_terms.2.refs_10_ = f32[4,16,320]{2,1,0:T(8,128)S(1)} custom-call(bf16[4,16,320]{2,1,0:T(8,128)(2,1)S(1)} %copy-done.4, bf16[16,320,320]{2,1,0:T(8,128)(2,1)S(1)} %copy-done, bf16[4,16,320]{2,1,0:T(8,128)(2,1)S(1)} %copy-done.3), custom_call_target="tpu_custom_call" | custom-call | flops 13107200 | bytes 3276800 | tf_op jit(solution)/shard_map/own_terms/pallas_call | solution.py:380
  10.2 0.0 collective-permute-done.refs_3_
  10.2 0.0 collective-permute-done.1.refs_4_
  10.2 0.7 %collective-permute-done.2.refs_5_ = bf16[8,512]{1,0:T(8,128)(2,1)S(1)} collective-permute-done((bf16[8,512]{1,0:T(8,128)(2,1)S(1)}, bf16[8,512]{1,0:T(8,128)(2,1)S(1)}, u32[]{:S(2)}, u32[]{:S(2)}) %collective-permute-start.2) | collective-permute-done | bytes 8224 | tf_op jit(solution)/shard_map/ppermute | solution.py:372
  10.9 0.0 collective-permute-done.3.refs_6_
  10.9 0.0 collective-permute-done.4.refs_8_
  10.9 0.0 copy-done.1
  11.0 0.9 %first_step.1 = (bf16[4,16,320]{2,1,0:T(8,128)(2,1)S(1)}, bf16[96,512]{1,0:T(8,128)(2,1)S(1)}, bf16[8,512]{1,0:T(8,128)(2,1)S(1)}, bf16[8,512]{1,0:T(8,128)(2,1)...) custom-call(s32[1]{0:T(128)} %bitcast.place_ref.refs_0_, f32[8,320]{1,0:T(8,128)S(1)} %get-tuple-element.19.refs_1_, ...), custom_call_target="tpu_custom_call" | custom-call | tf_op jit(solution)/shard_map/first_step/pallas_call | solution.py:419
  11.9 0.1 collective-permute-start.9
  12.0 1.9 %collective-permute-start.5 = (bf16[8,512]{1,0:T(8,128)(2,1)S(1)}, bf16[8,512]{1,0:T(8,128)(2,1)S(1)}, u32[]{:S(2)}, u32[]{:S(2)}) collective-permute-start(bf16[8,512]{1,0:T(8,128)(2,1)S(1)} %get-tuple-element.28), channel_id=1, source_target_pairs={{2,4},{3,5},{6,8},{7,9},{10,12},{11,13},{18,20},{19,21},{22,24},{2... | collective-permute-start | bytes 24584 | tf_op jit(solution)/shard_map/ppermute | solution.py:372
  14.0 0.1 collective-permute-start.6
  14.1 1.3 %collective-permute-start.7 = (bf16[8,512]{1,0:T(8,128)(2,1)S(1)}, bf16[8,512]{1,0:T(8,128)(2,1)S(1)}, u32[]{:S(2)}, u32[]{:S(2)}) collective-permute-start(bf16[8,512]{1,0:T(8,128)(2,1)S(1)} %get-tuple-element.30), channel_id=1, source_target_pairs={{0,2},{1,3},{4,6},{5,7},{8,10},{9,11},{12,14},{13,15},{16,18},{17,... | collective-permute-start | bytes 24584 | tf_op jit(solution)/shard_map/ppermute | solution.py:372
  15.4 0.9 %collective-permute-start.8 = (bf16[8,512]{1,0:T(8,128)(2,1)S(1)}, bf16[8,512]{1,0:T(8,128)(2,1)S(1)}, u32[]{:S(2)}, u32[]{:S(2)}) collective-permute-start(bf16[8,512]{1,0:T(8,128)(2,1)S(1)} %get-tuple-element.31), channel_id=1, source_target_pairs={{0,1},{2,3},{4,5},{6,7},{8,9},{10,11},{12,13},{14,15},{16,17},{18,... | collective-permute-start | bytes 24584 | tf_op jit(solution)/shard_map/ppermute | solution.py:372
  16.3 0.7 %own_terms.3.refs_10_ = f32[4,16,320]{2,1,0:T(8,128)S(1)} custom-call(bf16[4,16,320]{2,1,0:T(8,128)(2,1)S(1)} %get-tuple-element.32.state_ref.refs_7_, bf16[16,320,320]{2,1,0:T(8,128)(2,1)S(1)} %copy-done, bf16[4,16,320]{2,1,0:T(8,128)(2,1)S(1)} %copy-done.3), custom_call_target="tpu_custom_call" | custom-call | flops 13107200 | bytes 3276800 | tf_op jit(solution)/shard_map/own_terms/pallas_call | solution.py:380
  17.0 0.0 collective-permute-done.5.refs_3_
  17.0 0.7 %collective-permute-done.6.refs_4_ = bf16[8,512]{1,0:T(8,128)(2,1)S(1)} collective-permute-done((bf16[8,512]{1,0:T(8,128)(2,1)S(1)}, bf16[8,512]{1,0:T(8,128)(2,1)S(1)}, u32[]{:S(2)}, u32[]{:S(2)}) %collective-permute-start.6) | collective-permute-done | bytes 8224 | tf_op jit(solution)/shard_map/ppermute | solution.py:372
  17.6 0.1 collective-permute-done.7.refs_5_
  17.7 0.0 collective-permute-done.8.refs_6_
  17.7 0.0 collective-permute-done.9.refs_8_
  17.7 1.3 %last_step.1 = (bf16[4,16,320]{2,1,0:T(8,128)(2,1)}, f32[4,16,320]{2,1,0:T(8,128)}) custom-call(s32[1]{0:T(128)} %bitcast.place_ref.refs_0_, f32[8,320]{1,0:T(8,128)S(1)} %get-tuple-element.19.refs_1_, bf16[128,640]{1,0:T(8,128)(2,1)S(1)} %get-tuple-element.20.refs_2_, bf16[8,512]{1,0:T(8,128)(2,1)S(1)} %collective-permute-done.5.refs_3_, ...), custom_call_target="tpu_custom_call" | custom-call | tf_op jit(solution)/shard_map/last_step/pallas_call | solution.py:429
  (10 shorter events, 0.0 us)
Async XLA Ops:
  0.6 10.3 %collective-permute-start.4 = (bf16[4,16,320]{2,1,0:T(8,128)(2,1)}, bf16[4,16,320]{2,1,0:T(8,128)(2,1)S(1)}, u32[]{:S(2)}, u32[]{:S(2)}) collective-permute-start(bf16[4,16,320]{2,1,0:T(8,128)(2,1)} %refs_7_.1), channel_id=1, source_target_pairs={{16,0},{0,16},{17,1},{1,17},{18,2},{2,18},{19,3},{3,19},{20,4},{4,... | collective-permute-start | bytes 122888 | tf_op jit(solution)/shard_map/ppermute | solution.py:376
  3.6 1.0 %copy-start.2 = (bf16[320,768]{1,0:T(8,128)(2,1)S(1)}, bf16[320,768]{1,0:T(8,128)(2,1)}, u32[]{:S(2)}) copy-start(bf16[320,768]{1,0:T(8,128)(2,1)} %constant.8.clone.trace_ref.refs_14_) | copy-start | bytes 1474564
  3.6 1.0 %copy-start.4 = (bf16[4,16,320]{2,1,0:T(8,128)(2,1)S(1)}, bf16[4,16,320]{2,1,0:T(8,128)(2,1)}, u32[]{:S(2)}) copy-start(bf16[4,16,320]{2,1,0:T(8,128)(2,1)} %refs_7_.1) | copy-start | bytes 122884
  3.6 1.0 %copy-start.5 = (s32[1,4,8]{2,1,0:T(4,128)S(1)}, s32[1,4,8]{2,1,0:T(4,128)}, u32[]{:S(2)}) copy-start(s32[1,4,8]{2,1,0:T(4,128)} %refs_15_.1) | copy-start | bytes 388
  3.6 1.1 %copy-start.6 = (bf16[16,2400]{1,0:T(8,128)(2,1)S(1)}, bf16[16,2400]{1,0:T(8,128)(2,1)}, u32[]{:S(2)}) copy-start(bf16[16,2400]{1,0:T(8,128)(2,1)} %flux_ref.1) | copy-start | bytes 230404
  3.6 1.1 %copy-start.7 = (s32[16,6]{0,1:T(8,128)S(1)}, s32[16,6]{0,1:T(8,128)}, u32[]{:S(2)}) copy-start(s32[16,6]{0,1:T(8,128)} %param.14) | copy-start | bytes 1156
  4.7 4.8 %copy-start = (bf16[16,320,320]{2,1,0:T(8,128)(2,1)S(1)}, bf16[16,320,320]{2,1,0:T(8,128)(2,1)}, u32[]{:S(2)}) copy-start(bf16[16,320,320]{2,1,0:T(8,128)(2,1)} %diag_ref.3) | copy-start | bytes 9830404
  4.7 4.8 %copy-start.3 = (bf16[4,16,320]{2,1,0:T(8,128)(2,1)S(1)}, bf16[4,16,320]{2,1,0:T(8,128)(2,1)}, u32[]{:S(2)}) copy-start(bf16[4,16,320]{2,1,0:T(8,128)(2,1)} %forcing_ref.3) | copy-start | bytes 122884
  5.2 5.8 %copy-start.1 = (bf16[768,320]{1,0:T(8,128)(2,1)S(1)}, bf16[768,320]{1,0:T(8,128)(2,1)}, u32[]{:S(2)}) copy-start(bf16[768,320]{1,0:T(8,128)(2,1)} %constant.9.clone.refs_13_) | copy-start | bytes 1474564
  5.2 5.0 %collective-permute-start = (bf16[8,512]{1,0:T(8,128)(2,1)S(1)}, bf16[8,512]{1,0:T(8,128)(2,1)S(1)}, u32[]{:S(2)}, u32[]{:S(2)}) collective-permute-start(bf16[8,512]{1,0:T(8,128)(2,1)S(1)} %get-tuple-element.21), channel_id=1, source_target_pairs={{2,4},{3,5},{6,8},{7,9},{10,12},{11,13},{18,20},{19,21},{22,24},{2... | collective-permute-start | bytes 24584 | tf_op jit(solution)/shard_map/ppermute | solution.py:372
  5.3 5.0 %collective-permute-start.1 = (bf16[8,512]{1,0:T(8,128)(2,1)S(1)}, bf16[8,512]{1,0:T(8,128)(2,1)S(1)}, u32[]{:S(2)}, u32[]{:S(2)}) collective-permute-start(bf16[8,512]{1,0:T(8,128)(2,1)S(1)} %get-tuple-element.22), channel_id=1, source_target_pairs={{1,2},{3,4},{5,6},{7,8},{9,10},{11,12},{13,14},{17,18},{19,20},{21... | collective-permute-start | bytes 24584 | tf_op jit(solution)/shard_map/ppermute | solution.py:372
  7.3 3.7 %collective-permute-start.2 = (bf16[8,512]{1,0:T(8,128)(2,1)S(1)}, bf16[8,512]{1,0:T(8,128)(2,1)S(1)}, u32[]{:S(2)}, u32[]{:S(2)}) collective-permute-start(bf16[8,512]{1,0:T(8,128)(2,1)S(1)} %get-tuple-element.23), channel_id=1, source_target_pairs={{0,2},{1,3},{4,6},{5,7},{8,10},{9,11},{12,14},{13,15},{16,18},{17,... | collective-permute-start | bytes 24584 | tf_op jit(solution)/shard_map/ppermute | solution.py:372
  8.3 2.6 %collective-permute-start.3 = (bf16[8,512]{1,0:T(8,128)(2,1)S(1)}, bf16[8,512]{1,0:T(8,128)(2,1)S(1)}, u32[]{:S(2)}, u32[]{:S(2)}) collective-permute-start(bf16[8,512]{1,0:T(8,128)(2,1)S(1)} %get-tuple-element.24), channel_id=1, source_target_pairs={{0,1},{2,3},{4,5},{6,7},{8,9},{10,11},{12,13},{14,15},{16,17},{18,... | collective-permute-start | bytes 24584 | tf_op jit(solution)/shard_map/ppermute | solution.py:372
  11.9 5.8 %collective-permute-start.9 = (bf16[4,16,320]{2,1,0:T(8,128)(2,1)S(1)}, bf16[4,16,320]{2,1,0:T(8,128)(2,1)S(1)}, u32[]{:S(2)}, u32[]{:S(2)}) collective-permute-start(bf16[4,16,320]{2,1,0:T(8,128)(2,1)S(1)} %get-tuple-element.32.state_ref.refs_7_), channel_id=1, source_target_pairs={{16,0},{0,16},{17,1},{1,17},{18,2},{2,18},{19,3},{3,19},{20,4},{4,... | collective-permute-start | bytes 122888 | tf_op jit(solution)/shard_map/ppermute | solution.py:376
  12.0 4.9 %collective-permute-start.5 = (bf16[8,512]{1,0:T(8,128)(2,1)S(1)}, bf16[8,512]{1,0:T(8,128)(2,1)S(1)}, u32[]{:S(2)}, u32[]{:S(2)}) collective-permute-start(bf16[8,512]{1,0:T(8,128)(2,1)S(1)} %get-tuple-element.28), channel_id=1, source_target_pairs={{2,4},{3,5},{6,8},{7,9},{10,12},{11,13},{18,20},{19,21},{22,24},{2... | collective-permute-start | bytes 24584 | tf_op jit(solution)/shard_map/ppermute | solution.py:372
  14.0 3.7 %collective-permute-start.6 = (bf16[8,512]{1,0:T(8,128)(2,1)S(1)}, bf16[8,512]{1,0:T(8,128)(2,1)S(1)}, u32[]{:S(2)}, u32[]{:S(2)}) collective-permute-start(bf16[8,512]{1,0:T(8,128)(2,1)S(1)} %get-tuple-element.29), channel_id=1, source_target_pairs={{1,2},{3,4},{5,6},{7,8},{9,10},{11,12},{13,14},{17,18},{19,20},{21... | collective-permute-start | bytes 24584 | tf_op jit(solution)/shard_map/ppermute | solution.py:372
  14.1 3.7 %collective-permute-start.7 = (bf16[8,512]{1,0:T(8,128)(2,1)S(1)}, bf16[8,512]{1,0:T(8,128)(2,1)S(1)}, u32[]{:S(2)}, u32[]{:S(2)}) collective-permute-start(bf16[8,512]{1,0:T(8,128)(2,1)S(1)} %get-tuple-element.30), channel_id=1, source_target_pairs={{0,2},{1,3},{4,6},{5,7},{8,10},{9,11},{12,14},{13,15},{16,18},{17,... | collective-permute-start | bytes 24584 | tf_op jit(solution)/shard_map/ppermute | solution.py:372
  15.4 2.4 %collective-permute-start.8 = (bf16[8,512]{1,0:T(8,128)(2,1)S(1)}, bf16[8,512]{1,0:T(8,128)(2,1)S(1)}, u32[]{:S(2)}, u32[]{:S(2)}) collective-permute-start(bf16[8,512]{1,0:T(8,128)(2,1)S(1)} %get-tuple-element.31), channel_id=1, source_target_pairs={{0,1},{2,3},{4,5},{6,7},{8,9},{10,11},{12,13},{14,15},{16,17},{18,... | collective-permute-start | bytes 24584 | tf_op jit(solution)/shard_map/ppermute | solution.py:372

commit v3 on v1

--- a/solution.py
+++ b/solution.py
@@ -248,6 +248,67 @@
     return jnp.concatenate(hot, 0).astype(BF16)
 
 
+def face_flux(picked, flux, spread, insts):
+    count = picked.shape[0]
+    stacked = jnp.concatenate([picked[:, t * LANE : (t + 1) * LANE] for t in range(insts)], 0)
+    wide = jnp.dot(stacked, spread, preferred_element_type=F32)
+    normal = []
+    for t in range(insts):
+        rows = wide[t * count : (t + 1) * count]
+        summed = flux[:, 0:LANE] * rows[:, 0:LANE]
+        for d in range(1, FIELDS):
+            summed += flux[:, d * LANE : (d + 1) * LANE] * rows[:, d * LANE : (d + 1) * LANE]
+        normal.append(summed.astype(BF16))
+    return normal
+
+
+def lift_faces(normal, lift, elems):
+    rows = [
+        jnp.concatenate([n[f * elems : (f + 1) * elems] for f in range(FACES)], 1) for n in normal
+    ]
+    return jnp.dot(jnp.concatenate(rows, 0), lift, preferred_element_type=F32)
+
+
+def coupler_kernel(spectral, second, freq_ref, spread_ref, entry_ref):
+    freq = freq_ref[0]
+    for d in range(NI):
+        entry = freq * float(spectral[d]) - dissipation * float(second[d])
+        entry_ref[d : d + 1, :] = jnp.full((1, entry_ref.shape[1]), entry, F32)
+
+
+def couple(entry_ref, states, t, rank, insts):
+    summed = None
+    for s in range(insts):
+        d = (t - s - rank * insts) % NI
+        term = entry_ref[d : d + 1, :] * states[s].astype(F32)
+        summed = term if summed is None else summed + term
+    return summed
+
+
+def rotated(flux):
+    place = lax.broadcasted_iota(jnp.int32, (flux.shape[0], LANE), 1) // FPTS
+    blocks = []
+    for k in range(LANE // FPTS):
+        block = jnp.zeros((flux.shape[0], LANE), F32)
+        for d in range(FIELDS):
+            met = place == (d + k) % (LANE // FPTS)
+            block = jnp.where(met, flux[:, d * LANE : (d + 1) * LANE], block)
+        blocks.append(block)
+    return jnp.concatenate(blocks, 1)
+
+
+def slot_normal(blocks, factors, insts):
+    count = blocks.shape[0]
+    stacked = jnp.concatenate([blocks[:, t * LANE : (t + 1) * LANE] for t in range(insts)], 0)
+    summed = [None] * insts
+    for k in range(LANE // FPTS):
+        turned = stacked if k == 0 else pltpu.roll(stacked, k * FPTS, 1)
+        for t in range(insts):
+            term = factors[:, k * LANE : (k + 1) * LANE] * turned[t * count : (t + 1) * count]
+            summed[t] = term if k == 0 else summed[t] + term
+    return [rows.astype(BF16) for rows in summed]
+
+
 def table_kernel(spread_ref, order_ref):
     spread_ref[...] = spread_table()
     order_ref[...] = order_table()
@@ -260,7 +321,8 @@
     pool = trace_pool(state, trace_ref[...], insts, elems)
     pool_ref[...] = pool
     fill_outgoing(pool, send_ref[0], out_refs, place_ref[0], elems)
-    hot_ref[...] = source_table(source_ref[...].T, elems, send_ref.shape[1] * send_ref.shape[2])
+    slots = send_ref.shape[1] * send_ref.shape[2]
+    hot_ref[...] = source_table(source_ref[...].T, elems, slots)
     flux_out_ref[...] = flux_order(flux_ref[...], order_ref[...])
 
 
@@ -272,68 +334,102 @@
         base_ref[t] = products[t] - forcing_ref[t].astype(F32)
 
 
-def step_kernel(parts, ranks, last, spectral, second, *refs):
-    place_ref, freq_ref, spread_ref = refs[:3]
-    got_refs = {swap: refs[3 + i] for i, swap in enumerate(SWAP_ORDER)}
-    got_refs = [got_refs[swap] for swap in range(len(OFFSETS))]
-    refs = refs[3 + len(OFFSETS) :]
-    states = refs[:ranks]
-    pool_ref, refs = refs[ranks], refs[ranks + 1 :]
-    base_ref, hot_ref, flux_ref, lift_ref = refs[:4]
-    if last:
-        final_ref, residual_ref = refs[4:]
-    else:
-        trace_ref, send_ref, next_ref, next_pool_ref = refs[4:8]
-        out_refs = refs[8:]
-    insts, elems, width = states[0].shape
-    place = place_ref[0]
-    faces = FACES * elems
-
-    freq = freq_ref[...]
-    entries = [freq * float(spectral[d]) - dissipation * float(second[d]) for d in range(NI)]
-
-    arrived = by_offset(place, [ref[...].astype(F32) for ref in got_refs])
+def last_base_kernel(state_ref, diag_ref, forcing_ref, pool_ref, hot_ref, flux_ref, spread_ref,
+                     lift_ref, entry_ref, base_ref, part_ref, factor_ref, wide_ref, prod_ref):
+    insts, elems, width = state_ref.shape
+    flux = flux_ref[...]
+    hot = hot_ref[...]
+    faces = pool_ref.shape[0]
+    factors = lax.dot_general(hot, flux, (((0,), (0,)), ((), ())), preferred_element_type=F32)
+    factor_ref[...] = rotated(factors[faces:])
+    empty = jnp.zeros((hot.shape[1] - faces, pool_ref.shape[1]), BF16)
+    pool = jnp.concatenate([pool_ref[...], empty], 0)
+    picked = jnp.dot(hot, pool, preferred_element_type=F32).astype(BF16)
+    normal = face_flux(picked, flux.astype(F32), spread_ref[...], insts)
+    lifted = lift_faces(normal, lift_ref[...], elems)
+    states = [state_ref[t] for t in range(insts)]
+    products = diagonal(states, diag_ref, wide_ref, prod_ref, insts, elems)
+    for t in range(insts):
+        base_ref[t] = (
+            products[t] + lifted[t * elems : (t + 1) * elems] - forcing_ref[t].astype(F32)
+        )
+        part_ref[t] = couple(entry_ref, states, t, 0, insts)
+
+
+def received(parts, place, got_refs):
+    got_refs = {swap: got_refs[i] for i, swap in enumerate(SWAP_ORDER)}
+    arrived = by_offset(
+        place, [got_refs[swap][...].astype(F32) for swap in range(len(OFFSETS))]
+    )
     for k, offset in enumerate(OFFSETS):
         exists = (place + offset >= 0) & (place + offset < parts)
         arrived[k] = jnp.where(exists, arrived[k], jnp.zeros_like(arrived[k]))
-    pool = jnp.concatenate([pool_ref[...], jnp.concatenate(arrived, 0).astype(BF16)], 0)
+    return jnp.concatenate(arrived, 0)
+
+
+def step_kernel(parts, ranks, *refs):
+    place_ref, entry_ref, spread_ref = refs[:3]
+    got_refs, refs = refs[3 : 3 + len(OFFSETS)], refs[3 + len(OFFSETS) :]
+    states, refs = refs[:ranks], refs[ranks:]
+    (pool_ref, base_ref, hot_ref, flux_ref, lift_ref, trace_ref, send_ref,
+     next_ref, next_pool_ref) = refs[:9]
+    out_refs = refs[9:]
+    insts, elems, width = states[0].shape
+    place = place_ref[0]
+    blocks = received(parts, place, got_refs).astype(BF16)
+    pool = jnp.concatenate([pool_ref[...], blocks], 0)
     picked = jnp.dot(hot_ref[...], pool, preferred_element_type=F32).astype(BF16)
-    stacked = jnp.concatenate([picked[:, t * LANE : (t + 1) * LANE] for t in range(insts)], 0)
-    wide = jnp.dot(stacked, spread_ref[...], preferred_element_type=F32)
-
-    flux = flux_ref[...].astype(F32)
-    normal = []
-    for t in range(insts):
-        rows = wide[t * faces : (t + 1) * faces]
-        summed = flux[:, 0:LANE] * rows[:, 0:LANE]
-        for d in range(1, FIELDS):
-            summed += flux[:, d * LANE : (d + 1) * LANE] * rows[:, d * LANE : (d + 1) * LANE]
-        summed = summed.astype(BF16)
-        normal.append(
-            jnp.concatenate([summed[f * elems : (f + 1) * elems] for f in range(FACES)], 1)
-        )
-    lifted = jnp.dot(jnp.concatenate(normal, 0), lift_ref[...], preferred_element_type=F32)
-
+    normal = face_flux(picked, flux_ref[...].astype(F32), spread_ref[...], insts)
+    lifted = lift_faces(normal, lift_ref[...], elems)
     fresh = []
     for t in range(insts):
-        summed = jnp.zeros((elems, width), F32)
-        for rank in range(ranks):
-            for s in range(insts):
-                summed += entries[(t - s - rank * insts) % NI] * states[rank][s].astype(F32)
+        summed = couple(entry_ref, states[0], t, 0, insts)
+        for rank in range(1, ranks):
+            summed += couple(entry_ref, states[rank], t, rank, insts)
         residual = (
             base_ref[t] + lifted[t * elems : (t + 1) * elems] + summed.astype(BF16).astype(F32)
         )
         moved = (states[0][t].astype(F32) - pseudo_step * residual).astype(BF16)
-        if last:
-            final_ref[t] = moved
-            residual_ref[t] = residual
-        else:
-            next_ref[t] = moved
-            fresh.append(moved)
-    if not last:
-        pool = trace_pool(jnp.concatenate(fresh, 0), trace_ref[...], insts, elems)
-        next_pool_ref[...] = pool
-        fill_outgoing(pool, send_ref[0], out_refs, place, elems)
+        next_ref[t] = moved
+        fresh.append(moved)
+    pool = trace_pool(jnp.concatenate(fresh, 0), trace_ref[...], insts, elems)
+    next_pool_ref[...] = pool
+    fill_outgoing(pool, send_ref[0], out_refs, place, elems)
+
+
+def last_kernel(parts, ranks, *refs):
+    place_ref, entry_ref = refs[:2]
+    got_refs, refs = refs[2 : 2 + len(OFFSETS)], refs[2 + len(OFFSETS) :]
+    states, refs = refs[:ranks], refs[ranks:]
+    (base_ref, part_ref, hot_ref, factor_ref, lift_ref, final_hbm, residual_hbm,
+     final_ref, residual_ref, sems) = refs
+    insts, elems, width = states[0].shape
+    blocks = received(parts, place_ref[0], got_refs)
+    normal = slot_normal(blocks, factor_ref[...], insts)
+    empty = jnp.zeros((FACES * elems, insts * LANE), BF16)
+    rows = jnp.concatenate([empty, jnp.concatenate(normal, 1)], 0)
+    spots = jnp.dot(hot_ref[...], rows, preferred_element_type=F32).astype(BF16)
+    lifted = lift_faces(
+        [spots[:, t * LANE : (t + 1) * LANE] for t in range(insts)], lift_ref[...], elems
+    )
+    copies = []
+    for t in range(insts):
+        summed = part_ref[t]
+        for rank in range(1, ranks):
+            summed += couple(entry_ref, states[rank], t, rank, insts)
+        residual = (
+            base_ref[t] + lifted[t * elems : (t + 1) * elems] + summed.astype(BF16).astype(F32)
+        )
+        residual_ref[t] = residual
+        final_ref[t] = (states[0][t].astype(F32) - pseudo_step * residual).astype(BF16)
+        copies += [
+            pltpu.make_async_copy(residual_ref.at[t], residual_hbm.at[t], sems.at[0, t]),
+            pltpu.make_async_copy(final_ref.at[t], final_hbm.at[t], sems.at[1, t]),
+        ]
+        copies[-2].start()
+        copies[-1].start()
+    for copy in copies:
+        copy.wait()
 
 
 def on_device(
@@ -363,6 +459,7 @@
     out_shapes = [jax.ShapeDtypeStruct((capacity, insts * LANE), BF16)] * slots
     flux_shape = jax.ShapeDtypeStruct((faces, FIELDS * LANE), BF16)
     hot_shape = jax.ShapeDtypeStruct((faces, faces + slots * capacity), BF16)
+    factor_shape = jax.ShapeDtypeStruct((slots * capacity, LANE // FPTS * LANE), F32)
 
     def exchange(state, outgoing):
         got = [lax.ppermute(outgoing[swap], ("inst", "dom"), routes[swap]) for swap in SWAP_ORDER]
@@ -372,23 +469,11 @@
             states.append(lax.ppermute(state, "inst", route))
         return states, got
 
-    def own_terms(state, diag, force):
-        return pl.pallas_call(
-            base_kernel,
-            out_shape=wide_shape,
-            in_specs=[vmem] * 3,
-            out_specs=vmem,
-            scratch_shapes=[pltpu.VMEM((pl.cdiv(width, LANE) * insts * elems, LANE), F32)] * 2,
-            compiler_params=params,
-            cost_estimate=pl.CostEstimate(
-                flops=2 * insts * diagonal_blocks.size,
-                bytes_accessed=2 * diagonal_blocks.size,
-                transcendentals=0,
-            ),
-            name="own_terms",
-        )(state, diag, force)
-
-    freq = frequency.reshape(1, 1)
+    chunks = [pltpu.VMEM((pl.cdiv(width, LANE) * insts * elems, LANE), F32)] * 2
+    diag_cost = pl.CostEstimate(
+        flops=2 * insts * diagonal_blocks.size, bytes_accessed=2 * diagonal_blocks.size,
+        transcendentals=0,
+    )
     spread, order = pl.pallas_call(
         table_kernel,
         out_shape=[
@@ -400,6 +485,15 @@
         cost_estimate=pl.CostEstimate(flops=10**10, bytes_accessed=10**6, transcendentals=0),
         name="tables",
     )()
+    freq, _ = lax.optimization_barrier((frequency, spread))
+    entries = pl.pallas_call(
+        functools.partial(coupler_kernel, spectral, second),
+        out_shape=jax.ShapeDtypeStruct((NI, width), F32),
+        in_specs=[smem, vmem],
+        out_specs=vmem,
+        compiler_params=params,
+        name="couplers",
+    )(freq, spread)
     flux, hot, pool, *outgoing = pl.pallas_call(
         first_kernel,
         out_shape=[flux_shape, hot_shape, pool_shape] + out_shapes,
@@ -409,28 +503,51 @@
         cost_estimate=pl.CostEstimate(flops=10**10, bytes_accessed=10**6, transcendentals=0),
         name="first_traces",
     )(place, order, initial_state, trace_wide, send_list, flux_jacobian, sources)
-    state, trace, send = initial_state, trace_wide, send_list
-    force, lift, diag = forcing, lift_wide, diagonal_blocks
+    state, _ = lax.optimization_barrier((initial_state, entries))
     states, got = exchange(state, outgoing)
-    base = own_terms(state, diag, force)
+    base = pl.pallas_call(
+        base_kernel,
+        out_shape=wide_shape,
+        in_specs=[vmem] * 3,
+        out_specs=vmem,
+        scratch_shapes=chunks,
+        compiler_params=params,
+        cost_estimate=diag_cost,
+        name="own_terms",
+    )(state, diagonal_blocks, forcing)
     state, pool, *outgoing = pl.pallas_call(
-        functools.partial(step_kernel, parts, ranks, False, spectral, second),
+        functools.partial(step_kernel, parts, ranks),
         out_shape=[like(initial_state), pool_shape] + out_shapes,
         in_specs=[smem] + [vmem] * (ranks + slots + 9),
         out_specs=[vmem] * (2 + len(out_shapes)),
         compiler_params=params,
         name="first_step",
-    )(place, freq, spread, *got, *states, pool, base, hot, flux, lift, trace, send)
+    )(place, entries, spread, *got, *states, pool, base, hot, flux, lift_wide, trace_wide,
+      send_list)
     states, got = exchange(state, outgoing)
-    base = own_terms(state, diag, force)
+    base, part, factors = pl.pallas_call(
+        last_base_kernel,
+        out_shape=[wide_shape] * 2 + [factor_shape],
+        in_specs=[vmem] * 9,
+        out_specs=[vmem] * 3,
+        scratch_shapes=chunks,
+        compiler_params=params,
+        cost_estimate=diag_cost,
+        name="last_own_terms",
+    )(state, diagonal_blocks, forcing, pool, hot, flux, spread, lift_wide, entries)
     return pl.pallas_call(
-        functools.partial(step_kernel, parts, ranks, True, spectral, second),
+        functools.partial(last_kernel, parts, ranks),
         out_shape=[like(initial_state), wide_shape],
-        in_specs=[smem] + [vmem] * (ranks + slots + 7),
-        out_specs=[vmem] * 2,
+        in_specs=[smem] + [vmem] * (ranks + slots + 6),
+        out_specs=[pl.BlockSpec(memory_space=pl.ANY)] * 2,
+        scratch_shapes=[
+            pltpu.VMEM(initial_state.shape, BF16),
+            pltpu.VMEM(initial_state.shape, F32),
+            pltpu.SemaphoreType.DMA((2, insts)),
+        ],
         compiler_params=params,
         name="last_step",
-    )(place, freq, spread, *got, *states, pool, base, hot, flux, lift)
+    )(place, entries, *got, *states, base, part, hot, factors, lift_wide)
 
 
 def solution(mesh):

time: 19.6 us -> 19 us (0.969)
  local copies, waits for them, and re-layouts: 0.88 us -> 0.04 us
  Pallas kernels: 4.17 us -> 4.67 us
  waiting for transfers between devices: 1.24 us -> 0.86 us
    unnamed x16, local copies, waits for them, and re-layouts: 0.88 us -> 0.04 us
    pallas_call x4 -> x5, Pallas kernels: 3.53 us -> 4.04 us  [the longest x1 1.24 us: on_device(): pl.pallas_call(last_base_kernel, out_shape=[wide_shape] * 2 + [factor_sha...]
    ppermute x8, starting transfers between devices: 8.15 us -> 8.6 us  [exchange(): lax.ppermute(outgoing[swap], ('inst', 'dom'), routes[swap])]
    ppermute x2, starting transfers between devices: 3.6 us -> 3.15 us  [exchange(): states.append(lax.ppermute(state, 'inst', route))]
    ppermute x8, waiting for transfers between devices: 1.23 us -> 0.86 us  [exchange(): lax.ppermute(outgoing[swap], ('inst', 'dom'), routes[swap])]
  transfers between devices with their start and end apart: 10 -> 10, of which waited for: 2 -> 3; matrix products, arithmetic and copies ran while one was open for 0% -> 0% of each run, Pallas kernels for 10% -> 13%
where the time goes in v3:
time: 19 us; the launch traced here: 18.8 us
  starting transfers between devices  11.8 us (62%)
  Pallas kernels  4.67 us (25%)
  between operations  1.46 us (8%)
  waiting for transfers between devices  0.86 us (5%)
    ppermute x8, starting transfers between devices, exchange(): lax.ppermute(outgoing[swap], ('inst', 'dom'), routes[swap])  8.6 us
    ppermute x2, starting transfers between devices, exchange(): states.append(lax.ppermute(state, 'inst', route))  3.15 us
    pallas_call x1, Pallas kernels, on_device(): pl.pallas_call(last_base_kernel, out_shape=[wide_shape] * 2 + [factor_sha...  1.24 us
    pallas_call x1, Pallas kernels, on_device(): pl.pallas_call(functools.partial(last_kernel, parts, ranks), out_shape=[l...  1.17 us
    pallas_call x1, Pallas kernels, on_device(): pl.pallas_call(functools.partial(step_kernel, parts, ranks), out_shape=[l...  0.94 us
    ppermute x8, waiting for transfers between devices, exchange(): lax.ppermute(outgoing[swap], ('inst', 'dom'), routes[swap])  0.86 us
    pallas_call x1, Pallas kernels, on_device(): pl.pallas_call(base_kernel, out_shape=wide_shape, in_specs=[vmem] * 3, ou...  0.68 us
    pallas_call x1, Pallas kernels, on_device(): pl.pallas_call(first_kernel, out_shape=[flux_shape, hot_shape, pool_shape...  0.46 us
  transfers between devices with their start and end apart: 10, of which 3 were waited for; matrix products, arithmetic and copies ran while one was open for 0% of the time, Pallas kernels for 13%

profile of v3, /device:TPU:0, one launch (start us, length us, event | category | flops | bytes accessed | tf_op | source)
XLA Modules:
  0.0 18.8 jit_solution(8265192356341717581)
XLA Ops:
  0.6 0.0 copy-start.2
  0.6 0.0 copy-start.4
  0.7 0.0 copy-start.7
  0.7 0.2 tables.1
  1.6 3.0 %collective-permute-start.4 = (bf16[4,16,320]{2,1,0:T(8,128)(2,1)S(1)}, bf16[4,16,320]{2,1,0:T(8,128)(2,1)S(1)}, u32[]{:S(2)}, u32[]{:S(2)}) collective-permute-start(bf16[4,16,320]{2,1,0:T(8,128)(2,1)S(1)} %copy-done.4), channel_id=1, source_target_pairs={{16,0},{0,16},{17,1},{1,17},{18,2},{2,18},{19,3},{3,19},{20,4},{4,... | collective-permute-start | bytes 122888 | tf_op jit(solution)/shard_map/ppermute | solution.py:469
  4.6 0.0 copy-start
  4.6 0.0 copy-start.3
  4.6 0.5 %first_traces.1 = (bf16[96,640]{1,0:T(8,128)(2,1)S(1)}, bf16[96,128]{1,0:T(8,128)(2,1)S(1)}, bf16[96,512]{1,0:T(8,128)(2,1)S(1)}, bf16[8,512]{1,0:T(8,128)(2,1)S...) custom-call(s32[1]{0:T(128)} %bitcast.place_ref.refs_0_, ...), custom_call_target="tpu_custom_call" | custom-call | flops 10000000000 | bytes 1000000 | tf_op jit(solution)/shard_map/first_traces/pallas_call | solution.py:497
  5.1 0.0 copy-start.1
  5.1 0.1 collective-permute-start
  5.2 2.0 %collective-permute-start.1 = (bf16[8,512]{1,0:T(8,128)(2,1)S(1)}, bf16[8,512]{1,0:T(8,128)(2,1)S(1)}, u32[]{:S(2)}, u32[]{:S(2)}) collective-permute-start(bf16[8,512]{1,0:T(8,128)(2,1)S(1)} %get-tuple-element.26), channel_id=1, source_target_pairs={{1,2},{3,4},{5,6},{7,8},{9,10},{11,12},{13,14},{17,18},{19,20},{21... | collective-permute-start | bytes 24584 | tf_op jit(solution)/shard_map/ppermute | solution.py:465
  7.2 1.0 %collective-permute-start.2 = (bf16[8,512]{1,0:T(8,128)(2,1)S(1)}, bf16[8,512]{1,0:T(8,128)(2,1)S(1)}, u32[]{:S(2)}, u32[]{:S(2)}) collective-permute-start(bf16[8,512]{1,0:T(8,128)(2,1)S(1)} %get-tuple-element.27), channel_id=1, source_target_pairs={{0,2},{1,3},{4,6},{5,7},{8,10},{9,11},{12,14},{13,15},{16,18},{17,... | collective-permute-start | bytes 24584 | tf_op jit(solution)/shard_map/ppermute | solution.py:465
  8.2 1.2 %collective-permute-start.3 = (bf16[8,512]{1,0:T(8,128)(2,1)S(1)}, bf16[8,512]{1,0:T(8,128)(2,1)S(1)}, u32[]{:S(2)}, u32[]{:S(2)}) collective-permute-start(bf16[8,512]{1,0:T(8,128)(2,1)S(1)} %get-tuple-element.28), channel_id=1, source_target_pairs={{0,1},{2,3},{4,5},{6,7},{8,9},{10,11},{12,13},{14,15},{16,17},{18,... | collective-permute-start | bytes 24584 | tf_op jit(solution)/shard_map/ppermute | solution.py:465
  9.4 0.7 %own_terms.1.refs_10_ = f32[4,16,320]{2,1,0:T(8,128)S(1)} custom-call(bf16[4,16,320]{2,1,0:T(8,128)(2,1)S(1)} %copy-done.4, bf16[16,320,320]{2,1,0:T(8,128)(2,1)S(1)} %copy-done, bf16[4,16,320]{2,1,0:T(8,128)(2,1)S(1)} %copy-done.3), custom_call_target="tpu_custom_call" | custom-call | flops 13107200 | bytes 3276800 | tf_op jit(solution)/shard_map/own_terms/pallas_call | solution.py:508
  10.1 0.0 collective-permute-done.refs_3_
  10.1 0.0 collective-permute-done.1.refs_4_
  10.2 0.7 %collective-permute-done.2.refs_5_ = bf16[8,512]{1,0:T(8,128)(2,1)S(1)} collective-permute-done((bf16[8,512]{1,0:T(8,128)(2,1)S(1)}, bf16[8,512]{1,0:T(8,128)(2,1)S(1)}, u32[]{:S(2)}, u32[]{:S(2)}) %collective-permute-start.2) | collective-permute-done | bytes 8224 | tf_op jit(solution)/shard_map/ppermute | solution.py:465
  10.8 0.0 collective-permute-done.3.refs_6_
  10.8 0.0 collective-permute-done.4.refs_8_
  10.8 0.9 %first_step.1 = (bf16[4,16,320]{2,1,0:T(8,128)(2,1)S(1)}, bf16[96,512]{1,0:T(8,128)(2,1)S(1)}, bf16[8,512]{1,0:T(8,128)(2,1)S(1)}, bf16[8,512]{1,0:T(8,128)(2,1)...) custom-call(s32[1]{0:T(128)} %bitcast.place_ref.refs_0_, f32[8,320]{1,0:T(8,128)S(1)} %couplers.1.refs_1_.entry_ref, ...), custom_call_target="tpu_custom_call" | custom-call | tf_op jit(solution)/shard_map/first_step/pallas_call | solution.py:518
  11.8 0.1 collective-permute-start.9
  11.9 1.9 %collective-permute-start.5 = (bf16[8,512]{1,0:T(8,128)(2,1)S(1)}, bf16[8,512]{1,0:T(8,128)(2,1)S(1)}, u32[]{:S(2)}, u32[]{:S(2)}) collective-permute-start(bf16[8,512]{1,0:T(8,128)(2,1)S(1)} %get-tuple-element.33), channel_id=1, source_target_pairs={{2,4},{3,5},{6,8},{7,9},{10,12},{11,13},{18,20},{19,21},{22,24},{2... | collective-permute-start | bytes 24584 | tf_op jit(solution)/shard_map/ppermute | solution.py:465
  13.9 0.1 collective-permute-start.6
  14.0 1.3 %collective-permute-start.7 = (bf16[8,512]{1,0:T(8,128)(2,1)S(1)}, bf16[8,512]{1,0:T(8,128)(2,1)S(1)}, u32[]{:S(2)}, u32[]{:S(2)}) collective-permute-start(bf16[8,512]{1,0:T(8,128)(2,1)S(1)} %get-tuple-element.35), channel_id=1, source_target_pairs={{0,2},{1,3},{4,6},{5,7},{8,10},{9,11},{12,14},{13,15},{16,18},{17,... | collective-permute-start | bytes 24584 | tf_op jit(solution)/shard_map/ppermute | solution.py:465
  15.3 0.9 %collective-permute-start.8 = (bf16[8,512]{1,0:T(8,128)(2,1)S(1)}, bf16[8,512]{1,0:T(8,128)(2,1)S(1)}, u32[]{:S(2)}, u32[]{:S(2)}) collective-permute-start(bf16[8,512]{1,0:T(8,128)(2,1)S(1)} %get-tuple-element.36), channel_id=1, source_target_pairs={{0,1},{2,3},{4,5},{6,7},{8,9},{10,11},{12,13},{14,15},{16,17},{18,... | collective-permute-start | bytes 24584 | tf_op jit(solution)/shard_map/ppermute | solution.py:465
  16.2 1.2 %last_own_terms.1 = (f32[4,16,320]{2,1,0:T(8,128)S(1)}, f32[4,16,320]{2,1,0:T(8,128)S(1)}, f32[32,1024]{1,0:T(8,128)S(1)}) custom-call(bf16[4,16,320]{2,1,0:T(8,128)(2,1)S(1)} %get-tuple-element.37.state_ref.refs_6_, bf16[16,320,320]{2,1,0:T(8,128)(2,1)S(1)} %copy-done, bf16[4,16,320]{2,1,0:T(8,128)(2,1)S(1)} %copy-done.3, ...), custom_call_target="tpu_custom_call" | custom-call | flops 13107200 | bytes 3276800 | tf_op jit(solution)/shard_map/last_own_terms/pallas_call | solution.py:528
  17.4 0.0 collective-permute-done.5.refs_2_
  17.5 0.1 collective-permute-done.6.refs_3_
  17.5 0.1 collective-permute-done.7.refs_4_
  17.6 0.0 collective-permute-done.8.refs_5_
  17.6 0.0 collective-permute-done.9.refs_7_
  17.6 1.2 %last_step.1 = (bf16[4,16,320]{2,1,0:T(8,128)(2,1)}, f32[4,16,320]{2,1,0:T(8,128)}) custom-call(s32[1]{0:T(128)} %bitcast.place_ref.refs_0_, f32[8,320]{1,0:T(8,128)S(1)} %couplers.1.refs_1_.entry_ref, bf16[8,512]{1,0:T(8,128)(2,1)S(1)} %collective-permute-done.5.refs_2_, bf16[8,512]{1,0:T(8,128)(2,1)S(1)} %collective-permute-done.6.refs_3_, ...), custom_call_target="tpu_custom_call" | custom-call | tf_op jit(solution)/shard_map/last_step/pallas_call | solution.py:538
  (11 shorter events, 0.0 us)
Async XLA Ops:
  0.6 3.9 %copy-start.2 = (bf16[320,768]{1,0:T(8,128)(2,1)S(1)}, bf16[320,768]{1,0:T(8,128)(2,1)}, u32[]{:S(2)}) copy-start(bf16[320,768]{1,0:T(8,128)(2,1)} %constant.8.clone.trace_ref.refs_14_) | copy-start | bytes 1474564
  0.6 0.9 %copy-start.4 = (bf16[4,16,320]{2,1,0:T(8,128)(2,1)S(1)}, bf16[4,16,320]{2,1,0:T(8,128)(2,1)}, u32[]{:S(2)}) copy-start(bf16[4,16,320]{2,1,0:T(8,128)(2,1)} %refs_7_) | copy-start | bytes 122884
  0.7 3.9 %copy-start.7 = (s32[16,6]{0,1:T(8,128)S(1)}, s32[16,6]{0,1:T(8,128)}, u32[]{:S(2)}) copy-start(s32[16,6]{0,1:T(8,128)} %param.14) | copy-start | bytes 1156
  0.7 3.9 %copy-start.6 = (bf16[16,2400]{1,0:T(8,128)(2,1)S(1)}, bf16[16,2400]{1,0:T(8,128)(2,1)}, u32[]{:S(2)}) copy-start(bf16[16,2400]{1,0:T(8,128)(2,1)} %flux_ref.1) | copy-start | bytes 230404
  0.7 3.9 %copy-start.5 = (s32[1,4,8]{2,1,0:T(4,128)S(1)}, s32[1,4,8]{2,1,0:T(4,128)}, u32[]{:S(2)}) copy-start(s32[1,4,8]{2,1,0:T(4,128)} %refs_15_.1) | copy-start | bytes 388
  1.6 9.3 %collective-permute-start.4 = (bf16[4,16,320]{2,1,0:T(8,128)(2,1)S(1)}, bf16[4,16,320]{2,1,0:T(8,128)(2,1)S(1)}, u32[]{:S(2)}, u32[]{:S(2)}) collective-permute-start(bf16[4,16,320]{2,1,0:T(8,128)(2,1)S(1)} %copy-done.4), channel_id=1, source_target_pairs={{16,0},{0,16},{17,1},{1,17},{18,2},{2,18},{19,3},{3,19},{20,4},{4,... | collective-permute-start | bytes 122888 | tf_op jit(solution)/shard_map/ppermute | solution.py:469
  4.6 4.9 %copy-start = (bf16[16,320,320]{2,1,0:T(8,128)(2,1)S(1)}, bf16[16,320,320]{2,1,0:T(8,128)(2,1)}, u32[]{:S(2)}) copy-start(bf16[16,320,320]{2,1,0:T(8,128)(2,1)} %diag_ref.3) | copy-start | bytes 9830404
  4.6 4.8 %copy-start.3 = (bf16[4,16,320]{2,1,0:T(8,128)(2,1)S(1)}, bf16[4,16,320]{2,1,0:T(8,128)(2,1)}, u32[]{:S(2)}) copy-start(bf16[4,16,320]{2,1,0:T(8,128)(2,1)} %forcing_ref.3) | copy-start | bytes 122884
  5.1 5.8 %copy-start.1 = (bf16[768,320]{1,0:T(8,128)(2,1)S(1)}, bf16[768,320]{1,0:T(8,128)(2,1)}, u32[]{:S(2)}) copy-start(bf16[768,320]{1,0:T(8,128)(2,1)} %constant.9.clone.refs_13_.lift_ref.refs_12_) | copy-start | bytes 1474564
  5.1 5.0 %collective-permute-start = (bf16[8,512]{1,0:T(8,128)(2,1)S(1)}, bf16[8,512]{1,0:T(8,128)(2,1)S(1)}, u32[]{:S(2)}, u32[]{:S(2)}) collective-permute-start(bf16[8,512]{1,0:T(8,128)(2,1)S(1)} %get-tuple-element.25), channel_id=1, source_target_pairs={{2,4},{3,5},{6,8},{7,9},{10,12},{11,13},{18,20},{19,21},{22,24},{2... | collective-permute-start | bytes 24584 | tf_op jit(solution)/shard_map/ppermute | solution.py:465
  5.2 4.9 %collective-permute-start.1 = (bf16[8,512]{1,0:T(8,128)(2,1)S(1)}, bf16[8,512]{1,0:T(8,128)(2,1)S(1)}, u32[]{:S(2)}, u32[]{:S(2)}) collective-permute-start(bf16[8,512]{1,0:T(8,128)(2,1)S(1)} %get-tuple-element.26), channel_id=1, source_target_pairs={{1,2},{3,4},{5,6},{7,8},{9,10},{11,12},{13,14},{17,18},{19,20},{21... | collective-permute-start | bytes 24584 | tf_op jit(solution)/shard_map/ppermute | solution.py:465
  7.2 3.7 %collective-permute-start.2 = (bf16[8,512]{1,0:T(8,128)(2,1)S(1)}, bf16[8,512]{1,0:T(8,128)(2,1)S(1)}, u32[]{:S(2)}, u32[]{:S(2)}) collective-permute-start(bf16[8,512]{1,0:T(8,128)(2,1)S(1)} %get-tuple-element.27), channel_id=1, source_target_pairs={{0,2},{1,3},{4,6},{5,7},{8,10},{9,11},{12,14},{13,15},{16,18},{17,... | collective-permute-start | bytes 24584 | tf_op jit(solution)/shard_map/ppermute | solution.py:465
  8.2 2.6 %collective-permute-start.3 = (bf16[8,512]{1,0:T(8,128)(2,1)S(1)}, bf16[8,512]{1,0:T(8,128)(2,1)S(1)}, u32[]{:S(2)}, u32[]{:S(2)}) collective-permute-start(bf16[8,512]{1,0:T(8,128)(2,1)S(1)} %get-tuple-element.28), channel_id=1, source_target_pairs={{0,1},{2,3},{4,5},{6,7},{8,9},{10,11},{12,13},{14,15},{16,17},{18,... | collective-permute-start | bytes 24584 | tf_op jit(solution)/shard_map/ppermute | solution.py:465
  11.8 5.8 %collective-permute-start.9 = (bf16[4,16,320]{2,1,0:T(8,128)(2,1)S(1)}, bf16[4,16,320]{2,1,0:T(8,128)(2,1)S(1)}, u32[]{:S(2)}, u32[]{:S(2)}) collective-permute-start(bf16[4,16,320]{2,1,0:T(8,128)(2,1)S(1)} %get-tuple-element.37.state_ref.refs_6_), channel_id=1, source_target_pairs={{16,0},{0,16},{17,1},{1,17},{18,2},{2,18},{19,3},{3,19},{20,4},{4,... | collective-permute-start | bytes 122888 | tf_op jit(solution)/shard_map/ppermute | solution.py:469
  11.9 5.5 %collective-permute-start.5 = (bf16[8,512]{1,0:T(8,128)(2,1)S(1)}, bf16[8,512]{1,0:T(8,128)(2,1)S(1)}, u32[]{:S(2)}, u32[]{:S(2)}) collective-permute-start(bf16[8,512]{1,0:T(8,128)(2,1)S(1)} %get-tuple-element.33), channel_id=1, source_target_pairs={{2,4},{3,5},{6,8},{7,9},{10,12},{11,13},{18,20},{19,21},{22,24},{2... | collective-permute-start | bytes 24584 | tf_op jit(solution)/shard_map/ppermute | solution.py:465
  13.9 3.7 %collective-permute-start.6 = (bf16[8,512]{1,0:T(8,128)(2,1)S(1)}, bf16[8,512]{1,0:T(8,128)(2,1)S(1)}, u32[]{:S(2)}, u32[]{:S(2)}) collective-permute-start(bf16[8,512]{1,0:T(8,128)(2,1)S(1)} %get-tuple-element.34), channel_id=1, source_target_pairs={{1,2},{3,4},{5,6},{7,8},{9,10},{11,12},{13,14},{17,18},{19,20},{21... | collective-permute-start | bytes 24584 | tf_op jit(solution)/shard_map/ppermute | solution.py:465
  14.0 3.7 %collective-permute-start.7 = (bf16[8,512]{1,0:T(8,128)(2,1)S(1)}, bf16[8,512]{1,0:T(8,128)(2,1)S(1)}, u32[]{:S(2)}, u32[]{:S(2)}) collective-permute-start(bf16[8,512]{1,0:T(8,128)(2,1)S(1)} %get-tuple-element.35), channel_id=1, source_target_pairs={{0,2},{1,3},{4,6},{5,7},{8,10},{9,11},{12,14},{13,15},{16,18},{17,... | collective-permute-start | bytes 24584 | tf_op jit(solution)/shard_map/ppermute | solution.py:465
  15.3 2.4 %collective-permute-start.8 = (bf16[8,512]{1,0:T(8,128)(2,1)S(1)}, bf16[8,512]{1,0:T(8,128)(2,1)S(1)}, u32[]{:S(2)}, u32[]{:S(2)}) collective-permute-start(bf16[8,512]{1,0:T(8,128)(2,1)S(1)} %get-tuple-element.36), channel_id=1, source_target_pairs={{0,1},{2,3},{4,5},{6,7},{8,9},{10,11},{12,13},{14,15},{16,17},{18,... | collective-permute-start | bytes 24584 | tf_op jit(solution)/shard_map/ppermute | solution.py:465

commit v4 on v3

--- a/solution.py
+++ b/solution.py
@@ -269,17 +269,10 @@
     return jnp.dot(jnp.concatenate(rows, 0), lift, preferred_element_type=F32)
 
 
-def coupler_kernel(spectral, second, freq_ref, spread_ref, entry_ref):
-    freq = freq_ref[0]
-    for d in range(NI):
-        entry = freq * float(spectral[d]) - dissipation * float(second[d])
-        entry_ref[d : d + 1, :] = jnp.full((1, entry_ref.shape[1]), entry, F32)
-
-
-def couple(entry_ref, states, t, rank, insts):
+def couple(entry_ref, states, t, shift, insts):
     summed = None
     for s in range(insts):
-        d = (t - s - rank * insts) % NI
+        d = (t - s + shift * insts) % NI
         term = entry_ref[d : d + 1, :] * states[s].astype(F32)
         summed = term if summed is None else summed + term
     return summed
@@ -314,8 +307,8 @@
     order_ref[...] = order_table()
 
 
-def first_kernel(place_ref, order_ref, state_ref, trace_ref, send_ref, flux_ref, source_ref,
-                 flux_out_ref, hot_ref, pool_ref, *out_refs):
+def first_kernel(spectral, second, place_ref, freq_ref, order_ref, state_ref, trace_ref, send_ref, flux_ref, source_ref,
+                 flux_out_ref, hot_ref, entry_ref, pool_ref, *out_refs):
     insts, elems, width = state_ref.shape
     state = state_ref[...].reshape(insts * elems, width)
     pool = trace_pool(state, trace_ref[...], insts, elems)
@@ -324,36 +317,110 @@
     slots = send_ref.shape[1] * send_ref.shape[2]
     hot_ref[...] = source_table(source_ref[...].T, elems, slots)
     flux_out_ref[...] = flux_order(flux_ref[...], order_ref[...])
-
-
-def base_kernel(state_ref, diag_ref, forcing_ref, base_ref, wide_ref, prod_ref):
+    freq = freq_ref[0]
+    for d in range(NI):
+        entry = freq * float(spectral[d]) - dissipation * float(second[d])
+        entry_ref[d : d + 1, :] = jnp.full((1, width), entry, F32)
+
+
+def base_kernel(state_ref, diag_ref, forcing_ref, entry_ref, base_ref, wide_ref, prod_ref):
     insts, elems, width = state_ref.shape
     states = [state_ref[t] for t in range(insts)]
     products = diagonal(states, diag_ref, wide_ref, prod_ref, insts, elems)
     for t in range(insts):
-        base_ref[t] = products[t] - forcing_ref[t].astype(F32)
-
-
-def last_base_kernel(state_ref, diag_ref, forcing_ref, pool_ref, hot_ref, flux_ref, spread_ref,
-                     lift_ref, entry_ref, base_ref, part_ref, factor_ref, wide_ref, prod_ref):
-    insts, elems, width = state_ref.shape
+        own = couple(entry_ref, states, t, 0, insts)
+        base_ref[t] = products[t] + own - forcing_ref[t].astype(F32)
+
+
+def message_rows(insts, elems, slots):
+    per_row = pl.cdiv(WIDE, LANE)
+    tall = insts * elems
+    return tall, 2 * tall, 2 * tall + pl.cdiv(insts, per_row) * slots
+
+
+def fill_message(message_ref, states, partial, blocks, insts, elems):
+    slots = blocks.shape[0]
+    per_row = pl.cdiv(WIDE, LANE)
+    first, second, last = message_rows(insts, elems, slots)
+    message_ref[...] = jnp.zeros_like(message_ref)
+    for t in range(insts):
+        message_ref[t * elems : (t + 1) * elems, 0:WIDE] = states[t]
+        message_ref[first + t * elems : first + (t + 1) * elems, 0:WIDE] = partial[t]
+        low, at = second + t // per_row * slots, t % per_row * LANE
+        message_ref[low : low + slots, at : at + LANE] = blocks[:, t * LANE : (t + 1) * LANE]
+
+
+def from_message(message_ref, insts, elems, slots):
+    per_row = pl.cdiv(WIDE, LANE)
+    first, second, last = message_rows(insts, elems, slots)
+    states = [message_ref[t * elems : (t + 1) * elems, 0:WIDE] for t in range(insts)]
+    partial = [
+        message_ref[first + t * elems : first + (t + 1) * elems, 0:WIDE] for t in range(insts)
+    ]
+    blocks = []
+    for t in range(insts):
+        low, at = second + t // per_row * slots, t % per_row * LANE
+        blocks.append(message_ref[low : low + slots, at : at + LANE])
+    return states, partial, blocks
+
+
+def last_base_kernel(ranks, partial_ref, first_ref, *refs):
+    messages, refs = refs[: ranks - 1], refs[ranks - 1 :]
+    (diag_ref, forcing_ref, trace_ref, hot_ref, flux_ref, spread_ref, lift_ref, entry_ref,
+     state_ref, base_ref, factor_ref, mend_ref, wide_ref, prod_ref) = refs
+    insts, elems, width = first_ref.shape
     flux = flux_ref[...]
     hot = hot_ref[...]
-    faces = pool_ref.shape[0]
+    faces = hot.shape[0]
+    slots = hot.shape[1] - faces
+
+    firsts = [[first_ref[t] for t in range(insts)]]
+    partials = [[partial_ref[t] for t in range(insts)]]
+    traces = [None]
+    for message_ref in messages:
+        states, partial, blocks = from_message(message_ref, insts, elems, slots)
+        firsts.append(states)
+        partials.append(partial)
+        traces.append(blocks)
+    states = []
+    for k in range(ranks):
+        of_rank = []
+        for t in range(insts):
+            state = partials[k][t].astype(F32)
+            for j in range(ranks):
+                if j != k:
+                    state -= pseudo_step * couple(entry_ref, firsts[j], t, k - j, insts)
+            of_rank.append(state.astype(BF16))
+        states.append(of_rank)
+    for t in range(insts):
+        state_ref[t] = states[0][t]
+    for t in range(insts):
+        mend = jnp.zeros((slots, LANE), F32)
+        for k in range(1, ranks):
+            for s in range(insts):
+                d = (t - s - k * insts) % NI
+                mend -= pseudo_step * entry_ref[d : d + 1, 0:LANE] * traces[k][s].astype(F32)
+        mend_ref[:, t * LANE : (t + 1) * LANE] = mend
+
+    pool = trace_pool(jnp.concatenate(states[0], 0), trace_ref[...], insts, elems)
     factors = lax.dot_general(hot, flux, (((0,), (0,)), ((), ())), preferred_element_type=F32)
     factor_ref[...] = rotated(factors[faces:])
-    empty = jnp.zeros((hot.shape[1] - faces, pool_ref.shape[1]), BF16)
-    pool = jnp.concatenate([pool_ref[...], empty], 0)
+    empty = jnp.zeros((slots, insts * LANE), BF16)
+    pool = jnp.concatenate([pool, empty], 0)
     picked = jnp.dot(hot, pool, preferred_element_type=F32).astype(BF16)
     normal = face_flux(picked, flux.astype(F32), spread_ref[...], insts)
     lifted = lift_faces(normal, lift_ref[...], elems)
-    states = [state_ref[t] for t in range(insts)]
-    products = diagonal(states, diag_ref, wide_ref, prod_ref, insts, elems)
-    for t in range(insts):
+    products = diagonal(states[0], diag_ref, wide_ref, prod_ref, insts, elems)
+    for t in range(insts):
+        coupling = couple(entry_ref, states[0], t, 0, insts)
+        for k in range(1, ranks):
+            coupling += couple(entry_ref, states[k], t, -k, insts)
         base_ref[t] = (
-            products[t] + lifted[t * elems : (t + 1) * elems] - forcing_ref[t].astype(F32)
+            products[t]
+            + lifted[t * elems : (t + 1) * elems]
+            + coupling.astype(BF16).astype(F32)
+            - forcing_ref[t].astype(F32)
         )
-        part_ref[t] = couple(entry_ref, states, t, 0, insts)
 
 
 def received(parts, place, got_refs):
@@ -367,14 +434,11 @@
     return jnp.concatenate(arrived, 0)
 
 
-def step_kernel(parts, ranks, *refs):
-    place_ref, entry_ref, spread_ref = refs[:3]
-    got_refs, refs = refs[3 : 3 + len(OFFSETS)], refs[3 + len(OFFSETS) :]
-    states, refs = refs[:ranks], refs[ranks:]
-    (pool_ref, base_ref, hot_ref, flux_ref, lift_ref, trace_ref, send_ref,
-     next_ref, next_pool_ref) = refs[:9]
-    out_refs = refs[9:]
-    insts, elems, width = states[0].shape
+def step_kernel(parts, place_ref, spread_ref, *refs):
+    got_refs, refs = refs[: len(OFFSETS)], refs[len(OFFSETS) :]
+    (state_ref, pool_ref, base_ref, hot_ref, flux_ref, lift_ref, trace_ref, send_ref,
+     partial_ref, message_ref, *out_refs) = refs
+    insts, elems, width = state_ref.shape
     place = place_ref[0]
     blocks = received(parts, place, got_refs).astype(BF16)
     pool = jnp.concatenate([pool_ref[...], blocks], 0)
@@ -383,28 +447,21 @@
     lifted = lift_faces(normal, lift_ref[...], elems)
     fresh = []
     for t in range(insts):
-        summed = couple(entry_ref, states[0], t, 0, insts)
-        for rank in range(1, ranks):
-            summed += couple(entry_ref, states[rank], t, rank, insts)
-        residual = (
-            base_ref[t] + lifted[t * elems : (t + 1) * elems] + summed.astype(BF16).astype(F32)
-        )
-        moved = (states[0][t].astype(F32) - pseudo_step * residual).astype(BF16)
-        next_ref[t] = moved
-        fresh.append(moved)
+        residual = base_ref[t] + lifted[t * elems : (t + 1) * elems]
+        moved = state_ref[t].astype(F32) - pseudo_step * residual
+        partial_ref[t] = moved
+        fresh.append(moved.astype(BF16))
+    fill_message(message_ref, [state_ref[t] for t in range(insts)], fresh, blocks, insts, elems)
     pool = trace_pool(jnp.concatenate(fresh, 0), trace_ref[...], insts, elems)
-    next_pool_ref[...] = pool
     fill_outgoing(pool, send_ref[0], out_refs, place, elems)
 
 
-def last_kernel(parts, ranks, *refs):
-    place_ref, entry_ref = refs[:2]
-    got_refs, refs = refs[2 : 2 + len(OFFSETS)], refs[2 + len(OFFSETS) :]
-    states, refs = refs[:ranks], refs[ranks:]
-    (base_ref, part_ref, hot_ref, factor_ref, lift_ref, final_hbm, residual_hbm,
+def last_kernel(parts, place_ref, *refs):
+    got_refs, refs = refs[: len(OFFSETS)], refs[len(OFFSETS) :]
+    (state_ref, base_ref, hot_ref, factor_ref, mend_ref, lift_ref, final_hbm, residual_hbm,
      final_ref, residual_ref, sems) = refs
-    insts, elems, width = states[0].shape
-    blocks = received(parts, place_ref[0], got_refs)
+    insts, elems, width = state_ref.shape
+    blocks = received(parts, place_ref[0], got_refs) + mend_ref[...]
     normal = slot_normal(blocks, factor_ref[...], insts)
     empty = jnp.zeros((FACES * elems, insts * LANE), BF16)
     rows = jnp.concatenate([empty, jnp.concatenate(normal, 1)], 0)
@@ -414,14 +471,9 @@
     )
     copies = []
     for t in range(insts):
-        summed = part_ref[t]
-        for rank in range(1, ranks):
-            summed += couple(entry_ref, states[rank], t, rank, insts)
-        residual = (
-            base_ref[t] + lifted[t * elems : (t + 1) * elems] + summed.astype(BF16).astype(F32)
-        )
+        residual = base_ref[t] + lifted[t * elems : (t + 1) * elems]
         residual_ref[t] = residual
-        final_ref[t] = (states[0][t].astype(F32) - pseudo_step * residual).astype(BF16)
+        final_ref[t] = (state_ref[t].astype(F32) - pseudo_step * residual).astype(BF16)
         copies += [
             pltpu.make_async_copy(residual_ref.at[t], residual_hbm.at[t], sems.at[0, t]),
             pltpu.make_async_copy(final_ref.at[t], final_hbm.at[t], sems.at[1, t]),
@@ -461,14 +513,16 @@
     hot_shape = jax.ShapeDtypeStruct((faces, faces + slots * capacity), BF16)
     factor_shape = jax.ShapeDtypeStruct((slots * capacity, LANE // FPTS * LANE), F32)
 
-    def exchange(state, outgoing):
-        got = [lax.ppermute(outgoing[swap], ("inst", "dom"), routes[swap]) for swap in SWAP_ORDER]
-        states = [state]
-        for rank in range(1, ranks):
-            route = [((i + rank) % ranks, i) for i in range(ranks)]
-            states.append(lax.ppermute(state, "inst", route))
-        return states, got
-
+    def exchange(outgoing):
+        return [
+            lax.ppermute(outgoing[swap], ("inst", "dom"), routes[swap]) for swap in SWAP_ORDER
+        ]
+
+    entry_shape = jax.ShapeDtypeStruct((NI, width), F32)
+    mend_shape = jax.ShapeDtypeStruct((slots * capacity, insts * LANE), F32)
+    message_shape = jax.ShapeDtypeStruct(
+        (message_rows(insts, elems, slots * capacity)[-1], pl.cdiv(width, LANE) * LANE), BF16
+    )
     chunks = [pltpu.VMEM((pl.cdiv(width, LANE) * insts * elems, LANE), F32)] * 2
     diag_cost = pl.CostEstimate(
         flops=2 * insts * diagonal_blocks.size, bytes_accessed=2 * diagonal_blocks.size,
@@ -486,59 +540,54 @@
         name="tables",
     )()
     freq, _ = lax.optimization_barrier((frequency, spread))
-    entries = pl.pallas_call(
-        functools.partial(coupler_kernel, spectral, second),
-        out_shape=jax.ShapeDtypeStruct((NI, width), F32),
-        in_specs=[smem, vmem],
-        out_specs=vmem,
-        compiler_params=params,
-        name="couplers",
-    )(freq, spread)
-    flux, hot, pool, *outgoing = pl.pallas_call(
-        first_kernel,
-        out_shape=[flux_shape, hot_shape, pool_shape] + out_shapes,
-        in_specs=[smem] + [vmem] * 6,
-        out_specs=[vmem] * (3 + len(out_shapes)),
+    flux, hot, entries, pool, *outgoing = pl.pallas_call(
+        functools.partial(first_kernel, spectral, second),
+        out_shape=[flux_shape, hot_shape, entry_shape, pool_shape] + out_shapes,
+        in_specs=[smem] * 2 + [vmem] * 6,
+        out_specs=[vmem] * (4 + len(out_shapes)),
         compiler_params=params,
         cost_estimate=pl.CostEstimate(flops=10**10, bytes_accessed=10**6, transcendentals=0),
         name="first_traces",
-    )(place, order, initial_state, trace_wide, send_list, flux_jacobian, sources)
-    state, _ = lax.optimization_barrier((initial_state, entries))
-    states, got = exchange(state, outgoing)
+    )(place, freq, order, initial_state, trace_wide, send_list, flux_jacobian, sources)
+    got = exchange(outgoing)
     base = pl.pallas_call(
         base_kernel,
         out_shape=wide_shape,
-        in_specs=[vmem] * 3,
+        in_specs=[vmem] * 4,
         out_specs=vmem,
         scratch_shapes=chunks,
         compiler_params=params,
         cost_estimate=diag_cost,
         name="own_terms",
-    )(state, diagonal_blocks, forcing)
-    state, pool, *outgoing = pl.pallas_call(
-        functools.partial(step_kernel, parts, ranks),
-        out_shape=[like(initial_state), pool_shape] + out_shapes,
-        in_specs=[smem] + [vmem] * (ranks + slots + 9),
+    )(initial_state, diagonal_blocks, forcing, entries)
+    partial, message, *outgoing = pl.pallas_call(
+        functools.partial(step_kernel, parts),
+        out_shape=[wide_shape, message_shape] + out_shapes,
+        in_specs=[smem] + [vmem] * (slots + 9),
         out_specs=[vmem] * (2 + len(out_shapes)),
         compiler_params=params,
         name="first_step",
-    )(place, entries, spread, *got, *states, pool, base, hot, flux, lift_wide, trace_wide,
-      send_list)
-    states, got = exchange(state, outgoing)
-    base, part, factors = pl.pallas_call(
-        last_base_kernel,
-        out_shape=[wide_shape] * 2 + [factor_shape],
-        in_specs=[vmem] * 9,
-        out_specs=[vmem] * 3,
+    )(place, spread, *got, initial_state, pool, base, hot, flux, lift_wide, trace_wide, send_list)
+    messages = [
+        lax.ppermute(message, "inst", [((i + rank) % ranks, i) for i in range(ranks)])
+        for rank in range(1, ranks)
+    ]
+    got = exchange(outgoing)
+    state, base, factors, mend = pl.pallas_call(
+        functools.partial(last_base_kernel, ranks),
+        out_shape=[like(initial_state), wide_shape, factor_shape, mend_shape],
+        in_specs=[vmem] * (ranks + 9),
+        out_specs=[vmem] * 4,
         scratch_shapes=chunks,
         compiler_params=params,
         cost_estimate=diag_cost,
         name="last_own_terms",
-    )(state, diagonal_blocks, forcing, pool, hot, flux, spread, lift_wide, entries)
+    )(partial, initial_state, *messages, diagonal_blocks, forcing, trace_wide, hot, flux, spread,
+      lift_wide, entries)
     return pl.pallas_call(
-        functools.partial(last_kernel, parts, ranks),
+        functools.partial(last_kernel, parts),
         out_shape=[like(initial_state), wide_shape],
-        in_specs=[smem] + [vmem] * (ranks + slots + 6),
+        in_specs=[smem] + [vmem] * (slots + 6),
         out_specs=[pl.BlockSpec(memory_space=pl.ANY)] * 2,
         scratch_shapes=[
             pltpu.VMEM(initial_state.shape, BF16),
@@ -547,7 +596,7 @@
         ],
         compiler_params=params,
         name="last_step",
-    )(place, entries, *got, *states, base, part, hot, factors, lift_wide)
+    )(place, *got, state, base, hot, factors, mend, lift_wide)
 
 
 def solution(mesh):

time: 19 us -> 19.1 us (level)
  Pallas kernels: 4.67 us -> 4.91 us
  starting transfers between devices: 11.8 us -> 11.6 us
    ppermute x2 -> x1, starting transfers between devices: 3.15 us -> 2.02 us  [on_device(): lax.ppermute(message, 'inst', [((i + rank) % ranks, i) for i in range(ran...]
    ppermute x8, starting transfers between devices: 8.6 us -> 9.61 us  [exchange(): lax.ppermute(outgoing[swap], ('inst', 'dom'), routes[swap])]
    ppermute x8, waiting for transfers between devices: 0.86 us -> 0.23 us  [exchange(): lax.ppermute(outgoing[swap], ('inst', 'dom'), routes[swap])]
    ppermute x2 -> x1, waiting for transfers between devices: 0.01 us -> 0.52 us  [on_device(): lax.ppermute(message, 'inst', [((i + rank) % ranks, i) for i in range(ran...]
    pallas_call x6 -> x5, Pallas kernels: 4.5 us -> 4.73 us  [the longest x1 1.43 us: on_device(): pl.pallas_call(functools.partial(last_base_kernel, ranks), out_shape=[lik...]
  transfers between devices with their start and end apart: 10 -> 9, of which waited for: 3 -> 3; matrix products, arithmetic and copies ran while one was open for 0% -> 0% of each run, Pallas kernels for 13% -> 11%
where the time goes in v4:
time: 19.1 us; the launch traced here: 18.9 us
  starting transfers between devices  11.6 us (61%)
  Pallas kernels  4.91 us (26%)
  between operations  1.42 us (7%)
  waiting for transfers between devices  0.75 us (4%)
  local copies, waits for them, and re-layouts  0.22 us (1%)
    ppermute x8, starting transfers between devices, exchange(): lax.ppermute(outgoing[swap], ('inst', 'dom'), routes[swap])  9.61 us
    ppermute x1, starting transfers between devices, on_device(): lax.ppermute(message, 'inst', [((i + rank) % ranks, i) for i in range(ran...  2.02 us
    pallas_call x1, Pallas kernels, on_device(): pl.pallas_call(functools.partial(last_base_kernel, ranks), out_shape=[lik...  1.43 us
    pallas_call x1, Pallas kernels, on_device(): pl.pallas_call(functools.partial(last_kernel, parts), out_shape=[like(ini...  1.22 us
    pallas_call x1, Pallas kernels, on_device(): pl.pallas_call(functools.partial(step_kernel, parts), out_shape=[wide_sha...  0.92 us
    pallas_call x1, Pallas kernels, on_device(): pl.pallas_call(base_kernel, out_shape=wide_shape, in_specs=[vmem] * 4, ou...  0.7 us
    ppermute x1, waiting for transfers between devices, on_device(): lax.ppermute(message, 'inst', [((i + rank) % ranks, i) for i in range(ran...  0.52 us
    pallas_call x1, Pallas kernels, on_device(): pl.pallas_call(functools.partial(first_kernel, spectral, second), out_sha...  0.46 us
  transfers between devices with their start and end apart: 9, of which 3 were waited for; matrix products, arithmetic and copies ran while one was open for 0% of the time, Pallas kernels for 11%

profile of v4, /device:TPU:0, one launch (start us, length us, event | category | flops | bytes accessed | tf_op | source)
XLA Modules:
  0.0 18.9 jit_solution(5136774378514638703)
XLA Ops:
  0.6 0.0 copy-start.2
  0.6 0.0 copy-start.3
  0.7 0.0 copy-start.5
  0.7 0.0 copy-start.6
  0.7 0.0 copy-start.7
  0.7 0.2 tables.1
  1.5 0.1 copy-done.2
  1.7 0.0 copy-done.6
  1.7 0.5 %first_traces.1 = (bf16[96,640]{1,0:T(8,128)(2,1)S(1)}, bf16[96,128]{1,0:T(8,128)(2,1)S(1)}, f32[8,320]{1,0:T(8,128)S(1)}, bf16[96,512]{1,0:T(8,128)(2,1)S(1)}, ...) custom-call(s32[1]{0:T(128)} %bitcast.place_ref, ...), custom_call_target="tpu_custom_call" | custom-call | flops 10000000000 | bytes 1000000 | tf_op jit(solution)/shard_map/first_traces/pallas_call | solution.py:543
  2.2 0.0 copy-start.1
  2.2 3.0 %collective-permute-start = (bf16[8,512]{1,0:T(8,128)(2,1)S(1)}, bf16[8,512]{1,0:T(8,128)(2,1)S(1)}, u32[]{:S(2)}, u32[]{:S(2)}) collective-permute-start(bf16[8,512]{1,0:T(8,128)(2,1)S(1)} %get-tuple-element.26), channel_id=1, source_target_pairs={{2,4},{3,5},{6,8},{7,9},{10,12},{11,13},{18,20},{19,21},{22,24},{2... | collective-permute-start | bytes 24584 | tf_op jit(solution)/shard_map/ppermute | solution.py:518
  5.2 0.1 collective-permute-start.1
  5.3 1.5 %collective-permute-start.2 = (bf16[8,512]{1,0:T(8,128)(2,1)S(1)}, bf16[8,512]{1,0:T(8,128)(2,1)S(1)}, u32[]{:S(2)}, u32[]{:S(2)}) collective-permute-start(bf16[8,512]{1,0:T(8,128)(2,1)S(1)} %get-tuple-element.28), channel_id=1, source_target_pairs={{0,2},{1,3},{4,6},{5,7},{8,10},{9,11},{12,14},{13,15},{16,18},{17,... | collective-permute-start | bytes 24584 | tf_op jit(solution)/shard_map/ppermute | solution.py:518
  6.8 1.2 %collective-permute-start.3 = (bf16[8,512]{1,0:T(8,128)(2,1)S(1)}, bf16[8,512]{1,0:T(8,128)(2,1)S(1)}, u32[]{:S(2)}, u32[]{:S(2)}) collective-permute-start(bf16[8,512]{1,0:T(8,128)(2,1)S(1)} %get-tuple-element.29), channel_id=1, source_target_pairs={{0,1},{2,3},{4,5},{6,7},{8,9},{10,11},{12,13},{14,15},{16,17},{18,... | collective-permute-start | bytes 24584 | tf_op jit(solution)/shard_map/ppermute | solution.py:518
  8.0 0.7 %own_terms.1.refs_6_ = f32[4,16,320]{2,1,0:T(8,128)S(1)} custom-call(bf16[4,16,320]{2,1,0:T(8,128)(2,1)S(1)} %copy-done.3, bf16[16,320,320]{2,1,0:T(8,128)(2,1)S(1)} %copy-done, bf16[4,16,320]{2,1,0:T(8,128)(2,1)S(1)} %copy-done.4, f32[8,320]{1,0:T(8,128)S(1)} %get-tuple-element.31.entry_ref.refs_8_), custom_call_target="tpu_custom_call" | custom-call | flops 13107200 | bytes 3276800 | tf_op jit(solution)/shard_map/own_terms/pallas_call | solution.py:553
  8.7 0.0 collective-permute-done.refs_0_
  8.7 0.1 collective-permute-done.1.refs_1_
  8.9 0.1 collective-permute-done.2.refs_2_
  8.9 0.0 collective-permute-done.3.refs_3_
  8.9 0.9 %first_step.1 = (f32[4,16,320]{2,1,0:T(8,128)S(1)}, bf16[192,384]{1,0:T(8,128)(2,1)S(1)}, bf16[8,512]{1,0:T(8,128)(2,1)S(1)}, bf16[8,512]{1,0:T(8,128)(2,1)S(1)}...) custom-call(s32[1]{0:T(128)} %bitcast.place_ref, bf16[128,640]{1,0:T(8,128)(2,1)S(1)} %get-tuple-element.23.spread_ref.refs_6_, ...), custom_call_target="tpu_custom_call" | custom-call | tf_op jit(solution)/shard_map/first_step/pallas_call | solution.py:563
  9.9 2.0 %collective-permute-start.8 = (bf16[192,384]{1,0:T(8,128)(2,1)S(1)}, bf16[192,384]{1,0:T(8,128)(2,1)S(1)}, u32[]{:S(2)}, u32[]{:S(2)}) collective-permute-start(bf16[192,384]{1,0:T(8,128)(2,1)S(1)} %get-tuple-element.39), channel_id=1, source_target_pairs={{16,0},{0,16},{17,1},{1,17},{18,2},{2,18},{19,3},{3,19},{20,4},{4,... | collective-permute-start | bytes 442376 | tf_op jit(solution)/shard_map/ppermute | solution.py:572
  11.9 0.1 collective-permute-start.4
  12.0 1.9 %collective-permute-start.5 = (bf16[8,512]{1,0:T(8,128)(2,1)S(1)}, bf16[8,512]{1,0:T(8,128)(2,1)S(1)}, u32[]{:S(2)}, u32[]{:S(2)}) collective-permute-start(bf16[8,512]{1,0:T(8,128)(2,1)S(1)} %get-tuple-element.35), channel_id=1, source_target_pairs={{1,2},{3,4},{5,6},{7,8},{9,10},{11,12},{13,14},{17,18},{19,20},{21... | collective-permute-start | bytes 24584 | tf_op jit(solution)/shard_map/ppermute | solution.py:518
  13.9 1.1 %collective-permute-start.6 = (bf16[8,512]{1,0:T(8,128)(2,1)S(1)}, bf16[8,512]{1,0:T(8,128)(2,1)S(1)}, u32[]{:S(2)}, u32[]{:S(2)}) collective-permute-start(bf16[8,512]{1,0:T(8,128)(2,1)S(1)} %get-tuple-element.36), channel_id=1, source_target_pairs={{0,2},{1,3},{4,6},{5,7},{8,10},{9,11},{12,14},{13,15},{16,18},{17,... | collective-permute-start | bytes 24584 | tf_op jit(solution)/shard_map/ppermute | solution.py:518
  15.0 0.7 %collective-permute-start.7 = (bf16[8,512]{1,0:T(8,128)(2,1)S(1)}, bf16[8,512]{1,0:T(8,128)(2,1)S(1)}, u32[]{:S(2)}, u32[]{:S(2)}) collective-permute-start(bf16[8,512]{1,0:T(8,128)(2,1)S(1)} %get-tuple-element.37), channel_id=1, source_target_pairs={{0,1},{2,3},{4,5},{6,7},{8,9},{10,11},{12,13},{14,15},{16,17},{18,... | collective-permute-start | bytes 24584 | tf_op jit(solution)/shard_map/ppermute | solution.py:518
  15.7 0.5 %collective-permute-done.8.refs_0_ = bf16[192,384]{1,0:T(8,128)(2,1)S(1)} collective-permute-done((bf16[192,384]{1,0:T(8,128)(2,1)S(1)}, bf16[192,384]{1,0:T(8,128)(2,1)S(1)}, u32[]{:S(2)}, u32[]{:S(2)}) %collective-permute-start.8) | collective-permute-done | bytes 147488 | tf_op jit(solution)/shard_map/ppermute | solution.py:572
  16.2 1.4 %last_own_terms.1 = (bf16[4,16,320]{2,1,0:T(8,128)(2,1)S(1)}, f32[4,16,320]{2,1,0:T(8,128)S(1)}, f32[32,1024]{1,0:T(8,128)S(1)}, f32[32,512]{1,0:T(8,128)S(1)}) custom-call(f32[4,16,320]{2,1,0:T(8,128)S(1)} %get-tuple-element.38.partial_ref, bf16[4,16,320]{2,1,0:T(8,128)(2,1)S(1)} %copy-done.3, bf16[192,384]{1,0:T(8,128)(2,1)S(1)} %collective-permute-done.8.refs_0_, ...), custom_call_target="tpu_custom_call" | custom-call | flops 13107200 | bytes 3276800 | tf_op jit(solution)/shard_map/last_own_terms/pallas_call | solution.py:576
  17.7 0.0 collective-permute-done.4.refs_0_
  17.7 0.0 collective-permute-done.5.refs_1_
  17.7 0.0 collective-permute-done.6.refs_2_
  17.7 0.0 collective-permute-done.7.refs_3_
  17.7 1.2 %last_step.1 = (bf16[4,16,320]{2,1,0:T(8,128)(2,1)}, f32[4,16,320]{2,1,0:T(8,128)}) custom-call(s32[1]{0:T(128)} %bitcast.place_ref, bf16[8,512]{1,0:T(8,128)(2,1)S(1)} %collective-permute-done.4.refs_0_, bf16[8,512]{1,0:T(8,128)(2,1)S(1)} %collective-permute-done.5.refs_1_, bf16[8,512]{1,0:T(8,128)(2,1)S(1)} %collective-permute-done.6.refs_2_, ...), custom_call_target="tpu_custom_call" | custom-call | tf_op jit(solution)/shard_map/last_step/pallas_call | solution.py:587
  (8 shorter events, 0.0 us)
Async XLA Ops:
  0.6 1.0 %copy-start.2 = (bf16[320,768]{1,0:T(8,128)(2,1)S(1)}, bf16[320,768]{1,0:T(8,128)(2,1)}, u32[]{:S(2)}) copy-start(bf16[320,768]{1,0:T(8,128)(2,1)} %constant.8.clone.trace_ref.refs_10_.refs_3_) | copy-start | bytes 1474564
  0.6 1.0 %copy-start.3 = (bf16[4,16,320]{2,1,0:T(8,128)(2,1)S(1)}, bf16[4,16,320]{2,1,0:T(8,128)(2,1)}, u32[]{:S(2)}) copy-start(bf16[4,16,320]{2,1,0:T(8,128)(2,1)} %first_ref.1) | copy-start | bytes 122884
  0.7 1.0 %copy-start.5 = (s32[1,4,8]{2,1,0:T(4,128)S(1)}, s32[1,4,8]{2,1,0:T(4,128)}, u32[]{:S(2)}) copy-start(s32[1,4,8]{2,1,0:T(4,128)} %refs_11_.1) | copy-start | bytes 388
  0.7 1.0 %copy-start.6 = (bf16[16,2400]{1,0:T(8,128)(2,1)S(1)}, bf16[16,2400]{1,0:T(8,128)(2,1)}, u32[]{:S(2)}) copy-start(bf16[16,2400]{1,0:T(8,128)(2,1)} %flux_ref.1) | copy-start | bytes 230404
  0.7 1.0 %copy-start.7 = (s32[16,6]{0,1:T(8,128)S(1)}, s32[16,6]{0,1:T(8,128)}, u32[]{:S(2)}) copy-start(s32[16,6]{0,1:T(8,128)} %param.14) | copy-start | bytes 1156
  1.7 6.3 %copy-start = (bf16[16,320,320]{2,1,0:T(8,128)(2,1)S(1)}, bf16[16,320,320]{2,1,0:T(8,128)(2,1)}, u32[]{:S(2)}) copy-start(bf16[16,320,320]{2,1,0:T(8,128)(2,1)} %refs_1_.1) | copy-start | bytes 9830404
  1.7 6.3 %copy-start.4 = (bf16[4,16,320]{2,1,0:T(8,128)(2,1)S(1)}, bf16[4,16,320]{2,1,0:T(8,128)(2,1)}, u32[]{:S(2)}) copy-start(bf16[4,16,320]{2,1,0:T(8,128)(2,1)} %refs_2_.1) | copy-start | bytes 122884
  2.2 6.7 %copy-start.1 = (bf16[768,320]{1,0:T(8,128)(2,1)S(1)}, bf16[768,320]{1,0:T(8,128)(2,1)}, u32[]{:S(2)}) copy-start(bf16[768,320]{1,0:T(8,128)(2,1)} %constant.9.clone.refs_9_.refs_7_) | copy-start | bytes 1474564
  2.2 6.5 %collective-permute-start = (bf16[8,512]{1,0:T(8,128)(2,1)S(1)}, bf16[8,512]{1,0:T(8,128)(2,1)S(1)}, u32[]{:S(2)}, u32[]{:S(2)}) collective-permute-start(bf16[8,512]{1,0:T(8,128)(2,1)S(1)} %get-tuple-element.26), channel_id=1, source_target_pairs={{2,4},{3,5},{6,8},{7,9},{10,12},{11,13},{18,20},{19,21},{22,24},{2... | collective-permute-start | bytes 24584 | tf_op jit(solution)/shard_map/ppermute | solution.py:518
  5.2 3.7 %collective-permute-start.1 = (bf16[8,512]{1,0:T(8,128)(2,1)S(1)}, bf16[8,512]{1,0:T(8,128)(2,1)S(1)}, u32[]{:S(2)}, u32[]{:S(2)}) collective-permute-start(bf16[8,512]{1,0:T(8,128)(2,1)S(1)} %get-tuple-element.27), channel_id=1, source_target_pairs={{1,2},{3,4},{5,6},{7,8},{9,10},{11,12},{13,14},{17,18},{19,20},{21... | collective-permute-start | bytes 24584 | tf_op jit(solution)/shard_map/ppermute | solution.py:518
  5.3 3.7 %collective-permute-start.2 = (bf16[8,512]{1,0:T(8,128)(2,1)S(1)}, bf16[8,512]{1,0:T(8,128)(2,1)S(1)}, u32[]{:S(2)}, u32[]{:S(2)}) collective-permute-start(bf16[8,512]{1,0:T(8,128)(2,1)S(1)} %get-tuple-element.28), channel_id=1, source_target_pairs={{0,2},{1,3},{4,6},{5,7},{8,10},{9,11},{12,14},{13,15},{16,18},{17,... | collective-permute-start | bytes 24584 | tf_op jit(solution)/shard_map/ppermute | solution.py:518
  6.8 2.1 %collective-permute-start.3 = (bf16[8,512]{1,0:T(8,128)(2,1)S(1)}, bf16[8,512]{1,0:T(8,128)(2,1)S(1)}, u32[]{:S(2)}, u32[]{:S(2)}) collective-permute-start(bf16[8,512]{1,0:T(8,128)(2,1)S(1)} %get-tuple-element.29), channel_id=1, source_target_pairs={{0,1},{2,3},{4,5},{6,7},{8,9},{10,11},{12,13},{14,15},{16,17},{18,... | collective-permute-start | bytes 24584 | tf_op jit(solution)/shard_map/ppermute | solution.py:518
  9.9 6.4 %collective-permute-start.8 = (bf16[192,384]{1,0:T(8,128)(2,1)S(1)}, bf16[192,384]{1,0:T(8,128)(2,1)S(1)}, u32[]{:S(2)}, u32[]{:S(2)}) collective-permute-start(bf16[192,384]{1,0:T(8,128)(2,1)S(1)} %get-tuple-element.39), channel_id=1, source_target_pairs={{16,0},{0,16},{17,1},{1,17},{18,2},{2,18},{19,3},{3,19},{20,4},{4,... | collective-permute-start | bytes 442376 | tf_op jit(solution)/shard_map/ppermute | solution.py:572
  11.9 5.8 %collective-permute-start.4 = (bf16[8,512]{1,0:T(8,128)(2,1)S(1)}, bf16[8,512]{1,0:T(8,128)(2,1)S(1)}, u32[]{:S(2)}, u32[]{:S(2)}) collective-permute-start(bf16[8,512]{1,0:T(8,128)(2,1)S(1)} %get-tuple-element.34), channel_id=1, source_target_pairs={{2,4},{3,5},{6,8},{7,9},{10,12},{11,13},{18,20},{19,21},{22,24},{2... | collective-permute-start | bytes 24584 | tf_op jit(solution)/shard_map/ppermute | solution.py:518
  12.0 5.7 %collective-permute-start.5 = (bf16[8,512]{1,0:T(8,128)(2,1)S(1)}, bf16[8,512]{1,0:T(8,128)(2,1)S(1)}, u32[]{:S(2)}, u32[]{:S(2)}) collective-permute-start(bf16[8,512]{1,0:T(8,128)(2,1)S(1)} %get-tuple-element.35), channel_id=1, source_target_pairs={{1,2},{3,4},{5,6},{7,8},{9,10},{11,12},{13,14},{17,18},{19,20},{21... | collective-permute-start | bytes 24584 | tf_op jit(solution)/shard_map/ppermute | solution.py:518
  13.9 3.8 %collective-permute-start.6 = (bf16[8,512]{1,0:T(8,128)(2,1)S(1)}, bf16[8,512]{1,0:T(8,128)(2,1)S(1)}, u32[]{:S(2)}, u32[]{:S(2)}) collective-permute-start(bf16[8,512]{1,0:T(8,128)(2,1)S(1)} %get-tuple-element.36), channel_id=1, source_target_pairs={{0,2},{1,3},{4,6},{5,7},{8,10},{9,11},{12,14},{13,15},{16,18},{17,... | collective-permute-start | bytes 24584 | tf_op jit(solution)/shard_map/ppermute | solution.py:518
  15.0 2.7 %collective-permute-start.7 = (bf16[8,512]{1,0:T(8,128)(2,1)S(1)}, bf16[8,512]{1,0:T(8,128)(2,1)S(1)}, u32[]{:S(2)}, u32[]{:S(2)}) collective-permute-start(bf16[8,512]{1,0:T(8,128)(2,1)S(1)} %get-tuple-element.37), channel_id=1, source_target_pairs={{0,1},{2,3},{4,5},{6,7},{8,9},{10,11},{12,13},{14,15},{16,17},{18,... | collective-permute-start | bytes 24584 | tf_op jit(solution)/shard_map/ppermute | solution.py:518

commit v5 on v4

--- a/solution.py
+++ b/solution.py
@@ -323,65 +323,50 @@
         entry_ref[d : d + 1, :] = jnp.full((1, width), entry, F32)
 
 
-def base_kernel(state_ref, diag_ref, forcing_ref, entry_ref, base_ref, wide_ref, prod_ref):
+def base_kernel(state_ref, diag_ref, forcing_ref, entry_ref, prod_out_ref, rest_ref, wide_ref,
+                prod_ref):
     insts, elems, width = state_ref.shape
     states = [state_ref[t] for t in range(insts)]
     products = diagonal(states, diag_ref, wide_ref, prod_ref, insts, elems)
     for t in range(insts):
-        own = couple(entry_ref, states, t, 0, insts)
-        base_ref[t] = products[t] + own - forcing_ref[t].astype(F32)
-
-
-def message_rows(insts, elems, slots):
-    per_row = pl.cdiv(WIDE, LANE)
-    tall = insts * elems
-    return tall, 2 * tall, 2 * tall + pl.cdiv(insts, per_row) * slots
-
-
-def fill_message(message_ref, states, partial, blocks, insts, elems):
-    slots = blocks.shape[0]
-    per_row = pl.cdiv(WIDE, LANE)
-    first, second, last = message_rows(insts, elems, slots)
-    message_ref[...] = jnp.zeros_like(message_ref)
-    for t in range(insts):
-        message_ref[t * elems : (t + 1) * elems, 0:WIDE] = states[t]
-        message_ref[first + t * elems : first + (t + 1) * elems, 0:WIDE] = partial[t]
-        low, at = second + t // per_row * slots, t % per_row * LANE
-        message_ref[low : low + slots, at : at + LANE] = blocks[:, t * LANE : (t + 1) * LANE]
-
-
-def from_message(message_ref, insts, elems, slots):
-    per_row = pl.cdiv(WIDE, LANE)
-    first, second, last = message_rows(insts, elems, slots)
-    states = [message_ref[t * elems : (t + 1) * elems, 0:WIDE] for t in range(insts)]
-    partial = [
-        message_ref[first + t * elems : first + (t + 1) * elems, 0:WIDE] for t in range(insts)
-    ]
-    blocks = []
-    for t in range(insts):
-        low, at = second + t // per_row * slots, t % per_row * LANE
-        blocks.append(message_ref[low : low + slots, at : at + LANE])
-    return states, partial, blocks
-
-
-def last_base_kernel(ranks, partial_ref, first_ref, *refs):
-    messages, refs = refs[: ranks - 1], refs[ranks - 1 :]
-    (diag_ref, forcing_ref, trace_ref, hot_ref, flux_ref, spread_ref, lift_ref, entry_ref,
-     state_ref, base_ref, factor_ref, mend_ref, wide_ref, prod_ref) = refs
-    insts, elems, width = first_ref.shape
+        prod_out_ref[t] = products[t]
+        rest_ref[t] = couple(entry_ref, states, t, 0, insts) - forcing_ref[t].astype(F32)
+
+
+def last_base_kernel(state_ref, pool_ref, diag_ref, forcing_ref, hot_ref, flux_ref, spread_ref,
+                     lift_ref, base_ref, factor_ref, wide_ref, prod_ref):
+    insts, elems, width = state_ref.shape
     flux = flux_ref[...]
     hot = hot_ref[...]
     faces = hot.shape[0]
-    slots = hot.shape[1] - faces
-
+    factors = lax.dot_general(hot, flux, (((0,), (0,)), ((), ())), preferred_element_type=F32)
+    factor_ref[...] = rotated(factors[faces:])
+    empty = jnp.zeros((hot.shape[1] - faces, insts * LANE), BF16)
+    pool = jnp.concatenate([pool_ref[...], empty], 0)
+    picked = jnp.dot(hot, pool, preferred_element_type=F32).astype(BF16)
+    normal = face_flux(picked, flux.astype(F32), spread_ref[...], insts)
+    lifted = lift_faces(normal, lift_ref[...], elems)
+    states = [state_ref[t].astype(BF16) for t in range(insts)]
+    products = diagonal(states, diag_ref, wide_ref, prod_ref, insts, elems)
+    for t in range(insts):
+        base_ref[t] = (
+            products[t] + lifted[t * elems : (t + 1) * elems] - forcing_ref[t].astype(F32)
+        )
+
+
+def message_kernel(ranks, partial_ref, first_ref, base_ref, entry_ref, *refs):
+    message_refs, (state_ref, out_ref) = refs[: ranks - 1], refs[ranks - 1 :]
+    insts, elems, width = base_ref.shape
     firsts = [[first_ref[t] for t in range(insts)]]
     partials = [[partial_ref[t] for t in range(insts)]]
-    traces = [None]
-    for message_ref in messages:
-        states, partial, blocks = from_message(message_ref, insts, elems, slots)
-        firsts.append(states)
-        partials.append(partial)
-        traces.append(blocks)
+    spatial = [None]
+    for message_ref in message_refs:
+        rows = [
+            message_ref[i * elems : (i + 1) * elems, 0:width] for i in range(3 * insts)
+        ]
+        firsts.append(rows[:insts])
+        partials.append(rows[insts : 2 * insts])
+        spatial.append(rows[2 * insts :])
     states = []
     for k in range(ranks):
         of_rank = []
@@ -394,33 +379,12 @@
         states.append(of_rank)
     for t in range(insts):
         state_ref[t] = states[0][t]
-    for t in range(insts):
-        mend = jnp.zeros((slots, LANE), F32)
-        for k in range(1, ranks):
-            for s in range(insts):
-                d = (t - s - k * insts) % NI
-                mend -= pseudo_step * entry_ref[d : d + 1, 0:LANE] * traces[k][s].astype(F32)
-        mend_ref[:, t * LANE : (t + 1) * LANE] = mend
-
-    pool = trace_pool(jnp.concatenate(states[0], 0), trace_ref[...], insts, elems)
-    factors = lax.dot_general(hot, flux, (((0,), (0,)), ((), ())), preferred_element_type=F32)
-    factor_ref[...] = rotated(factors[faces:])
-    empty = jnp.zeros((slots, insts * LANE), BF16)
-    pool = jnp.concatenate([pool, empty], 0)
-    picked = jnp.dot(hot, pool, preferred_element_type=F32).astype(BF16)
-    normal = face_flux(picked, flux.astype(F32), spread_ref[...], insts)
-    lifted = lift_faces(normal, lift_ref[...], elems)
-    products = diagonal(states[0], diag_ref, wide_ref, prod_ref, insts, elems)
-    for t in range(insts):
         coupling = couple(entry_ref, states[0], t, 0, insts)
+        missing = jnp.zeros((elems, width), F32)
         for k in range(1, ranks):
             coupling += couple(entry_ref, states[k], t, -k, insts)
-        base_ref[t] = (
-            products[t]
-            + lifted[t * elems : (t + 1) * elems]
-            + coupling.astype(BF16).astype(F32)
-            - forcing_ref[t].astype(F32)
-        )
+            missing += couple(entry_ref, spatial[k], t, -k, insts)
+        out_ref[t] = base_ref[t] + coupling.astype(BF16).astype(F32) - pseudo_step * missing
 
 
 def received(parts, place, got_refs):
@@ -436,8 +400,8 @@
 
 def step_kernel(parts, place_ref, spread_ref, *refs):
     got_refs, refs = refs[: len(OFFSETS)], refs[len(OFFSETS) :]
-    (state_ref, pool_ref, base_ref, hot_ref, flux_ref, lift_ref, trace_ref, send_ref,
-     partial_ref, message_ref, *out_refs) = refs
+    (state_ref, pool_ref, prod_ref, rest_ref, hot_ref, flux_ref, lift_ref, trace_ref, send_ref,
+     partial_ref, message_ref, next_pool_ref, *out_refs) = refs
     insts, elems, width = state_ref.shape
     place = place_ref[0]
     blocks = received(parts, place, got_refs).astype(BF16)
@@ -445,23 +409,27 @@
     picked = jnp.dot(hot_ref[...], pool, preferred_element_type=F32).astype(BF16)
     normal = face_flux(picked, flux_ref[...].astype(F32), spread_ref[...], insts)
     lifted = lift_faces(normal, lift_ref[...], elems)
+    message_ref[...] = jnp.zeros_like(message_ref)
     fresh = []
     for t in range(insts):
-        residual = base_ref[t] + lifted[t * elems : (t + 1) * elems]
-        moved = state_ref[t].astype(F32) - pseudo_step * residual
+        spatial = prod_ref[t] + lifted[t * elems : (t + 1) * elems]
+        moved = state_ref[t].astype(F32) - pseudo_step * (spatial + rest_ref[t])
         partial_ref[t] = moved
         fresh.append(moved.astype(BF16))
-    fill_message(message_ref, [state_ref[t] for t in range(insts)], fresh, blocks, insts, elems)
+        for i, block in enumerate((state_ref[t], fresh[t], spatial.astype(BF16))):
+            low = (i * insts + t) * elems
+            message_ref[low : low + elems, 0:width] = block
     pool = trace_pool(jnp.concatenate(fresh, 0), trace_ref[...], insts, elems)
+    next_pool_ref[...] = pool
     fill_outgoing(pool, send_ref[0], out_refs, place, elems)
 
 
 def last_kernel(parts, place_ref, *refs):
     got_refs, refs = refs[: len(OFFSETS)], refs[len(OFFSETS) :]
-    (state_ref, base_ref, hot_ref, factor_ref, mend_ref, lift_ref, final_hbm, residual_hbm,
+    (state_ref, base_ref, hot_ref, factor_ref, lift_ref, final_hbm, residual_hbm,
      final_ref, residual_ref, sems) = refs
     insts, elems, width = state_ref.shape
-    blocks = received(parts, place_ref[0], got_refs) + mend_ref[...]
+    blocks = received(parts, place_ref[0], got_refs)
     normal = slot_normal(blocks, factor_ref[...], insts)
     empty = jnp.zeros((FACES * elems, insts * LANE), BF16)
     rows = jnp.concatenate([empty, jnp.concatenate(normal, 1)], 0)
@@ -519,10 +487,7 @@
         ]
 
     entry_shape = jax.ShapeDtypeStruct((NI, width), F32)
-    mend_shape = jax.ShapeDtypeStruct((slots * capacity, insts * LANE), F32)
-    message_shape = jax.ShapeDtypeStruct(
-        (message_rows(insts, elems, slots * capacity)[-1], pl.cdiv(width, LANE) * LANE), BF16
-    )
+    message_shape = jax.ShapeDtypeStruct((3 * insts * elems, pl.cdiv(width, LANE) * LANE), BF16)
     chunks = [pltpu.VMEM((pl.cdiv(width, LANE) * insts * elems, LANE), F32)] * 2
     diag_cost = pl.CostEstimate(
         flops=2 * insts * diagonal_blocks.size, bytes_accessed=2 * diagonal_blocks.size,
@@ -550,44 +515,52 @@
         name="first_traces",
     )(place, freq, order, initial_state, trace_wide, send_list, flux_jacobian, sources)
     got = exchange(outgoing)
-    base = pl.pallas_call(
+    product, rest = pl.pallas_call(
         base_kernel,
-        out_shape=wide_shape,
+        out_shape=[wide_shape] * 2,
         in_specs=[vmem] * 4,
-        out_specs=vmem,
+        out_specs=[vmem] * 2,
         scratch_shapes=chunks,
         compiler_params=params,
         cost_estimate=diag_cost,
         name="own_terms",
     )(initial_state, diagonal_blocks, forcing, entries)
-    partial, message, *outgoing = pl.pallas_call(
+    partial, message, pool, *outgoing = pl.pallas_call(
         functools.partial(step_kernel, parts),
-        out_shape=[wide_shape, message_shape] + out_shapes,
-        in_specs=[smem] + [vmem] * (slots + 9),
-        out_specs=[vmem] * (2 + len(out_shapes)),
+        out_shape=[wide_shape, message_shape, pool_shape] + out_shapes,
+        in_specs=[smem] + [vmem] * (slots + 10),
+        out_specs=[vmem] * (3 + len(out_shapes)),
         compiler_params=params,
         name="first_step",
-    )(place, spread, *got, initial_state, pool, base, hot, flux, lift_wide, trace_wide, send_list)
+    )(place, spread, *got, initial_state, pool, product, rest, hot, flux, lift_wide, trace_wide,
+      send_list)
     messages = [
         lax.ppermute(message, "inst", [((i + rank) % ranks, i) for i in range(ranks)])
         for rank in range(1, ranks)
     ]
     got = exchange(outgoing)
-    state, base, factors, mend = pl.pallas_call(
-        functools.partial(last_base_kernel, ranks),
-        out_shape=[like(initial_state), wide_shape, factor_shape, mend_shape],
-        in_specs=[vmem] * (ranks + 9),
-        out_specs=[vmem] * 4,
+    base, factors = pl.pallas_call(
+        last_base_kernel,
+        out_shape=[wide_shape, factor_shape],
+        in_specs=[vmem] * 8,
+        out_specs=[vmem] * 2,
         scratch_shapes=chunks,
         compiler_params=params,
         cost_estimate=diag_cost,
         name="last_own_terms",
-    )(partial, initial_state, *messages, diagonal_blocks, forcing, trace_wide, hot, flux, spread,
-      lift_wide, entries)
+    )(partial, pool, diagonal_blocks, forcing, hot, flux, spread, lift_wide)
+    state, base = pl.pallas_call(
+        functools.partial(message_kernel, ranks),
+        out_shape=[like(initial_state), wide_shape],
+        in_specs=[vmem] * (ranks + 3),
+        out_specs=[vmem] * 2,
+        compiler_params=params,
+        name="message_terms",
+    )(partial, initial_state, base, entries, *messages)
     return pl.pallas_call(
         functools.partial(last_kernel, parts),
         out_shape=[like(initial_state), wide_shape],
-        in_specs=[smem] + [vmem] * (slots + 6),
+        in_specs=[smem] + [vmem] * (slots + 5),
         out_specs=[pl.BlockSpec(memory_space=pl.ANY)] * 2,
         scratch_shapes=[
             pltpu.VMEM(initial_state.shape, BF16),
@@ -596,7 +569,7 @@
         ],
         compiler_params=params,
         name="last_step",
-    )(place, *got, state, base, hot, factors, mend, lift_wide)
+    )(place, *got, state, base, hot, factors, lift_wide)
 
 
 def solution(mesh):

time: 19.1 us -> 18.9 us (0.990)
    ppermute x1, waiting for transfers between devices: 0.52 us -> 0.01 us  [on_device(): lax.ppermute(message, 'inst', [((i + rank) % ranks, i) for i in range(ran...]
    ppermute x8, waiting for transfers between devices: 0.23 us -> 0.67 us  [exchange(): lax.ppermute(outgoing[swap], ('inst', 'dom'), routes[swap])]
    pallas_call x2 -> x3, Pallas kernels: 2.13 us -> 2.08 us  [the longest x1 1.22 us: on_device(): pl.pallas_call(last_base_kernel, out_shape=[wide_shape, factor_shape], in...]
where the time goes in v5:
time: 18.9 us; the launch traced here: 18.7 us
  starting transfers between devices  11.6 us (61%)
  Pallas kernels  4.81 us (25%)
  between operations  1.41 us (7%)
  waiting for transfers between devices  0.67 us (4%)
  local copies, waits for them, and re-layouts  0.22 us (1%)
    ppermute x8, starting transfers between devices, exchange(): lax.ppermute(outgoing[swap], ('inst', 'dom'), routes[swap])  9.61 us
    ppermute x1, starting transfers between devices, on_device(): lax.ppermute(message, 'inst', [((i + rank) % ranks, i) for i in range(ran...  2.02 us
    pallas_call x1, Pallas kernels, on_device(): pl.pallas_call(last_base_kernel, out_shape=[wide_shape, factor_shape], in...  1.22 us
    pallas_call x1, Pallas kernels, on_device(): pl.pallas_call(functools.partial(last_kernel, parts), out_shape=[like(ini...  1.17 us
    pallas_call x1, Pallas kernels, on_device(): pl.pallas_call(functools.partial(step_kernel, parts), out_shape=[wide_sha...  0.92 us
    ppermute x8, waiting for transfers between devices, exchange(): lax.ppermute(outgoing[swap], ('inst', 'dom'), routes[swap])  0.67 us
    pallas_call x1, Pallas kernels, on_device(): pl.pallas_call(base_kernel, out_shape=[wide_shape] * 2, in_specs=[vmem] *...  0.67 us
    pallas_call x1, Pallas kernels, on_device(): pl.pallas_call(functools.partial(first_kernel, spectral, second), out_sha...  0.46 us
  transfers between devices with their start and end apart: 9, of which 3 were waited for; matrix products, arithmetic and copies ran while one was open for 0% of the time, Pallas kernels for 11%

profile of v5, /device:TPU:0, one launch (start us, length us, event | category | flops | bytes accessed | tf_op | source)
XLA Modules:
  0.0 18.7 jit_solution(5205151527814301253)
XLA Ops:
  0.6 0.0 copy-start.2
  0.6 0.0 copy-start.3
  0.7 0.0 copy-start.5
  0.7 0.2 tables.1
  1.5 0.1 copy-done.2
  1.7 0.0 copy-done.6
  1.7 0.5 %first_traces.1 = (bf16[96,640]{1,0:T(8,128)(2,1)S(1)}, bf16[96,128]{1,0:T(8,128)(2,1)S(1)}, f32[8,320]{1,0:T(8,128)S(1)}, bf16[96,512]{1,0:T(8,128)(2,1)S(1)}, ...) custom-call(s32[1]{0:T(128)} %bitcast.place_ref, ...), custom_call_target="tpu_custom_call" | custom-call | flops 10000000000 | bytes 1000000 | tf_op jit(solution)/shard_map/first_traces/pallas_call | solution.py:508
  2.2 0.0 copy-start.1
  2.2 3.0 %collective-permute-start = (bf16[8,512]{1,0:T(8,128)(2,1)S(1)}, bf16[8,512]{1,0:T(8,128)(2,1)S(1)}, u32[]{:S(2)}, u32[]{:S(2)}) collective-permute-start(bf16[8,512]{1,0:T(8,128)(2,1)S(1)} %get-tuple-element.29), channel_id=1, source_target_pairs={{2,4},{3,5},{6,8},{7,9},{10,12},{11,13},{18,20},{19,21},{22,24},{2... | collective-permute-start | bytes 24584 | tf_op jit(solution)/shard_map/ppermute | solution.py:486
  5.2 0.1 collective-permute-start.1
  5.3 1.5 %collective-permute-start.2 = (bf16[8,512]{1,0:T(8,128)(2,1)S(1)}, bf16[8,512]{1,0:T(8,128)(2,1)S(1)}, u32[]{:S(2)}, u32[]{:S(2)}) collective-permute-start(bf16[8,512]{1,0:T(8,128)(2,1)S(1)} %get-tuple-element.31), channel_id=1, source_target_pairs={{0,2},{1,3},{4,6},{5,7},{8,10},{9,11},{12,14},{13,15},{16,18},{17,... | collective-permute-start | bytes 24584 | tf_op jit(solution)/shard_map/ppermute | solution.py:486
  6.8 1.2 %collective-permute-start.3 = (bf16[8,512]{1,0:T(8,128)(2,1)S(1)}, bf16[8,512]{1,0:T(8,128)(2,1)S(1)}, u32[]{:S(2)}, u32[]{:S(2)}) collective-permute-start(bf16[8,512]{1,0:T(8,128)(2,1)S(1)} %get-tuple-element.32), channel_id=1, source_target_pairs={{0,1},{2,3},{4,5},{6,7},{8,9},{10,11},{12,13},{14,15},{16,17},{18,... | collective-permute-start | bytes 24584 | tf_op jit(solution)/shard_map/ppermute | solution.py:486
  8.0 0.0 copy-done.4
  8.0 0.7 %own_terms.1 = (f32[4,16,320]{2,1,0:T(8,128)S(1)}, f32[4,16,320]{2,1,0:T(8,128)S(1)}) custom-call(bf16[4,16,320]{2,1,0:T(8,128)(2,1)S(1)} %copy-done.3, bf16[16,320,320]{2,1,0:T(8,128)(2,1)S(1)} %copy-done, bf16[4,16,320]{2,1,0:T(8,128)(2,1)S(1)} %copy-done.4, f32[8,320]{1,0:T(8,128)S(1)} %get-tuple-element.34.entry_ref), custom_call_target="tpu_custom_call" | custom-call | flops 13107200 | bytes 3276800 | tf_op jit(solution)/shard_map/own_terms/pallas_call | solution.py:518
  8.7 0.0 collective-permute-done.refs_0_
  8.7 0.2 collective-permute-done.1.refs_1_
  8.9 0.1 collective-permute-done.2.refs_2_
  8.9 0.0 collective-permute-done.3.refs_3_
  8.9 0.9 %first_step.1 = (f32[4,16,320]{2,1,0:T(8,128)S(1)}, bf16[192,384]{1,0:T(8,128)(2,1)S(1)}, bf16[96,512]{1,0:T(8,128)(2,1)S(1)}, bf16[8,512]{1,0:T(8,128)(2,1)S(1)...) custom-call(s32[1]{0:T(128)} %bitcast.place_ref, ...), custom_call_target="tpu_custom_call" | custom-call | tf_op jit(solution)/shard_map/first_step/pallas_call | solution.py:528
  9.9 2.0 %collective-permute-start.8 = (bf16[192,384]{1,0:T(8,128)(2,1)S(1)}, bf16[192,384]{1,0:T(8,128)(2,1)S(1)}, u32[]{:S(2)}, u32[]{:S(2)}) collective-permute-start(bf16[192,384]{1,0:T(8,128)(2,1)S(1)} %get-tuple-element.46), channel_id=1, source_target_pairs={{16,0},{0,16},{17,1},{1,17},{18,2},{2,18},{19,3},{3,19},{20,4},{4,... | collective-permute-start | bytes 442376 | tf_op jit(solution)/shard_map/ppermute | solution.py:538
  11.9 0.1 collective-permute-start.4
  12.0 1.9 %collective-permute-start.5 = (bf16[8,512]{1,0:T(8,128)(2,1)S(1)}, bf16[8,512]{1,0:T(8,128)(2,1)S(1)}, u32[]{:S(2)}, u32[]{:S(2)}) collective-permute-start(bf16[8,512]{1,0:T(8,128)(2,1)S(1)} %get-tuple-element.40), channel_id=1, source_target_pairs={{1,2},{3,4},{5,6},{7,8},{9,10},{11,12},{13,14},{17,18},{19,20},{21... | collective-permute-start | bytes 24584 | tf_op jit(solution)/shard_map/ppermute | solution.py:486
  13.9 1.1 %collective-permute-start.6 = (bf16[8,512]{1,0:T(8,128)(2,1)S(1)}, bf16[8,512]{1,0:T(8,128)(2,1)S(1)}, u32[]{:S(2)}, u32[]{:S(2)}) collective-permute-start(bf16[8,512]{1,0:T(8,128)(2,1)S(1)} %get-tuple-element.41), channel_id=1, source_target_pairs={{0,2},{1,3},{4,6},{5,7},{8,10},{9,11},{12,14},{13,15},{16,18},{17,... | collective-permute-start | bytes 24584 | tf_op jit(solution)/shard_map/ppermute | solution.py:486
  15.0 0.7 %collective-permute-start.7 = (bf16[8,512]{1,0:T(8,128)(2,1)S(1)}, bf16[8,512]{1,0:T(8,128)(2,1)S(1)}, u32[]{:S(2)}, u32[]{:S(2)}) collective-permute-start(bf16[8,512]{1,0:T(8,128)(2,1)S(1)} %get-tuple-element.42), channel_id=1, source_target_pairs={{0,1},{2,3},{4,5},{6,7},{8,9},{10,11},{12,13},{14,15},{16,17},{18,... | collective-permute-start | bytes 24584 | tf_op jit(solution)/shard_map/ppermute | solution.py:486
  15.7 1.2 %last_own_terms.1 = (f32[4,16,320]{2,1,0:T(8,128)S(1)}, f32[32,1024]{1,0:T(8,128)S(1)}) custom-call(f32[4,16,320]{2,1,0:T(8,128)S(1)} %get-tuple-element.43.state_ref.partial_ref, bf16[96,512]{1,0:T(8,128)(2,1)S(1)} %get-tuple-element.44.pool_ref, bf16[16,320,320]{2,1,0:T(8,128)(2,1)S(1)} %copy-done, bf16[4,16,320]{2,1,0:T(8,128)(2,1)S(1)} %copy-done.4, ...), custom_call_target="tpu_custom_call" | custom-call | flops 13107200 | bytes 3276800 | tf_op jit(solution)/shard_map/last_own_terms/pallas_call | solution.py:542
  16.9 0.0 collective-permute-done.8.refs_0_
  16.9 0.2 message_terms.1
  17.1 0.0 collective-permute-done.4.refs_0_
  17.1 0.0 collective-permute-done.5.refs_1_
  17.2 0.4 %collective-permute-done.6.refs_2_ = bf16[8,512]{1,0:T(8,128)(2,1)S(1)} collective-permute-done((bf16[8,512]{1,0:T(8,128)(2,1)S(1)}, bf16[8,512]{1,0:T(8,128)(2,1)S(1)}, u32[]{:S(2)}, u32[]{:S(2)}) %collective-permute-start.6) | collective-permute-done | bytes 8224 | tf_op jit(solution)/shard_map/ppermute | solution.py:486
  17.6 0.0 collective-permute-done.7.refs_3_
  17.6 1.2 %last_step.1 = (bf16[4,16,320]{2,1,0:T(8,128)(2,1)}, f32[4,16,320]{2,1,0:T(8,128)}) custom-call(s32[1]{0:T(128)} %bitcast.place_ref, bf16[8,512]{1,0:T(8,128)(2,1)S(1)} %collective-permute-done.4.refs_0_, bf16[8,512]{1,0:T(8,128)(2,1)S(1)} %collective-permute-done.5.refs_1_, bf16[8,512]{1,0:T(8,128)(2,1)S(1)} %collective-permute-done.6.refs_2_, ...), custom_call_target="tpu_custom_call" | custom-call | tf_op jit(solution)/shard_map/last_step/pallas_call | solution.py:560
  (9 shorter events, 0.0 us)
Async XLA Ops:
  0.6 1.0 %copy-start.2 = (bf16[320,768]{1,0:T(8,128)(2,1)S(1)}, bf16[320,768]{1,0:T(8,128)(2,1)}, u32[]{:S(2)}) copy-start(bf16[320,768]{1,0:T(8,128)(2,1)} %constant.8.clone.trace_ref.refs_11_) | copy-start | bytes 1474564
  0.6 1.0 %copy-start.3 = (bf16[4,16,320]{2,1,0:T(8,128)(2,1)S(1)}, bf16[4,16,320]{2,1,0:T(8,128)(2,1)}, u32[]{:S(2)}) copy-start(bf16[4,16,320]{2,1,0:T(8,128)(2,1)} %first_ref.1) | copy-start | bytes 122884
  0.7 1.0 %copy-start.5 = (s32[1,4,8]{2,1,0:T(4,128)S(1)}, s32[1,4,8]{2,1,0:T(4,128)}, u32[]{:S(2)}) copy-start(s32[1,4,8]{2,1,0:T(4,128)} %refs_12_.1) | copy-start | bytes 388
  0.7 1.0 %copy-start.6 = (bf16[16,2400]{1,0:T(8,128)(2,1)S(1)}, bf16[16,2400]{1,0:T(8,128)(2,1)}, u32[]{:S(2)}) copy-start(bf16[16,2400]{1,0:T(8,128)(2,1)} %flux_ref.1) | copy-start | bytes 230404
  0.7 1.0 %copy-start.7 = (s32[16,6]{0,1:T(8,128)S(1)}, s32[16,6]{0,1:T(8,128)}, u32[]{:S(2)}) copy-start(s32[16,6]{0,1:T(8,128)} %param.14) | copy-start | bytes 1156
  1.7 6.3 %copy-start = (bf16[16,320,320]{2,1,0:T(8,128)(2,1)S(1)}, bf16[16,320,320]{2,1,0:T(8,128)(2,1)}, u32[]{:S(2)}) copy-start(bf16[16,320,320]{2,1,0:T(8,128)(2,1)} %diag_ref.3) | copy-start | bytes 9830404
  1.7 6.3 %copy-start.4 = (bf16[4,16,320]{2,1,0:T(8,128)(2,1)S(1)}, bf16[4,16,320]{2,1,0:T(8,128)(2,1)}, u32[]{:S(2)}) copy-start(bf16[4,16,320]{2,1,0:T(8,128)(2,1)} %forcing_ref.3) | copy-start | bytes 122884
  2.2 6.7 %copy-start.1 = (bf16[768,320]{1,0:T(8,128)(2,1)S(1)}, bf16[768,320]{1,0:T(8,128)(2,1)}, u32[]{:S(2)}) copy-start(bf16[768,320]{1,0:T(8,128)(2,1)} %constant.9.clone.refs_10_.lift_ref.refs_8_) | copy-start | bytes 1474564
  2.2 6.5 %collective-permute-start = (bf16[8,512]{1,0:T(8,128)(2,1)S(1)}, bf16[8,512]{1,0:T(8,128)(2,1)S(1)}, u32[]{:S(2)}, u32[]{:S(2)}) collective-permute-start(bf16[8,512]{1,0:T(8,128)(2,1)S(1)} %get-tuple-element.29), channel_id=1, source_target_pairs={{2,4},{3,5},{6,8},{7,9},{10,12},{11,13},{18,20},{19,21},{22,24},{2... | collective-permute-start | bytes 24584 | tf_op jit(solution)/shard_map/ppermute | solution.py:486
  5.2 3.7 %collective-permute-start.1 = (bf16[8,512]{1,0:T(8,128)(2,1)S(1)}, bf16[8,512]{1,0:T(8,128)(2,1)S(1)}, u32[]{:S(2)}, u32[]{:S(2)}) collective-permute-start(bf16[8,512]{1,0:T(8,128)(2,1)S(1)} %get-tuple-element.30), channel_id=1, source_target_pairs={{1,2},{3,4},{5,6},{7,8},{9,10},{11,12},{13,14},{17,18},{19,20},{21... | collective-permute-start | bytes 24584 | tf_op jit(solution)/shard_map/ppermute | solution.py:486
  5.3 3.7 %collective-permute-start.2 = (bf16[8,512]{1,0:T(8,128)(2,1)S(1)}, bf16[8,512]{1,0:T(8,128)(2,1)S(1)}, u32[]{:S(2)}, u32[]{:S(2)}) collective-permute-start(bf16[8,512]{1,0:T(8,128)(2,1)S(1)} %get-tuple-element.31), channel_id=1, source_target_pairs={{0,2},{1,3},{4,6},{5,7},{8,10},{9,11},{12,14},{13,15},{16,18},{17,... | collective-permute-start | bytes 24584 | tf_op jit(solution)/shard_map/ppermute | solution.py:486
  6.8 2.1 %collective-permute-start.3 = (bf16[8,512]{1,0:T(8,128)(2,1)S(1)}, bf16[8,512]{1,0:T(8,128)(2,1)S(1)}, u32[]{:S(2)}, u32[]{:S(2)}) collective-permute-start(bf16[8,512]{1,0:T(8,128)(2,1)S(1)} %get-tuple-element.32), channel_id=1, source_target_pairs={{0,1},{2,3},{4,5},{6,7},{8,9},{10,11},{12,13},{14,15},{16,17},{18,... | collective-permute-start | bytes 24584 | tf_op jit(solution)/shard_map/ppermute | solution.py:486
  9.9 7.1 %collective-permute-start.8 = (bf16[192,384]{1,0:T(8,128)(2,1)S(1)}, bf16[192,384]{1,0:T(8,128)(2,1)S(1)}, u32[]{:S(2)}, u32[]{:S(2)}) collective-permute-start(bf16[192,384]{1,0:T(8,128)(2,1)S(1)} %get-tuple-element.46), channel_id=1, source_target_pairs={{16,0},{0,16},{17,1},{1,17},{18,2},{2,18},{19,3},{3,19},{20,4},{4,... | collective-permute-start | bytes 442376 | tf_op jit(solution)/shard_map/ppermute | solution.py:538
  11.9 5.2 %collective-permute-start.4 = (bf16[8,512]{1,0:T(8,128)(2,1)S(1)}, bf16[8,512]{1,0:T(8,128)(2,1)S(1)}, u32[]{:S(2)}, u32[]{:S(2)}) collective-permute-start(bf16[8,512]{1,0:T(8,128)(2,1)S(1)} %get-tuple-element.39), channel_id=1, source_target_pairs={{2,4},{3,5},{6,8},{7,9},{10,12},{11,13},{18,20},{19,21},{22,24},{2... | collective-permute-start | bytes 24584 | tf_op jit(solution)/shard_map/ppermute | solution.py:486
  12.0 5.2 %collective-permute-start.5 = (bf16[8,512]{1,0:T(8,128)(2,1)S(1)}, bf16[8,512]{1,0:T(8,128)(2,1)S(1)}, u32[]{:S(2)}, u32[]{:S(2)}) collective-permute-start(bf16[8,512]{1,0:T(8,128)(2,1)S(1)} %get-tuple-element.40), channel_id=1, source_target_pairs={{1,2},{3,4},{5,6},{7,8},{9,10},{11,12},{13,14},{17,18},{19,20},{21... | collective-permute-start | bytes 24584 | tf_op jit(solution)/shard_map/ppermute | solution.py:486
  13.9 3.7 %collective-permute-start.6 = (bf16[8,512]{1,0:T(8,128)(2,1)S(1)}, bf16[8,512]{1,0:T(8,128)(2,1)S(1)}, u32[]{:S(2)}, u32[]{:S(2)}) collective-permute-start(bf16[8,512]{1,0:T(8,128)(2,1)S(1)} %get-tuple-element.41), channel_id=1, source_target_pairs={{0,2},{1,3},{4,6},{5,7},{8,10},{9,11},{12,14},{13,15},{16,18},{17,... | collective-permute-start | bytes 24584 | tf_op jit(solution)/shard_map/ppermute | solution.py:486
  15.0 2.5 %collective-permute-start.7 = (bf16[8,512]{1,0:T(8,128)(2,1)S(1)}, bf16[8,512]{1,0:T(8,128)(2,1)S(1)}, u32[]{:S(2)}, u32[]{:S(2)}) collective-permute-start(bf16[8,512]{1,0:T(8,128)(2,1)S(1)} %get-tuple-element.42), channel_id=1, source_target_pairs={{0,1},{2,3},{4,5},{6,7},{8,9},{10,11},{12,13},{14,15},{16,17},{18,... | collective-permute-start | bytes 24584 | tf_op jit(solution)/shard_map/ppermute | solution.py:486

commit v6 on v5

--- a/solution.py
+++ b/solution.py
@@ -100,7 +100,8 @@
 BF16 = jnp.bfloat16
 F32 = jnp.float32
 OFFSETS = list(range(-REACH, 0)) + list(range(1, REACH + 1))
-SWAP_ORDER = (3, 1, 2, 0)
+FIRST_ORDER = (3, 1, 2, 0)
+LAST_ORDER = (2, 1, 3, 0)
 
 
 def wide_tables():
@@ -159,7 +160,9 @@
     for pairs in near + far:
         met = {p for pair in pairs for p in pair}
         alone = [p for p in range(parts) if p not in met]
-        swaps = [(r * parts + p, r * parts + q) for r in range(ranks) for p, q in pairs]
+        idle = [(p, p + 1) for p in alone if p + 1 in alone]
+        alone = [p for p in alone if p + 1 not in alone and p - 1 not in alone]
+        swaps = [(r * parts + p, r * parts + q) for r in range(ranks) for p, q in pairs + idle]
         swaps += [(r * parts + p, (r ^ 1) * parts + p) for r in range(0, ranks, 2) for p in alone]
         routes.append(swaps + [(q, p) for p, q in swaps])
     return routes
@@ -387,8 +390,8 @@
         out_ref[t] = base_ref[t] + coupling.astype(BF16).astype(F32) - pseudo_step * missing
 
 
-def received(parts, place, got_refs):
-    got_refs = {swap: got_refs[i] for i, swap in enumerate(SWAP_ORDER)}
+def received(parts, place, got_refs, order):
+    got_refs = {swap: got_refs[i] for i, swap in enumerate(order)}
     arrived = by_offset(
         place, [got_refs[swap][...].astype(F32) for swap in range(len(OFFSETS))]
     )
@@ -404,7 +407,7 @@
      partial_ref, message_ref, next_pool_ref, *out_refs) = refs
     insts, elems, width = state_ref.shape
     place = place_ref[0]
-    blocks = received(parts, place, got_refs).astype(BF16)
+    blocks = received(parts, place, got_refs, FIRST_ORDER).astype(BF16)
     pool = jnp.concatenate([pool_ref[...], blocks], 0)
     picked = jnp.dot(hot_ref[...], pool, preferred_element_type=F32).astype(BF16)
     normal = face_flux(picked, flux_ref[...].astype(F32), spread_ref[...], insts)
@@ -429,7 +432,7 @@
     (state_ref, base_ref, hot_ref, factor_ref, lift_ref, final_hbm, residual_hbm,
      final_ref, residual_ref, sems) = refs
     insts, elems, width = state_ref.shape
-    blocks = received(parts, place_ref[0], got_refs)
+    blocks = received(parts, place_ref[0], got_refs, LAST_ORDER)
     normal = slot_normal(blocks, factor_ref[...], insts)
     empty = jnp.zeros((FACES * elems, insts * LANE), BF16)
     rows = jnp.concatenate([empty, jnp.concatenate(normal, 1)], 0)
@@ -481,9 +484,9 @@
     hot_shape = jax.ShapeDtypeStruct((faces, faces + slots * capacity), BF16)
     factor_shape = jax.ShapeDtypeStruct((slots * capacity, LANE // FPTS * LANE), F32)
 
-    def exchange(outgoing):
+    def exchange(outgoing, order):
         return [
-            lax.ppermute(outgoing[swap], ("inst", "dom"), routes[swap]) for swap in SWAP_ORDER
+            lax.ppermute(outgoing[swap], ("inst", "dom"), routes[swap]) for swap in order
         ]
 
     entry_shape = jax.ShapeDtypeStruct((NI, width), F32)
@@ -514,7 +517,7 @@
         cost_estimate=pl.CostEstimate(flops=10**10, bytes_accessed=10**6, transcendentals=0),
         name="first_traces",
     )(place, freq, order, initial_state, trace_wide, send_list, flux_jacobian, sources)
-    got = exchange(outgoing)
+    got = exchange(outgoing, FIRST_ORDER)
     product, rest = pl.pallas_call(
         base_kernel,
         out_shape=[wide_shape] * 2,
@@ -538,7 +541,7 @@
         lax.ppermute(message, "inst", [((i + rank) % ranks, i) for i in range(ranks)])
         for rank in range(1, ranks)
     ]
-    got = exchange(outgoing)
+    got = exchange(outgoing, LAST_ORDER)
     base, factors = pl.pallas_call(
         last_base_kernel,
         out_shape=[wide_shape, factor_shape],

time: 18.9 us -> 18 us (0.952)
  starting transfers between devices: 11.6 us -> 9.91 us
  waiting for transfers between devices: 0.67 us -> 1.43 us
    ppermute x8, starting transfers between devices: 9.61 us -> 8.47 us  [exchange(): lax.ppermute(outgoing[swap], ('inst', 'dom'), routes[swap])]
    ppermute x1, waiting for transfers between devices: 0.01 us -> 0.91 us  [on_device(): lax.ppermute(message, 'inst', [((i + rank) % ranks, i) for i in range(ran...]
    ppermute x1, starting transfers between devices: 2.02 us -> 1.45 us  [on_device(): lax.ppermute(message, 'inst', [((i + rank) % ranks, i) for i in range(ran...]
  transfers between devices with their start and end apart: 9 -> 9, of which waited for: 3 -> 3; matrix products, arithmetic and copies ran while one was open for 0% -> 0% of each run, Pallas kernels for 11% -> 12%
where the time goes in v6:
time: 18 us; the launch traced here: 17.8 us
  starting transfers between devices  9.91 us (55%)
  Pallas kernels  4.81 us (27%)
  waiting for transfers between devices  1.43 us (8%)
  between operations  1.41 us (8%)
  local copies, waits for them, and re-layouts  0.22 us (1%)
    ppermute x8, starting transfers between devices, exchange(): lax.ppermute(outgoing[swap], ('inst', 'dom'), routes[swap])  8.47 us
    ppermute x1, starting transfers between devices, on_device(): lax.ppermute(message, 'inst', [((i + rank) % ranks, i) for i in range(ran...  1.45 us
    pallas_call x1, Pallas kernels, on_device(): pl.pallas_call(last_base_kernel, out_shape=[wide_shape, factor_shape], in...  1.22 us
    pallas_call x1, Pallas kernels, on_device(): pl.pallas_call(functools.partial(last_kernel, parts), out_shape=[like(ini...  1.17 us
    pallas_call x1, Pallas kernels, on_device(): pl.pallas_call(functools.partial(step_kernel, parts), out_shape=[wide_sha...  0.92 us
    ppermute x1, waiting for transfers between devices, on_device(): lax.ppermute(message, 'inst', [((i + rank) % ranks, i) for i in range(ran...  0.91 us
    pallas_call x1, Pallas kernels, on_device(): pl.pallas_call(base_kernel, out_shape=[wide_shape] * 2, in_specs=[vmem] *...  0.67 us
    ppermute x8, waiting for transfers between devices, exchange(): lax.ppermute(outgoing[swap], ('inst', 'dom'), routes[swap])  0.52 us
  transfers between devices with their start and end apart: 9, of which 3 were waited for; matrix products, arithmetic and copies ran while one was open for 0% of the time, Pallas kernels for 12%

profile of v6, /device:TPU:0, one launch (start us, length us, event | category | flops | bytes accessed | tf_op | source)
XLA Modules:
  0.0 17.8 jit_solution(14432127384111174971)
XLA Ops:
  0.6 0.0 copy-start.2
  0.6 0.0 copy-start.3
  0.7 0.2 %tables.1 = (bf16[128,640]{1,0:T(8,128)(2,1)S(1)}, bf16[400,640]{1,0:T(8,128)(2,1)S(1)}) custom-call(), custom_call_target="tpu_custom_call" | custom-call | flops 10000000000 | bytes 1000000 | tf_op jit(solution)/shard_map/tables/pallas_call | solution.py:499
  1.5 0.1 copy-done.2
  1.7 0.0 copy-done.6
  1.7 0.0 copy-done.7
  1.7 0.5 %first_traces.1 = (bf16[96,640]{1,0:T(8,128)(2,1)S(1)}, bf16[96,128]{1,0:T(8,128)(2,1)S(1)}, f32[8,320]{1,0:T(8,128)S(1)}, bf16[96,512]{1,0:T(8,128)(2,1)S(1)}, ...) custom-call(s32[1]{0:T(128)} %bitcast.place_ref, ...), custom_call_target="tpu_custom_call" | custom-call | flops 10000000000 | bytes 1000000 | tf_op jit(solution)/shard_map/first_traces/pallas_call | solution.py:511
  2.2 0.0 copy-start.1
  2.2 0.5 %collective-permute-start = (bf16[8,512]{1,0:T(8,128)(2,1)S(1)}, bf16[8,512]{1,0:T(8,128)(2,1)S(1)}, u32[]{:S(2)}, u32[]{:S(2)}) collective-permute-start(bf16[8,512]{1,0:T(8,128)(2,1)S(1)} %get-tuple-element.29), channel_id=1, source_target_pairs={{2,4},{3,5},{6,8},{7,9},{10,12},{11,13},{0,1},{14,15},{18,20},{19,... | collective-permute-start | bytes 24584 | tf_op jit(solution)/shard_map/ppermute | solution.py:489
  2.7 2.6 %collective-permute-start.1 = (bf16[8,512]{1,0:T(8,128)(2,1)S(1)}, bf16[8,512]{1,0:T(8,128)(2,1)S(1)}, u32[]{:S(2)}, u32[]{:S(2)}) collective-permute-start(bf16[8,512]{1,0:T(8,128)(2,1)S(1)} %get-tuple-element.30), channel_id=1, source_target_pairs={{1,2},{3,4},{5,6},{7,8},{9,10},{11,12},{13,14},{17,18},{19,20},{21... | collective-permute-start | bytes 24584 | tf_op jit(solution)/shard_map/ppermute | solution.py:489
  5.3 1.5 %collective-permute-start.2 = (bf16[8,512]{1,0:T(8,128)(2,1)S(1)}, bf16[8,512]{1,0:T(8,128)(2,1)S(1)}, u32[]{:S(2)}, u32[]{:S(2)}) collective-permute-start(bf16[8,512]{1,0:T(8,128)(2,1)S(1)} %get-tuple-element.31), channel_id=1, source_target_pairs={{0,2},{1,3},{4,6},{5,7},{8,10},{9,11},{12,14},{13,15},{16,18},{17,... | collective-permute-start | bytes 24584 | tf_op jit(solution)/shard_map/ppermute | solution.py:489
  6.8 1.2 %collective-permute-start.3 = (bf16[8,512]{1,0:T(8,128)(2,1)S(1)}, bf16[8,512]{1,0:T(8,128)(2,1)S(1)}, u32[]{:S(2)}, u32[]{:S(2)}) collective-permute-start(bf16[8,512]{1,0:T(8,128)(2,1)S(1)} %get-tuple-element.32), channel_id=1, source_target_pairs={{0,1},{2,3},{4,5},{6,7},{8,9},{10,11},{12,13},{14,15},{16,17},{18,... | collective-permute-start | bytes 24584 | tf_op jit(solution)/shard_map/ppermute | solution.py:489
  8.0 0.0 copy-done
  8.0 0.7 %own_terms.1 = (f32[4,16,320]{2,1,0:T(8,128)S(1)}, f32[4,16,320]{2,1,0:T(8,128)S(1)}) custom-call(bf16[4,16,320]{2,1,0:T(8,128)(2,1)S(1)} %copy-done.3, bf16[16,320,320]{2,1,0:T(8,128)(2,1)S(1)} %copy-done, bf16[4,16,320]{2,1,0:T(8,128)(2,1)S(1)} %copy-done.4, f32[8,320]{1,0:T(8,128)S(1)} %get-tuple-element.34.entry_ref), custom_call_target="tpu_custom_call" | custom-call | flops 13107200 | bytes 3276800 | tf_op jit(solution)/shard_map/own_terms/pallas_call | solution.py:521
  8.7 0.0 collective-permute-done.refs_0_
  8.7 0.0 collective-permute-done.1.refs_1_
  8.7 0.2 %collective-permute-done.2.refs_2_ = bf16[8,512]{1,0:T(8,128)(2,1)S(1)} collective-permute-done((bf16[8,512]{1,0:T(8,128)(2,1)S(1)}, bf16[8,512]{1,0:T(8,128)(2,1)S(1)}, u32[]{:S(2)}, u32[]{:S(2)}) %collective-permute-start.2) | collective-permute-done | bytes 8224 | tf_op jit(solution)/shard_map/ppermute | solution.py:489
  8.9 0.0 collective-permute-done.3.refs_3_
  8.9 0.9 %first_step.1 = (f32[4,16,320]{2,1,0:T(8,128)S(1)}, bf16[192,384]{1,0:T(8,128)(2,1)S(1)}, bf16[96,512]{1,0:T(8,128)(2,1)S(1)}, bf16[8,512]{1,0:T(8,128)(2,1)S(1)...) custom-call(s32[1]{0:T(128)} %bitcast.place_ref, ...), custom_call_target="tpu_custom_call" | custom-call | tf_op jit(solution)/shard_map/first_step/pallas_call | solution.py:531
  9.9 1.4 %collective-permute-start.8 = (bf16[192,384]{1,0:T(8,128)(2,1)S(1)}, bf16[192,384]{1,0:T(8,128)(2,1)S(1)}, u32[]{:S(2)}, u32[]{:S(2)}) collective-permute-start(bf16[192,384]{1,0:T(8,128)(2,1)S(1)} %get-tuple-element.46), channel_id=1, source_target_pairs={{16,0},{0,16},{17,1},{1,17},{18,2},{2,18},{19,3},{3,19},{20,4},{4,... | collective-permute-start | bytes 442376 | tf_op jit(solution)/shard_map/ppermute | solution.py:541
  11.3 1.6 %collective-permute-start.4 = (bf16[8,512]{1,0:T(8,128)(2,1)S(1)}, bf16[8,512]{1,0:T(8,128)(2,1)S(1)}, u32[]{:S(2)}, u32[]{:S(2)}) collective-permute-start(bf16[8,512]{1,0:T(8,128)(2,1)S(1)} %get-tuple-element.39), channel_id=1, source_target_pairs={{0,2},{1,3},{4,6},{5,7},{8,10},{9,11},{12,14},{13,15},{16,18},{17,... | collective-permute-start | bytes 24584 | tf_op jit(solution)/shard_map/ppermute | solution.py:489
  12.9 0.5 %collective-permute-start.5 = (bf16[8,512]{1,0:T(8,128)(2,1)S(1)}, bf16[8,512]{1,0:T(8,128)(2,1)S(1)}, u32[]{:S(2)}, u32[]{:S(2)}) collective-permute-start(bf16[8,512]{1,0:T(8,128)(2,1)S(1)} %get-tuple-element.40), channel_id=1, source_target_pairs={{1,2},{3,4},{5,6},{7,8},{9,10},{11,12},{13,14},{17,18},{19,20},{21... | collective-permute-start | bytes 24584 | tf_op jit(solution)/shard_map/ppermute | solution.py:489
  13.5 0.0 collective-permute-start.6
  13.5 0.5 %collective-permute-start.7 = (bf16[8,512]{1,0:T(8,128)(2,1)S(1)}, bf16[8,512]{1,0:T(8,128)(2,1)S(1)}, u32[]{:S(2)}, u32[]{:S(2)}) collective-permute-start(bf16[8,512]{1,0:T(8,128)(2,1)S(1)} %get-tuple-element.42), channel_id=1, source_target_pairs={{0,1},{2,3},{4,5},{6,7},{8,9},{10,11},{12,13},{14,15},{16,17},{18,... | collective-permute-start | bytes 24584 | tf_op jit(solution)/shard_map/ppermute | solution.py:489
  14.0 1.2 %last_own_terms.1 = (f32[4,16,320]{2,1,0:T(8,128)S(1)}, f32[32,1024]{1,0:T(8,128)S(1)}) custom-call(f32[4,16,320]{2,1,0:T(8,128)S(1)} %get-tuple-element.43.state_ref.partial_ref, bf16[96,512]{1,0:T(8,128)(2,1)S(1)} %get-tuple-element.44.pool_ref, bf16[16,320,320]{2,1,0:T(8,128)(2,1)S(1)} %copy-done, bf16[4,16,320]{2,1,0:T(8,128)(2,1)S(1)} %copy-done.4, ...), custom_call_target="tpu_custom_call" | custom-call | flops 13107200 | bytes 3276800 | tf_op jit(solution)/shard_map/last_own_terms/pallas_call | solution.py:545
  15.2 0.9 %collective-permute-done.8.refs_0_ = bf16[192,384]{1,0:T(8,128)(2,1)S(1)} collective-permute-done((bf16[192,384]{1,0:T(8,128)(2,1)S(1)}, bf16[192,384]{1,0:T(8,128)(2,1)S(1)}, u32[]{:S(2)}, u32[]{:S(2)}) %collective-permute-start.8) | collective-permute-done | bytes 147488 | tf_op jit(solution)/shard_map/ppermute | solution.py:541
  16.1 0.2 %message_terms.1 = (bf16[4,16,320]{2,1,0:T(8,128)(2,1)S(1)}, f32[4,16,320]{2,1,0:T(8,128)S(1)}) custom-call(f32[4,16,320]{2,1,0:T(8,128)S(1)} %get-tuple-element.43.state_ref.partial_ref, bf16[4,16,320]{2,1,0:T(8,128)(2,1)S(1)} %copy-done.3, f32[4,16,320]{2,1,0:T(8,128)S(1)} %get-tuple-element.45.base_ref, f32[8,320]{1,0:T(8,128)S(1)} %get-tuple-element.34.entry_ref, ...), custom_call_target="tpu_custom_call" | custom-call | tf_op jit(solution)/shard_map/message_terms/pallas_call | solution.py:555
  16.3 0.0 collective-permute-done.4.refs_0_
  16.3 0.3 %collective-permute-done.5.refs_1_ = bf16[8,512]{1,0:T(8,128)(2,1)S(1)} collective-permute-done((bf16[8,512]{1,0:T(8,128)(2,1)S(1)}, bf16[8,512]{1,0:T(8,128)(2,1)S(1)}, u32[]{:S(2)}, u32[]{:S(2)}) %collective-permute-start.5) | collective-permute-done | bytes 8224 | tf_op jit(solution)/shard_map/ppermute | solution.py:489
  16.6 0.0 collective-permute-done.6.refs_2_
  16.6 0.0 collective-permute-done.7.refs_3_
  16.6 1.2 %last_step.1 = (bf16[4,16,320]{2,1,0:T(8,128)(2,1)}, f32[4,16,320]{2,1,0:T(8,128)}) custom-call(s32[1]{0:T(128)} %bitcast.place_ref, bf16[8,512]{1,0:T(8,128)(2,1)S(1)} %collective-permute-done.4.refs_0_, bf16[8,512]{1,0:T(8,128)(2,1)S(1)} %collective-permute-done.5.refs_1_, bf16[8,512]{1,0:T(8,128)(2,1)S(1)} %collective-permute-done.6.refs_2_, ...), custom_call_target="tpu_custom_call" | custom-call | tf_op jit(solution)/shard_map/last_step/pallas_call | solution.py:563
  (9 shorter events, 0.0 us)
Async XLA Ops:
  0.6 1.0 %copy-start.2 = (bf16[320,768]{1,0:T(8,128)(2,1)S(1)}, bf16[320,768]{1,0:T(8,128)(2,1)}, u32[]{:S(2)}) copy-start(bf16[320,768]{1,0:T(8,128)(2,1)} %constant.8.clone.trace_ref.refs_11_) | copy-start | bytes 1474564
  0.6 1.0 %copy-start.3 = (bf16[4,16,320]{2,1,0:T(8,128)(2,1)S(1)}, bf16[4,16,320]{2,1,0:T(8,128)(2,1)}, u32[]{:S(2)}) copy-start(bf16[4,16,320]{2,1,0:T(8,128)(2,1)} %first_ref.1) | copy-start | bytes 122884
  0.7 1.0 %copy-start.5 = (s32[1,4,8]{2,1,0:T(4,128)S(1)}, s32[1,4,8]{2,1,0:T(4,128)}, u32[]{:S(2)}) copy-start(s32[1,4,8]{2,1,0:T(4,128)} %refs_12_.1) | copy-start | bytes 388
  0.7 1.0 %copy-start.6 = (bf16[16,2400]{1,0:T(8,128)(2,1)S(1)}, bf16[16,2400]{1,0:T(8,128)(2,1)}, u32[]{:S(2)}) copy-start(bf16[16,2400]{1,0:T(8,128)(2,1)} %flux_ref.1) | copy-start | bytes 230404
  0.7 1.0 %copy-start.7 = (s32[16,6]{0,1:T(8,128)S(1)}, s32[16,6]{0,1:T(8,128)}, u32[]{:S(2)}) copy-start(s32[16,6]{0,1:T(8,128)} %param.14) | copy-start | bytes 1156
  1.7 6.3 %copy-start = (bf16[16,320,320]{2,1,0:T(8,128)(2,1)S(1)}, bf16[16,320,320]{2,1,0:T(8,128)(2,1)}, u32[]{:S(2)}) copy-start(bf16[16,320,320]{2,1,0:T(8,128)(2,1)} %diag_ref.3) | copy-start | bytes 9830404
  1.7 6.3 %copy-start.4 = (bf16[4,16,320]{2,1,0:T(8,128)(2,1)S(1)}, bf16[4,16,320]{2,1,0:T(8,128)(2,1)}, u32[]{:S(2)}) copy-start(bf16[4,16,320]{2,1,0:T(8,128)(2,1)} %forcing_ref.3) | copy-start | bytes 122884
  2.2 6.7 %copy-start.1 = (bf16[768,320]{1,0:T(8,128)(2,1)S(1)}, bf16[768,320]{1,0:T(8,128)(2,1)}, u32[]{:S(2)}) copy-start(bf16[768,320]{1,0:T(8,128)(2,1)} %constant.9.clone.refs_10_.lift_ref.refs_8_) | copy-start | bytes 1474564
  2.2 6.5 %collective-permute-start = (bf16[8,512]{1,0:T(8,128)(2,1)S(1)}, bf16[8,512]{1,0:T(8,128)(2,1)S(1)}, u32[]{:S(2)}, u32[]{:S(2)}) collective-permute-start(bf16[8,512]{1,0:T(8,128)(2,1)S(1)} %get-tuple-element.29), channel_id=1, source_target_pairs={{2,4},{3,5},{6,8},{7,9},{10,12},{11,13},{0,1},{14,15},{18,20},{19,... | collective-permute-start | bytes 24584 | tf_op jit(solution)/shard_map/ppermute | solution.py:489
  2.7 6.0 %collective-permute-start.1 = (bf16[8,512]{1,0:T(8,128)(2,1)S(1)}, bf16[8,512]{1,0:T(8,128)(2,1)S(1)}, u32[]{:S(2)}, u32[]{:S(2)}) collective-permute-start(bf16[8,512]{1,0:T(8,128)(2,1)S(1)} %get-tuple-element.30), channel_id=1, source_target_pairs={{1,2},{3,4},{5,6},{7,8},{9,10},{11,12},{13,14},{17,18},{19,20},{21... | collective-permute-start | bytes 24584 | tf_op jit(solution)/shard_map/ppermute | solution.py:489
  5.3 3.7 %collective-permute-start.2 = (bf16[8,512]{1,0:T(8,128)(2,1)S(1)}, bf16[8,512]{1,0:T(8,128)(2,1)S(1)}, u32[]{:S(2)}, u32[]{:S(2)}) collective-permute-start(bf16[8,512]{1,0:T(8,128)(2,1)S(1)} %get-tuple-element.31), channel_id=1, source_target_pairs={{0,2},{1,3},{4,6},{5,7},{8,10},{9,11},{12,14},{13,15},{16,18},{17,... | collective-permute-start | bytes 24584 | tf_op jit(solution)/shard_map/ppermute | solution.py:489
  6.8 2.1 %collective-permute-start.3 = (bf16[8,512]{1,0:T(8,128)(2,1)S(1)}, bf16[8,512]{1,0:T(8,128)(2,1)S(1)}, u32[]{:S(2)}, u32[]{:S(2)}) collective-permute-start(bf16[8,512]{1,0:T(8,128)(2,1)S(1)} %get-tuple-element.32), channel_id=1, source_target_pairs={{0,1},{2,3},{4,5},{6,7},{8,9},{10,11},{12,13},{14,15},{16,17},{18,... | collective-permute-start | bytes 24584 | tf_op jit(solution)/shard_map/ppermute | solution.py:489
  9.9 6.3 %collective-permute-start.8 = (bf16[192,384]{1,0:T(8,128)(2,1)S(1)}, bf16[192,384]{1,0:T(8,128)(2,1)S(1)}, u32[]{:S(2)}, u32[]{:S(2)}) collective-permute-start(bf16[192,384]{1,0:T(8,128)(2,1)S(1)} %get-tuple-element.46), channel_id=1, source_target_pairs={{16,0},{0,16},{17,1},{1,17},{18,2},{2,18},{19,3},{3,19},{20,4},{4,... | collective-permute-start | bytes 442376 | tf_op jit(solution)/shard_map/ppermute | solution.py:541
  11.3 5.0 %collective-permute-start.4 = (bf16[8,512]{1,0:T(8,128)(2,1)S(1)}, bf16[8,512]{1,0:T(8,128)(2,1)S(1)}, u32[]{:S(2)}, u32[]{:S(2)}) collective-permute-start(bf16[8,512]{1,0:T(8,128)(2,1)S(1)} %get-tuple-element.39), channel_id=1, source_target_pairs={{0,2},{1,3},{4,6},{5,7},{8,10},{9,11},{12,14},{13,15},{16,18},{17,... | collective-permute-start | bytes 24584 | tf_op jit(solution)/shard_map/ppermute | solution.py:489
  12.9 3.7 %collective-permute-start.5 = (bf16[8,512]{1,0:T(8,128)(2,1)S(1)}, bf16[8,512]{1,0:T(8,128)(2,1)S(1)}, u32[]{:S(2)}, u32[]{:S(2)}) collective-permute-start(bf16[8,512]{1,0:T(8,128)(2,1)S(1)} %get-tuple-element.40), channel_id=1, source_target_pairs={{1,2},{3,4},{5,6},{7,8},{9,10},{11,12},{13,14},{17,18},{19,20},{21... | collective-permute-start | bytes 24584 | tf_op jit(solution)/shard_map/ppermute | solution.py:489
  13.5 3.1 %collective-permute-start.6 = (bf16[8,512]{1,0:T(8,128)(2,1)S(1)}, bf16[8,512]{1,0:T(8,128)(2,1)S(1)}, u32[]{:S(2)}, u32[]{:S(2)}) collective-permute-start(bf16[8,512]{1,0:T(8,128)(2,1)S(1)} %get-tuple-element.41), channel_id=1, source_target_pairs={{2,4},{3,5},{6,8},{7,9},{10,12},{11,13},{0,1},{14,15},{18,20},{19,... | collective-permute-start | bytes 24584 | tf_op jit(solution)/shard_map/ppermute | solution.py:489
  13.5 3.1 %collective-permute-start.7 = (bf16[8,512]{1,0:T(8,128)(2,1)S(1)}, bf16[8,512]{1,0:T(8,128)(2,1)S(1)}, u32[]{:S(2)}, u32[]{:S(2)}) collective-permute-start(bf16[8,512]{1,0:T(8,128)(2,1)S(1)} %get-tuple-element.42), channel_id=1, source_target_pairs={{0,1},{2,3},{4,5},{6,7},{8,9},{10,11},{12,13},{14,15},{16,17},{18,... | collective-permute-start | bytes 24584 | tf_op jit(solution)/shard_map/ppermute | solution.py:489

commit v7 on v6

--- a/solution.py
+++ b/solution.py
@@ -310,25 +310,24 @@
     order_ref[...] = order_table()
 
 
-def first_kernel(spectral, second, place_ref, freq_ref, order_ref, state_ref, trace_ref, send_ref, flux_ref, source_ref,
-                 flux_out_ref, hot_ref, entry_ref, pool_ref, *out_refs):
+def first_kernel(spectral, second, place_ref, freq_ref, spread_ref, state_ref, trace_ref, send_ref,
+                 entry_ref, pool_ref, *out_refs):
     insts, elems, width = state_ref.shape
     state = state_ref[...].reshape(insts * elems, width)
     pool = trace_pool(state, trace_ref[...], insts, elems)
     pool_ref[...] = pool
     fill_outgoing(pool, send_ref[0], out_refs, place_ref[0], elems)
-    slots = send_ref.shape[1] * send_ref.shape[2]
-    hot_ref[...] = source_table(source_ref[...].T, elems, slots)
-    flux_out_ref[...] = flux_order(flux_ref[...], order_ref[...])
     freq = freq_ref[0]
     for d in range(NI):
         entry = freq * float(spectral[d]) - dissipation * float(second[d])
         entry_ref[d : d + 1, :] = jnp.full((1, width), entry, F32)
 
 
-def base_kernel(state_ref, diag_ref, forcing_ref, entry_ref, prod_out_ref, rest_ref, wide_ref,
-                prod_ref):
+def base_kernel(slots, state_ref, diag_ref, forcing_ref, entry_ref, flux_ref, source_ref, order_ref,
+                prod_out_ref, rest_ref, flux_out_ref, hot_ref, wide_ref, prod_ref):
     insts, elems, width = state_ref.shape
+    hot_ref[...] = source_table(source_ref[...].T, elems, slots)
+    flux_out_ref[...] = flux_order(flux_ref[...], order_ref[...])
     states = [state_ref[t] for t in range(insts)]
     products = diagonal(states, diag_ref, wide_ref, prod_ref, insts, elems)
     for t in range(insts):
@@ -362,14 +361,12 @@
     insts, elems, width = base_ref.shape
     firsts = [[first_ref[t] for t in range(insts)]]
     partials = [[partial_ref[t] for t in range(insts)]]
-    spatial = [None]
     for message_ref in message_refs:
         rows = [
-            message_ref[i * elems : (i + 1) * elems, 0:width] for i in range(3 * insts)
+            message_ref[i * elems : (i + 1) * elems, 0:width] for i in range(2 * insts)
         ]
         firsts.append(rows[:insts])
-        partials.append(rows[insts : 2 * insts])
-        spatial.append(rows[2 * insts :])
+        partials.append(rows[insts:])
     states = []
     for k in range(ranks):
         of_rank = []
@@ -378,16 +375,14 @@
             for j in range(ranks):
                 if j != k:
                     state -= pseudo_step * couple(entry_ref, firsts[j], t, k - j, insts)
-            of_rank.append(state.astype(BF16))
+            of_rank.append(state.astype(BF16) if k == 0 else state)
         states.append(of_rank)
     for t in range(insts):
         state_ref[t] = states[0][t]
-        coupling = couple(entry_ref, states[0], t, 0, insts)
-        missing = jnp.zeros((elems, width), F32)
-        for k in range(1, ranks):
+        coupling = base_ref[t]
+        for k in range(ranks):
             coupling += couple(entry_ref, states[k], t, -k, insts)
-            missing += couple(entry_ref, spatial[k], t, -k, insts)
-        out_ref[t] = base_ref[t] + coupling.astype(BF16).astype(F32) - pseudo_step * missing
+        out_ref[t] = coupling
 
 
 def received(parts, place, got_refs, order):
@@ -419,7 +414,8 @@
         moved = state_ref[t].astype(F32) - pseudo_step * (spatial + rest_ref[t])
         partial_ref[t] = moved
         fresh.append(moved.astype(BF16))
-        for i, block in enumerate((state_ref[t], fresh[t], spatial.astype(BF16))):
+        lean = (moved - pseudo_step * spatial).astype(BF16)
+        for i, block in enumerate((state_ref[t], lean)):
             low = (i * insts + t) * elems
             message_ref[low : low + elems, 0:width] = block
     pool = trace_pool(jnp.concatenate(fresh, 0), trace_ref[...], insts, elems)
@@ -490,7 +486,7 @@
         ]
 
     entry_shape = jax.ShapeDtypeStruct((NI, width), F32)
-    message_shape = jax.ShapeDtypeStruct((3 * insts * elems, pl.cdiv(width, LANE) * LANE), BF16)
+    message_shape = jax.ShapeDtypeStruct((2 * insts * elems, pl.cdiv(width, LANE) * LANE), BF16)
     chunks = [pltpu.VMEM((pl.cdiv(width, LANE) * insts * elems, LANE), F32)] * 2
     diag_cost = pl.CostEstimate(
         flops=2 * insts * diagonal_blocks.size, bytes_accessed=2 * diagonal_blocks.size,
@@ -508,26 +504,26 @@
         name="tables",
     )()
     freq, _ = lax.optimization_barrier((frequency, spread))
-    flux, hot, entries, pool, *outgoing = pl.pallas_call(
+    entries, pool, *outgoing = pl.pallas_call(
         functools.partial(first_kernel, spectral, second),
-        out_shape=[flux_shape, hot_shape, entry_shape, pool_shape] + out_shapes,
-        in_specs=[smem] * 2 + [vmem] * 6,
-        out_specs=[vmem] * (4 + len(out_shapes)),
+        out_shape=[entry_shape, pool_shape] + out_shapes,
+        in_specs=[smem] * 2 + [vmem] * 4,
+        out_specs=[vmem] * (2 + len(out_shapes)),
         compiler_params=params,
         cost_estimate=pl.CostEstimate(flops=10**10, bytes_accessed=10**6, transcendentals=0),
         name="first_traces",
-    )(place, freq, order, initial_state, trace_wide, send_list, flux_jacobian, sources)
+    )(place, freq, spread, initial_state, trace_wide, send_list)
     got = exchange(outgoing, FIRST_ORDER)
-    product, rest = pl.pallas_call(
-        base_kernel,
-        out_shape=[wide_shape] * 2,
-        in_specs=[vmem] * 4,
-        out_specs=[vmem] * 2,
+    product, rest, flux, hot = pl.pallas_call(
+        functools.partial(base_kernel, slots * capacity),
+        out_shape=[wide_shape] * 2 + [flux_shape, hot_shape],
+        in_specs=[vmem] * 7,
+        out_specs=[vmem] * 4,
         scratch_shapes=chunks,
         compiler_params=params,
         cost_estimate=diag_cost,
         name="own_terms",
-    )(initial_state, diagonal_blocks, forcing, entries)
+    )(initial_state, diagonal_blocks, forcing, entries, flux_jacobian, sources, order)
     partial, message, pool, *outgoing = pl.pallas_call(
         functools.partial(step_kernel, parts),
         out_shape=[wide_shape, message_shape, pool_shape] + out_shapes,

time: 18 us -> 17.9 us (level)
    ppermute x1, waiting for transfers between devices: 0.91 us -> 0.01 us  [on_device(): lax.ppermute(message, 'inst', [((i + rank) % ranks, i) for i in range(ran...]
    ppermute x8, waiting for transfers between devices: 0.52 us -> 1.3 us  [exchange(): lax.ppermute(outgoing[swap], ('inst', 'dom'), routes[swap])]
  transfers between devices with their start and end apart: 9 -> 9, of which waited for: 3 -> 2; matrix products, arithmetic and copies ran while one was open for 0% -> 0% of each run, Pallas kernels for 12% -> 12%
where the time goes in v7:
time: 17.9 us; the launch traced here: 17.6 us
  starting transfers between devices  9.91 us (55%)
  Pallas kernels  4.79 us (27%)
  between operations  1.42 us (8%)
  waiting for transfers between devices  1.31 us (7%)
  local copies, waits for them, and re-layouts  0.2 us (1%)
    ppermute x8, starting transfers between devices, exchange(): lax.ppermute(outgoing[swap], ('inst', 'dom'), routes[swap])  8.4 us
    ppermute x1, starting transfers between devices, on_device(): lax.ppermute(message, 'inst', [((i + rank) % ranks, i) for i in range(ran...  1.52 us
    ppermute x8, waiting for transfers between devices, exchange(): lax.ppermute(outgoing[swap], ('inst', 'dom'), routes[swap])  1.3 us
    pallas_call x1, Pallas kernels, on_device(): pl.pallas_call(last_base_kernel, out_shape=[wide_shape, factor_shape], in...  1.22 us
    pallas_call x1, Pallas kernels, on_device(): pl.pallas_call(functools.partial(last_kernel, parts), out_shape=[like(ini...  1.17 us
    pallas_call x1, Pallas kernels, on_device(): pl.pallas_call(functools.partial(step_kernel, parts), out_shape=[wide_sha...  0.92 us
    pallas_call x1, Pallas kernels, on_device(): pl.pallas_call(functools.partial(base_kernel, slots * capacity), out_shap...  0.82 us
  transfers between devices with their start and end apart: 9, of which 2 were waited for; matrix products, arithmetic and copies ran while one was open for 0% of the time, Pallas kernels for 12%

profile of v7, /device:TPU:0, one launch (start us, length us, event | category | flops | bytes accessed | tf_op | source)
XLA Modules:
  0.0 17.6 jit_solution(8809559279166891153)
XLA Ops:
  0.6 0.0 copy-start.2
  0.6 0.0 copy-start.3
  0.7 0.0 copy-start.7
  0.7 0.2 %tables.1 = (bf16[128,640]{1,0:T(8,128)(2,1)S(1)}, bf16[400,640]{1,0:T(8,128)(2,1)S(1)}) custom-call(), custom_call_target="tpu_custom_call" | custom-call | flops 10000000000 | bytes 1000000 | tf_op jit(solution)/shard_map/tables/pallas_call | solution.py:495
  1.5 0.2 copy-done.2
  1.7 0.0 copy-start.5
  1.7 0.0 copy-start.6
  1.7 0.3 %first_traces.1 = (f32[8,320]{1,0:T(8,128)S(1)}, bf16[96,512]{1,0:T(8,128)(2,1)S(1)}, bf16[8,512]{1,0:T(8,128)(2,1)S(1)}, bf16[8,512]{1,0:T(8,128)(2,1)S(1)}, bf...) custom-call(s32[1]{0:T(128)} %bitcast.place_ref, f32[1]{0:T(128)S(6)} %copy.11.freq_ref, ...), custom_call_target="tpu_custom_call" | custom-call | flops 10000000000 | bytes 1000000 | tf_op jit(solution)/shard_map/first_traces/pallas_call | solution.py:507
  2.1 0.0 copy-start.1
  2.1 0.5 %collective-permute-start = (bf16[8,512]{1,0:T(8,128)(2,1)S(1)}, bf16[8,512]{1,0:T(8,128)(2,1)S(1)}, u32[]{:S(2)}, u32[]{:S(2)}) collective-permute-start(bf16[8,512]{1,0:T(8,128)(2,1)S(1)} %get-tuple-element.28), channel_id=1, source_target_pairs={{2,4},{3,5},{6,8},{7,9},{10,12},{11,13},{0,1},{14,15},{18,20},{19,... | collective-permute-start | bytes 24584 | tf_op jit(solution)/shard_map/ppermute | solution.py:485
  2.6 2.6 %collective-permute-start.1 = (bf16[8,512]{1,0:T(8,128)(2,1)S(1)}, bf16[8,512]{1,0:T(8,128)(2,1)S(1)}, u32[]{:S(2)}, u32[]{:S(2)}) collective-permute-start(bf16[8,512]{1,0:T(8,128)(2,1)S(1)} %get-tuple-element.29), channel_id=1, source_target_pairs={{1,2},{3,4},{5,6},{7,8},{9,10},{11,12},{13,14},{17,18},{19,20},{21... | collective-permute-start | bytes 24584 | tf_op jit(solution)/shard_map/ppermute | solution.py:485
  5.1 1.5 %collective-permute-start.2 = (bf16[8,512]{1,0:T(8,128)(2,1)S(1)}, bf16[8,512]{1,0:T(8,128)(2,1)S(1)}, u32[]{:S(2)}, u32[]{:S(2)}) collective-permute-start(bf16[8,512]{1,0:T(8,128)(2,1)S(1)} %get-tuple-element.30), channel_id=1, source_target_pairs={{0,2},{1,3},{4,6},{5,7},{8,10},{9,11},{12,14},{13,15},{16,18},{17,... | collective-permute-start | bytes 24584 | tf_op jit(solution)/shard_map/ppermute | solution.py:485
  6.7 1.2 %collective-permute-start.3 = (bf16[8,512]{1,0:T(8,128)(2,1)S(1)}, bf16[8,512]{1,0:T(8,128)(2,1)S(1)}, u32[]{:S(2)}, u32[]{:S(2)}) collective-permute-start(bf16[8,512]{1,0:T(8,128)(2,1)S(1)} %get-tuple-element.31), channel_id=1, source_target_pairs={{0,1},{2,3},{4,5},{6,7},{8,9},{10,11},{12,13},{14,15},{16,17},{18,... | collective-permute-start | bytes 24584 | tf_op jit(solution)/shard_map/ppermute | solution.py:485
  7.9 0.8 %own_terms.1 = (f32[4,16,320]{2,1,0:T(8,128)S(1)}, f32[4,16,320]{2,1,0:T(8,128)S(1)}, bf16[96,640]{1,0:T(8,128)(2,1)S(1)}, bf16[96,128]{1,0:T(8,128)(2,1)S(1)}) custom-call(bf16[4,16,320]{2,1,0:T(8,128)(2,1)S(1)} %copy-done.3, bf16[16,320,320]{2,1,0:T(8,128)(2,1)S(1)} %copy-done, bf16[4,16,320]{2,1,0:T(8,128)(2,1)S(1)} %copy-done.4, ...), custom_call_target="tpu_custom_call" | custom-call | flops 13107200 | bytes 3276800 | tf_op jit(solution)/shard_map/own_terms/pallas_call | solution.py:517
  8.7 0.0 collective-permute-done.refs_0_
  8.7 0.0 collective-permute-done.1.refs_1_
  8.7 0.1 collective-permute-done.2.refs_2_
  8.8 0.0 collective-permute-done.3.refs_3_
  8.8 0.9 %first_step.1 = (f32[4,16,320]{2,1,0:T(8,128)S(1)}, bf16[128,384]{1,0:T(8,128)(2,1)S(1)}, bf16[96,512]{1,0:T(8,128)(2,1)S(1)}, bf16[8,512]{1,0:T(8,128)(2,1)S(1)...) custom-call(s32[1]{0:T(128)} %bitcast.place_ref, ...), custom_call_target="tpu_custom_call" | custom-call | tf_op jit(solution)/shard_map/first_step/pallas_call | solution.py:527
  9.7 1.5 %collective-permute-start.8 = (bf16[128,384]{1,0:T(8,128)(2,1)S(1)}, bf16[128,384]{1,0:T(8,128)(2,1)S(1)}, u32[]{:S(2)}, u32[]{:S(2)}) collective-permute-start(bf16[128,384]{1,0:T(8,128)(2,1)S(1)} %get-tuple-element.46), channel_id=1, source_target_pairs={{16,0},{0,16},{17,1},{1,17},{18,2},{2,18},{19,3},{3,19},{20,4},{4,... | collective-permute-start | bytes 294920 | tf_op jit(solution)/shard_map/ppermute | solution.py:537
  11.2 1.6 %collective-permute-start.4 = (bf16[8,512]{1,0:T(8,128)(2,1)S(1)}, bf16[8,512]{1,0:T(8,128)(2,1)S(1)}, u32[]{:S(2)}, u32[]{:S(2)}) collective-permute-start(bf16[8,512]{1,0:T(8,128)(2,1)S(1)} %get-tuple-element.39), channel_id=1, source_target_pairs={{0,2},{1,3},{4,6},{5,7},{8,10},{9,11},{12,14},{13,15},{16,18},{17,... | collective-permute-start | bytes 24584 | tf_op jit(solution)/shard_map/ppermute | solution.py:485
  12.8 0.5 %collective-permute-start.5 = (bf16[8,512]{1,0:T(8,128)(2,1)S(1)}, bf16[8,512]{1,0:T(8,128)(2,1)S(1)}, u32[]{:S(2)}, u32[]{:S(2)}) collective-permute-start(bf16[8,512]{1,0:T(8,128)(2,1)S(1)} %get-tuple-element.40), channel_id=1, source_target_pairs={{1,2},{3,4},{5,6},{7,8},{9,10},{11,12},{13,14},{17,18},{19,20},{21... | collective-permute-start | bytes 24584 | tf_op jit(solution)/shard_map/ppermute | solution.py:485
  13.3 0.0 collective-permute-start.6
  13.4 0.5 %collective-permute-start.7 = (bf16[8,512]{1,0:T(8,128)(2,1)S(1)}, bf16[8,512]{1,0:T(8,128)(2,1)S(1)}, u32[]{:S(2)}, u32[]{:S(2)}) collective-permute-start(bf16[8,512]{1,0:T(8,128)(2,1)S(1)} %get-tuple-element.42), channel_id=1, source_target_pairs={{0,1},{2,3},{4,5},{6,7},{8,9},{10,11},{12,13},{14,15},{16,17},{18,... | collective-permute-start | bytes 24584 | tf_op jit(solution)/shard_map/ppermute | solution.py:485
  13.9 1.2 %last_own_terms.1 = (f32[4,16,320]{2,1,0:T(8,128)S(1)}, f32[32,1024]{1,0:T(8,128)S(1)}) custom-call(f32[4,16,320]{2,1,0:T(8,128)S(1)} %get-tuple-element.43.state_ref.partial_ref, bf16[96,512]{1,0:T(8,128)(2,1)S(1)} %get-tuple-element.44.pool_ref, bf16[16,320,320]{2,1,0:T(8,128)(2,1)S(1)} %copy-done, bf16[4,16,320]{2,1,0:T(8,128)(2,1)S(1)} %copy-done.4, ...), custom_call_target="tpu_custom_call" | custom-call | flops 13107200 | bytes 3276800 | tf_op jit(solution)/shard_map/last_own_terms/pallas_call | solution.py:541
  15.1 0.0 collective-permute-done.8.refs_0_
  15.1 0.1 message_terms.1
  15.2 0.0 collective-permute-done.4.refs_0_
  15.2 1.2 %collective-permute-done.5.refs_1_ = bf16[8,512]{1,0:T(8,128)(2,1)S(1)} collective-permute-done((bf16[8,512]{1,0:T(8,128)(2,1)S(1)}, bf16[8,512]{1,0:T(8,128)(2,1)S(1)}, u32[]{:S(2)}, u32[]{:S(2)}) %collective-permute-start.5) | collective-permute-done | bytes 8224 | tf_op jit(solution)/shard_map/ppermute | solution.py:485
  16.5 0.0 collective-permute-done.6.refs_2_
  16.5 0.0 collective-permute-done.7.refs_3_
  16.5 1.2 %last_step.1 = (bf16[4,16,320]{2,1,0:T(8,128)(2,1)}, f32[4,16,320]{2,1,0:T(8,128)}) custom-call(s32[1]{0:T(128)} %bitcast.place_ref, bf16[8,512]{1,0:T(8,128)(2,1)S(1)} %collective-permute-done.4.refs_0_, bf16[8,512]{1,0:T(8,128)(2,1)S(1)} %collective-permute-done.5.refs_1_, bf16[8,512]{1,0:T(8,128)(2,1)S(1)} %collective-permute-done.6.refs_2_, ...), custom_call_target="tpu_custom_call" | custom-call | tf_op jit(solution)/shard_map/last_step/pallas_call | solution.py:559
  (9 shorter events, 0.0 us)
Async XLA Ops:
  0.6 1.0 %copy-start.2 = (bf16[320,768]{1,0:T(8,128)(2,1)S(1)}, bf16[320,768]{1,0:T(8,128)(2,1)}, u32[]{:S(2)}) copy-start(bf16[320,768]{1,0:T(8,128)(2,1)} %constant.8.clone.trace_ref.refs_11_) | copy-start | bytes 1474564
  0.6 1.0 %copy-start.3 = (bf16[4,16,320]{2,1,0:T(8,128)(2,1)S(1)}, bf16[4,16,320]{2,1,0:T(8,128)(2,1)}, u32[]{:S(2)}) copy-start(bf16[4,16,320]{2,1,0:T(8,128)(2,1)} %first_ref.1) | copy-start | bytes 122884
  0.7 1.0 %copy-start.7 = (s32[1,4,8]{2,1,0:T(4,128)S(1)}, s32[1,4,8]{2,1,0:T(4,128)}, u32[]{:S(2)}) copy-start(s32[1,4,8]{2,1,0:T(4,128)} %refs_12_.1) | copy-start | bytes 388
  1.7 6.2 %copy-start = (bf16[16,320,320]{2,1,0:T(8,128)(2,1)S(1)}, bf16[16,320,320]{2,1,0:T(8,128)(2,1)}, u32[]{:S(2)}) copy-start(bf16[16,320,320]{2,1,0:T(8,128)(2,1)} %diag_ref.3) | copy-start | bytes 9830404
  1.7 6.2 %copy-start.4 = (bf16[4,16,320]{2,1,0:T(8,128)(2,1)S(1)}, bf16[4,16,320]{2,1,0:T(8,128)(2,1)}, u32[]{:S(2)}) copy-start(bf16[4,16,320]{2,1,0:T(8,128)(2,1)} %forcing_ref.3) | copy-start | bytes 122884
  1.7 6.2 %copy-start.5 = (bf16[16,2400]{1,0:T(8,128)(2,1)S(1)}, bf16[16,2400]{1,0:T(8,128)(2,1)}, u32[]{:S(2)}) copy-start(bf16[16,2400]{1,0:T(8,128)(2,1)} %flux_ref.1) | copy-start | bytes 230404
  1.7 6.2 %copy-start.6 = (s32[16,6]{0,1:T(8,128)S(1)}, s32[16,6]{0,1:T(8,128)}, u32[]{:S(2)}) copy-start(s32[16,6]{0,1:T(8,128)} %param.14) | copy-start | bytes 1156
  2.1 6.8 %copy-start.1 = (bf16[768,320]{1,0:T(8,128)(2,1)S(1)}, bf16[768,320]{1,0:T(8,128)(2,1)}, u32[]{:S(2)}) copy-start(bf16[768,320]{1,0:T(8,128)(2,1)} %constant.9.clone.refs_10_.lift_ref.refs_8_) | copy-start | bytes 1474564
  2.1 6.6 %collective-permute-start = (bf16[8,512]{1,0:T(8,128)(2,1)S(1)}, bf16[8,512]{1,0:T(8,128)(2,1)S(1)}, u32[]{:S(2)}, u32[]{:S(2)}) collective-permute-start(bf16[8,512]{1,0:T(8,128)(2,1)S(1)} %get-tuple-element.28), channel_id=1, source_target_pairs={{2,4},{3,5},{6,8},{7,9},{10,12},{11,13},{0,1},{14,15},{18,20},{19,... | collective-permute-start | bytes 24584 | tf_op jit(solution)/shard_map/ppermute | solution.py:485
  2.6 6.1 %collective-permute-start.1 = (bf16[8,512]{1,0:T(8,128)(2,1)S(1)}, bf16[8,512]{1,0:T(8,128)(2,1)S(1)}, u32[]{:S(2)}, u32[]{:S(2)}) collective-permute-start(bf16[8,512]{1,0:T(8,128)(2,1)S(1)} %get-tuple-element.29), channel_id=1, source_target_pairs={{1,2},{3,4},{5,6},{7,8},{9,10},{11,12},{13,14},{17,18},{19,20},{21... | collective-permute-start | bytes 24584 | tf_op jit(solution)/shard_map/ppermute | solution.py:485
  5.1 3.7 %collective-permute-start.2 = (bf16[8,512]{1,0:T(8,128)(2,1)S(1)}, bf16[8,512]{1,0:T(8,128)(2,1)S(1)}, u32[]{:S(2)}, u32[]{:S(2)}) collective-permute-start(bf16[8,512]{1,0:T(8,128)(2,1)S(1)} %get-tuple-element.30), channel_id=1, source_target_pairs={{0,2},{1,3},{4,6},{5,7},{8,10},{9,11},{12,14},{13,15},{16,18},{17,... | collective-permute-start | bytes 24584 | tf_op jit(solution)/shard_map/ppermute | solution.py:485
  6.7 2.1 %collective-permute-start.3 = (bf16[8,512]{1,0:T(8,128)(2,1)S(1)}, bf16[8,512]{1,0:T(8,128)(2,1)S(1)}, u32[]{:S(2)}, u32[]{:S(2)}) collective-permute-start(bf16[8,512]{1,0:T(8,128)(2,1)S(1)} %get-tuple-element.31), channel_id=1, source_target_pairs={{0,1},{2,3},{4,5},{6,7},{8,9},{10,11},{12,13},{14,15},{16,17},{18,... | collective-permute-start | bytes 24584 | tf_op jit(solution)/shard_map/ppermute | solution.py:485
  9.7 5.4 %collective-permute-start.8 = (bf16[128,384]{1,0:T(8,128)(2,1)S(1)}, bf16[128,384]{1,0:T(8,128)(2,1)S(1)}, u32[]{:S(2)}, u32[]{:S(2)}) collective-permute-start(bf16[128,384]{1,0:T(8,128)(2,1)S(1)} %get-tuple-element.46), channel_id=1, source_target_pairs={{16,0},{0,16},{17,1},{1,17},{18,2},{2,18},{19,3},{3,19},{20,4},{4,... | collective-permute-start | bytes 294920 | tf_op jit(solution)/shard_map/ppermute | solution.py:537
  11.2 4.0 %collective-permute-start.4 = (bf16[8,512]{1,0:T(8,128)(2,1)S(1)}, bf16[8,512]{1,0:T(8,128)(2,1)S(1)}, u32[]{:S(2)}, u32[]{:S(2)}) collective-permute-start(bf16[8,512]{1,0:T(8,128)(2,1)S(1)} %get-tuple-element.39), channel_id=1, source_target_pairs={{0,2},{1,3},{4,6},{5,7},{8,10},{9,11},{12,14},{13,15},{16,18},{17,... | collective-permute-start | bytes 24584 | tf_op jit(solution)/shard_map/ppermute | solution.py:485
  12.8 3.7 %collective-permute-start.5 = (bf16[8,512]{1,0:T(8,128)(2,1)S(1)}, bf16[8,512]{1,0:T(8,128)(2,1)S(1)}, u32[]{:S(2)}, u32[]{:S(2)}) collective-permute-start(bf16[8,512]{1,0:T(8,128)(2,1)S(1)} %get-tuple-element.40), channel_id=1, source_target_pairs={{1,2},{3,4},{5,6},{7,8},{9,10},{11,12},{13,14},{17,18},{19,20},{21... | collective-permute-start | bytes 24584 | tf_op jit(solution)/shard_map/ppermute | solution.py:485
  13.3 3.1 %collective-permute-start.6 = (bf16[8,512]{1,0:T(8,128)(2,1)S(1)}, bf16[8,512]{1,0:T(8,128)(2,1)S(1)}, u32[]{:S(2)}, u32[]{:S(2)}) collective-permute-start(bf16[8,512]{1,0:T(8,128)(2,1)S(1)} %get-tuple-element.41), channel_id=1, source_target_pairs={{2,4},{3,5},{6,8},{7,9},{10,12},{11,13},{0,1},{14,15},{18,20},{19,... | collective-permute-start | bytes 24584 | tf_op jit(solution)/shard_map/ppermute | solution.py:485
  13.4 3.1 %collective-permute-start.7 = (bf16[8,512]{1,0:T(8,128)(2,1)S(1)}, bf16[8,512]{1,0:T(8,128)(2,1)S(1)}, u32[]{:S(2)}, u32[]{:S(2)}) collective-permute-start(bf16[8,512]{1,0:T(8,128)(2,1)S(1)} %get-tuple-element.42), channel_id=1, source_target_pairs={{0,1},{2,3},{4,5},{6,7},{8,9},{10,11},{12,13},{14,15},{16,17},{18,... | collective-permute-start | bytes 24584 | tf_op jit(solution)/shard_map/ppermute | solution.py:485

commit v8 on v7

--- a/solution.py
+++ b/solution.py
@@ -126,17 +126,13 @@
     return jnp.where(mask, 1.0, 0.0).astype(BF16)
 
 
-def spread_table():
-    row, col = iotas((LANE, FIELDS * LANE))
-    inside = col % LANE < FIELDS * FPTS
-    return one_hot(inside & (row == col // LANE * FPTS + col % FPTS))
-
-
 def order_table():
-    row, col = iotas((FIELDS * FIELDS * FPTS, FIELDS * LANE))
-    place = col % LANE
-    source = place // FPTS * FIELDS * FPTS + col // LANE * FPTS + col % FPTS
-    return one_hot((place < FIELDS * FPTS) & (row == source))
+    turns = LANE // FPTS
+    row, col = iotas((FIELDS * FIELDS * FPTS, turns * LANE))
+    c = col % LANE // FPTS
+    d = (c + turns - col // LANE) % turns
+    source = (c * FIELDS + d) * FPTS + col % FPTS
+    return one_hot((c < FIELDS) & (d < FIELDS) & (row == source))
 
 
 def trace_pool(state, trace_wide, insts, elems):
@@ -251,49 +247,7 @@
     return jnp.concatenate(hot, 0).astype(BF16)
 
 
-def face_flux(picked, flux, spread, insts):
-    count = picked.shape[0]
-    stacked = jnp.concatenate([picked[:, t * LANE : (t + 1) * LANE] for t in range(insts)], 0)
-    wide = jnp.dot(stacked, spread, preferred_element_type=F32)
-    normal = []
-    for t in range(insts):
-        rows = wide[t * count : (t + 1) * count]
-        summed = flux[:, 0:LANE] * rows[:, 0:LANE]
-        for d in range(1, FIELDS):
-            summed += flux[:, d * LANE : (d + 1) * LANE] * rows[:, d * LANE : (d + 1) * LANE]
-        normal.append(summed.astype(BF16))
-    return normal
-
-
-def lift_faces(normal, lift, elems):
-    rows = [
-        jnp.concatenate([n[f * elems : (f + 1) * elems] for f in range(FACES)], 1) for n in normal
-    ]
-    return jnp.dot(jnp.concatenate(rows, 0), lift, preferred_element_type=F32)
-
-
-def couple(entry_ref, states, t, shift, insts):
-    summed = None
-    for s in range(insts):
-        d = (t - s + shift * insts) % NI
-        term = entry_ref[d : d + 1, :] * states[s].astype(F32)
-        summed = term if summed is None else summed + term
-    return summed
-
-
-def rotated(flux):
-    place = lax.broadcasted_iota(jnp.int32, (flux.shape[0], LANE), 1) // FPTS
-    blocks = []
-    for k in range(LANE // FPTS):
-        block = jnp.zeros((flux.shape[0], LANE), F32)
-        for d in range(FIELDS):
-            met = place == (d + k) % (LANE // FPTS)
-            block = jnp.where(met, flux[:, d * LANE : (d + 1) * LANE], block)
-        blocks.append(block)
-    return jnp.concatenate(blocks, 1)
-
-
-def slot_normal(blocks, factors, insts):
+def normal_flux(blocks, factors, insts):
     count = blocks.shape[0]
     stacked = jnp.concatenate([blocks[:, t * LANE : (t + 1) * LANE] for t in range(insts)], 0)
     summed = [None] * insts
@@ -305,12 +259,27 @@
     return [rows.astype(BF16) for rows in summed]
 
 
-def table_kernel(spread_ref, order_ref):
-    spread_ref[...] = spread_table()
+def lift_faces(normal, lift, elems):
+    rows = [
+        jnp.concatenate([n[f * elems : (f + 1) * elems] for f in range(FACES)], 1) for n in normal
+    ]
+    return jnp.dot(jnp.concatenate(rows, 0), lift, preferred_element_type=F32)
+
+
+def couple(entry_ref, states, t, shift, insts):
+    summed = None
+    for s in range(insts):
+        d = (t - s + shift * insts) % NI
+        term = entry_ref[d : d + 1, :] * states[s].astype(F32)
+        summed = term if summed is None else summed + term
+    return summed
+
+
+def table_kernel(order_ref):
     order_ref[...] = order_table()
 
 
-def first_kernel(spectral, second, place_ref, freq_ref, spread_ref, state_ref, trace_ref, send_ref,
+def first_kernel(spectral, second, place_ref, freq_ref, order_ref, state_ref, trace_ref, send_ref,
                  entry_ref, pool_ref, *out_refs):
     insts, elems, width = state_ref.shape
     state = state_ref[...].reshape(insts * elems, width)
@@ -335,18 +304,18 @@
         rest_ref[t] = couple(entry_ref, states, t, 0, insts) - forcing_ref[t].astype(F32)
 
 
-def last_base_kernel(state_ref, pool_ref, diag_ref, forcing_ref, hot_ref, flux_ref, spread_ref,
-                     lift_ref, base_ref, factor_ref, wide_ref, prod_ref):
+def last_base_kernel(state_ref, pool_ref, diag_ref, forcing_ref, hot_ref, flux_ref, lift_ref,
+                     base_ref, factor_ref, wide_ref, prod_ref):
     insts, elems, width = state_ref.shape
     flux = flux_ref[...]
     hot = hot_ref[...]
     faces = hot.shape[0]
     factors = lax.dot_general(hot, flux, (((0,), (0,)), ((), ())), preferred_element_type=F32)
-    factor_ref[...] = rotated(factors[faces:])
+    factor_ref[...] = factors[faces:]
     empty = jnp.zeros((hot.shape[1] - faces, insts * LANE), BF16)
     pool = jnp.concatenate([pool_ref[...], empty], 0)
-    picked = jnp.dot(hot, pool, preferred_element_type=F32).astype(BF16)
-    normal = face_flux(picked, flux.astype(F32), spread_ref[...], insts)
+    picked = jnp.dot(hot, pool, preferred_element_type=F32)
+    normal = normal_flux(picked, flux.astype(F32), insts)
     lifted = lift_faces(normal, lift_ref[...], elems)
     states = [state_ref[t].astype(BF16) for t in range(insts)]
     products = diagonal(states, diag_ref, wide_ref, prod_ref, insts, elems)
@@ -396,7 +365,7 @@
     return jnp.concatenate(arrived, 0)
 
 
-def step_kernel(parts, place_ref, spread_ref, *refs):
+def step_kernel(parts, place_ref, *refs):
     got_refs, refs = refs[: len(OFFSETS)], refs[len(OFFSETS) :]
     (state_ref, pool_ref, prod_ref, rest_ref, hot_ref, flux_ref, lift_ref, trace_ref, send_ref,
      partial_ref, message_ref, next_pool_ref, *out_refs) = refs
@@ -404,8 +373,8 @@
     place = place_ref[0]
     blocks = received(parts, place, got_refs, FIRST_ORDER).astype(BF16)
     pool = jnp.concatenate([pool_ref[...], blocks], 0)
-    picked = jnp.dot(hot_ref[...], pool, preferred_element_type=F32).astype(BF16)
-    normal = face_flux(picked, flux_ref[...].astype(F32), spread_ref[...], insts)
+    picked = jnp.dot(hot_ref[...], pool, preferred_element_type=F32)
+    normal = normal_flux(picked, flux_ref[...].astype(F32), insts)
     lifted = lift_faces(normal, lift_ref[...], elems)
     message_ref[...] = jnp.zeros_like(message_ref)
     fresh = []
@@ -429,7 +398,7 @@
      final_ref, residual_ref, sems) = refs
     insts, elems, width = state_ref.shape
     blocks = received(parts, place_ref[0], got_refs, LAST_ORDER)
-    normal = slot_normal(blocks, factor_ref[...], insts)
+    normal = normal_flux(blocks, factor_ref[...], insts)
     empty = jnp.zeros((FACES * elems, insts * LANE), BF16)
     rows = jnp.concatenate([empty, jnp.concatenate(normal, 1)], 0)
     spots = jnp.dot(hot_ref[...], rows, preferred_element_type=F32).astype(BF16)
@@ -476,7 +445,7 @@
     wide_shape = jax.ShapeDtypeStruct(initial_state.shape, F32)
     pool_shape = jax.ShapeDtypeStruct((faces, insts * LANE), BF16)
     out_shapes = [jax.ShapeDtypeStruct((capacity, insts * LANE), BF16)] * slots
-    flux_shape = jax.ShapeDtypeStruct((faces, FIELDS * LANE), BF16)
+    flux_shape = jax.ShapeDtypeStruct((faces, LANE // FPTS * LANE), BF16)
     hot_shape = jax.ShapeDtypeStruct((faces, faces + slots * capacity), BF16)
     factor_shape = jax.ShapeDtypeStruct((slots * capacity, LANE // FPTS * LANE), F32)
 
@@ -492,18 +461,15 @@
         flops=2 * insts * diagonal_blocks.size, bytes_accessed=2 * diagonal_blocks.size,
         transcendentals=0,
     )
-    spread, order = pl.pallas_call(
+    order = pl.pallas_call(
         table_kernel,
-        out_shape=[
-            jax.ShapeDtypeStruct((LANE, FIELDS * LANE), BF16),
-            jax.ShapeDtypeStruct((FIELDS * FIELDS * FPTS, FIELDS * LANE), BF16),
-        ],
-        out_specs=[vmem] * 2,
+        out_shape=jax.ShapeDtypeStruct((FIELDS * FIELDS * FPTS, LANE // FPTS * LANE), BF16),
+        out_specs=vmem,
         compiler_params=params,
         cost_estimate=pl.CostEstimate(flops=10**10, bytes_accessed=10**6, transcendentals=0),
         name="tables",
     )()
-    freq, _ = lax.optimization_barrier((frequency, spread))
+    freq, _ = lax.optimization_barrier((frequency, order))
     entries, pool, *outgoing = pl.pallas_call(
         functools.partial(first_kernel, spectral, second),
         out_shape=[entry_shape, pool_shape] + out_shapes,
@@ -512,7 +478,7 @@
         compiler_params=params,
         cost_estimate=pl.CostEstimate(flops=10**10, bytes_accessed=10**6, transcendentals=0),
         name="first_traces",
-    )(place, freq, spread, initial_state, trace_wide, send_list)
+    )(place, freq, order, initial_state, trace_wide, send_list)
     got = exchange(outgoing, FIRST_ORDER)
     product, rest, flux, hot = pl.pallas_call(
         functools.partial(base_kernel, slots * capacity),
@@ -527,11 +493,11 @@
     partial, message, pool, *outgoing = pl.pallas_call(
         functools.partial(step_kernel, parts),
         out_shape=[wide_shape, message_shape, pool_shape] + out_shapes,
-        in_specs=[smem] + [vmem] * (slots + 10),
+        in_specs=[smem] + [vmem] * (slots + 9),
         out_specs=[vmem] * (3 + len(out_shapes)),
         compiler_params=params,
         name="first_step",
-    )(place, spread, *got, initial_state, pool, product, rest, hot, flux, lift_wide, trace_wide,
+    )(place, *got, initial_state, pool, product, rest, hot, flux, lift_wide, trace_wide,
       send_list)
     messages = [
         lax.ppermute(message, "inst", [((i + rank) % ranks, i) for i in range(ranks)])
@@ -541,13 +507,13 @@
     base, factors = pl.pallas_call(
         last_base_kernel,
         out_shape=[wide_shape, factor_shape],
-        in_specs=[vmem] * 8,
+        in_specs=[vmem] * 7,
         out_specs=[vmem] * 2,
         scratch_shapes=chunks,
         compiler_params=params,
         cost_estimate=diag_cost,
         name="last_own_terms",
-    )(partial, pool, diagonal_blocks, forcing, hot, flux, spread, lift_wide)
+    )(partial, pool, diagonal_blocks, forcing, hot, flux, lift_wide)
     state, base = pl.pallas_call(
         functools.partial(message_kernel, ranks),
         out_shape=[like(initial_state), wide_shape],

time: 17.9 us -> 18 us (level)
  Pallas kernels: 4.79 us -> 5.18 us
  waiting for transfers between devices: 1.31 us -> 1.08 us
    ppermute x8, waiting for transfers between devices: 1.3 us -> 1.07 us  [exchange(): lax.ppermute(outgoing[swap], ('inst', 'dom'), routes[swap])]
  transfers between devices with their start and end apart: 9 -> 9, of which waited for: 2 -> 1; matrix products, arithmetic and copies ran while one was open for 0% -> 0% of each run, Pallas kernels for 12% -> 14%
where the time goes in v8:
time: 18 us; the launch traced here: 17.7 us
  starting transfers between devices  9.89 us (55%)
  Pallas kernels  5.18 us (29%)
  between operations  1.42 us (8%)
  waiting for transfers between devices  1.08 us (6%)
    ppermute x8, starting transfers between devices, exchange(): lax.ppermute(outgoing[swap], ('inst', 'dom'), routes[swap])  8.33 us
    ppermute x1, starting transfers between devices, on_device(): lax.ppermute(message, 'inst', [((i + rank) % ranks, i) for i in range(ran...  1.56 us
    pallas_call x1, Pallas kernels, on_device(): pl.pallas_call(last_base_kernel, out_shape=[wide_shape, factor_shape], in...  1.39 us
    pallas_call x1, Pallas kernels, on_device(): pl.pallas_call(functools.partial(last_kernel, parts), out_shape=[like(ini...  1.17 us
    ppermute x8, waiting for transfers between devices, exchange(): lax.ppermute(outgoing[swap], ('inst', 'dom'), routes[swap])  1.07 us
    pallas_call x1, Pallas kernels, on_device(): pl.pallas_call(functools.partial(step_kernel, parts), out_shape=[wide_sha...  1.03 us
    pallas_call x1, Pallas kernels, on_device(): pl.pallas_call(functools.partial(base_kernel, slots * capacity), out_shap...  0.88 us
  transfers between devices with their start and end apart: 9, of which 1 were waited for; matrix products, arithmetic and copies ran while one was open for 0% of the time, Pallas kernels for 14%

profile of v8, /device:TPU:0, one launch (start us, length us, event | category | flops | bytes accessed | tf_op | source)
XLA Modules:
  0.0 17.7 jit_solution(13816218769030422341)
XLA Ops:
  0.6 0.0 copy-start.2
  0.6 0.0 copy-start.3
  0.7 0.0 copy-start.7
  0.7 0.2 %tables.1.order_ref = bf16[400,1024]{1,0:T(8,128)(2,1)S(1)} custom-call(), custom_call_target="tpu_custom_call" | custom-call | flops 10000000000 | bytes 1000000 | tf_op jit(solution)/shard_map/tables/pallas_call | solution.py:464
  1.5 0.1 copy-done.2
  1.7 0.0 copy-start.5
  1.7 0.0 copy-start.6
  1.7 0.3 %first_traces.1 = (f32[8,320]{1,0:T(8,128)S(1)}, bf16[96,512]{1,0:T(8,128)(2,1)S(1)}, bf16[8,512]{1,0:T(8,128)(2,1)S(1)}, bf16[8,512]{1,0:T(8,128)(2,1)S(1)}, bf...) custom-call(s32[1]{0:T(128)} %bitcast.place_ref, f32[1]{0:T(128)S(6)} %copy.11.freq_ref, ...), custom_call_target="tpu_custom_call" | custom-call | flops 10000000000 | bytes 1000000 | tf_op jit(solution)/shard_map/first_traces/pallas_call | solution.py:473
  2.1 0.0 copy-start.1
  2.1 0.5 %collective-permute-start = (bf16[8,512]{1,0:T(8,128)(2,1)S(1)}, bf16[8,512]{1,0:T(8,128)(2,1)S(1)}, u32[]{:S(2)}, u32[]{:S(2)}) collective-permute-start(bf16[8,512]{1,0:T(8,128)(2,1)S(1)} %get-tuple-element.25), channel_id=1, source_target_pairs={{2,4},{3,5},{6,8},{7,9},{10,12},{11,13},{0,1},{14,15},{18,20},{19,... | collective-permute-start | bytes 24584 | tf_op jit(solution)/shard_map/ppermute | solution.py:454
  2.6 2.6 %collective-permute-start.1 = (bf16[8,512]{1,0:T(8,128)(2,1)S(1)}, bf16[8,512]{1,0:T(8,128)(2,1)S(1)}, u32[]{:S(2)}, u32[]{:S(2)}) collective-permute-start(bf16[8,512]{1,0:T(8,128)(2,1)S(1)} %get-tuple-element.26), channel_id=1, source_target_pairs={{1,2},{3,4},{5,6},{7,8},{9,10},{11,12},{13,14},{17,18},{19,20},{21... | collective-permute-start | bytes 24584 | tf_op jit(solution)/shard_map/ppermute | solution.py:454
  5.1 1.5 %collective-permute-start.2 = (bf16[8,512]{1,0:T(8,128)(2,1)S(1)}, bf16[8,512]{1,0:T(8,128)(2,1)S(1)}, u32[]{:S(2)}, u32[]{:S(2)}) collective-permute-start(bf16[8,512]{1,0:T(8,128)(2,1)S(1)} %get-tuple-element.27), channel_id=1, source_target_pairs={{0,2},{1,3},{4,6},{5,7},{8,10},{9,11},{12,14},{13,15},{16,18},{17,... | collective-permute-start | bytes 24584 | tf_op jit(solution)/shard_map/ppermute | solution.py:454
  6.7 1.2 %collective-permute-start.3 = (bf16[8,512]{1,0:T(8,128)(2,1)S(1)}, bf16[8,512]{1,0:T(8,128)(2,1)S(1)}, u32[]{:S(2)}, u32[]{:S(2)}) collective-permute-start(bf16[8,512]{1,0:T(8,128)(2,1)S(1)} %get-tuple-element.28), channel_id=1, source_target_pairs={{0,1},{2,3},{4,5},{6,7},{8,9},{10,11},{12,13},{14,15},{16,17},{18,... | collective-permute-start | bytes 24584 | tf_op jit(solution)/shard_map/ppermute | solution.py:454
  7.9 0.9 %own_terms.1 = (f32[4,16,320]{2,1,0:T(8,128)S(1)}, f32[4,16,320]{2,1,0:T(8,128)S(1)}, bf16[96,1024]{1,0:T(8,128)(2,1)S(1)}, bf16[96,128]{1,0:T(8,128)(2,1)S(1)}) custom-call(bf16[4,16,320]{2,1,0:T(8,128)(2,1)S(1)} %copy-done.3, bf16[16,320,320]{2,1,0:T(8,128)(2,1)S(1)} %copy-done, bf16[4,16,320]{2,1,0:T(8,128)(2,1)S(1)} %copy-done.4, ...), custom_call_target="tpu_custom_call" | custom-call | flops 13107200 | bytes 3276800 | tf_op jit(solution)/shard_map/own_terms/pallas_call | solution.py:483
  8.8 0.0 collective-permute-done.refs_0_
  8.8 0.0 collective-permute-done.1.refs_1_
  8.8 0.0 collective-permute-done.2.refs_2_
  8.8 0.0 collective-permute-done.3.refs_3_
  8.8 1.0 %first_step.1 = (f32[4,16,320]{2,1,0:T(8,128)S(1)}, bf16[128,384]{1,0:T(8,128)(2,1)S(1)}, bf16[96,512]{1,0:T(8,128)(2,1)S(1)}, bf16[8,512]{1,0:T(8,128)(2,1)S(1)...) custom-call(s32[1]{0:T(128)} %bitcast.place_ref, ...), custom_call_target="tpu_custom_call" | custom-call | tf_op jit(solution)/shard_map/first_step/pallas_call | solution.py:493
  9.8 1.6 %collective-permute-start.8 = (bf16[128,384]{1,0:T(8,128)(2,1)S(1)}, bf16[128,384]{1,0:T(8,128)(2,1)S(1)}, u32[]{:S(2)}, u32[]{:S(2)}) collective-permute-start(bf16[128,384]{1,0:T(8,128)(2,1)S(1)} %get-tuple-element.42), channel_id=1, source_target_pairs={{16,0},{0,16},{17,1},{1,17},{18,2},{2,18},{19,3},{3,19},{20,4},{4,... | collective-permute-start | bytes 294920 | tf_op jit(solution)/shard_map/ppermute | solution.py:503
  11.4 1.5 %collective-permute-start.4 = (bf16[8,512]{1,0:T(8,128)(2,1)S(1)}, bf16[8,512]{1,0:T(8,128)(2,1)S(1)}, u32[]{:S(2)}, u32[]{:S(2)}) collective-permute-start(bf16[8,512]{1,0:T(8,128)(2,1)S(1)} %get-tuple-element.35), channel_id=1, source_target_pairs={{0,2},{1,3},{4,6},{5,7},{8,10},{9,11},{12,14},{13,15},{16,18},{17,... | collective-permute-start | bytes 24584 | tf_op jit(solution)/shard_map/ppermute | solution.py:454
  12.9 0.5 %collective-permute-start.5 = (bf16[8,512]{1,0:T(8,128)(2,1)S(1)}, bf16[8,512]{1,0:T(8,128)(2,1)S(1)}, u32[]{:S(2)}, u32[]{:S(2)}) collective-permute-start(bf16[8,512]{1,0:T(8,128)(2,1)S(1)} %get-tuple-element.36), channel_id=1, source_target_pairs={{1,2},{3,4},{5,6},{7,8},{9,10},{11,12},{13,14},{17,18},{19,20},{21... | collective-permute-start | bytes 24584 | tf_op jit(solution)/shard_map/ppermute | solution.py:454
  13.4 0.1 collective-permute-start.6
  13.5 0.4 %collective-permute-start.7 = (bf16[8,512]{1,0:T(8,128)(2,1)S(1)}, bf16[8,512]{1,0:T(8,128)(2,1)S(1)}, u32[]{:S(2)}, u32[]{:S(2)}) collective-permute-start(bf16[8,512]{1,0:T(8,128)(2,1)S(1)} %get-tuple-element.38), channel_id=1, source_target_pairs={{0,1},{2,3},{4,5},{6,7},{8,9},{10,11},{12,13},{14,15},{16,17},{18,... | collective-permute-start | bytes 24584 | tf_op jit(solution)/shard_map/ppermute | solution.py:454
  13.9 1.4 %last_own_terms.1 = (f32[4,16,320]{2,1,0:T(8,128)S(1)}, f32[32,1024]{1,0:T(8,128)S(1)}) custom-call(f32[4,16,320]{2,1,0:T(8,128)S(1)} %get-tuple-element.39.state_ref.partial_ref, bf16[96,512]{1,0:T(8,128)(2,1)S(1)} %get-tuple-element.40.pool_ref, bf16[16,320,320]{2,1,0:T(8,128)(2,1)S(1)} %copy-done, bf16[4,16,320]{2,1,0:T(8,128)(2,1)S(1)} %copy-done.4, ...), custom_call_target="tpu_custom_call" | custom-call | flops 13107200 | bytes 3276800 | tf_op jit(solution)/shard_map/last_own_terms/pallas_call | solution.py:507
  15.3 0.0 collective-permute-done.8.refs_0_
  15.4 0.1 message_terms.1
  15.5 0.0 collective-permute-done.4.refs_0_
  15.5 1.0 %collective-permute-done.5.refs_1_ = bf16[8,512]{1,0:T(8,128)(2,1)S(1)} collective-permute-done((bf16[8,512]{1,0:T(8,128)(2,1)S(1)}, bf16[8,512]{1,0:T(8,128)(2,1)S(1)}, u32[]{:S(2)}, u32[]{:S(2)}) %collective-permute-start.5) | collective-permute-done | bytes 8224 | tf_op jit(solution)/shard_map/ppermute | solution.py:454
  16.6 0.0 collective-permute-done.6.refs_2_
  16.6 0.0 collective-permute-done.7.refs_3_
  16.6 1.2 %last_step.1 = (bf16[4,16,320]{2,1,0:T(8,128)(2,1)}, f32[4,16,320]{2,1,0:T(8,128)}) custom-call(s32[1]{0:T(128)} %bitcast.place_ref, bf16[8,512]{1,0:T(8,128)(2,1)S(1)} %collective-permute-done.4.refs_0_, bf16[8,512]{1,0:T(8,128)(2,1)S(1)} %collective-permute-done.5.refs_1_, bf16[8,512]{1,0:T(8,128)(2,1)S(1)} %collective-permute-done.6.refs_2_, ...), custom_call_target="tpu_custom_call" | custom-call | tf_op jit(solution)/shard_map/last_step/pallas_call | solution.py:525
  (9 shorter events, 0.0 us)
Async XLA Ops:
  0.6 1.0 %copy-start.2 = (bf16[320,768]{1,0:T(8,128)(2,1)S(1)}, bf16[320,768]{1,0:T(8,128)(2,1)}, u32[]{:S(2)}) copy-start(bf16[320,768]{1,0:T(8,128)(2,1)} %constant.8.clone.trace_ref.refs_11_) | copy-start | bytes 1474564
  0.6 1.0 %copy-start.3 = (bf16[4,16,320]{2,1,0:T(8,128)(2,1)S(1)}, bf16[4,16,320]{2,1,0:T(8,128)(2,1)}, u32[]{:S(2)}) copy-start(bf16[4,16,320]{2,1,0:T(8,128)(2,1)} %first_ref.1) | copy-start | bytes 122884
  0.7 1.0 %copy-start.7 = (s32[1,4,8]{2,1,0:T(4,128)S(1)}, s32[1,4,8]{2,1,0:T(4,128)}, u32[]{:S(2)}) copy-start(s32[1,4,8]{2,1,0:T(4,128)} %refs_12_.1) | copy-start | bytes 388
  1.7 6.2 %copy-start = (bf16[16,320,320]{2,1,0:T(8,128)(2,1)S(1)}, bf16[16,320,320]{2,1,0:T(8,128)(2,1)}, u32[]{:S(2)}) copy-start(bf16[16,320,320]{2,1,0:T(8,128)(2,1)} %diag_ref.3) | copy-start | bytes 9830404
  1.7 6.2 %copy-start.4 = (bf16[4,16,320]{2,1,0:T(8,128)(2,1)S(1)}, bf16[4,16,320]{2,1,0:T(8,128)(2,1)}, u32[]{:S(2)}) copy-start(bf16[4,16,320]{2,1,0:T(8,128)(2,1)} %forcing_ref.3) | copy-start | bytes 122884
  1.7 6.2 %copy-start.5 = (bf16[16,2400]{1,0:T(8,128)(2,1)S(1)}, bf16[16,2400]{1,0:T(8,128)(2,1)}, u32[]{:S(2)}) copy-start(bf16[16,2400]{1,0:T(8,128)(2,1)} %flux_ref.1) | copy-start | bytes 230404
  1.7 6.2 %copy-start.6 = (s32[16,6]{0,1:T(8,128)S(1)}, s32[16,6]{0,1:T(8,128)}, u32[]{:S(2)}) copy-start(s32[16,6]{0,1:T(8,128)} %param.14) | copy-start | bytes 1156
  2.1 6.8 %copy-start.1 = (bf16[768,320]{1,0:T(8,128)(2,1)S(1)}, bf16[768,320]{1,0:T(8,128)(2,1)}, u32[]{:S(2)}) copy-start(bf16[768,320]{1,0:T(8,128)(2,1)} %constant.9.clone.refs_10_.lift_ref.refs_8_) | copy-start | bytes 1474564
  2.1 6.7 %collective-permute-start = (bf16[8,512]{1,0:T(8,128)(2,1)S(1)}, bf16[8,512]{1,0:T(8,128)(2,1)S(1)}, u32[]{:S(2)}, u32[]{:S(2)}) collective-permute-start(bf16[8,512]{1,0:T(8,128)(2,1)S(1)} %get-tuple-element.25), channel_id=1, source_target_pairs={{2,4},{3,5},{6,8},{7,9},{10,12},{11,13},{0,1},{14,15},{18,20},{19,... | collective-permute-start | bytes 24584 | tf_op jit(solution)/shard_map/ppermute | solution.py:454
  2.6 6.2 %collective-permute-start.1 = (bf16[8,512]{1,0:T(8,128)(2,1)S(1)}, bf16[8,512]{1,0:T(8,128)(2,1)S(1)}, u32[]{:S(2)}, u32[]{:S(2)}) collective-permute-start(bf16[8,512]{1,0:T(8,128)(2,1)S(1)} %get-tuple-element.26), channel_id=1, source_target_pairs={{1,2},{3,4},{5,6},{7,8},{9,10},{11,12},{13,14},{17,18},{19,20},{21... | collective-permute-start | bytes 24584 | tf_op jit(solution)/shard_map/ppermute | solution.py:454
  5.1 3.7 %collective-permute-start.2 = (bf16[8,512]{1,0:T(8,128)(2,1)S(1)}, bf16[8,512]{1,0:T(8,128)(2,1)S(1)}, u32[]{:S(2)}, u32[]{:S(2)}) collective-permute-start(bf16[8,512]{1,0:T(8,128)(2,1)S(1)} %get-tuple-element.27), channel_id=1, source_target_pairs={{0,2},{1,3},{4,6},{5,7},{8,10},{9,11},{12,14},{13,15},{16,18},{17,... | collective-permute-start | bytes 24584 | tf_op jit(solution)/shard_map/ppermute | solution.py:454
  6.7 2.1 %collective-permute-start.3 = (bf16[8,512]{1,0:T(8,128)(2,1)S(1)}, bf16[8,512]{1,0:T(8,128)(2,1)S(1)}, u32[]{:S(2)}, u32[]{:S(2)}) collective-permute-start(bf16[8,512]{1,0:T(8,128)(2,1)S(1)} %get-tuple-element.28), channel_id=1, source_target_pairs={{0,1},{2,3},{4,5},{6,7},{8,9},{10,11},{12,13},{14,15},{16,17},{18,... | collective-permute-start | bytes 24584 | tf_op jit(solution)/shard_map/ppermute | solution.py:454
  9.8 5.5 %collective-permute-start.8 = (bf16[128,384]{1,0:T(8,128)(2,1)S(1)}, bf16[128,384]{1,0:T(8,128)(2,1)S(1)}, u32[]{:S(2)}, u32[]{:S(2)}) collective-permute-start(bf16[128,384]{1,0:T(8,128)(2,1)S(1)} %get-tuple-element.42), channel_id=1, source_target_pairs={{16,0},{0,16},{17,1},{1,17},{18,2},{2,18},{19,3},{3,19},{20,4},{4,... | collective-permute-start | bytes 294920 | tf_op jit(solution)/shard_map/ppermute | solution.py:503
  11.4 4.1 %collective-permute-start.4 = (bf16[8,512]{1,0:T(8,128)(2,1)S(1)}, bf16[8,512]{1,0:T(8,128)(2,1)S(1)}, u32[]{:S(2)}, u32[]{:S(2)}) collective-permute-start(bf16[8,512]{1,0:T(8,128)(2,1)S(1)} %get-tuple-element.35), channel_id=1, source_target_pairs={{0,2},{1,3},{4,6},{5,7},{8,10},{9,11},{12,14},{13,15},{16,18},{17,... | collective-permute-start | bytes 24584 | tf_op jit(solution)/shard_map/ppermute | solution.py:454
  12.9 3.7 %collective-permute-start.5 = (bf16[8,512]{1,0:T(8,128)(2,1)S(1)}, bf16[8,512]{1,0:T(8,128)(2,1)S(1)}, u32[]{:S(2)}, u32[]{:S(2)}) collective-permute-start(bf16[8,512]{1,0:T(8,128)(2,1)S(1)} %get-tuple-element.36), channel_id=1, source_target_pairs={{1,2},{3,4},{5,6},{7,8},{9,10},{11,12},{13,14},{17,18},{19,20},{21... | collective-permute-start | bytes 24584 | tf_op jit(solution)/shard_map/ppermute | solution.py:454
  13.4 3.1 %collective-permute-start.6 = (bf16[8,512]{1,0:T(8,128)(2,1)S(1)}, bf16[8,512]{1,0:T(8,128)(2,1)S(1)}, u32[]{:S(2)}, u32[]{:S(2)}) collective-permute-start(bf16[8,512]{1,0:T(8,128)(2,1)S(1)} %get-tuple-element.37), channel_id=1, source_target_pairs={{2,4},{3,5},{6,8},{7,9},{10,12},{11,13},{0,1},{14,15},{18,20},{19,... | collective-permute-start | bytes 24584 | tf_op jit(solution)/shard_map/ppermute | solution.py:454
  13.5 3.0 %collective-permute-start.7 = (bf16[8,512]{1,0:T(8,128)(2,1)S(1)}, bf16[8,512]{1,0:T(8,128)(2,1)S(1)}, u32[]{:S(2)}, u32[]{:S(2)}) collective-permute-start(bf16[8,512]{1,0:T(8,128)(2,1)S(1)} %get-tuple-element.38), channel_id=1, source_target_pairs={{0,1},{2,3},{4,5},{6,7},{8,9},{10,11},{12,13},{14,15},{16,17},{18,... | collective-permute-start | bytes 24584 | tf_op jit(solution)/shard_map/ppermute | solution.py:454

commit v9 on v7

--- a/solution.py
+++ b/solution.py
@@ -96,6 +96,7 @@
 LANE = 128
 WIDE = FIELDS * NODES
 FACES = 6
+TRACE_TABLES = 3
 VMEM_LIMIT = 16 * 1024 * 1024
 BF16 = jnp.bfloat16
 F32 = jnp.float32
@@ -139,14 +140,14 @@
     return one_hot((place < FIELDS * FPTS) & (row == source))
 
 
-def trace_pool(state, trace_wide, insts, elems):
-    wide = jnp.dot(state, trace_wide, preferred_element_type=F32).astype(BF16)
+def trace_pool(state, trace_tables, insts, elems):
+    faces = []
+    for table in trace_tables:
+        wide = jnp.dot(state, table, preferred_element_type=F32).astype(BF16)
+        faces += [wide[:, at : at + LANE] for at in range(0, table.shape[1], LANE)]
     by_inst = []
     for t in range(insts):
-        rows = wide[t * elems : (t + 1) * elems]
-        by_inst.append(
-            jnp.concatenate([rows[:, f * LANE : (f + 1) * LANE] for f in range(FACES)], 0)
-        )
+        by_inst.append(jnp.concatenate([rows[t * elems : (t + 1) * elems] for rows in faces], 0))
     return jnp.concatenate(by_inst, 1)
 
 
@@ -310,11 +311,11 @@
     order_ref[...] = order_table()
 
 
-def first_kernel(spectral, second, place_ref, freq_ref, spread_ref, state_ref, trace_ref, send_ref,
-                 entry_ref, pool_ref, *out_refs):
+def first_kernel(spectral, second, place_ref, freq_ref, spread_ref, state_ref, send_ref, *refs):
     insts, elems, width = state_ref.shape
+    trace_refs, (entry_ref, pool_ref, *out_refs) = refs[:TRACE_TABLES], refs[TRACE_TABLES:]
     state = state_ref[...].reshape(insts * elems, width)
-    pool = trace_pool(state, trace_ref[...], insts, elems)
+    pool = trace_pool(state, [ref[...] for ref in trace_refs], insts, elems)
     pool_ref[...] = pool
     fill_outgoing(pool, send_ref[0], out_refs, place_ref[0], elems)
     freq = freq_ref[0]
@@ -398,7 +399,8 @@
 
 def step_kernel(parts, place_ref, spread_ref, *refs):
     got_refs, refs = refs[: len(OFFSETS)], refs[len(OFFSETS) :]
-    (state_ref, pool_ref, prod_ref, rest_ref, hot_ref, flux_ref, lift_ref, trace_ref, send_ref,
+    trace_refs, refs = refs[:TRACE_TABLES], refs[TRACE_TABLES:]
+    (state_ref, pool_ref, prod_ref, rest_ref, hot_ref, flux_ref, lift_ref, send_ref,
      partial_ref, message_ref, next_pool_ref, *out_refs) = refs
     insts, elems, width = state_ref.shape
     place = place_ref[0]
@@ -418,7 +420,8 @@
         for i, block in enumerate((state_ref[t], lean)):
             low = (i * insts + t) * elems
             message_ref[low : low + elems, 0:width] = block
-    pool = trace_pool(jnp.concatenate(fresh, 0), trace_ref[...], insts, elems)
+    tables_of_traces = [ref[...] for ref in trace_refs]
+    pool = trace_pool(jnp.concatenate(fresh, 0), tables_of_traces, insts, elems)
     next_pool_ref[...] = pool
     fill_outgoing(pool, send_ref[0], out_refs, place, elems)
 
@@ -436,17 +439,16 @@
     lifted = lift_faces(
         [spots[:, t * LANE : (t + 1) * LANE] for t in range(insts)], lift_ref[...], elems
     )
-    copies = []
     for t in range(insts):
         residual = base_ref[t] + lifted[t * elems : (t + 1) * elems]
         residual_ref[t] = residual
         final_ref[t] = (state_ref[t].astype(F32) - pseudo_step * residual).astype(BF16)
-        copies += [
-            pltpu.make_async_copy(residual_ref.at[t], residual_hbm.at[t], sems.at[0, t]),
-            pltpu.make_async_copy(final_ref.at[t], final_hbm.at[t], sems.at[1, t]),
-        ]
-        copies[-2].start()
-        copies[-1].start()
+    copies = [
+        pltpu.make_async_copy(residual_ref, residual_hbm, sems.at[0]),
+        pltpu.make_async_copy(final_ref, final_hbm, sems.at[1]),
+    ]
+    for copy in copies:
+        copy.start()
     for copy in copies:
         copy.wait()
 
@@ -460,7 +462,7 @@
     slots, capacity = send_list.shape[1:]
     faces = FACES * elems
     trace_np, lift_np, spectral, second = wide_tables()
-    trace_wide = jnp.asarray(trace_np, BF16)
+    trace_wide = [jnp.asarray(part, BF16) for part in np.split(trace_np, TRACE_TABLES, 1)]
     lift_wide = jnp.asarray(lift_np, BF16)
     place = lax.axis_index("dom").reshape(1)
     sources = source_index.T
@@ -507,12 +509,12 @@
     entries, pool, *outgoing = pl.pallas_call(
         functools.partial(first_kernel, spectral, second),
         out_shape=[entry_shape, pool_shape] + out_shapes,
-        in_specs=[smem] * 2 + [vmem] * 4,
+        in_specs=[smem] * 2 + [vmem] * (3 + TRACE_TABLES),
         out_specs=[vmem] * (2 + len(out_shapes)),
         compiler_params=params,
         cost_estimate=pl.CostEstimate(flops=10**10, bytes_accessed=10**6, transcendentals=0),
         name="first_traces",
-    )(place, freq, spread, initial_state, trace_wide, send_list)
+    )(place, freq, spread, initial_state, send_list, *trace_wide)
     got = exchange(outgoing, FIRST_ORDER)
     product, rest, flux, hot = pl.pallas_call(
         functools.partial(base_kernel, slots * capacity),
@@ -527,11 +529,11 @@
     partial, message, pool, *outgoing = pl.pallas_call(
         functools.partial(step_kernel, parts),
         out_shape=[wide_shape, message_shape, pool_shape] + out_shapes,
-        in_specs=[smem] + [vmem] * (slots + 10),
+        in_specs=[smem] + [vmem] * (slots + 9 + TRACE_TABLES),
         out_specs=[vmem] * (3 + len(out_shapes)),
         compiler_params=params,
         name="first_step",
-    )(place, spread, *got, initial_state, pool, product, rest, hot, flux, lift_wide, trace_wide,
+    )(place, spread, *got, *trace_wide, initial_state, pool, product, rest, hot, flux, lift_wide,
       send_list)
     messages = [
         lax.ppermute(message, "inst", [((i + rank) % ranks, i) for i in range(ranks)])
@@ -564,7 +566,7 @@
         scratch_shapes=[
             pltpu.VMEM(initial_state.shape, BF16),
             pltpu.VMEM(initial_state.shape, F32),
-            pltpu.SemaphoreType.DMA((2, insts)),
+            pltpu.SemaphoreType.DMA((2,)),
         ],
         compiler_params=params,
         name="last_step",

time: 17.9 us -> 17.9 us (level)
  no operation moved by 1% of the time
where the time goes in v9:
time: 17.9 us; the launch traced here: 17.6 us
  starting transfers between devices  9.91 us (55%)
  Pallas kernels  4.76 us (27%)
  between operations  1.47 us (8%)
  waiting for transfers between devices  1.31 us (7%)
  local copies, waits for them, and re-layouts  0.19 us (1%)
    ppermute x8, starting transfers between devices, exchange(): lax.ppermute(outgoing[swap], ('inst', 'dom'), routes[swap])  8.39 us
    ppermute x1, starting transfers between devices, on_device(): lax.ppermute(message, 'inst', [((i + rank) % ranks, i) for i in range(ran...  1.52 us
    ppermute x8, waiting for transfers between devices, exchange(): lax.ppermute(outgoing[swap], ('inst', 'dom'), routes[swap])  1.3 us
    pallas_call x1, Pallas kernels, on_device(): pl.pallas_call(last_base_kernel, out_shape=[wide_shape, factor_shape], in...  1.22 us
    pallas_call x1, Pallas kernels, on_device(): pl.pallas_call(functools.partial(last_kernel, parts), out_shape=[like(ini...  1.14 us
    pallas_call x1, Pallas kernels, on_device(): pl.pallas_call(functools.partial(step_kernel, parts), out_shape=[wide_sha...  0.92 us
    pallas_call x1, Pallas kernels, on_device(): pl.pallas_call(functools.partial(base_kernel, slots * capacity), out_shap...  0.82 us
  transfers between devices with their start and end apart: 9, of which 2 were waited for; matrix products, arithmetic and copies ran while one was open for 0% of the time, Pallas kernels for 12%

profile of v9, /device:TPU:0, one launch (start us, length us, event | category | flops | bytes accessed | tf_op | source)
XLA Modules:
  0.0 17.6 jit_solution(2485473762234483036)
XLA Ops:
  0.6 0.0 copy-start.4
  0.6 0.0 copy-start.5
  0.7 0.0 copy-start.6
  0.7 0.2 %tables.1 = (bf16[128,640]{1,0:T(8,128)(2,1)S(1)}, bf16[400,640]{1,0:T(8,128)(2,1)S(1)}) custom-call(), custom_call_target="tpu_custom_call" | custom-call | flops 10000000000 | bytes 1000000 | tf_op jit(solution)/shard_map/tables/pallas_call | solution.py:497
  1.6 0.1 copy-done.5
  1.6 0.1 copy-done.6
  1.7 0.0 copy-start.7
  1.7 0.0 copy-start.8
  1.8 0.3 %first_traces.1 = (f32[8,320]{1,0:T(8,128)S(1)}, bf16[96,512]{1,0:T(8,128)(2,1)S(1)}, bf16[8,512]{1,0:T(8,128)(2,1)S(1)}, bf16[8,512]{1,0:T(8,128)(2,1)S(1)}, bf...) custom-call(s32[1]{0:T(128)} %bitcast.place_ref, f32[1]{0:T(128)S(6)} %copy.13.freq_ref, ...), custom_call_target="tpu_custom_call" | custom-call | flops 10000000000 | bytes 1000000 | tf_op jit(solution)/shard_map/first_traces/pallas_call | solution.py:509
  2.1 0.0 copy-start.1
  2.1 0.5 %collective-permute-start = (bf16[8,512]{1,0:T(8,128)(2,1)S(1)}, bf16[8,512]{1,0:T(8,128)(2,1)S(1)}, u32[]{:S(2)}, u32[]{:S(2)}) collective-permute-start(bf16[8,512]{1,0:T(8,128)(2,1)S(1)} %get-tuple-element.28), channel_id=1, source_target_pairs={{2,4},{3,5},{6,8},{7,9},{10,12},{11,13},{0,1},{14,15},{18,20},{19,... | collective-permute-start | bytes 24584 | tf_op jit(solution)/shard_map/ppermute | solution.py:487
  2.6 2.6 %collective-permute-start.1 = (bf16[8,512]{1,0:T(8,128)(2,1)S(1)}, bf16[8,512]{1,0:T(8,128)(2,1)S(1)}, u32[]{:S(2)}, u32[]{:S(2)}) collective-permute-start(bf16[8,512]{1,0:T(8,128)(2,1)S(1)} %get-tuple-element.29), channel_id=1, source_target_pairs={{1,2},{3,4},{5,6},{7,8},{9,10},{11,12},{13,14},{17,18},{19,20},{21... | collective-permute-start | bytes 24584 | tf_op jit(solution)/shard_map/ppermute | solution.py:487
  5.2 1.5 %collective-permute-start.2 = (bf16[8,512]{1,0:T(8,128)(2,1)S(1)}, bf16[8,512]{1,0:T(8,128)(2,1)S(1)}, u32[]{:S(2)}, u32[]{:S(2)}) collective-permute-start(bf16[8,512]{1,0:T(8,128)(2,1)S(1)} %get-tuple-element.30), channel_id=1, source_target_pairs={{0,2},{1,3},{4,6},{5,7},{8,10},{9,11},{12,14},{13,15},{16,18},{17,... | collective-permute-start | bytes 24584 | tf_op jit(solution)/shard_map/ppermute | solution.py:487
  6.7 1.2 %collective-permute-start.3 = (bf16[8,512]{1,0:T(8,128)(2,1)S(1)}, bf16[8,512]{1,0:T(8,128)(2,1)S(1)}, u32[]{:S(2)}, u32[]{:S(2)}) collective-permute-start(bf16[8,512]{1,0:T(8,128)(2,1)S(1)} %get-tuple-element.31), channel_id=1, source_target_pairs={{0,1},{2,3},{4,5},{6,7},{8,9},{10,11},{12,13},{14,15},{16,17},{18,... | collective-permute-start | bytes 24584 | tf_op jit(solution)/shard_map/ppermute | solution.py:487
  7.9 0.8 %own_terms.1 = (f32[4,16,320]{2,1,0:T(8,128)S(1)}, f32[4,16,320]{2,1,0:T(8,128)S(1)}, bf16[96,640]{1,0:T(8,128)(2,1)S(1)}, bf16[96,128]{1,0:T(8,128)(2,1)S(1)}) custom-call(bf16[4,16,320]{2,1,0:T(8,128)(2,1)S(1)} %copy-done.2, bf16[16,320,320]{2,1,0:T(8,128)(2,1)S(1)} %copy-done, bf16[4,16,320]{2,1,0:T(8,128)(2,1)S(1)} %copy-done.3, ...), custom_call_target="tpu_custom_call" | custom-call | flops 13107200 | bytes 3276800 | tf_op jit(solution)/shard_map/own_terms/pallas_call | solution.py:519
  8.8 0.0 collective-permute-done.refs_0_
  8.8 0.0 collective-permute-done.1.refs_1_
  8.8 0.1 collective-permute-done.2.refs_2_
  8.8 0.0 collective-permute-done.3.refs_3_
  8.9 0.9 %first_step.1 = (f32[4,16,320]{2,1,0:T(8,128)S(1)}, bf16[128,384]{1,0:T(8,128)(2,1)S(1)}, bf16[96,512]{1,0:T(8,128)(2,1)S(1)}, bf16[8,512]{1,0:T(8,128)(2,1)S(1)...) custom-call(s32[1]{0:T(128)} %bitcast.place_ref, ...), custom_call_target="tpu_custom_call" | custom-call | tf_op jit(solution)/shard_map/first_step/pallas_call | solution.py:529
  9.8 1.5 %collective-permute-start.8 = (bf16[128,384]{1,0:T(8,128)(2,1)S(1)}, bf16[128,384]{1,0:T(8,128)(2,1)S(1)}, u32[]{:S(2)}, u32[]{:S(2)}) collective-permute-start(bf16[128,384]{1,0:T(8,128)(2,1)S(1)} %get-tuple-element.46), channel_id=1, source_target_pairs={{16,0},{0,16},{17,1},{1,17},{18,2},{2,18},{19,3},{3,19},{20,4},{4,... | collective-permute-start | bytes 294920 | tf_op jit(solution)/shard_map/ppermute | solution.py:539
  11.3 1.5 %collective-permute-start.4 = (bf16[8,512]{1,0:T(8,128)(2,1)S(1)}, bf16[8,512]{1,0:T(8,128)(2,1)S(1)}, u32[]{:S(2)}, u32[]{:S(2)}) collective-permute-start(bf16[8,512]{1,0:T(8,128)(2,1)S(1)} %get-tuple-element.39), channel_id=1, source_target_pairs={{0,2},{1,3},{4,6},{5,7},{8,10},{9,11},{12,14},{13,15},{16,18},{17,... | collective-permute-start | bytes 24584 | tf_op jit(solution)/shard_map/ppermute | solution.py:487
  12.9 0.5 %collective-permute-start.5 = (bf16[8,512]{1,0:T(8,128)(2,1)S(1)}, bf16[8,512]{1,0:T(8,128)(2,1)S(1)}, u32[]{:S(2)}, u32[]{:S(2)}) collective-permute-start(bf16[8,512]{1,0:T(8,128)(2,1)S(1)} %get-tuple-element.40), channel_id=1, source_target_pairs={{1,2},{3,4},{5,6},{7,8},{9,10},{11,12},{13,14},{17,18},{19,20},{21... | collective-permute-start | bytes 24584 | tf_op jit(solution)/shard_map/ppermute | solution.py:487
  13.4 0.1 collective-permute-start.6
  13.4 0.5 %collective-permute-start.7 = (bf16[8,512]{1,0:T(8,128)(2,1)S(1)}, bf16[8,512]{1,0:T(8,128)(2,1)S(1)}, u32[]{:S(2)}, u32[]{:S(2)}) collective-permute-start(bf16[8,512]{1,0:T(8,128)(2,1)S(1)} %get-tuple-element.42), channel_id=1, source_target_pairs={{0,1},{2,3},{4,5},{6,7},{8,9},{10,11},{12,13},{14,15},{16,17},{18,... | collective-permute-start | bytes 24584 | tf_op jit(solution)/shard_map/ppermute | solution.py:487
  13.9 1.2 %last_own_terms.1 = (f32[4,16,320]{2,1,0:T(8,128)S(1)}, f32[32,1024]{1,0:T(8,128)S(1)}) custom-call(f32[4,16,320]{2,1,0:T(8,128)S(1)} %get-tuple-element.43.state_ref.partial_ref, bf16[96,512]{1,0:T(8,128)(2,1)S(1)} %get-tuple-element.44.pool_ref, bf16[16,320,320]{2,1,0:T(8,128)(2,1)S(1)} %copy-done, bf16[4,16,320]{2,1,0:T(8,128)(2,1)S(1)} %copy-done.3, ...), custom_call_target="tpu_custom_call" | custom-call | flops 13107200 | bytes 3276800 | tf_op jit(solution)/shard_map/last_own_terms/pallas_call | solution.py:543
  15.1 0.0 collective-permute-done.8.refs_0_
  15.1 0.1 message_terms.1
  15.3 0.0 collective-permute-done.4.refs_0_
  15.3 1.2 %collective-permute-done.5.refs_1_ = bf16[8,512]{1,0:T(8,128)(2,1)S(1)} collective-permute-done((bf16[8,512]{1,0:T(8,128)(2,1)S(1)}, bf16[8,512]{1,0:T(8,128)(2,1)S(1)}, u32[]{:S(2)}, u32[]{:S(2)}) %collective-permute-start.5) | collective-permute-done | bytes 8224 | tf_op jit(solution)/shard_map/ppermute | solution.py:487
  16.5 0.0 collective-permute-done.6.refs_2_
  16.5 1.1 %last_step.1 = (bf16[4,16,320]{2,1,0:T(8,128)(2,1)}, f32[4,16,320]{2,1,0:T(8,128)}) custom-call(s32[1]{0:T(128)} %bitcast.place_ref, bf16[8,512]{1,0:T(8,128)(2,1)S(1)} %collective-permute-done.4.refs_0_, bf16[8,512]{1,0:T(8,128)(2,1)S(1)} %collective-permute-done.5.refs_1_, bf16[8,512]{1,0:T(8,128)(2,1)S(1)} %collective-permute-done.6.refs_2_, ...), custom_call_target="tpu_custom_call" | custom-call | tf_op jit(solution)/shard_map/last_step/pallas_call | solution.py:561
  (13 shorter events, 0.0 us)
Async XLA Ops:
  0.6 0.9 %copy-start.4 = (bf16[320,256]{1,0:T(8,128)(2,1)S(1)}, bf16[320,256]{1,0:T(8,128)(2,1)}, u32[]{:S(2)}) copy-start(bf16[320,256]{1,0:T(8,128)(2,1)} %constant.12.clone.refs_0_.refs_4_) | copy-start | bytes 491524
  0.6 1.0 %copy-start.5 = (bf16[320,256]{1,0:T(8,128)(2,1)S(1)}, bf16[320,256]{1,0:T(8,128)(2,1)}, u32[]{:S(2)}) copy-start(bf16[320,256]{1,0:T(8,128)(2,1)} %constant.13.clone.refs_1_.refs_5_) | copy-start | bytes 491524
  0.7 1.1 %copy-start.6 = (bf16[320,256]{1,0:T(8,128)(2,1)S(1)}, bf16[320,256]{1,0:T(8,128)(2,1)}, u32[]{:S(2)}) copy-start(bf16[320,256]{1,0:T(8,128)(2,1)} %constant.14.clone.refs_2_.refs_6_) | copy-start | bytes 491524
  0.7 1.0 %copy-start.2 = (bf16[4,16,320]{2,1,0:T(8,128)(2,1)S(1)}, bf16[4,16,320]{2,1,0:T(8,128)(2,1)}, u32[]{:S(2)}) copy-start(bf16[4,16,320]{2,1,0:T(8,128)(2,1)} %first_ref.1) | copy-start | bytes 122884
  0.7 1.0 %copy-start.9 = (s32[1,4,8]{2,1,0:T(4,128)S(1)}, s32[1,4,8]{2,1,0:T(4,128)}, u32[]{:S(2)}) copy-start(s32[1,4,8]{2,1,0:T(4,128)} %refs_14_.1) | copy-start | bytes 388
  1.7 6.2 %copy-start = (bf16[16,320,320]{2,1,0:T(8,128)(2,1)S(1)}, bf16[16,320,320]{2,1,0:T(8,128)(2,1)}, u32[]{:S(2)}) copy-start(bf16[16,320,320]{2,1,0:T(8,128)(2,1)} %diag_ref.3) | copy-start | bytes 9830404
  1.7 6.2 %copy-start.3 = (bf16[4,16,320]{2,1,0:T(8,128)(2,1)S(1)}, bf16[4,16,320]{2,1,0:T(8,128)(2,1)}, u32[]{:S(2)}) copy-start(bf16[4,16,320]{2,1,0:T(8,128)(2,1)} %forcing_ref.3) | copy-start | bytes 122884
  1.7 6.2 %copy-start.7 = (bf16[16,2400]{1,0:T(8,128)(2,1)S(1)}, bf16[16,2400]{1,0:T(8,128)(2,1)}, u32[]{:S(2)}) copy-start(bf16[16,2400]{1,0:T(8,128)(2,1)} %flux_ref.1) | copy-start | bytes 230404
  1.7 6.2 %copy-start.8 = (s32[16,6]{0,1:T(8,128)S(1)}, s32[16,6]{0,1:T(8,128)}, u32[]{:S(2)}) copy-start(s32[16,6]{0,1:T(8,128)} %param.16) | copy-start | bytes 1156
  2.1 6.8 %copy-start.1 = (bf16[768,320]{1,0:T(8,128)(2,1)S(1)}, bf16[768,320]{1,0:T(8,128)(2,1)}, u32[]{:S(2)}) copy-start(bf16[768,320]{1,0:T(8,128)(2,1)} %constant.15.clone.refs_13_.lift_ref.refs_8_) | copy-start | bytes 1474564
  2.1 6.6 %collective-permute-start = (bf16[8,512]{1,0:T(8,128)(2,1)S(1)}, bf16[8,512]{1,0:T(8,128)(2,1)S(1)}, u32[]{:S(2)}, u32[]{:S(2)}) collective-permute-start(bf16[8,512]{1,0:T(8,128)(2,1)S(1)} %get-tuple-element.28), channel_id=1, source_target_pairs={{2,4},{3,5},{6,8},{7,9},{10,12},{11,13},{0,1},{14,15},{18,20},{19,... | collective-permute-start | bytes 24584 | tf_op jit(solution)/shard_map/ppermute | solution.py:487
  2.6 6.1 %collective-permute-start.1 = (bf16[8,512]{1,0:T(8,128)(2,1)S(1)}, bf16[8,512]{1,0:T(8,128)(2,1)S(1)}, u32[]{:S(2)}, u32[]{:S(2)}) collective-permute-start(bf16[8,512]{1,0:T(8,128)(2,1)S(1)} %get-tuple-element.29), channel_id=1, source_target_pairs={{1,2},{3,4},{5,6},{7,8},{9,10},{11,12},{13,14},{17,18},{19,20},{21... | collective-permute-start | bytes 24584 | tf_op jit(solution)/shard_map/ppermute | solution.py:487
  5.2 3.7 %collective-permute-start.2 = (bf16[8,512]{1,0:T(8,128)(2,1)S(1)}, bf16[8,512]{1,0:T(8,128)(2,1)S(1)}, u32[]{:S(2)}, u32[]{:S(2)}) collective-permute-start(bf16[8,512]{1,0:T(8,128)(2,1)S(1)} %get-tuple-element.30), channel_id=1, source_target_pairs={{0,2},{1,3},{4,6},{5,7},{8,10},{9,11},{12,14},{13,15},{16,18},{17,... | collective-permute-start | bytes 24584 | tf_op jit(solution)/shard_map/ppermute | solution.py:487
  6.7 2.1 %collective-permute-start.3 = (bf16[8,512]{1,0:T(8,128)(2,1)S(1)}, bf16[8,512]{1,0:T(8,128)(2,1)S(1)}, u32[]{:S(2)}, u32[]{:S(2)}) collective-permute-start(bf16[8,512]{1,0:T(8,128)(2,1)S(1)} %get-tuple-element.31), channel_id=1, source_target_pairs={{0,1},{2,3},{4,5},{6,7},{8,9},{10,11},{12,13},{14,15},{16,17},{18,... | collective-permute-start | bytes 24584 | tf_op jit(solution)/shard_map/ppermute | solution.py:487
  9.8 5.4 %collective-permute-start.8 = (bf16[128,384]{1,0:T(8,128)(2,1)S(1)}, bf16[128,384]{1,0:T(8,128)(2,1)S(1)}, u32[]{:S(2)}, u32[]{:S(2)}) collective-permute-start(bf16[128,384]{1,0:T(8,128)(2,1)S(1)} %get-tuple-element.46), channel_id=1, source_target_pairs={{16,0},{0,16},{17,1},{1,17},{18,2},{2,18},{19,3},{3,19},{20,4},{4,... | collective-permute-start | bytes 294920 | tf_op jit(solution)/shard_map/ppermute | solution.py:539
  11.3 4.0 %collective-permute-start.4 = (bf16[8,512]{1,0:T(8,128)(2,1)S(1)}, bf16[8,512]{1,0:T(8,128)(2,1)S(1)}, u32[]{:S(2)}, u32[]{:S(2)}) collective-permute-start(bf16[8,512]{1,0:T(8,128)(2,1)S(1)} %get-tuple-element.39), channel_id=1, source_target_pairs={{0,2},{1,3},{4,6},{5,7},{8,10},{9,11},{12,14},{13,15},{16,18},{17,... | collective-permute-start | bytes 24584 | tf_op jit(solution)/shard_map/ppermute | solution.py:487
  12.9 3.7 %collective-permute-start.5 = (bf16[8,512]{1,0:T(8,128)(2,1)S(1)}, bf16[8,512]{1,0:T(8,128)(2,1)S(1)}, u32[]{:S(2)}, u32[]{:S(2)}) collective-permute-start(bf16[8,512]{1,0:T(8,128)(2,1)S(1)} %get-tuple-element.40), channel_id=1, source_target_pairs={{1,2},{3,4},{5,6},{7,8},{9,10},{11,12},{13,14},{17,18},{19,20},{21... | collective-permute-start | bytes 24584 | tf_op jit(solution)/shard_map/ppermute | solution.py:487
  13.4 3.1 %collective-permute-start.6 = (bf16[8,512]{1,0:T(8,128)(2,1)S(1)}, bf16[8,512]{1,0:T(8,128)(2,1)S(1)}, u32[]{:S(2)}, u32[]{:S(2)}) collective-permute-start(bf16[8,512]{1,0:T(8,128)(2,1)S(1)} %get-tuple-element.41), channel_id=1, source_target_pairs={{2,4},{3,5},{6,8},{7,9},{10,12},{11,13},{0,1},{14,15},{18,20},{19,... | collective-permute-start | bytes 24584 | tf_op jit(solution)/shard_map/ppermute | solution.py:487
  13.4 3.1 %collective-permute-start.7 = (bf16[8,512]{1,0:T(8,128)(2,1)S(1)}, bf16[8,512]{1,0:T(8,128)(2,1)S(1)}, u32[]{:S(2)}, u32[]{:S(2)}) collective-permute-start(bf16[8,512]{1,0:T(8,128)(2,1)S(1)} %get-tuple-element.42), channel_id=1, source_target_pairs={{0,1},{2,3},{4,5},{6,7},{8,9},{10,11},{12,13},{14,15},{16,17},{18,... | collective-permute-start | bytes 24584 | tf_op jit(solution)/shard_map/ppermute | solution.py:487

commit v10 on v7

--- a/solution.py
+++ b/solution.py
@@ -323,31 +323,46 @@
         entry_ref[d : d + 1, :] = jnp.full((1, width), entry, F32)
 
 
-def base_kernel(slots, state_ref, diag_ref, forcing_ref, entry_ref, flux_ref, source_ref, order_ref,
-                prod_out_ref, rest_ref, flux_out_ref, hot_ref, wide_ref, prod_ref):
+def local_lift(pool, hot, flux, spread, lift, insts, elems):
+    empty = jnp.zeros((hot.shape[1] - pool.shape[0], pool.shape[1]), BF16)
+    pool = jnp.concatenate([pool, empty], 0)
+    picked = jnp.dot(hot, pool, preferred_element_type=F32).astype(BF16)
+    normal = face_flux(picked, flux.astype(F32), spread, insts)
+    return lift_faces(normal, lift, elems)
+
+
+def slot_lift(blocks, factors, hot, lift, insts, elems):
+    normal = slot_normal(blocks, factors, insts)
+    empty = jnp.zeros((FACES * elems, insts * LANE), BF16)
+    rows = jnp.concatenate([empty, jnp.concatenate(normal, 1)], 0)
+    spots = jnp.dot(hot, rows, preferred_element_type=F32).astype(BF16)
+    return lift_faces([spots[:, t * LANE : (t + 1) * LANE] for t in range(insts)], lift, elems)
+
+
+def base_kernel(slots, state_ref, diag_ref, forcing_ref, entry_ref, pool_ref, flux_ref, source_ref,
+                order_ref, spread_ref, lift_ref, spatial_ref, rest_ref, flux_out_ref, hot_ref,
+                factor_ref, wide_ref, prod_ref):
     insts, elems, width = state_ref.shape
-    hot_ref[...] = source_table(source_ref[...].T, elems, slots)
-    flux_out_ref[...] = flux_order(flux_ref[...], order_ref[...])
+    hot = source_table(source_ref[...].T, elems, slots)
+    flux = flux_order(flux_ref[...], order_ref[...])
+    hot_ref[...] = hot
+    flux_out_ref[...] = flux
+    factors = lax.dot_general(hot, flux, (((0,), (0,)), ((), ())), preferred_element_type=F32)
+    factor_ref[...] = rotated(factors[FACES * elems :])
+    lifted = local_lift(pool_ref[...], hot, flux, spread_ref[...], lift_ref[...], insts, elems)
     states = [state_ref[t] for t in range(insts)]
     products = diagonal(states, diag_ref, wide_ref, prod_ref, insts, elems)
     for t in range(insts):
-        prod_out_ref[t] = products[t]
+        spatial_ref[t] = products[t] + lifted[t * elems : (t + 1) * elems]
         rest_ref[t] = couple(entry_ref, states, t, 0, insts) - forcing_ref[t].astype(F32)
 
 
 def last_base_kernel(state_ref, pool_ref, diag_ref, forcing_ref, hot_ref, flux_ref, spread_ref,
-                     lift_ref, base_ref, factor_ref, wide_ref, prod_ref):
+                     lift_ref, base_ref, wide_ref, prod_ref):
     insts, elems, width = state_ref.shape
-    flux = flux_ref[...]
-    hot = hot_ref[...]
-    faces = hot.shape[0]
-    factors = lax.dot_general(hot, flux, (((0,), (0,)), ((), ())), preferred_element_type=F32)
-    factor_ref[...] = rotated(factors[faces:])
-    empty = jnp.zeros((hot.shape[1] - faces, insts * LANE), BF16)
-    pool = jnp.concatenate([pool_ref[...], empty], 0)
-    picked = jnp.dot(hot, pool, preferred_element_type=F32).astype(BF16)
-    normal = face_flux(picked, flux.astype(F32), spread_ref[...], insts)
-    lifted = lift_faces(normal, lift_ref[...], elems)
+    lifted = local_lift(
+        pool_ref[...], hot_ref[...], flux_ref[...], spread_ref[...], lift_ref[...], insts, elems
+    )
     states = [state_ref[t].astype(BF16) for t in range(insts)]
     products = diagonal(states, diag_ref, wide_ref, prod_ref, insts, elems)
     for t in range(insts):
@@ -396,21 +411,18 @@
     return jnp.concatenate(arrived, 0)
 
 
-def step_kernel(parts, place_ref, spread_ref, *refs):
+def step_kernel(parts, place_ref, *refs):
     got_refs, refs = refs[: len(OFFSETS)], refs[len(OFFSETS) :]
-    (state_ref, pool_ref, prod_ref, rest_ref, hot_ref, flux_ref, lift_ref, trace_ref, send_ref,
+    (state_ref, local_ref, rest_ref, hot_ref, factor_ref, lift_ref, trace_ref, send_ref,
      partial_ref, message_ref, next_pool_ref, *out_refs) = refs
     insts, elems, width = state_ref.shape
     place = place_ref[0]
-    blocks = received(parts, place, got_refs, FIRST_ORDER).astype(BF16)
-    pool = jnp.concatenate([pool_ref[...], blocks], 0)
-    picked = jnp.dot(hot_ref[...], pool, preferred_element_type=F32).astype(BF16)
-    normal = face_flux(picked, flux_ref[...].astype(F32), spread_ref[...], insts)
-    lifted = lift_faces(normal, lift_ref[...], elems)
+    blocks = received(parts, place, got_refs, FIRST_ORDER)
+    lifted = slot_lift(blocks, factor_ref[...], hot_ref[...], lift_ref[...], insts, elems)
     message_ref[...] = jnp.zeros_like(message_ref)
     fresh = []
     for t in range(insts):
-        spatial = prod_ref[t] + lifted[t * elems : (t + 1) * elems]
+        spatial = local_ref[t] + lifted[t * elems : (t + 1) * elems]
         moved = state_ref[t].astype(F32) - pseudo_step * (spatial + rest_ref[t])
         partial_ref[t] = moved
         fresh.append(moved.astype(BF16))
@@ -429,13 +441,7 @@
      final_ref, residual_ref, sems) = refs
     insts, elems, width = state_ref.shape
     blocks = received(parts, place_ref[0], got_refs, LAST_ORDER)
-    normal = slot_normal(blocks, factor_ref[...], insts)
-    empty = jnp.zeros((FACES * elems, insts * LANE), BF16)
-    rows = jnp.concatenate([empty, jnp.concatenate(normal, 1)], 0)
-    spots = jnp.dot(hot_ref[...], rows, preferred_element_type=F32).astype(BF16)
-    lifted = lift_faces(
-        [spots[:, t * LANE : (t + 1) * LANE] for t in range(insts)], lift_ref[...], elems
-    )
+    lifted = slot_lift(blocks, factor_ref[...], hot_ref[...], lift_ref[...], insts, elems)
     copies = []
     for t in range(insts):
         residual = base_ref[t] + lifted[t * elems : (t + 1) * elems]
@@ -514,35 +520,35 @@
         name="first_traces",
     )(place, freq, spread, initial_state, trace_wide, send_list)
     got = exchange(outgoing, FIRST_ORDER)
-    product, rest, flux, hot = pl.pallas_call(
+    local, rest, flux, hot, factors = pl.pallas_call(
         functools.partial(base_kernel, slots * capacity),
-        out_shape=[wide_shape] * 2 + [flux_shape, hot_shape],
-        in_specs=[vmem] * 7,
-        out_specs=[vmem] * 4,
+        out_shape=[wide_shape] * 2 + [flux_shape, hot_shape, factor_shape],
+        in_specs=[vmem] * 10,
+        out_specs=[vmem] * 5,
         scratch_shapes=chunks,
         compiler_params=params,
         cost_estimate=diag_cost,
         name="own_terms",
-    )(initial_state, diagonal_blocks, forcing, entries, flux_jacobian, sources, order)
+    )(initial_state, diagonal_blocks, forcing, entries, pool, flux_jacobian, sources, order, spread,
+      lift_wide)
     partial, message, pool, *outgoing = pl.pallas_call(
         functools.partial(step_kernel, parts),
         out_shape=[wide_shape, message_shape, pool_shape] + out_shapes,
-        in_specs=[smem] + [vmem] * (slots + 10),
+        in_specs=[smem] + [vmem] * (slots + 8),
         out_specs=[vmem] * (3 + len(out_shapes)),
         compiler_params=params,
         name="first_step",
-    )(place, spread, *got, initial_state, pool, product, rest, hot, flux, lift_wide, trace_wide,
-      send_list)
+    )(place, *got, initial_state, local, rest, hot, factors, lift_wide, trace_wide, send_list)
     messages = [
         lax.ppermute(message, "inst", [((i + rank) % ranks, i) for i in range(ranks)])
         for rank in range(1, ranks)
     ]
     got = exchange(outgoing, LAST_ORDER)
-    base, factors = pl.pallas_call(
+    base = pl.pallas_call(
         last_base_kernel,
-        out_shape=[wide_shape, factor_shape],
+        out_shape=wide_shape,
         in_specs=[vmem] * 8,
-        out_specs=[vmem] * 2,
+        out_specs=vmem,
         scratch_shapes=chunks,
         compiler_params=params,
         cost_estimate=diag_cost,

time: 17.9 us -> 17.8 us (level)
  Pallas kernels: 4.79 us -> 5.22 us
  starting transfers between devices: 9.91 us -> 9.49 us
    pallas_call x1, Pallas kernels: 0.82 us -> 1.44 us  [on_device(): pl.pallas_call(functools.partial(base_kernel, slots * capacity), out_shap...]
    ppermute x8, starting transfers between devices: 8.4 us -> 7.94 us  [exchange(): lax.ppermute(outgoing[swap], ('inst', 'dom'), routes[swap])]
  transfers between devices with their start and end apart: 9 -> 9, of which waited for: 2 -> 2; matrix products, arithmetic and copies ran while one was open for 0% -> 0% of each run, Pallas kernels for 12% -> 16%
where the time goes in v10:
time: 17.8 us; the launch traced here: 17.5 us
  starting transfers between devices  9.49 us (53%)
  Pallas kernels  5.22 us (29%)
  between operations  1.43 us (8%)
  waiting for transfers between devices  1.18 us (7%)
  local copies, waits for them, and re-layouts  0.2 us (1%)
    ppermute x8, starting transfers between devices, exchange(): lax.ppermute(outgoing[swap], ('inst', 'dom'), routes[swap])  7.94 us
    ppermute x1, starting transfers between devices, on_device(): lax.ppermute(message, 'inst', [((i + rank) % ranks, i) for i in range(ran...  1.55 us
    pallas_call x1, Pallas kernels, on_device(): pl.pallas_call(functools.partial(base_kernel, slots * capacity), out_shap...  1.44 us
    ppermute x8, waiting for transfers between devices, exchange(): lax.ppermute(outgoing[swap], ('inst', 'dom'), routes[swap])  1.17 us
    pallas_call x1, Pallas kernels, on_device(): pl.pallas_call(functools.partial(last_kernel, parts), out_shape=[like(ini...  1.17 us
    pallas_call x1, Pallas kernels, on_device(): pl.pallas_call(last_base_kernel, out_shape=wide_shape, in_specs=[vmem] *...  1.13 us
    pallas_call x1, Pallas kernels, on_device(): pl.pallas_call(functools.partial(step_kernel, parts), out_shape=[wide_sha...  0.81 us
  transfers between devices with their start and end apart: 9, of which 2 were waited for; matrix products, arithmetic and copies ran while one was open for 0% of the time, Pallas kernels for 16%

profile of v10, /device:TPU:0, one launch (start us, length us, event | category | flops | bytes accessed | tf_op | source)
XLA Modules:
  0.0 17.5 jit_solution(5023951054238083329)
XLA Ops:
  0.6 0.0 copy-start.2
  0.6 0.0 copy-start.3
  0.7 0.0 copy-start.7
  0.7 0.2 %tables.1 = (bf16[128,640]{1,0:T(8,128)(2,1)S(1)}, bf16[400,640]{1,0:T(8,128)(2,1)S(1)}) custom-call(), custom_call_target="tpu_custom_call" | custom-call | flops 10000000000 | bytes 1000000 | tf_op jit(solution)/shard_map/tables/pallas_call | solution.py:501
  1.5 0.2 copy-done.2
  1.7 0.0 copy-start.4
  1.7 0.0 copy-start.5
  1.7 0.0 copy-start.6
  1.7 0.3 %first_traces.1 = (f32[8,320]{1,0:T(8,128)S(1)}, bf16[96,512]{1,0:T(8,128)(2,1)S(1)}, bf16[8,512]{1,0:T(8,128)(2,1)S(1)}, bf16[8,512]{1,0:T(8,128)(2,1)S(1)}, bf...) custom-call(s32[1]{0:T(128)} %bitcast.place_ref, f32[1]{0:T(128)S(6)} %copy.11.freq_ref, ...), custom_call_target="tpu_custom_call" | custom-call | flops 10000000000 | bytes 1000000 | tf_op jit(solution)/shard_map/first_traces/pallas_call | solution.py:513
  2.1 0.5 %collective-permute-start = (bf16[8,512]{1,0:T(8,128)(2,1)S(1)}, bf16[8,512]{1,0:T(8,128)(2,1)S(1)}, u32[]{:S(2)}, u32[]{:S(2)}) collective-permute-start(bf16[8,512]{1,0:T(8,128)(2,1)S(1)} %get-tuple-element.27), channel_id=1, source_target_pairs={{2,4},{3,5},{6,8},{7,9},{10,12},{11,13},{0,1},{14,15},{18,20},{19,... | collective-permute-start | bytes 24584 | tf_op jit(solution)/shard_map/ppermute | solution.py:491
  2.6 2.6 %collective-permute-start.1 = (bf16[8,512]{1,0:T(8,128)(2,1)S(1)}, bf16[8,512]{1,0:T(8,128)(2,1)S(1)}, u32[]{:S(2)}, u32[]{:S(2)}) collective-permute-start(bf16[8,512]{1,0:T(8,128)(2,1)S(1)} %get-tuple-element.28), channel_id=1, source_target_pairs={{1,2},{3,4},{5,6},{7,8},{9,10},{11,12},{13,14},{17,18},{19,20},{21... | collective-permute-start | bytes 24584 | tf_op jit(solution)/shard_map/ppermute | solution.py:491
  5.2 1.5 %collective-permute-start.2 = (bf16[8,512]{1,0:T(8,128)(2,1)S(1)}, bf16[8,512]{1,0:T(8,128)(2,1)S(1)}, u32[]{:S(2)}, u32[]{:S(2)}) collective-permute-start(bf16[8,512]{1,0:T(8,128)(2,1)S(1)} %get-tuple-element.29), channel_id=1, source_target_pairs={{0,2},{1,3},{4,6},{5,7},{8,10},{9,11},{12,14},{13,15},{16,18},{17,... | collective-permute-start | bytes 24584 | tf_op jit(solution)/shard_map/ppermute | solution.py:491
  6.7 1.2 %collective-permute-start.3 = (bf16[8,512]{1,0:T(8,128)(2,1)S(1)}, bf16[8,512]{1,0:T(8,128)(2,1)S(1)}, u32[]{:S(2)}, u32[]{:S(2)}) collective-permute-start(bf16[8,512]{1,0:T(8,128)(2,1)S(1)} %get-tuple-element.30), channel_id=1, source_target_pairs={{0,1},{2,3},{4,5},{6,7},{8,9},{10,11},{12,13},{14,15},{16,17},{18,... | collective-permute-start | bytes 24584 | tf_op jit(solution)/shard_map/ppermute | solution.py:491
  7.9 1.4 %own_terms.1 = (f32[4,16,320]{2,1,0:T(8,128)S(1)}, f32[4,16,320]{2,1,0:T(8,128)S(1)}, bf16[96,640]{1,0:T(8,128)(2,1)S(1)}, bf16[96,128]{1,0:T(8,128)(2,1)S(1)}, f32[32,1024]{1,0:T(8,128)S(1)}) custom-call(bf16[4,16,320]{2,1,0:T(8,128)(2,1)S(1)} %copy-done.3, bf16[16,320,320]{2,1,0:T(8,128)(2,1)S(1)} %copy-done, bf16[4,16,320]{2,1,0:T(8,128)(2,1)S(1)} %copy-done.4, ...), custom_call_target="tpu_custom_call" | custom-call | flops 13107200 | bytes 3276800 | tf_op jit(solution)/shard_map/own_terms/pallas_call | solution.py:523
  9.3 0.0 collective-permute-done.refs_0_
  9.3 0.0 collective-permute-done.1.refs_1_
  9.3 0.0 collective-permute-done.2.refs_2_
  9.4 0.0 collective-permute-done.3.refs_3_
  9.4 0.8 %first_step.1 = (f32[4,16,320]{2,1,0:T(8,128)S(1)}, bf16[128,384]{1,0:T(8,128)(2,1)S(1)}, bf16[96,512]{1,0:T(8,128)(2,1)S(1)}, bf16[8,512]{1,0:T(8,128)(2,1)S(1)...) custom-call(s32[1]{0:T(128)} %bitcast.place_ref, ...), custom_call_target="tpu_custom_call" | custom-call | tf_op jit(solution)/shard_map/first_step/pallas_call | solution.py:534
  10.2 1.6 %collective-permute-start.8 = (bf16[128,384]{1,0:T(8,128)(2,1)S(1)}, bf16[128,384]{1,0:T(8,128)(2,1)S(1)}, u32[]{:S(2)}, u32[]{:S(2)}) collective-permute-start(bf16[128,384]{1,0:T(8,128)(2,1)S(1)} %get-tuple-element.45), channel_id=1, source_target_pairs={{16,0},{0,16},{17,1},{1,17},{18,2},{2,18},{19,3},{3,19},{20,4},{4,... | collective-permute-start | bytes 294920 | tf_op jit(solution)/shard_map/ppermute | solution.py:543
  11.7 0.9 %collective-permute-start.4 = (bf16[8,512]{1,0:T(8,128)(2,1)S(1)}, bf16[8,512]{1,0:T(8,128)(2,1)S(1)}, u32[]{:S(2)}, u32[]{:S(2)}) collective-permute-start(bf16[8,512]{1,0:T(8,128)(2,1)S(1)} %get-tuple-element.38), channel_id=1, source_target_pairs={{0,2},{1,3},{4,6},{5,7},{8,10},{9,11},{12,14},{13,15},{16,18},{17,... | collective-permute-start | bytes 24584 | tf_op jit(solution)/shard_map/ppermute | solution.py:491
  12.7 0.5 %collective-permute-start.5 = (bf16[8,512]{1,0:T(8,128)(2,1)S(1)}, bf16[8,512]{1,0:T(8,128)(2,1)S(1)}, u32[]{:S(2)}, u32[]{:S(2)}) collective-permute-start(bf16[8,512]{1,0:T(8,128)(2,1)S(1)} %get-tuple-element.39), channel_id=1, source_target_pairs={{1,2},{3,4},{5,6},{7,8},{9,10},{11,12},{13,14},{17,18},{19,20},{21... | collective-permute-start | bytes 24584 | tf_op jit(solution)/shard_map/ppermute | solution.py:491
  13.2 0.7 %collective-permute-start.6 = (bf16[8,512]{1,0:T(8,128)(2,1)S(1)}, bf16[8,512]{1,0:T(8,128)(2,1)S(1)}, u32[]{:S(2)}, u32[]{:S(2)}) collective-permute-start(bf16[8,512]{1,0:T(8,128)(2,1)S(1)} %get-tuple-element.40), channel_id=1, source_target_pairs={{2,4},{3,5},{6,8},{7,9},{10,12},{11,13},{0,1},{14,15},{18,20},{19,... | collective-permute-start | bytes 24584 | tf_op jit(solution)/shard_map/ppermute | solution.py:491
  13.9 0.0 collective-permute-start.7
  13.9 1.1 %last_own_terms.1.base_ref = f32[4,16,320]{2,1,0:T(8,128)S(1)} custom-call(f32[4,16,320]{2,1,0:T(8,128)S(1)} %get-tuple-element.42.state_ref.partial_ref, bf16[96,512]{1,0:T(8,128)(2,1)S(1)} %get-tuple-element.43.pool_ref, bf16[16,320,320]{2,1,0:T(8,128)(2,1)S(1)} %copy-done, bf16[4,16,320]{2,1,0:T(8,128)(2,1)S(1)} %copy-done.4, ...), custom_call_target="tpu_custom_call" | custom-call | flops 13107200 | bytes 3276800 | tf_op jit(solution)/shard_map/last_own_terms/pallas_call | solution.py:547
  15.0 0.0 collective-permute-done.8.refs_0_
  15.0 0.1 message_terms.1
  15.2 0.2 %collective-permute-done.4.refs_0_ = bf16[8,512]{1,0:T(8,128)(2,1)S(1)} collective-permute-done((bf16[8,512]{1,0:T(8,128)(2,1)S(1)}, bf16[8,512]{1,0:T(8,128)(2,1)S(1)}, u32[]{:S(2)}, u32[]{:S(2)}) %collective-permute-start.4) | collective-permute-done | bytes 8224 | tf_op jit(solution)/shard_map/ppermute | solution.py:491
  15.4 0.9 %collective-permute-done.5.refs_1_ = bf16[8,512]{1,0:T(8,128)(2,1)S(1)} collective-permute-done((bf16[8,512]{1,0:T(8,128)(2,1)S(1)}, bf16[8,512]{1,0:T(8,128)(2,1)S(1)}, u32[]{:S(2)}, u32[]{:S(2)}) %collective-permute-start.5) | collective-permute-done | bytes 8224 | tf_op jit(solution)/shard_map/ppermute | solution.py:491
  16.3 0.0 collective-permute-done.6.refs_2_
  16.3 0.0 collective-permute-done.7.refs_3_
  16.3 1.2 %last_step.1 = (bf16[4,16,320]{2,1,0:T(8,128)(2,1)}, f32[4,16,320]{2,1,0:T(8,128)}) custom-call(s32[1]{0:T(128)} %bitcast.place_ref, bf16[8,512]{1,0:T(8,128)(2,1)S(1)} %collective-permute-done.4.refs_0_, bf16[8,512]{1,0:T(8,128)(2,1)S(1)} %collective-permute-done.5.refs_1_, bf16[8,512]{1,0:T(8,128)(2,1)S(1)} %collective-permute-done.6.refs_2_, ...), custom_call_target="tpu_custom_call" | custom-call | tf_op jit(solution)/shard_map/last_step/pallas_call | solution.py:565
  (9 shorter events, 0.0 us)
Async XLA Ops:
  0.6 1.0 %copy-start.2 = (bf16[320,768]{1,0:T(8,128)(2,1)S(1)}, bf16[320,768]{1,0:T(8,128)(2,1)}, u32[]{:S(2)}) copy-start(bf16[320,768]{1,0:T(8,128)(2,1)} %constant.8.clone.trace_ref.refs_10_) | copy-start | bytes 1474564
  0.6 1.0 %copy-start.3 = (bf16[4,16,320]{2,1,0:T(8,128)(2,1)S(1)}, bf16[4,16,320]{2,1,0:T(8,128)(2,1)}, u32[]{:S(2)}) copy-start(bf16[4,16,320]{2,1,0:T(8,128)(2,1)} %first_ref.1) | copy-start | bytes 122884
  0.7 1.0 %copy-start.7 = (s32[1,4,8]{2,1,0:T(4,128)S(1)}, s32[1,4,8]{2,1,0:T(4,128)}, u32[]{:S(2)}) copy-start(s32[1,4,8]{2,1,0:T(4,128)} %refs_11_.1) | copy-start | bytes 388
  1.7 6.2 %copy-start = (bf16[16,320,320]{2,1,0:T(8,128)(2,1)S(1)}, bf16[16,320,320]{2,1,0:T(8,128)(2,1)}, u32[]{:S(2)}) copy-start(bf16[16,320,320]{2,1,0:T(8,128)(2,1)} %diag_ref.3) | copy-start | bytes 9830404
  1.7 6.2 %copy-start.1 = (bf16[768,320]{1,0:T(8,128)(2,1)S(1)}, bf16[768,320]{1,0:T(8,128)(2,1)}, u32[]{:S(2)}) copy-start(bf16[768,320]{1,0:T(8,128)(2,1)} %constant.9.clone.lift_ref.refs_9_.refs_8_) | copy-start | bytes 1474564
  1.7 6.2 %copy-start.4 = (bf16[4,16,320]{2,1,0:T(8,128)(2,1)S(1)}, bf16[4,16,320]{2,1,0:T(8,128)(2,1)}, u32[]{:S(2)}) copy-start(bf16[4,16,320]{2,1,0:T(8,128)(2,1)} %forcing_ref.3) | copy-start | bytes 122884
  1.7 6.2 %copy-start.5 = (bf16[16,2400]{1,0:T(8,128)(2,1)S(1)}, bf16[16,2400]{1,0:T(8,128)(2,1)}, u32[]{:S(2)}) copy-start(bf16[16,2400]{1,0:T(8,128)(2,1)} %flux_ref.1) | copy-start | bytes 230404
  1.7 6.2 %copy-start.6 = (s32[16,6]{0,1:T(8,128)S(1)}, s32[16,6]{0,1:T(8,128)}, u32[]{:S(2)}) copy-start(s32[16,6]{0,1:T(8,128)} %param.14) | copy-start | bytes 1156
  2.1 7.3 %collective-permute-start = (bf16[8,512]{1,0:T(8,128)(2,1)S(1)}, bf16[8,512]{1,0:T(8,128)(2,1)S(1)}, u32[]{:S(2)}, u32[]{:S(2)}) collective-permute-start(bf16[8,512]{1,0:T(8,128)(2,1)S(1)} %get-tuple-element.27), channel_id=1, source_target_pairs={{2,4},{3,5},{6,8},{7,9},{10,12},{11,13},{0,1},{14,15},{18,20},{19,... | collective-permute-start | bytes 24584 | tf_op jit(solution)/shard_map/ppermute | solution.py:491
  2.6 6.8 %collective-permute-start.1 = (bf16[8,512]{1,0:T(8,128)(2,1)S(1)}, bf16[8,512]{1,0:T(8,128)(2,1)S(1)}, u32[]{:S(2)}, u32[]{:S(2)}) collective-permute-start(bf16[8,512]{1,0:T(8,128)(2,1)S(1)} %get-tuple-element.28), channel_id=1, source_target_pairs={{1,2},{3,4},{5,6},{7,8},{9,10},{11,12},{13,14},{17,18},{19,20},{21... | collective-permute-start | bytes 24584 | tf_op jit(solution)/shard_map/ppermute | solution.py:491
  5.2 4.2 %collective-permute-start.2 = (bf16[8,512]{1,0:T(8,128)(2,1)S(1)}, bf16[8,512]{1,0:T(8,128)(2,1)S(1)}, u32[]{:S(2)}, u32[]{:S(2)}) collective-permute-start(bf16[8,512]{1,0:T(8,128)(2,1)S(1)} %get-tuple-element.29), channel_id=1, source_target_pairs={{0,2},{1,3},{4,6},{5,7},{8,10},{9,11},{12,14},{13,15},{16,18},{17,... | collective-permute-start | bytes 24584 | tf_op jit(solution)/shard_map/ppermute | solution.py:491
  6.7 2.7 %collective-permute-start.3 = (bf16[8,512]{1,0:T(8,128)(2,1)S(1)}, bf16[8,512]{1,0:T(8,128)(2,1)S(1)}, u32[]{:S(2)}, u32[]{:S(2)}) collective-permute-start(bf16[8,512]{1,0:T(8,128)(2,1)S(1)} %get-tuple-element.30), channel_id=1, source_target_pairs={{0,1},{2,3},{4,5},{6,7},{8,9},{10,11},{12,13},{14,15},{16,17},{18,... | collective-permute-start | bytes 24584 | tf_op jit(solution)/shard_map/ppermute | solution.py:491
  10.2 4.8 %collective-permute-start.8 = (bf16[128,384]{1,0:T(8,128)(2,1)S(1)}, bf16[128,384]{1,0:T(8,128)(2,1)S(1)}, u32[]{:S(2)}, u32[]{:S(2)}) collective-permute-start(bf16[128,384]{1,0:T(8,128)(2,1)S(1)} %get-tuple-element.45), channel_id=1, source_target_pairs={{16,0},{0,16},{17,1},{1,17},{18,2},{2,18},{19,3},{3,19},{20,4},{4,... | collective-permute-start | bytes 294920 | tf_op jit(solution)/shard_map/ppermute | solution.py:543
  11.7 3.7 %collective-permute-start.4 = (bf16[8,512]{1,0:T(8,128)(2,1)S(1)}, bf16[8,512]{1,0:T(8,128)(2,1)S(1)}, u32[]{:S(2)}, u32[]{:S(2)}) collective-permute-start(bf16[8,512]{1,0:T(8,128)(2,1)S(1)} %get-tuple-element.38), channel_id=1, source_target_pairs={{0,2},{1,3},{4,6},{5,7},{8,10},{9,11},{12,14},{13,15},{16,18},{17,... | collective-permute-start | bytes 24584 | tf_op jit(solution)/shard_map/ppermute | solution.py:491
  12.7 3.7 %collective-permute-start.5 = (bf16[8,512]{1,0:T(8,128)(2,1)S(1)}, bf16[8,512]{1,0:T(8,128)(2,1)S(1)}, u32[]{:S(2)}, u32[]{:S(2)}) collective-permute-start(bf16[8,512]{1,0:T(8,128)(2,1)S(1)} %get-tuple-element.39), channel_id=1, source_target_pairs={{1,2},{3,4},{5,6},{7,8},{9,10},{11,12},{13,14},{17,18},{19,20},{21... | collective-permute-start | bytes 24584 | tf_op jit(solution)/shard_map/ppermute | solution.py:491
  13.2 3.1 %collective-permute-start.6 = (bf16[8,512]{1,0:T(8,128)(2,1)S(1)}, bf16[8,512]{1,0:T(8,128)(2,1)S(1)}, u32[]{:S(2)}, u32[]{:S(2)}) collective-permute-start(bf16[8,512]{1,0:T(8,128)(2,1)S(1)} %get-tuple-element.40), channel_id=1, source_target_pairs={{2,4},{3,5},{6,8},{7,9},{10,12},{11,13},{0,1},{14,15},{18,20},{19,... | collective-permute-start | bytes 24584 | tf_op jit(solution)/shard_map/ppermute | solution.py:491
  13.9 2.5 %collective-permute-start.7 = (bf16[8,512]{1,0:T(8,128)(2,1)S(1)}, bf16[8,512]{1,0:T(8,128)(2,1)S(1)}, u32[]{:S(2)}, u32[]{:S(2)}) collective-permute-start(bf16[8,512]{1,0:T(8,128)(2,1)S(1)} %get-tuple-element.41), channel_id=1, source_target_pairs={{0,1},{2,3},{4,5},{6,7},{8,9},{10,11},{12,13},{14,15},{16,17},{18,... | collective-permute-start | bytes 24584 | tf_op jit(solution)/shard_map/ppermute | solution.py:491

commit v11 on v10

--- a/solution.py
+++ b/solution.py
@@ -96,6 +96,7 @@
 LANE = 128
 WIDE = FIELDS * NODES
 FACES = 6
+TRACE_TABLES = 3
 VMEM_LIMIT = 16 * 1024 * 1024
 BF16 = jnp.bfloat16
 F32 = jnp.float32
@@ -139,14 +140,14 @@
     return one_hot((place < FIELDS * FPTS) & (row == source))
 
 
-def trace_pool(state, trace_wide, insts, elems):
-    wide = jnp.dot(state, trace_wide, preferred_element_type=F32).astype(BF16)
+def trace_pool(state, trace_tables, insts, elems):
+    faces = []
+    for table in trace_tables:
+        wide = jnp.dot(state, table, preferred_element_type=F32).astype(BF16)
+        faces += [wide[:, at : at + LANE] for at in range(0, table.shape[1], LANE)]
     by_inst = []
     for t in range(insts):
-        rows = wide[t * elems : (t + 1) * elems]
-        by_inst.append(
-            jnp.concatenate([rows[:, f * LANE : (f + 1) * LANE] for f in range(FACES)], 0)
-        )
+        by_inst.append(jnp.concatenate([rows[t * elems : (t + 1) * elems] for rows in faces], 0))
     return jnp.concatenate(by_inst, 1)
 
 
@@ -160,8 +161,11 @@
     for pairs in near + far:
         met = {p for pair in pairs for p in pair}
         alone = [p for p in range(parts) if p not in met]
-        idle = [(p, p + 1) for p in alone if p + 1 in alone]
-        alone = [p for p in alone if p + 1 not in alone and p - 1 not in alone]
+        idle = []
+        for p in list(alone):
+            if p in alone and p + 1 in alone:
+                idle.append((p, p + 1))
+                alone = [q for q in alone if q not in idle[-1]]
         swaps = [(r * parts + p, r * parts + q) for r in range(ranks) for p, q in pairs + idle]
         swaps += [(r * parts + p, (r ^ 1) * parts + p) for r in range(0, ranks, 2) for p in alone]
         routes.append(swaps + [(q, p) for p, q in swaps])
@@ -310,11 +314,11 @@
     order_ref[...] = order_table()
 
 
-def first_kernel(spectral, second, place_ref, freq_ref, spread_ref, state_ref, trace_ref, send_ref,
-                 entry_ref, pool_ref, *out_refs):
+def first_kernel(spectral, second, place_ref, freq_ref, spread_ref, state_ref, send_ref, *refs):
     insts, elems, width = state_ref.shape
+    trace_refs, (entry_ref, pool_ref, *out_refs) = refs[:TRACE_TABLES], refs[TRACE_TABLES:]
     state = state_ref[...].reshape(insts * elems, width)
-    pool = trace_pool(state, trace_ref[...], insts, elems)
+    pool = trace_pool(state, [ref[...] for ref in trace_refs], insts, elems)
     pool_ref[...] = pool
     fill_outgoing(pool, send_ref[0], out_refs, place_ref[0], elems)
     freq = freq_ref[0]
@@ -413,7 +417,8 @@
 
 def step_kernel(parts, place_ref, *refs):
     got_refs, refs = refs[: len(OFFSETS)], refs[len(OFFSETS) :]
-    (state_ref, local_ref, rest_ref, hot_ref, factor_ref, lift_ref, trace_ref, send_ref,
+    trace_refs, refs = refs[:TRACE_TABLES], refs[TRACE_TABLES:]
+    (state_ref, local_ref, rest_ref, hot_ref, factor_ref, lift_ref, send_ref,
      partial_ref, message_ref, next_pool_ref, *out_refs) = refs
     insts, elems, width = state_ref.shape
     place = place_ref[0]
@@ -430,7 +435,8 @@
         for i, block in enumerate((state_ref[t], lean)):
             low = (i * insts + t) * elems
             message_ref[low : low + elems, 0:width] = block
-    pool = trace_pool(jnp.concatenate(fresh, 0), trace_ref[...], insts, elems)
+    tables_of_traces = [ref[...] for ref in trace_refs]
+    pool = trace_pool(jnp.concatenate(fresh, 0), tables_of_traces, insts, elems)
     next_pool_ref[...] = pool
     fill_outgoing(pool, send_ref[0], out_refs, place, elems)
 
@@ -442,17 +448,16 @@
     insts, elems, width = state_ref.shape
     blocks = received(parts, place_ref[0], got_refs, LAST_ORDER)
     lifted = slot_lift(blocks, factor_ref[...], hot_ref[...], lift_ref[...], insts, elems)
-    copies = []
     for t in range(insts):
         residual = base_ref[t] + lifted[t * elems : (t + 1) * elems]
         residual_ref[t] = residual
         final_ref[t] = (state_ref[t].astype(F32) - pseudo_step * residual).astype(BF16)
-        copies += [
-            pltpu.make_async_copy(residual_ref.at[t], residual_hbm.at[t], sems.at[0, t]),
-            pltpu.make_async_copy(final_ref.at[t], final_hbm.at[t], sems.at[1, t]),
-        ]
-        copies[-2].start()
-        copies[-1].start()
+    copies = [
+        pltpu.make_async_copy(residual_ref, residual_hbm, sems.at[0]),
+        pltpu.make_async_copy(final_ref, final_hbm, sems.at[1]),
+    ]
+    for copy in copies:
+        copy.start()
     for copy in copies:
         copy.wait()
 
@@ -466,7 +471,7 @@
     slots, capacity = send_list.shape[1:]
     faces = FACES * elems
     trace_np, lift_np, spectral, second = wide_tables()
-    trace_wide = jnp.asarray(trace_np, BF16)
+    trace_wide = [jnp.asarray(part, BF16) for part in np.split(trace_np, TRACE_TABLES, 1)]
     lift_wide = jnp.asarray(lift_np, BF16)
     place = lax.axis_index("dom").reshape(1)
     sources = source_index.T
@@ -513,12 +518,12 @@
     entries, pool, *outgoing = pl.pallas_call(
         functools.partial(first_kernel, spectral, second),
         out_shape=[entry_shape, pool_shape] + out_shapes,
-        in_specs=[smem] * 2 + [vmem] * 4,
+        in_specs=[smem] * 2 + [vmem] * (3 + TRACE_TABLES),
         out_specs=[vmem] * (2 + len(out_shapes)),
         compiler_params=params,
         cost_estimate=pl.CostEstimate(flops=10**10, bytes_accessed=10**6, transcendentals=0),
         name="first_traces",
-    )(place, freq, spread, initial_state, trace_wide, send_list)
+    )(place, freq, spread, initial_state, send_list, *trace_wide)
     got = exchange(outgoing, FIRST_ORDER)
     local, rest, flux, hot, factors = pl.pallas_call(
         functools.partial(base_kernel, slots * capacity),
@@ -534,11 +539,11 @@
     partial, message, pool, *outgoing = pl.pallas_call(
         functools.partial(step_kernel, parts),
         out_shape=[wide_shape, message_shape, pool_shape] + out_shapes,
-        in_specs=[smem] + [vmem] * (slots + 8),
+        in_specs=[smem] + [vmem] * (slots + 7 + TRACE_TABLES),
         out_specs=[vmem] * (3 + len(out_shapes)),
         compiler_params=params,
         name="first_step",
-    )(place, *got, initial_state, local, rest, hot, factors, lift_wide, trace_wide, send_list)
+    )(place, *got, *trace_wide, initial_state, local, rest, hot, factors, lift_wide, send_list)
     messages = [
         lax.ppermute(message, "inst", [((i + rank) % ranks, i) for i in range(ranks)])
         for rank in range(1, ranks)
@@ -570,7 +575,7 @@
         scratch_shapes=[
             pltpu.VMEM(initial_state.shape, BF16),
             pltpu.VMEM(initial_state.shape, F32),
-            pltpu.SemaphoreType.DMA((2, insts)),
+            pltpu.SemaphoreType.DMA((2,)),
         ],
         compiler_params=params,
         name="last_step",

time: 17.8 us -> 17.8 us (level)
  transfers between devices with their start and end apart: 9 -> 9, of which waited for: 2 -> 2; matrix products, arithmetic and copies ran while one was open for 0% -> 0% of each run, Pallas kernels for 16% -> 15%
where the time goes in v11:
time: 17.8 us; the launch traced here: 17.5 us
  starting transfers between devices  9.49 us (53%)
  Pallas kernels  5.18 us (29%)
  between operations  1.48 us (8%)
  waiting for transfers between devices  1.17 us (7%)
  local copies, waits for them, and re-layouts  0.19 us (1%)
    ppermute x8, starting transfers between devices, exchange(): lax.ppermute(outgoing[swap], ('inst', 'dom'), routes[swap])  7.94 us
    ppermute x1, starting transfers between devices, on_device(): lax.ppermute(message, 'inst', [((i + rank) % ranks, i) for i in range(ran...  1.56 us
    pallas_call x1, Pallas kernels, on_device(): pl.pallas_call(functools.partial(base_kernel, slots * capacity), out_shap...  1.44 us
    ppermute x8, waiting for transfers between devices, exchange(): lax.ppermute(outgoing[swap], ('inst', 'dom'), routes[swap])  1.17 us
    pallas_call x1, Pallas kernels, on_device(): pl.pallas_call(functools.partial(last_kernel, parts), out_shape=[like(ini...  1.14 us
    pallas_call x1, Pallas kernels, on_device(): pl.pallas_call(last_base_kernel, out_shape=wide_shape, in_specs=[vmem] *...  1.13 us
    pallas_call x1, Pallas kernels, on_device(): pl.pallas_call(functools.partial(step_kernel, parts), out_shape=[wide_sha...  0.81 us
  transfers between devices with their start and end apart: 9, of which 2 were waited for; matrix products, arithmetic and copies ran while one was open for 0% of the time, Pallas kernels for 15%

profile of v11, /device:TPU:0, one launch (start us, length us, event | category | flops | bytes accessed | tf_op | source)
XLA Modules:
  0.0 17.5 jit_solution(11541275732307158491)
XLA Ops:
  0.6 0.0 copy-start.4
  0.6 0.0 copy-start.5
  0.7 0.0 copy-start.6
  0.7 0.2 %tables.1 = (bf16[128,640]{1,0:T(8,128)(2,1)S(1)}, bf16[400,640]{1,0:T(8,128)(2,1)S(1)}) custom-call(), custom_call_target="tpu_custom_call" | custom-call | flops 10000000000 | bytes 1000000 | tf_op jit(solution)/shard_map/tables/pallas_call | solution.py:506
  1.6 0.1 copy-done.5
  1.6 0.1 copy-done.6
  1.7 0.0 copy-start.3
  1.7 0.0 copy-start.7
  1.8 0.0 copy-start.8
  1.8 0.3 %first_traces.1 = (f32[8,320]{1,0:T(8,128)S(1)}, bf16[96,512]{1,0:T(8,128)(2,1)S(1)}, bf16[8,512]{1,0:T(8,128)(2,1)S(1)}, bf16[8,512]{1,0:T(8,128)(2,1)S(1)}, bf...) custom-call(s32[1]{0:T(128)} %bitcast.place_ref, f32[1]{0:T(128)S(6)} %copy.13.freq_ref, ...), custom_call_target="tpu_custom_call" | custom-call | flops 10000000000 | bytes 1000000 | tf_op jit(solution)/shard_map/first_traces/pallas_call | solution.py:518
  2.1 0.5 %collective-permute-start = (bf16[8,512]{1,0:T(8,128)(2,1)S(1)}, bf16[8,512]{1,0:T(8,128)(2,1)S(1)}, u32[]{:S(2)}, u32[]{:S(2)}) collective-permute-start(bf16[8,512]{1,0:T(8,128)(2,1)S(1)} %get-tuple-element.27), channel_id=1, source_target_pairs={{2,4},{3,5},{6,8},{7,9},{10,12},{11,13},{0,1},{14,15},{18,20},{19,... | collective-permute-start | bytes 24584 | tf_op jit(solution)/shard_map/ppermute | solution.py:496
  2.6 2.6 %collective-permute-start.1 = (bf16[8,512]{1,0:T(8,128)(2,1)S(1)}, bf16[8,512]{1,0:T(8,128)(2,1)S(1)}, u32[]{:S(2)}, u32[]{:S(2)}) collective-permute-start(bf16[8,512]{1,0:T(8,128)(2,1)S(1)} %get-tuple-element.28), channel_id=1, source_target_pairs={{1,2},{3,4},{5,6},{7,8},{9,10},{11,12},{13,14},{17,18},{19,20},{21... | collective-permute-start | bytes 24584 | tf_op jit(solution)/shard_map/ppermute | solution.py:496
  5.2 1.5 %collective-permute-start.2 = (bf16[8,512]{1,0:T(8,128)(2,1)S(1)}, bf16[8,512]{1,0:T(8,128)(2,1)S(1)}, u32[]{:S(2)}, u32[]{:S(2)}) collective-permute-start(bf16[8,512]{1,0:T(8,128)(2,1)S(1)} %get-tuple-element.29), channel_id=1, source_target_pairs={{0,2},{1,3},{4,6},{5,7},{8,10},{9,11},{12,14},{13,15},{16,18},{17,... | collective-permute-start | bytes 24584 | tf_op jit(solution)/shard_map/ppermute | solution.py:496
  6.7 1.2 %collective-permute-start.3 = (bf16[8,512]{1,0:T(8,128)(2,1)S(1)}, bf16[8,512]{1,0:T(8,128)(2,1)S(1)}, u32[]{:S(2)}, u32[]{:S(2)}) collective-permute-start(bf16[8,512]{1,0:T(8,128)(2,1)S(1)} %get-tuple-element.30), channel_id=1, source_target_pairs={{0,1},{2,3},{4,5},{6,7},{8,9},{10,11},{12,13},{14,15},{16,17},{18,... | collective-permute-start | bytes 24584 | tf_op jit(solution)/shard_map/ppermute | solution.py:496
  7.9 1.4 %own_terms.1 = (f32[4,16,320]{2,1,0:T(8,128)S(1)}, f32[4,16,320]{2,1,0:T(8,128)S(1)}, bf16[96,640]{1,0:T(8,128)(2,1)S(1)}, bf16[96,128]{1,0:T(8,128)(2,1)S(1)}, f32[32,1024]{1,0:T(8,128)S(1)}) custom-call(bf16[4,16,320]{2,1,0:T(8,128)(2,1)S(1)} %copy-done.2, bf16[16,320,320]{2,1,0:T(8,128)(2,1)S(1)} %copy-done, bf16[4,16,320]{2,1,0:T(8,128)(2,1)S(1)} %copy-done.3, ...), custom_call_target="tpu_custom_call" | custom-call | flops 13107200 | bytes 3276800 | tf_op jit(solution)/shard_map/own_terms/pallas_call | solution.py:528
  9.4 0.0 collective-permute-done.refs_0_
  9.4 0.0 collective-permute-done.1.refs_1_
  9.4 0.0 collective-permute-done.2.refs_2_
  9.4 0.0 collective-permute-done.3.refs_3_
  9.4 0.8 %first_step.1 = (f32[4,16,320]{2,1,0:T(8,128)S(1)}, bf16[128,384]{1,0:T(8,128)(2,1)S(1)}, bf16[96,512]{1,0:T(8,128)(2,1)S(1)}, bf16[8,512]{1,0:T(8,128)(2,1)S(1)...) custom-call(s32[1]{0:T(128)} %bitcast.place_ref, ...), custom_call_target="tpu_custom_call" | custom-call | tf_op jit(solution)/shard_map/first_step/pallas_call | solution.py:539
  10.2 1.6 %collective-permute-start.8 = (bf16[128,384]{1,0:T(8,128)(2,1)S(1)}, bf16[128,384]{1,0:T(8,128)(2,1)S(1)}, u32[]{:S(2)}, u32[]{:S(2)}) collective-permute-start(bf16[128,384]{1,0:T(8,128)(2,1)S(1)} %get-tuple-element.45), channel_id=1, source_target_pairs={{16,0},{0,16},{17,1},{1,17},{18,2},{2,18},{19,3},{3,19},{20,4},{4,... | collective-permute-start | bytes 294920 | tf_op jit(solution)/shard_map/ppermute | solution.py:548
  11.8 0.9 %collective-permute-start.4 = (bf16[8,512]{1,0:T(8,128)(2,1)S(1)}, bf16[8,512]{1,0:T(8,128)(2,1)S(1)}, u32[]{:S(2)}, u32[]{:S(2)}) collective-permute-start(bf16[8,512]{1,0:T(8,128)(2,1)S(1)} %get-tuple-element.38), channel_id=1, source_target_pairs={{0,2},{1,3},{4,6},{5,7},{8,10},{9,11},{12,14},{13,15},{16,18},{17,... | collective-permute-start | bytes 24584 | tf_op jit(solution)/shard_map/ppermute | solution.py:496
  12.7 0.5 %collective-permute-start.5 = (bf16[8,512]{1,0:T(8,128)(2,1)S(1)}, bf16[8,512]{1,0:T(8,128)(2,1)S(1)}, u32[]{:S(2)}, u32[]{:S(2)}) collective-permute-start(bf16[8,512]{1,0:T(8,128)(2,1)S(1)} %get-tuple-element.39), channel_id=1, source_target_pairs={{1,2},{3,4},{5,6},{7,8},{9,10},{11,12},{13,14},{17,18},{19,20},{21... | collective-permute-start | bytes 24584 | tf_op jit(solution)/shard_map/ppermute | solution.py:496
  13.3 0.7 %collective-permute-start.6 = (bf16[8,512]{1,0:T(8,128)(2,1)S(1)}, bf16[8,512]{1,0:T(8,128)(2,1)S(1)}, u32[]{:S(2)}, u32[]{:S(2)}) collective-permute-start(bf16[8,512]{1,0:T(8,128)(2,1)S(1)} %get-tuple-element.40), channel_id=1, source_target_pairs={{2,4},{3,5},{6,8},{7,9},{10,12},{11,13},{0,1},{14,15},{18,20},{19,... | collective-permute-start | bytes 24584 | tf_op jit(solution)/shard_map/ppermute | solution.py:496
  13.9 0.0 collective-permute-start.7
  13.9 1.1 %last_own_terms.1.base_ref = f32[4,16,320]{2,1,0:T(8,128)S(1)} custom-call(f32[4,16,320]{2,1,0:T(8,128)S(1)} %get-tuple-element.42.state_ref.partial_ref, bf16[96,512]{1,0:T(8,128)(2,1)S(1)} %get-tuple-element.43.pool_ref, bf16[16,320,320]{2,1,0:T(8,128)(2,1)S(1)} %copy-done, bf16[4,16,320]{2,1,0:T(8,128)(2,1)S(1)} %copy-done.3, ...), custom_call_target="tpu_custom_call" | custom-call | flops 13107200 | bytes 3276800 | tf_op jit(solution)/shard_map/last_own_terms/pallas_call | solution.py:552
  15.1 0.0 collective-permute-done.8.refs_0_
  15.1 0.1 message_terms.1
  15.2 0.2 %collective-permute-done.4.refs_0_ = bf16[8,512]{1,0:T(8,128)(2,1)S(1)} collective-permute-done((bf16[8,512]{1,0:T(8,128)(2,1)S(1)}, bf16[8,512]{1,0:T(8,128)(2,1)S(1)}, u32[]{:S(2)}, u32[]{:S(2)}) %collective-permute-start.4) | collective-permute-done | bytes 8224 | tf_op jit(solution)/shard_map/ppermute | solution.py:496
  15.4 0.9 %collective-permute-done.5.refs_1_ = bf16[8,512]{1,0:T(8,128)(2,1)S(1)} collective-permute-done((bf16[8,512]{1,0:T(8,128)(2,1)S(1)}, bf16[8,512]{1,0:T(8,128)(2,1)S(1)}, u32[]{:S(2)}, u32[]{:S(2)}) %collective-permute-start.5) | collective-permute-done | bytes 8224 | tf_op jit(solution)/shard_map/ppermute | solution.py:496
  16.4 0.0 collective-permute-done.6.refs_2_
  16.4 1.1 %last_step.1 = (bf16[4,16,320]{2,1,0:T(8,128)(2,1)}, f32[4,16,320]{2,1,0:T(8,128)}) custom-call(s32[1]{0:T(128)} %bitcast.place_ref, bf16[8,512]{1,0:T(8,128)(2,1)S(1)} %collective-permute-done.4.refs_0_, bf16[8,512]{1,0:T(8,128)(2,1)S(1)} %collective-permute-done.5.refs_1_, bf16[8,512]{1,0:T(8,128)(2,1)S(1)} %collective-permute-done.6.refs_2_, ...), custom_call_target="tpu_custom_call" | custom-call | tf_op jit(solution)/shard_map/last_step/pallas_call | solution.py:570
  (13 shorter events, 0.0 us)
Async XLA Ops:
  0.6 0.9 %copy-start.4 = (bf16[320,256]{1,0:T(8,128)(2,1)S(1)}, bf16[320,256]{1,0:T(8,128)(2,1)}, u32[]{:S(2)}) copy-start(bf16[320,256]{1,0:T(8,128)(2,1)} %constant.12.clone.refs_0_.refs_4_) | copy-start | bytes 491524
  0.6 1.0 %copy-start.5 = (bf16[320,256]{1,0:T(8,128)(2,1)S(1)}, bf16[320,256]{1,0:T(8,128)(2,1)}, u32[]{:S(2)}) copy-start(bf16[320,256]{1,0:T(8,128)(2,1)} %constant.13.clone.refs_1_.refs_5_) | copy-start | bytes 491524
  0.7 1.1 %copy-start.6 = (bf16[320,256]{1,0:T(8,128)(2,1)S(1)}, bf16[320,256]{1,0:T(8,128)(2,1)}, u32[]{:S(2)}) copy-start(bf16[320,256]{1,0:T(8,128)(2,1)} %constant.14.clone.refs_2_.refs_6_) | copy-start | bytes 491524
  0.7 1.0 %copy-start.2 = (bf16[4,16,320]{2,1,0:T(8,128)(2,1)S(1)}, bf16[4,16,320]{2,1,0:T(8,128)(2,1)}, u32[]{:S(2)}) copy-start(bf16[4,16,320]{2,1,0:T(8,128)(2,1)} %first_ref.1) | copy-start | bytes 122884
  0.7 1.0 %copy-start.9 = (s32[1,4,8]{2,1,0:T(4,128)S(1)}, s32[1,4,8]{2,1,0:T(4,128)}, u32[]{:S(2)}) copy-start(s32[1,4,8]{2,1,0:T(4,128)} %refs_13_.1) | copy-start | bytes 388
  1.7 6.2 %copy-start = (bf16[16,320,320]{2,1,0:T(8,128)(2,1)S(1)}, bf16[16,320,320]{2,1,0:T(8,128)(2,1)}, u32[]{:S(2)}) copy-start(bf16[16,320,320]{2,1,0:T(8,128)(2,1)} %diag_ref.3) | copy-start | bytes 9830404
  1.7 6.2 %copy-start.1 = (bf16[768,320]{1,0:T(8,128)(2,1)S(1)}, bf16[768,320]{1,0:T(8,128)(2,1)}, u32[]{:S(2)}) copy-start(bf16[768,320]{1,0:T(8,128)(2,1)} %constant.15.clone.lift_ref.refs_12_.refs_8_) | copy-start | bytes 1474564
  1.7 6.2 %copy-start.3 = (bf16[4,16,320]{2,1,0:T(8,128)(2,1)S(1)}, bf16[4,16,320]{2,1,0:T(8,128)(2,1)}, u32[]{:S(2)}) copy-start(bf16[4,16,320]{2,1,0:T(8,128)(2,1)} %forcing_ref.3) | copy-start | bytes 122884
  1.7 6.2 %copy-start.7 = (bf16[16,2400]{1,0:T(8,128)(2,1)S(1)}, bf16[16,2400]{1,0:T(8,128)(2,1)}, u32[]{:S(2)}) copy-start(bf16[16,2400]{1,0:T(8,128)(2,1)} %flux_ref.1) | copy-start | bytes 230404
  1.8 6.2 %copy-start.8 = (s32[16,6]{0,1:T(8,128)S(1)}, s32[16,6]{0,1:T(8,128)}, u32[]{:S(2)}) copy-start(s32[16,6]{0,1:T(8,128)} %param.16) | copy-start | bytes 1156
  2.1 7.3 %collective-permute-start = (bf16[8,512]{1,0:T(8,128)(2,1)S(1)}, bf16[8,512]{1,0:T(8,128)(2,1)S(1)}, u32[]{:S(2)}, u32[]{:S(2)}) collective-permute-start(bf16[8,512]{1,0:T(8,128)(2,1)S(1)} %get-tuple-element.27), channel_id=1, source_target_pairs={{2,4},{3,5},{6,8},{7,9},{10,12},{11,13},{0,1},{14,15},{18,20},{19,... | collective-permute-start | bytes 24584 | tf_op jit(solution)/shard_map/ppermute | solution.py:496
  2.6 6.8 %collective-permute-start.1 = (bf16[8,512]{1,0:T(8,128)(2,1)S(1)}, bf16[8,512]{1,0:T(8,128)(2,1)S(1)}, u32[]{:S(2)}, u32[]{:S(2)}) collective-permute-start(bf16[8,512]{1,0:T(8,128)(2,1)S(1)} %get-tuple-element.28), channel_id=1, source_target_pairs={{1,2},{3,4},{5,6},{7,8},{9,10},{11,12},{13,14},{17,18},{19,20},{21... | collective-permute-start | bytes 24584 | tf_op jit(solution)/shard_map/ppermute | solution.py:496
  5.2 4.2 %collective-permute-start.2 = (bf16[8,512]{1,0:T(8,128)(2,1)S(1)}, bf16[8,512]{1,0:T(8,128)(2,1)S(1)}, u32[]{:S(2)}, u32[]{:S(2)}) collective-permute-start(bf16[8,512]{1,0:T(8,128)(2,1)S(1)} %get-tuple-element.29), channel_id=1, source_target_pairs={{0,2},{1,3},{4,6},{5,7},{8,10},{9,11},{12,14},{13,15},{16,18},{17,... | collective-permute-start | bytes 24584 | tf_op jit(solution)/shard_map/ppermute | solution.py:496
  6.7 2.7 %collective-permute-start.3 = (bf16[8,512]{1,0:T(8,128)(2,1)S(1)}, bf16[8,512]{1,0:T(8,128)(2,1)S(1)}, u32[]{:S(2)}, u32[]{:S(2)}) collective-permute-start(bf16[8,512]{1,0:T(8,128)(2,1)S(1)} %get-tuple-element.30), channel_id=1, source_target_pairs={{0,1},{2,3},{4,5},{6,7},{8,9},{10,11},{12,13},{14,15},{16,17},{18,... | collective-permute-start | bytes 24584 | tf_op jit(solution)/shard_map/ppermute | solution.py:496
  10.2 4.8 %collective-permute-start.8 = (bf16[128,384]{1,0:T(8,128)(2,1)S(1)}, bf16[128,384]{1,0:T(8,128)(2,1)S(1)}, u32[]{:S(2)}, u32[]{:S(2)}) collective-permute-start(bf16[128,384]{1,0:T(8,128)(2,1)S(1)} %get-tuple-element.45), channel_id=1, source_target_pairs={{16,0},{0,16},{17,1},{1,17},{18,2},{2,18},{19,3},{3,19},{20,4},{4,... | collective-permute-start | bytes 294920 | tf_op jit(solution)/shard_map/ppermute | solution.py:548
  11.8 3.7 %collective-permute-start.4 = (bf16[8,512]{1,0:T(8,128)(2,1)S(1)}, bf16[8,512]{1,0:T(8,128)(2,1)S(1)}, u32[]{:S(2)}, u32[]{:S(2)}) collective-permute-start(bf16[8,512]{1,0:T(8,128)(2,1)S(1)} %get-tuple-element.38), channel_id=1, source_target_pairs={{0,2},{1,3},{4,6},{5,7},{8,10},{9,11},{12,14},{13,15},{16,18},{17,... | collective-permute-start | bytes 24584 | tf_op jit(solution)/shard_map/ppermute | solution.py:496
  12.7 3.7 %collective-permute-start.5 = (bf16[8,512]{1,0:T(8,128)(2,1)S(1)}, bf16[8,512]{1,0:T(8,128)(2,1)S(1)}, u32[]{:S(2)}, u32[]{:S(2)}) collective-permute-start(bf16[8,512]{1,0:T(8,128)(2,1)S(1)} %get-tuple-element.39), channel_id=1, source_target_pairs={{1,2},{3,4},{5,6},{7,8},{9,10},{11,12},{13,14},{17,18},{19,20},{21... | collective-permute-start | bytes 24584 | tf_op jit(solution)/shard_map/ppermute | solution.py:496
  13.3 3.1 %collective-permute-start.6 = (bf16[8,512]{1,0:T(8,128)(2,1)S(1)}, bf16[8,512]{1,0:T(8,128)(2,1)S(1)}, u32[]{:S(2)}, u32[]{:S(2)}) collective-permute-start(bf16[8,512]{1,0:T(8,128)(2,1)S(1)} %get-tuple-element.40), channel_id=1, source_target_pairs={{2,4},{3,5},{6,8},{7,9},{10,12},{11,13},{0,1},{14,15},{18,20},{19,... | collective-permute-start | bytes 24584 | tf_op jit(solution)/shard_map/ppermute | solution.py:496
  13.9 2.5 %collective-permute-start.7 = (bf16[8,512]{1,0:T(8,128)(2,1)S(1)}, bf16[8,512]{1,0:T(8,128)(2,1)S(1)}, u32[]{:S(2)}, u32[]{:S(2)}) collective-permute-start(bf16[8,512]{1,0:T(8,128)(2,1)S(1)} %get-tuple-element.41), channel_id=1, source_target_pairs={{0,1},{2,3},{4,5},{6,7},{8,9},{10,11},{12,13},{14,15},{16,17},{18,... | collective-permute-start | bytes 24584 | tf_op jit(solution)/shard_map/ppermute | solution.py:496

commit v12 on v11

--- a/solution.py
+++ b/solution.py
@@ -208,7 +208,7 @@
         ref[...] = block.astype(BF16)
 
 
-def diagonal(states, diag, wide_ref, prod_ref, insts, elems):
+def diagonal_steps(states, diag, wide_ref, prod_ref, insts, elems):
     tall = insts * elems
     width = diag.shape[1]
     cuts = [(j, j * LANE, min((j + 1) * LANE, width)) for j in range(pl.cdiv(width, LANE))]
@@ -217,26 +217,33 @@
         for j, low, high in cuts:
             first = j * tall + t * elems
             wide_ref[first : first + elems, 0 : high - low] = rows[:, low:high]
-    for e in range(elems):
-        rows = jnp.concatenate(
-            [wide_ref[pl.ds(j * tall + e, insts, stride=elems), :] for j, low, high in cuts], 1
-        )
-        product = jnp.dot(rows[:, 0:width].astype(BF16), diag[e], preferred_element_type=F32)
-        for j, low, high in cuts:
-            chunk = product[:, low:high]
-            if high - low < LANE:
-                chunk = jnp.concatenate([chunk, jnp.zeros((insts, LANE - high + low), F32)], 1)
-            prod_ref[pl.ds(j * tall + e, insts, stride=elems), :] = chunk
-    return [
-        jnp.concatenate(
-            [
-                prod_ref[j * tall + t * elems : j * tall + (t + 1) * elems, 0 : high - low]
-                for j, low, high in cuts
-            ],
-            1,
-        )
-        for t in range(insts)
-    ]
+
+    def some(begin, end):
+        for e in range(begin, end):
+            rows = jnp.concatenate(
+                [wide_ref[pl.ds(j * tall + e, insts, stride=elems), :] for j, low, high in cuts], 1
+            )
+            product = jnp.dot(rows[:, 0:width].astype(BF16), diag[e], preferred_element_type=F32)
+            for j, low, high in cuts:
+                chunk = product[:, low:high]
+                if high - low < LANE:
+                    empty = jnp.zeros((insts, LANE - high + low), F32)
+                    chunk = jnp.concatenate([chunk, empty], 1)
+                prod_ref[pl.ds(j * tall + e, insts, stride=elems), :] = chunk
+
+    def collect():
+        return [
+            jnp.concatenate(
+                [
+                    prod_ref[j * tall + t * elems : j * tall + (t + 1) * elems, 0 : high - low]
+                    for j, low, high in cuts
+                ],
+                1,
+            )
+            for t in range(insts)
+        ]
+
+    return some, collect
 
 
 def flux_order(rows, order):
@@ -255,10 +262,8 @@
     return jnp.concatenate(hot, 0).astype(BF16)
 
 
-def face_flux(picked, flux, spread, insts):
-    count = picked.shape[0]
-    stacked = jnp.concatenate([picked[:, t * LANE : (t + 1) * LANE] for t in range(insts)], 0)
-    wide = jnp.dot(stacked, spread, preferred_element_type=F32)
+def spread_flux(wide, flux, insts):
+    count = flux.shape[0]
     normal = []
     for t in range(insts):
         rows = wide[t * count : (t + 1) * count]
@@ -327,12 +332,22 @@
         entry_ref[d : d + 1, :] = jnp.full((1, width), entry, F32)
 
 
-def local_lift(pool, hot, flux, spread, lift, insts, elems):
+def local_terms(states, diag, wide_ref, prod_ref, pool, hot, flux, spread, lift, insts, elems):
+    some, collect = diagonal_steps(states, diag, wide_ref, prod_ref, insts, elems)
+    quarter = elems // 4
     empty = jnp.zeros((hot.shape[1] - pool.shape[0], pool.shape[1]), BF16)
     pool = jnp.concatenate([pool, empty], 0)
     picked = jnp.dot(hot, pool, preferred_element_type=F32).astype(BF16)
-    normal = face_flux(picked, flux.astype(F32), spread, insts)
-    return lift_faces(normal, lift, elems)
+    some(0, quarter)
+    stacked = jnp.concatenate([picked[:, t * LANE : (t + 1) * LANE] for t in range(insts)], 0)
+    wide = jnp.dot(stacked, spread, preferred_element_type=F32)
+    some(quarter, 2 * quarter)
+    normal = spread_flux(wide, flux.astype(F32), insts)
+    some(2 * quarter, 3 * quarter)
+    lifted = lift_faces(normal, lift, elems)
+    some(3 * quarter, elems)
+    products = collect()
+    return [products[t] + lifted[t * elems : (t + 1) * elems] for t in range(insts)]
 
 
 def slot_lift(blocks, factors, hot, lift, insts, elems):
@@ -353,26 +368,26 @@
     flux_out_ref[...] = flux
     factors = lax.dot_general(hot, flux, (((0,), (0,)), ((), ())), preferred_element_type=F32)
     factor_ref[...] = rotated(factors[FACES * elems :])
-    lifted = local_lift(pool_ref[...], hot, flux, spread_ref[...], lift_ref[...], insts, elems)
     states = [state_ref[t] for t in range(insts)]
-    products = diagonal(states, diag_ref, wide_ref, prod_ref, insts, elems)
-    for t in range(insts):
-        spatial_ref[t] = products[t] + lifted[t * elems : (t + 1) * elems]
+    spatial = local_terms(
+        states, diag_ref, wide_ref, prod_ref, pool_ref[...], hot, flux, spread_ref[...],
+        lift_ref[...], insts, elems,
+    )
+    for t in range(insts):
+        spatial_ref[t] = spatial[t]
         rest_ref[t] = couple(entry_ref, states, t, 0, insts) - forcing_ref[t].astype(F32)
 
 
 def last_base_kernel(state_ref, pool_ref, diag_ref, forcing_ref, hot_ref, flux_ref, spread_ref,
                      lift_ref, base_ref, wide_ref, prod_ref):
     insts, elems, width = state_ref.shape
-    lifted = local_lift(
-        pool_ref[...], hot_ref[...], flux_ref[...], spread_ref[...], lift_ref[...], insts, elems
+    states = [state_ref[t].astype(BF16) for t in range(insts)]
+    spatial = local_terms(
+        states, diag_ref, wide_ref, prod_ref, pool_ref[...], hot_ref[...], flux_ref[...],
+        spread_ref[...], lift_ref[...], insts, elems,
     )
-    states = [state_ref[t].astype(BF16) for t in range(insts)]
-    products = diagonal(states, diag_ref, wide_ref, prod_ref, insts, elems)
-    for t in range(insts):
-        base_ref[t] = (
-            products[t] + lifted[t * elems : (t + 1) * elems] - forcing_ref[t].astype(F32)
-        )
+    for t in range(insts):
+        base_ref[t] = spatial[t] - forcing_ref[t].astype(F32)
 
 
 def message_kernel(ranks, partial_ref, first_ref, base_ref, entry_ref, *refs):

time: 17.8 us -> 17.8 us (level)
  Pallas kernels: 5.18 us -> 4.75 us
  waiting for transfers between devices: 1.17 us -> 1.55 us
    ppermute x8, waiting for transfers between devices: 1.17 us -> 1.4 us  [exchange(): lax.ppermute(outgoing[swap], ('inst', 'dom'), routes[swap])]
    pallas_call x1, Pallas kernels: 1.44 us -> 1.23 us  [on_device(): pl.pallas_call(functools.partial(base_kernel, slots * capacity), out_shap...]
    pallas_call x1, Pallas kernels: 1.13 us -> 0.92 us  [on_device(): pl.pallas_call(last_base_kernel, out_shape=wide_shape, in_specs=[vmem] *...]
  transfers between devices with their start and end apart: 9 -> 9, of which waited for: 2 -> 3; matrix products, arithmetic and copies ran while one was open for 0% -> 0% of each run, Pallas kernels for 15% -> 13%
where the time goes in v12:
time: 17.8 us; the launch traced here: 17.5 us
  starting transfers between devices  9.54 us (54%)
  Pallas kernels  4.75 us (27%)
  waiting for transfers between devices  1.55 us (9%)
  between operations  1.48 us (8%)
  local copies, waits for them, and re-layouts  0.19 us (1%)
    ppermute x8, starting transfers between devices, exchange(): lax.ppermute(outgoing[swap], ('inst', 'dom'), routes[swap])  7.97 us
    ppermute x1, starting transfers between devices, on_device(): lax.ppermute(message, 'inst', [((i + rank) % ranks, i) for i in range(ran...  1.57 us
    ppermute x8, waiting for transfers between devices, exchange(): lax.ppermute(outgoing[swap], ('inst', 'dom'), routes[swap])  1.4 us
    pallas_call x1, Pallas kernels, on_device(): pl.pallas_call(functools.partial(base_kernel, slots * capacity), out_shap...  1.23 us
    pallas_call x1, Pallas kernels, on_device(): pl.pallas_call(functools.partial(last_kernel, parts), out_shape=[like(ini...  1.14 us
    pallas_call x1, Pallas kernels, on_device(): pl.pallas_call(last_base_kernel, out_shape=wide_shape, in_specs=[vmem] *...  0.92 us
    pallas_call x1, Pallas kernels, on_device(): pl.pallas_call(functools.partial(step_kernel, parts), out_shape=[wide_sha...  0.81 us
  transfers between devices with their start and end apart: 9, of which 3 were waited for; matrix products, arithmetic and copies ran while one was open for 0% of the time, Pallas kernels for 13%

profile of v12, /device:TPU:0, one launch (start us, length us, event | category | flops | bytes accessed | tf_op | source)
XLA Modules:
  0.0 17.5 jit_solution(2275384022140485648)
XLA Ops:
  0.6 0.0 copy-start.4
  0.6 0.0 copy-start.5
  0.7 0.0 copy-start.6
  0.7 0.2 %tables.1 = (bf16[128,640]{1,0:T(8,128)(2,1)S(1)}, bf16[400,640]{1,0:T(8,128)(2,1)S(1)}) custom-call(), custom_call_target="tpu_custom_call" | custom-call | flops 10000000000 | bytes 1000000 | tf_op jit(solution)/shard_map/tables/pallas_call | solution.py:521
  1.6 0.1 copy-done.5
  1.6 0.1 copy-done.6
  1.7 0.0 copy-start.3
  1.7 0.0 copy-start.7
  1.8 0.0 copy-start.8
  1.8 0.3 %first_traces.1 = (f32[8,320]{1,0:T(8,128)S(1)}, bf16[96,512]{1,0:T(8,128)(2,1)S(1)}, bf16[8,512]{1,0:T(8,128)(2,1)S(1)}, bf16[8,512]{1,0:T(8,128)(2,1)S(1)}, bf...) custom-call(s32[1]{0:T(128)} %bitcast.place_ref, f32[1]{0:T(128)S(6)} %copy.13.freq_ref, ...), custom_call_target="tpu_custom_call" | custom-call | flops 10000000000 | bytes 1000000 | tf_op jit(solution)/shard_map/first_traces/pallas_call | solution.py:533
  2.1 0.5 %collective-permute-start = (bf16[8,512]{1,0:T(8,128)(2,1)S(1)}, bf16[8,512]{1,0:T(8,128)(2,1)S(1)}, u32[]{:S(2)}, u32[]{:S(2)}) collective-permute-start(bf16[8,512]{1,0:T(8,128)(2,1)S(1)} %get-tuple-element.27), channel_id=1, source_target_pairs={{2,4},{3,5},{6,8},{7,9},{10,12},{11,13},{0,1},{14,15},{18,20},{19,... | collective-permute-start | bytes 24584 | tf_op jit(solution)/shard_map/ppermute | solution.py:511
  2.6 2.6 %collective-permute-start.1 = (bf16[8,512]{1,0:T(8,128)(2,1)S(1)}, bf16[8,512]{1,0:T(8,128)(2,1)S(1)}, u32[]{:S(2)}, u32[]{:S(2)}) collective-permute-start(bf16[8,512]{1,0:T(8,128)(2,1)S(1)} %get-tuple-element.28), channel_id=1, source_target_pairs={{1,2},{3,4},{5,6},{7,8},{9,10},{11,12},{13,14},{17,18},{19,20},{21... | collective-permute-start | bytes 24584 | tf_op jit(solution)/shard_map/ppermute | solution.py:511
  5.2 1.5 %collective-permute-start.2 = (bf16[8,512]{1,0:T(8,128)(2,1)S(1)}, bf16[8,512]{1,0:T(8,128)(2,1)S(1)}, u32[]{:S(2)}, u32[]{:S(2)}) collective-permute-start(bf16[8,512]{1,0:T(8,128)(2,1)S(1)} %get-tuple-element.29), channel_id=1, source_target_pairs={{0,2},{1,3},{4,6},{5,7},{8,10},{9,11},{12,14},{13,15},{16,18},{17,... | collective-permute-start | bytes 24584 | tf_op jit(solution)/shard_map/ppermute | solution.py:511
  6.7 1.2 %collective-permute-start.3 = (bf16[8,512]{1,0:T(8,128)(2,1)S(1)}, bf16[8,512]{1,0:T(8,128)(2,1)S(1)}, u32[]{:S(2)}, u32[]{:S(2)}) collective-permute-start(bf16[8,512]{1,0:T(8,128)(2,1)S(1)} %get-tuple-element.30), channel_id=1, source_target_pairs={{0,1},{2,3},{4,5},{6,7},{8,9},{10,11},{12,13},{14,15},{16,17},{18,... | collective-permute-start | bytes 24584 | tf_op jit(solution)/shard_map/ppermute | solution.py:511
  7.9 1.2 %own_terms.1 = (f32[4,16,320]{2,1,0:T(8,128)S(1)}, f32[4,16,320]{2,1,0:T(8,128)S(1)}, bf16[96,640]{1,0:T(8,128)(2,1)S(1)}, bf16[96,128]{1,0:T(8,128)(2,1)S(1)}, f32[32,1024]{1,0:T(8,128)S(1)}) custom-call(bf16[4,16,320]{2,1,0:T(8,128)(2,1)S(1)} %copy-done.2, bf16[16,320,320]{2,1,0:T(8,128)(2,1)S(1)} %copy-done, bf16[4,16,320]{2,1,0:T(8,128)(2,1)S(1)} %copy-done.3, ...), custom_call_target="tpu_custom_call" | custom-call | flops 13107200 | bytes 3276800 | tf_op jit(solution)/shard_map/own_terms/pallas_call | solution.py:543
  9.2 0.0 collective-permute-done.refs_0_
  9.2 0.0 collective-permute-done.1.refs_1_
  9.2 0.0 collective-permute-done.2.refs_2_
  9.2 0.0 collective-permute-done.3.refs_3_
  9.2 0.8 %first_step.1 = (f32[4,16,320]{2,1,0:T(8,128)S(1)}, bf16[128,384]{1,0:T(8,128)(2,1)S(1)}, bf16[96,512]{1,0:T(8,128)(2,1)S(1)}, bf16[8,512]{1,0:T(8,128)(2,1)S(1)...) custom-call(s32[1]{0:T(128)} %bitcast.place_ref, ...), custom_call_target="tpu_custom_call" | custom-call | tf_op jit(solution)/shard_map/first_step/pallas_call | solution.py:554
  10.0 1.6 %collective-permute-start.8 = (bf16[128,384]{1,0:T(8,128)(2,1)S(1)}, bf16[128,384]{1,0:T(8,128)(2,1)S(1)}, u32[]{:S(2)}, u32[]{:S(2)}) collective-permute-start(bf16[128,384]{1,0:T(8,128)(2,1)S(1)} %get-tuple-element.45), channel_id=1, source_target_pairs={{16,0},{0,16},{17,1},{1,17},{18,2},{2,18},{19,3},{3,19},{20,4},{4,... | collective-permute-start | bytes 294920 | tf_op jit(solution)/shard_map/ppermute | solution.py:563
  11.6 1.1 %collective-permute-start.4 = (bf16[8,512]{1,0:T(8,128)(2,1)S(1)}, bf16[8,512]{1,0:T(8,128)(2,1)S(1)}, u32[]{:S(2)}, u32[]{:S(2)}) collective-permute-start(bf16[8,512]{1,0:T(8,128)(2,1)S(1)} %get-tuple-element.38), channel_id=1, source_target_pairs={{0,2},{1,3},{4,6},{5,7},{8,10},{9,11},{12,14},{13,15},{16,18},{17,... | collective-permute-start | bytes 24584 | tf_op jit(solution)/shard_map/ppermute | solution.py:511
  12.7 0.5 %collective-permute-start.5 = (bf16[8,512]{1,0:T(8,128)(2,1)S(1)}, bf16[8,512]{1,0:T(8,128)(2,1)S(1)}, u32[]{:S(2)}, u32[]{:S(2)}) collective-permute-start(bf16[8,512]{1,0:T(8,128)(2,1)S(1)} %get-tuple-element.39), channel_id=1, source_target_pairs={{1,2},{3,4},{5,6},{7,8},{9,10},{11,12},{13,14},{17,18},{19,20},{21... | collective-permute-start | bytes 24584 | tf_op jit(solution)/shard_map/ppermute | solution.py:511
  13.3 0.5 %collective-permute-start.6 = (bf16[8,512]{1,0:T(8,128)(2,1)S(1)}, bf16[8,512]{1,0:T(8,128)(2,1)S(1)}, u32[]{:S(2)}, u32[]{:S(2)}) collective-permute-start(bf16[8,512]{1,0:T(8,128)(2,1)S(1)} %get-tuple-element.40), channel_id=1, source_target_pairs={{2,4},{3,5},{6,8},{7,9},{10,12},{11,13},{0,1},{14,15},{18,20},{19,... | collective-permute-start | bytes 24584 | tf_op jit(solution)/shard_map/ppermute | solution.py:511
  13.7 0.0 collective-permute-start.7
  13.8 0.9 %last_own_terms.1.base_ref = f32[4,16,320]{2,1,0:T(8,128)S(1)} custom-call(f32[4,16,320]{2,1,0:T(8,128)S(1)} %get-tuple-element.42.state_ref.partial_ref, bf16[96,512]{1,0:T(8,128)(2,1)S(1)} %get-tuple-element.43.pool_ref, bf16[16,320,320]{2,1,0:T(8,128)(2,1)S(1)} %copy-done, bf16[4,16,320]{2,1,0:T(8,128)(2,1)S(1)} %copy-done.3, ...), custom_call_target="tpu_custom_call" | custom-call | flops 13107200 | bytes 3276800 | tf_op jit(solution)/shard_map/last_own_terms/pallas_call | solution.py:567
  14.7 0.2 collective-permute-done.8.refs_0_
  14.9 0.1 message_terms.1
  15.0 0.2 %collective-permute-done.4.refs_0_ = bf16[8,512]{1,0:T(8,128)(2,1)S(1)} collective-permute-done((bf16[8,512]{1,0:T(8,128)(2,1)S(1)}, bf16[8,512]{1,0:T(8,128)(2,1)S(1)}, u32[]{:S(2)}, u32[]{:S(2)}) %collective-permute-start.4) | collective-permute-done | bytes 8224 | tf_op jit(solution)/shard_map/ppermute | solution.py:511
  15.2 1.1 %collective-permute-done.5.refs_1_ = bf16[8,512]{1,0:T(8,128)(2,1)S(1)} collective-permute-done((bf16[8,512]{1,0:T(8,128)(2,1)S(1)}, bf16[8,512]{1,0:T(8,128)(2,1)S(1)}, u32[]{:S(2)}, u32[]{:S(2)}) %collective-permute-start.5) | collective-permute-done | bytes 8224 | tf_op jit(solution)/shard_map/ppermute | solution.py:511
  16.4 0.0 collective-permute-done.6.refs_2_
  16.4 1.1 %last_step.1 = (bf16[4,16,320]{2,1,0:T(8,128)(2,1)}, f32[4,16,320]{2,1,0:T(8,128)}) custom-call(s32[1]{0:T(128)} %bitcast.place_ref, bf16[8,512]{1,0:T(8,128)(2,1)S(1)} %collective-permute-done.4.refs_0_, bf16[8,512]{1,0:T(8,128)(2,1)S(1)} %collective-permute-done.5.refs_1_, bf16[8,512]{1,0:T(8,128)(2,1)S(1)} %collective-permute-done.6.refs_2_, ...), custom_call_target="tpu_custom_call" | custom-call | tf_op jit(solution)/shard_map/last_step/pallas_call | solution.py:585
  (13 shorter events, 0.0 us)
Async XLA Ops:
  0.6 0.9 %copy-start.4 = (bf16[320,256]{1,0:T(8,128)(2,1)S(1)}, bf16[320,256]{1,0:T(8,128)(2,1)}, u32[]{:S(2)}) copy-start(bf16[320,256]{1,0:T(8,128)(2,1)} %constant.12.clone.refs_0_.refs_4_) | copy-start | bytes 491524
  0.6 1.0 %copy-start.5 = (bf16[320,256]{1,0:T(8,128)(2,1)S(1)}, bf16[320,256]{1,0:T(8,128)(2,1)}, u32[]{:S(2)}) copy-start(bf16[320,256]{1,0:T(8,128)(2,1)} %constant.13.clone.refs_1_.refs_5_) | copy-start | bytes 491524
  0.7 1.1 %copy-start.6 = (bf16[320,256]{1,0:T(8,128)(2,1)S(1)}, bf16[320,256]{1,0:T(8,128)(2,1)}, u32[]{:S(2)}) copy-start(bf16[320,256]{1,0:T(8,128)(2,1)} %constant.14.clone.refs_2_.refs_6_) | copy-start | bytes 491524
  0.7 1.0 %copy-start.2 = (bf16[4,16,320]{2,1,0:T(8,128)(2,1)S(1)}, bf16[4,16,320]{2,1,0:T(8,128)(2,1)}, u32[]{:S(2)}) copy-start(bf16[4,16,320]{2,1,0:T(8,128)(2,1)} %first_ref.1) | copy-start | bytes 122884
  0.7 1.0 %copy-start.9 = (s32[1,4,8]{2,1,0:T(4,128)S(1)}, s32[1,4,8]{2,1,0:T(4,128)}, u32[]{:S(2)}) copy-start(s32[1,4,8]{2,1,0:T(4,128)} %refs_13_.1) | copy-start | bytes 388
  1.7 6.2 %copy-start = (bf16[16,320,320]{2,1,0:T(8,128)(2,1)S(1)}, bf16[16,320,320]{2,1,0:T(8,128)(2,1)}, u32[]{:S(2)}) copy-start(bf16[16,320,320]{2,1,0:T(8,128)(2,1)} %diag_ref.3) | copy-start | bytes 9830404
  1.7 6.2 %copy-start.1 = (bf16[768,320]{1,0:T(8,128)(2,1)S(1)}, bf16[768,320]{1,0:T(8,128)(2,1)}, u32[]{:S(2)}) copy-start(bf16[768,320]{1,0:T(8,128)(2,1)} %constant.15.clone.lift_ref.refs_12_.refs_8_) | copy-start | bytes 1474564
  1.7 6.2 %copy-start.3 = (bf16[4,16,320]{2,1,0:T(8,128)(2,1)S(1)}, bf16[4,16,320]{2,1,0:T(8,128)(2,1)}, u32[]{:S(2)}) copy-start(bf16[4,16,320]{2,1,0:T(8,128)(2,1)} %forcing_ref.3) | copy-start | bytes 122884
  1.7 6.2 %copy-start.7 = (bf16[16,2400]{1,0:T(8,128)(2,1)S(1)}, bf16[16,2400]{1,0:T(8,128)(2,1)}, u32[]{:S(2)}) copy-start(bf16[16,2400]{1,0:T(8,128)(2,1)} %flux_ref.1) | copy-start | bytes 230404
  1.8 6.2 %copy-start.8 = (s32[16,6]{0,1:T(8,128)S(1)}, s32[16,6]{0,1:T(8,128)}, u32[]{:S(2)}) copy-start(s32[16,6]{0,1:T(8,128)} %param.16) | copy-start | bytes 1156
  2.1 7.1 %collective-permute-start = (bf16[8,512]{1,0:T(8,128)(2,1)S(1)}, bf16[8,512]{1,0:T(8,128)(2,1)S(1)}, u32[]{:S(2)}, u32[]{:S(2)}) collective-permute-start(bf16[8,512]{1,0:T(8,128)(2,1)S(1)} %get-tuple-element.27), channel_id=1, source_target_pairs={{2,4},{3,5},{6,8},{7,9},{10,12},{11,13},{0,1},{14,15},{18,20},{19,... | collective-permute-start | bytes 24584 | tf_op jit(solution)/shard_map/ppermute | solution.py:511
  2.6 6.5 %collective-permute-start.1 = (bf16[8,512]{1,0:T(8,128)(2,1)S(1)}, bf16[8,512]{1,0:T(8,128)(2,1)S(1)}, u32[]{:S(2)}, u32[]{:S(2)}) collective-permute-start(bf16[8,512]{1,0:T(8,128)(2,1)S(1)} %get-tuple-element.28), channel_id=1, source_target_pairs={{1,2},{3,4},{5,6},{7,8},{9,10},{11,12},{13,14},{17,18},{19,20},{21... | collective-permute-start | bytes 24584 | tf_op jit(solution)/shard_map/ppermute | solution.py:511
  5.2 4.0 %collective-permute-start.2 = (bf16[8,512]{1,0:T(8,128)(2,1)S(1)}, bf16[8,512]{1,0:T(8,128)(2,1)S(1)}, u32[]{:S(2)}, u32[]{:S(2)}) collective-permute-start(bf16[8,512]{1,0:T(8,128)(2,1)S(1)} %get-tuple-element.29), channel_id=1, source_target_pairs={{0,2},{1,3},{4,6},{5,7},{8,10},{9,11},{12,14},{13,15},{16,18},{17,... | collective-permute-start | bytes 24584 | tf_op jit(solution)/shard_map/ppermute | solution.py:511
  6.7 2.5 %collective-permute-start.3 = (bf16[8,512]{1,0:T(8,128)(2,1)S(1)}, bf16[8,512]{1,0:T(8,128)(2,1)S(1)}, u32[]{:S(2)}, u32[]{:S(2)}) collective-permute-start(bf16[8,512]{1,0:T(8,128)(2,1)S(1)} %get-tuple-element.30), channel_id=1, source_target_pairs={{0,1},{2,3},{4,5},{6,7},{8,9},{10,11},{12,13},{14,15},{16,17},{18,... | collective-permute-start | bytes 24584 | tf_op jit(solution)/shard_map/ppermute | solution.py:511
  10.0 4.8 %collective-permute-start.8 = (bf16[128,384]{1,0:T(8,128)(2,1)S(1)}, bf16[128,384]{1,0:T(8,128)(2,1)S(1)}, u32[]{:S(2)}, u32[]{:S(2)}) collective-permute-start(bf16[128,384]{1,0:T(8,128)(2,1)S(1)} %get-tuple-element.45), channel_id=1, source_target_pairs={{16,0},{0,16},{17,1},{1,17},{18,2},{2,18},{19,3},{3,19},{20,4},{4,... | collective-permute-start | bytes 294920 | tf_op jit(solution)/shard_map/ppermute | solution.py:563
  11.6 3.7 %collective-permute-start.4 = (bf16[8,512]{1,0:T(8,128)(2,1)S(1)}, bf16[8,512]{1,0:T(8,128)(2,1)S(1)}, u32[]{:S(2)}, u32[]{:S(2)}) collective-permute-start(bf16[8,512]{1,0:T(8,128)(2,1)S(1)} %get-tuple-element.38), channel_id=1, source_target_pairs={{0,2},{1,3},{4,6},{5,7},{8,10},{9,11},{12,14},{13,15},{16,18},{17,... | collective-permute-start | bytes 24584 | tf_op jit(solution)/shard_map/ppermute | solution.py:511
  12.7 3.7 %collective-permute-start.5 = (bf16[8,512]{1,0:T(8,128)(2,1)S(1)}, bf16[8,512]{1,0:T(8,128)(2,1)S(1)}, u32[]{:S(2)}, u32[]{:S(2)}) collective-permute-start(bf16[8,512]{1,0:T(8,128)(2,1)S(1)} %get-tuple-element.39), channel_id=1, source_target_pairs={{1,2},{3,4},{5,6},{7,8},{9,10},{11,12},{13,14},{17,18},{19,20},{21... | collective-permute-start | bytes 24584 | tf_op jit(solution)/shard_map/ppermute | solution.py:511
  13.3 3.1 %collective-permute-start.6 = (bf16[8,512]{1,0:T(8,128)(2,1)S(1)}, bf16[8,512]{1,0:T(8,128)(2,1)S(1)}, u32[]{:S(2)}, u32[]{:S(2)}) collective-permute-start(bf16[8,512]{1,0:T(8,128)(2,1)S(1)} %get-tuple-element.40), channel_id=1, source_target_pairs={{2,4},{3,5},{6,8},{7,9},{10,12},{11,13},{0,1},{14,15},{18,20},{19,... | collective-permute-start | bytes 24584 | tf_op jit(solution)/shard_map/ppermute | solution.py:511
  13.7 2.6 %collective-permute-start.7 = (bf16[8,512]{1,0:T(8,128)(2,1)S(1)}, bf16[8,512]{1,0:T(8,128)(2,1)S(1)}, u32[]{:S(2)}, u32[]{:S(2)}) collective-permute-start(bf16[8,512]{1,0:T(8,128)(2,1)S(1)} %get-tuple-element.41), channel_id=1, source_target_pairs={{0,1},{2,3},{4,5},{6,7},{8,9},{10,11},{12,13},{14,15},{16,17},{18,... | collective-permute-start | bytes 24584 | tf_op jit(solution)/shard_map/ppermute | solution.py:511

commit v13 on v12

--- a/solution.py
+++ b/solution.py
@@ -140,15 +140,19 @@
     return one_hot((place < FIELDS * FPTS) & (row == source))
 
 
+def pooled(faces, insts, elems):
+    by_inst = []
+    for t in range(insts):
+        by_inst.append(jnp.concatenate([rows[t * elems : (t + 1) * elems] for rows in faces], 0))
+    return jnp.concatenate(by_inst, 1)
+
+
 def trace_pool(state, trace_tables, insts, elems):
     faces = []
     for table in trace_tables:
-        wide = jnp.dot(state, table, preferred_element_type=F32).astype(BF16)
+        wide = jnp.dot(state, table, preferred_element_type=F32)
         faces += [wide[:, at : at + LANE] for at in range(0, table.shape[1], LANE)]
-    by_inst = []
-    for t in range(insts):
-        by_inst.append(jnp.concatenate([rows[t * elems : (t + 1) * elems] for rows in faces], 0))
-    return jnp.concatenate(by_inst, 1)
+    return pooled(faces, insts, elems)
 
 
 def swap_routes(ranks, parts):
@@ -274,11 +278,15 @@
     return normal
 
 
-def lift_faces(normal, lift, elems):
+def face_rows(normal, elems):
     rows = [
         jnp.concatenate([n[f * elems : (f + 1) * elems] for f in range(FACES)], 1) for n in normal
     ]
-    return jnp.dot(jnp.concatenate(rows, 0), lift, preferred_element_type=F32)
+    return jnp.concatenate(rows, 0)
+
+
+def lift_faces(normal, lift, elems):
+    return jnp.dot(face_rows(normal, elems), lift, preferred_element_type=F32)
 
 
 def couple(entry_ref, states, t, shift, insts):
@@ -323,7 +331,7 @@
     insts, elems, width = state_ref.shape
     trace_refs, (entry_ref, pool_ref, *out_refs) = refs[:TRACE_TABLES], refs[TRACE_TABLES:]
     state = state_ref[...].reshape(insts * elems, width)
-    pool = trace_pool(state, [ref[...] for ref in trace_refs], insts, elems)
+    pool = trace_pool(state, [ref[...] for ref in trace_refs], insts, elems).astype(BF16)
     pool_ref[...] = pool
     fill_outgoing(pool, send_ref[0], out_refs, place_ref[0], elems)
     freq = freq_ref[0]
@@ -350,17 +358,19 @@
     return [products[t] + lifted[t * elems : (t + 1) * elems] for t in range(insts)]
 
 
-def slot_lift(blocks, factors, hot, lift, insts, elems):
+def slot_faces(blocks, factors, hot, insts, elems):
     normal = slot_normal(blocks, factors, insts)
     empty = jnp.zeros((FACES * elems, insts * LANE), BF16)
     rows = jnp.concatenate([empty, jnp.concatenate(normal, 1)], 0)
     spots = jnp.dot(hot, rows, preferred_element_type=F32).astype(BF16)
-    return lift_faces([spots[:, t * LANE : (t + 1) * LANE] for t in range(insts)], lift, elems)
+    return [spots[:, t * LANE : (t + 1) * LANE] for t in range(insts)]
 
 
 def base_kernel(slots, state_ref, diag_ref, forcing_ref, entry_ref, pool_ref, flux_ref, source_ref,
-                order_ref, spread_ref, lift_ref, spatial_ref, rest_ref, flux_out_ref, hot_ref,
-                factor_ref, wide_ref, prod_ref):
+                order_ref, spread_ref, lift_ref, *refs):
+    trace_refs, refs = refs[:TRACE_TABLES], refs[TRACE_TABLES:]
+    (spatial_ref, rest_ref, flux_out_ref, hot_ref, factor_ref, early_ref, wide_ref,
+     prod_ref) = refs
     insts, elems, width = state_ref.shape
     hot = source_table(source_ref[...].T, elems, slots)
     flux = flux_order(flux_ref[...], order_ref[...])
@@ -373,9 +383,14 @@
         states, diag_ref, wide_ref, prod_ref, pool_ref[...], hot, flux, spread_ref[...],
         lift_ref[...], insts, elems,
     )
+    early = []
     for t in range(insts):
         spatial_ref[t] = spatial[t]
-        rest_ref[t] = couple(entry_ref, states, t, 0, insts) - forcing_ref[t].astype(F32)
+        rest = couple(entry_ref, states, t, 0, insts) - forcing_ref[t].astype(F32)
+        rest_ref[t] = rest
+        early.append((states[t].astype(F32) - pseudo_step * (spatial[t] + rest)).astype(BF16))
+    tables_of_traces = [ref[...] for ref in trace_refs]
+    early_ref[...] = trace_pool(jnp.concatenate(early, 0), tables_of_traces, insts, elems)
 
 
 def last_base_kernel(state_ref, pool_ref, diag_ref, forcing_ref, hot_ref, flux_ref, spread_ref,
@@ -432,28 +447,27 @@
 
 def step_kernel(parts, place_ref, *refs):
     got_refs, refs = refs[: len(OFFSETS)], refs[len(OFFSETS) :]
-    trace_refs, refs = refs[:TRACE_TABLES], refs[TRACE_TABLES:]
-    (state_ref, local_ref, rest_ref, hot_ref, factor_ref, lift_ref, send_ref,
-     partial_ref, message_ref, next_pool_ref, *out_refs) = refs
+    (state_ref, local_ref, rest_ref, hot_ref, factor_ref, early_ref, lift_ref, through_ref,
+     send_ref, partial_ref, message_ref, next_pool_ref, *out_refs) = refs
     insts, elems, width = state_ref.shape
     place = place_ref[0]
     blocks = received(parts, place, got_refs, FIRST_ORDER)
-    lifted = slot_lift(blocks, factor_ref[...], hot_ref[...], lift_ref[...], insts, elems)
+    rows = face_rows(slot_faces(blocks, factor_ref[...], hot_ref[...], insts, elems), elems)
+    late = jnp.dot(rows, through_ref[...], preferred_element_type=F32)
+    late = [late[:, f * LANE : (f + 1) * LANE] for f in range(FACES)]
+    pool = (early_ref[...] - pseudo_step * pooled(late, insts, elems)).astype(BF16)
+    next_pool_ref[...] = pool
+    fill_outgoing(pool, send_ref[0], out_refs, place, elems)
+    lifted = jnp.dot(rows, lift_ref[...], preferred_element_type=F32)
     message_ref[...] = jnp.zeros_like(message_ref)
-    fresh = []
     for t in range(insts):
         spatial = local_ref[t] + lifted[t * elems : (t + 1) * elems]
         moved = state_ref[t].astype(F32) - pseudo_step * (spatial + rest_ref[t])
         partial_ref[t] = moved
-        fresh.append(moved.astype(BF16))
         lean = (moved - pseudo_step * spatial).astype(BF16)
         for i, block in enumerate((state_ref[t], lean)):
             low = (i * insts + t) * elems
             message_ref[low : low + elems, 0:width] = block
-    tables_of_traces = [ref[...] for ref in trace_refs]
-    pool = trace_pool(jnp.concatenate(fresh, 0), tables_of_traces, insts, elems)
-    next_pool_ref[...] = pool
-    fill_outgoing(pool, send_ref[0], out_refs, place, elems)
 
 
 def last_kernel(parts, place_ref, *refs):
@@ -462,7 +476,8 @@
      final_ref, residual_ref, sems) = refs
     insts, elems, width = state_ref.shape
     blocks = received(parts, place_ref[0], got_refs, LAST_ORDER)
-    lifted = slot_lift(blocks, factor_ref[...], hot_ref[...], lift_ref[...], insts, elems)
+    normal = slot_faces(blocks, factor_ref[...], hot_ref[...], insts, elems)
+    lifted = lift_faces(normal, lift_ref[...], elems)
     for t in range(insts):
         residual = base_ref[t] + lifted[t * elems : (t + 1) * elems]
         residual_ref[t] = residual
@@ -486,6 +501,7 @@
     slots, capacity = send_list.shape[1:]
     faces = FACES * elems
     trace_np, lift_np, spectral, second = wide_tables()
+    through = jnp.asarray(lift_np @ trace_np, BF16)
     trace_wide = [jnp.asarray(part, BF16) for part in np.split(trace_np, TRACE_TABLES, 1)]
     lift_wide = jnp.asarray(lift_np, BF16)
     place = lax.axis_index("dom").reshape(1)
@@ -511,6 +527,7 @@
             lax.ppermute(outgoing[swap], ("inst", "dom"), routes[swap]) for swap in order
         ]
 
+    early_shape = jax.ShapeDtypeStruct((faces, insts * LANE), F32)
     entry_shape = jax.ShapeDtypeStruct((NI, width), F32)
     message_shape = jax.ShapeDtypeStruct((2 * insts * elems, pl.cdiv(width, LANE) * LANE), BF16)
     chunks = [pltpu.VMEM((pl.cdiv(width, LANE) * insts * elems, LANE), F32)] * 2
@@ -540,25 +557,25 @@
         name="first_traces",
     )(place, freq, spread, initial_state, send_list, *trace_wide)
     got = exchange(outgoing, FIRST_ORDER)
-    local, rest, flux, hot, factors = pl.pallas_call(
+    local, rest, flux, hot, factors, early = pl.pallas_call(
         functools.partial(base_kernel, slots * capacity),
-        out_shape=[wide_shape] * 2 + [flux_shape, hot_shape, factor_shape],
-        in_specs=[vmem] * 10,
-        out_specs=[vmem] * 5,
+        out_shape=[wide_shape] * 2 + [flux_shape, hot_shape, factor_shape, early_shape],
+        in_specs=[vmem] * (10 + TRACE_TABLES),
+        out_specs=[vmem] * 6,
         scratch_shapes=chunks,
         compiler_params=params,
         cost_estimate=diag_cost,
         name="own_terms",
     )(initial_state, diagonal_blocks, forcing, entries, pool, flux_jacobian, sources, order, spread,
-      lift_wide)
+      lift_wide, *trace_wide)
     partial, message, pool, *outgoing = pl.pallas_call(
         functools.partial(step_kernel, parts),
         out_shape=[wide_shape, message_shape, pool_shape] + out_shapes,
-        in_specs=[smem] + [vmem] * (slots + 7 + TRACE_TABLES),
+        in_specs=[smem] + [vmem] * (slots + 9),
         out_specs=[vmem] * (3 + len(out_shapes)),
         compiler_params=params,
         name="first_step",
-    )(place, *got, *trace_wide, initial_state, local, rest, hot, factors, lift_wide, send_list)
+    )(place, *got, initial_state, local, rest, hot, factors, early, lift_wide, through, send_list)
     messages = [
         lax.ppermute(message, "inst", [((i + rank) % ranks, i) for i in range(ranks)])
         for rank in range(1, ranks)

time: 17.8 us -> 17.9 us (level)
  Pallas kernels: 4.75 us -> 5.05 us
  waiting for transfers between devices: 1.55 us -> 1.35 us
    pallas_call x1, Pallas kernels: 1.23 us -> 1.46 us  [on_device(): pl.pallas_call(functools.partial(base_kernel, slots * capacity), out_shap...]
    ppermute x8, waiting for transfers between devices: 1.4 us -> 1.21 us  [exchange(): lax.ppermute(outgoing[swap], ('inst', 'dom'), routes[swap])]
  transfers between devices with their start and end apart: 9 -> 9, of which waited for: 3 -> 3; matrix products, arithmetic and copies ran while one was open for 0% -> 0% of each run, Pallas kernels for 13% -> 14%
where the time goes in v13:
time: 17.9 us; the launch traced here: 17.6 us
  starting transfers between devices  9.5 us (53%)
  Pallas kernels  5.05 us (28%)
  between operations  1.48 us (8%)
  waiting for transfers between devices  1.35 us (8%)
  local copies, waits for them, and re-layouts  0.22 us (1%)
    ppermute x8, starting transfers between devices, exchange(): lax.ppermute(outgoing[swap], ('inst', 'dom'), routes[swap])  7.94 us
    ppermute x1, starting transfers between devices, on_device(): lax.ppermute(message, 'inst', [((i + rank) % ranks, i) for i in range(ran...  1.56 us
    pallas_call x1, Pallas kernels, on_device(): pl.pallas_call(functools.partial(base_kernel, slots * capacity), out_shap...  1.46 us
    ppermute x8, waiting for transfers between devices, exchange(): lax.ppermute(outgoing[swap], ('inst', 'dom'), routes[swap])  1.21 us
    pallas_call x1, Pallas kernels, on_device(): pl.pallas_call(functools.partial(last_kernel, parts), out_shape=[like(ini...  1.13 us
    pallas_call x1, Pallas kernels, on_device(): pl.pallas_call(last_base_kernel, out_shape=wide_shape, in_specs=[vmem] *...  0.92 us
    pallas_call x1, Pallas kernels, on_device(): pl.pallas_call(functools.partial(step_kernel, parts), out_shape=[wide_sha...  0.87 us
  transfers between devices with their start and end apart: 9, of which 3 were waited for; matrix products, arithmetic and copies ran while one was open for 0% of the time, Pallas kernels for 14%

profile of v13, /device:TPU:0, one launch (start us, length us, event | category | flops | bytes accessed | tf_op | source)
XLA Modules:
  0.0 17.6 jit_solution(10361558195963838532)
XLA Ops:
  0.6 0.0 copy-start.5
  0.7 0.0 copy-start.6
  0.7 0.0 copy-start.7
  0.7 0.2 %tables.1 = (bf16[128,640]{1,0:T(8,128)(2,1)S(1)}, bf16[400,640]{1,0:T(8,128)(2,1)S(1)}) custom-call(), custom_call_target="tpu_custom_call" | custom-call | flops 10000000000 | bytes 1000000 | tf_op jit(solution)/shard_map/tables/pallas_call | solution.py:538
  1.6 0.0 copy-done.5
  1.6 0.1 copy-done.6
  1.7 0.1 copy-done.7
  1.7 0.0 copy-start.8
  1.8 0.0 copy-start.9
  1.8 0.3 %first_traces.1 = (f32[8,320]{1,0:T(8,128)S(1)}, bf16[96,512]{1,0:T(8,128)(2,1)S(1)}, bf16[8,512]{1,0:T(8,128)(2,1)S(1)}, bf16[8,512]{1,0:T(8,128)(2,1)S(1)}, bf...) custom-call(s32[1]{0:T(128)} %bitcast.place_ref, f32[1]{0:T(128)S(6)} %copy.14.freq_ref, ...), custom_call_target="tpu_custom_call" | custom-call | flops 10000000000 | bytes 1000000 | tf_op jit(solution)/shard_map/first_traces/pallas_call | solution.py:550
  2.1 0.0 copy-start.2
  2.1 0.5 %collective-permute-start = (bf16[8,512]{1,0:T(8,128)(2,1)S(1)}, bf16[8,512]{1,0:T(8,128)(2,1)S(1)}, u32[]{:S(2)}, u32[]{:S(2)}) collective-permute-start(bf16[8,512]{1,0:T(8,128)(2,1)S(1)} %get-tuple-element.28), channel_id=1, source_target_pairs={{2,4},{3,5},{6,8},{7,9},{10,12},{11,13},{0,1},{14,15},{18,20},{19,... | collective-permute-start | bytes 24584 | tf_op jit(solution)/shard_map/ppermute | solution.py:527
  2.7 2.6 %collective-permute-start.1 = (bf16[8,512]{1,0:T(8,128)(2,1)S(1)}, bf16[8,512]{1,0:T(8,128)(2,1)S(1)}, u32[]{:S(2)}, u32[]{:S(2)}) collective-permute-start(bf16[8,512]{1,0:T(8,128)(2,1)S(1)} %get-tuple-element.29), channel_id=1, source_target_pairs={{1,2},{3,4},{5,6},{7,8},{9,10},{11,12},{13,14},{17,18},{19,20},{21... | collective-permute-start | bytes 24584 | tf_op jit(solution)/shard_map/ppermute | solution.py:527
  5.2 1.5 %collective-permute-start.2 = (bf16[8,512]{1,0:T(8,128)(2,1)S(1)}, bf16[8,512]{1,0:T(8,128)(2,1)S(1)}, u32[]{:S(2)}, u32[]{:S(2)}) collective-permute-start(bf16[8,512]{1,0:T(8,128)(2,1)S(1)} %get-tuple-element.30), channel_id=1, source_target_pairs={{0,2},{1,3},{4,6},{5,7},{8,10},{9,11},{12,14},{13,15},{16,18},{17,... | collective-permute-start | bytes 24584 | tf_op jit(solution)/shard_map/ppermute | solution.py:527
  6.7 1.2 %collective-permute-start.3 = (bf16[8,512]{1,0:T(8,128)(2,1)S(1)}, bf16[8,512]{1,0:T(8,128)(2,1)S(1)}, u32[]{:S(2)}, u32[]{:S(2)}) collective-permute-start(bf16[8,512]{1,0:T(8,128)(2,1)S(1)} %get-tuple-element.31), channel_id=1, source_target_pairs={{0,1},{2,3},{4,5},{6,7},{8,9},{10,11},{12,13},{14,15},{16,17},{18,... | collective-permute-start | bytes 24584 | tf_op jit(solution)/shard_map/ppermute | solution.py:527
  8.0 1.5 %own_terms.1 = (f32[4,16,320]{2,1,0:T(8,128)S(1)}, f32[4,16,320]{2,1,0:T(8,128)S(1)}, bf16[96,640]{1,0:T(8,128)(2,1)S(1)}, bf16[96,128]{1,0:T(8,128)(2,1)S(1)}, ...) custom-call(bf16[4,16,320]{2,1,0:T(8,128)(2,1)S(1)} %copy-done.3, bf16[16,320,320]{2,1,0:T(8,128)(2,1)S(1)} %copy-done, ...), custom_call_target="tpu_custom_call" | custom-call | flops 13107200 | bytes 3276800 | tf_op jit(solution)/shard_map/own_terms/pallas_call | solution.py:560
  9.4 0.0 collective-permute-done.refs_0_
  9.4 0.0 collective-permute-done.1.refs_1_
  9.5 0.9 %first_step.1 = (f32[4,16,320]{2,1,0:T(8,128)S(1)}, bf16[128,384]{1,0:T(8,128)(2,1)S(1)}, bf16[96,512]{1,0:T(8,128)(2,1)S(1)}, bf16[8,512]{1,0:T(8,128)(2,1)S(1)...) custom-call(s32[1]{0:T(128)} %bitcast.place_ref, ...), custom_call_target="tpu_custom_call" | custom-call | tf_op jit(solution)/shard_map/first_step/pallas_call | solution.py:571
  10.3 1.6 %collective-permute-start.8 = (bf16[128,384]{1,0:T(8,128)(2,1)S(1)}, bf16[128,384]{1,0:T(8,128)(2,1)S(1)}, u32[]{:S(2)}, u32[]{:S(2)}) collective-permute-start(bf16[128,384]{1,0:T(8,128)(2,1)S(1)} %get-tuple-element.47), channel_id=1, source_target_pairs={{16,0},{0,16},{17,1},{1,17},{18,2},{2,18},{19,3},{3,19},{20,4},{4,... | collective-permute-start | bytes 294920 | tf_op jit(solution)/shard_map/ppermute | solution.py:580
  11.9 0.9 %collective-permute-start.4 = (bf16[8,512]{1,0:T(8,128)(2,1)S(1)}, bf16[8,512]{1,0:T(8,128)(2,1)S(1)}, u32[]{:S(2)}, u32[]{:S(2)}) collective-permute-start(bf16[8,512]{1,0:T(8,128)(2,1)S(1)} %get-tuple-element.40), channel_id=1, source_target_pairs={{0,2},{1,3},{4,6},{5,7},{8,10},{9,11},{12,14},{13,15},{16,18},{17,... | collective-permute-start | bytes 24584 | tf_op jit(solution)/shard_map/ppermute | solution.py:527
  12.8 0.5 %collective-permute-start.5 = (bf16[8,512]{1,0:T(8,128)(2,1)S(1)}, bf16[8,512]{1,0:T(8,128)(2,1)S(1)}, u32[]{:S(2)}, u32[]{:S(2)}) collective-permute-start(bf16[8,512]{1,0:T(8,128)(2,1)S(1)} %get-tuple-element.41), channel_id=1, source_target_pairs={{1,2},{3,4},{5,6},{7,8},{9,10},{11,12},{13,14},{17,18},{19,20},{21... | collective-permute-start | bytes 24584 | tf_op jit(solution)/shard_map/ppermute | solution.py:527
  13.3 0.7 %collective-permute-start.6 = (bf16[8,512]{1,0:T(8,128)(2,1)S(1)}, bf16[8,512]{1,0:T(8,128)(2,1)S(1)}, u32[]{:S(2)}, u32[]{:S(2)}) collective-permute-start(bf16[8,512]{1,0:T(8,128)(2,1)S(1)} %get-tuple-element.42), channel_id=1, source_target_pairs={{2,4},{3,5},{6,8},{7,9},{10,12},{11,13},{0,1},{14,15},{18,20},{19,... | collective-permute-start | bytes 24584 | tf_op jit(solution)/shard_map/ppermute | solution.py:527
  14.0 0.0 collective-permute-start.7
  14.0 0.9 %last_own_terms.1.base_ref = f32[4,16,320]{2,1,0:T(8,128)S(1)} custom-call(f32[4,16,320]{2,1,0:T(8,128)S(1)} %get-tuple-element.44.state_ref.partial_ref, bf16[96,512]{1,0:T(8,128)(2,1)S(1)} %get-tuple-element.45.pool_ref, bf16[16,320,320]{2,1,0:T(8,128)(2,1)S(1)} %copy-done, bf16[4,16,320]{2,1,0:T(8,128)(2,1)S(1)} %copy-done.4, ...), custom_call_target="tpu_custom_call" | custom-call | flops 13107200 | bytes 3276800 | tf_op jit(solution)/shard_map/last_own_terms/pallas_call | solution.py:584
  15.0 0.1 collective-permute-done.8.refs_0_
  15.1 0.1 message_terms.1
  15.3 0.3 %collective-permute-done.4.refs_0_ = bf16[8,512]{1,0:T(8,128)(2,1)S(1)} collective-permute-done((bf16[8,512]{1,0:T(8,128)(2,1)S(1)}, bf16[8,512]{1,0:T(8,128)(2,1)S(1)}, u32[]{:S(2)}, u32[]{:S(2)}) %collective-permute-start.4) | collective-permute-done | bytes 8224 | tf_op jit(solution)/shard_map/ppermute | solution.py:527
  15.6 0.9 %collective-permute-done.5.refs_1_ = bf16[8,512]{1,0:T(8,128)(2,1)S(1)} collective-permute-done((bf16[8,512]{1,0:T(8,128)(2,1)S(1)}, bf16[8,512]{1,0:T(8,128)(2,1)S(1)}, u32[]{:S(2)}, u32[]{:S(2)}) %collective-permute-start.5) | collective-permute-done | bytes 8224 | tf_op jit(solution)/shard_map/ppermute | solution.py:527
  16.5 0.0 collective-permute-done.6.refs_2_
  16.5 0.0 collective-permute-done.7.refs_3_
  16.5 1.1 %last_step.1 = (bf16[4,16,320]{2,1,0:T(8,128)(2,1)}, f32[4,16,320]{2,1,0:T(8,128)}) custom-call(s32[1]{0:T(128)} %bitcast.place_ref, bf16[8,512]{1,0:T(8,128)(2,1)S(1)} %collective-permute-done.4.refs_0_, bf16[8,512]{1,0:T(8,128)(2,1)S(1)} %collective-permute-done.5.refs_1_, bf16[8,512]{1,0:T(8,128)(2,1)S(1)} %collective-permute-done.6.refs_2_, ...), custom_call_target="tpu_custom_call" | custom-call | tf_op jit(solution)/shard_map/last_step/pallas_call | solution.py:602
  (15 shorter events, 0.0 us)
Async XLA Ops:
  0.6 0.9 %copy-start.3 = (bf16[4,16,320]{2,1,0:T(8,128)(2,1)S(1)}, bf16[4,16,320]{2,1,0:T(8,128)(2,1)}, u32[]{:S(2)}) copy-start(bf16[4,16,320]{2,1,0:T(8,128)(2,1)} %first_ref.1) | copy-start | bytes 122884
  0.6 0.9 %copy-start.5 = (bf16[320,256]{1,0:T(8,128)(2,1)S(1)}, bf16[320,256]{1,0:T(8,128)(2,1)}, u32[]{:S(2)}) copy-start(bf16[320,256]{1,0:T(8,128)(2,1)} %constant.17.clone.refs_2_) | copy-start | bytes 491524
  0.7 1.0 %copy-start.6 = (bf16[320,256]{1,0:T(8,128)(2,1)S(1)}, bf16[320,256]{1,0:T(8,128)(2,1)}, u32[]{:S(2)}) copy-start(bf16[320,256]{1,0:T(8,128)(2,1)} %constant.16.clone.refs_1_) | copy-start | bytes 491524
  0.7 1.1 %copy-start.7 = (bf16[320,256]{1,0:T(8,128)(2,1)S(1)}, bf16[320,256]{1,0:T(8,128)(2,1)}, u32[]{:S(2)}) copy-start(bf16[320,256]{1,0:T(8,128)(2,1)} %constant.15.clone.refs_0_) | copy-start | bytes 491524
  0.7 1.1 %copy-start.10 = (s32[1,4,8]{2,1,0:T(4,128)S(1)}, s32[1,4,8]{2,1,0:T(4,128)}, u32[]{:S(2)}) copy-start(s32[1,4,8]{2,1,0:T(4,128)} %refs_12_.1) | copy-start | bytes 388
  1.7 6.2 %copy-start = (bf16[16,320,320]{2,1,0:T(8,128)(2,1)S(1)}, bf16[16,320,320]{2,1,0:T(8,128)(2,1)}, u32[]{:S(2)}) copy-start(bf16[16,320,320]{2,1,0:T(8,128)(2,1)} %diag_ref.3) | copy-start | bytes 9830404
  1.7 6.2 %copy-start.1 = (bf16[768,320]{1,0:T(8,128)(2,1)S(1)}, bf16[768,320]{1,0:T(8,128)(2,1)}, u32[]{:S(2)}) copy-start(bf16[768,320]{1,0:T(8,128)(2,1)} %constant.18.clone.lift_ref.refs_10_.refs_8_) | copy-start | bytes 1474564
  1.7 6.2 %copy-start.4 = (bf16[4,16,320]{2,1,0:T(8,128)(2,1)S(1)}, bf16[4,16,320]{2,1,0:T(8,128)(2,1)}, u32[]{:S(2)}) copy-start(bf16[4,16,320]{2,1,0:T(8,128)(2,1)} %forcing_ref.3) | copy-start | bytes 122884
  1.7 6.2 %copy-start.8 = (bf16[16,2400]{1,0:T(8,128)(2,1)S(1)}, bf16[16,2400]{1,0:T(8,128)(2,1)}, u32[]{:S(2)}) copy-start(bf16[16,2400]{1,0:T(8,128)(2,1)} %flux_ref.1) | copy-start | bytes 230404
  1.8 6.2 %copy-start.9 = (s32[16,6]{0,1:T(8,128)S(1)}, s32[16,6]{0,1:T(8,128)}, u32[]{:S(2)}) copy-start(s32[16,6]{0,1:T(8,128)} %param.17) | copy-start | bytes 1156
  2.1 7.3 %copy-start.2 = (bf16[768,768]{1,0:T(8,128)(2,1)S(1)}, bf16[768,768]{1,0:T(8,128)(2,1)}, u32[]{:S(2)}) copy-start(bf16[768,768]{1,0:T(8,128)(2,1)} %constant.14.clone.refs_11_) | copy-start | bytes 3538948
  2.1 7.3 %collective-permute-start = (bf16[8,512]{1,0:T(8,128)(2,1)S(1)}, bf16[8,512]{1,0:T(8,128)(2,1)S(1)}, u32[]{:S(2)}, u32[]{:S(2)}) collective-permute-start(bf16[8,512]{1,0:T(8,128)(2,1)S(1)} %get-tuple-element.28), channel_id=1, source_target_pairs={{2,4},{3,5},{6,8},{7,9},{10,12},{11,13},{0,1},{14,15},{18,20},{19,... | collective-permute-start | bytes 24584 | tf_op jit(solution)/shard_map/ppermute | solution.py:527
  2.7 6.8 %collective-permute-start.1 = (bf16[8,512]{1,0:T(8,128)(2,1)S(1)}, bf16[8,512]{1,0:T(8,128)(2,1)S(1)}, u32[]{:S(2)}, u32[]{:S(2)}) collective-permute-start(bf16[8,512]{1,0:T(8,128)(2,1)S(1)} %get-tuple-element.29), channel_id=1, source_target_pairs={{1,2},{3,4},{5,6},{7,8},{9,10},{11,12},{13,14},{17,18},{19,20},{21... | collective-permute-start | bytes 24584 | tf_op jit(solution)/shard_map/ppermute | solution.py:527
  5.2 4.2 %collective-permute-start.2 = (bf16[8,512]{1,0:T(8,128)(2,1)S(1)}, bf16[8,512]{1,0:T(8,128)(2,1)S(1)}, u32[]{:S(2)}, u32[]{:S(2)}) collective-permute-start(bf16[8,512]{1,0:T(8,128)(2,1)S(1)} %get-tuple-element.30), channel_id=1, source_target_pairs={{0,2},{1,3},{4,6},{5,7},{8,10},{9,11},{12,14},{13,15},{16,18},{17,... | collective-permute-start | bytes 24584 | tf_op jit(solution)/shard_map/ppermute | solution.py:527
  6.7 2.7 %collective-permute-start.3 = (bf16[8,512]{1,0:T(8,128)(2,1)S(1)}, bf16[8,512]{1,0:T(8,128)(2,1)S(1)}, u32[]{:S(2)}, u32[]{:S(2)}) collective-permute-start(bf16[8,512]{1,0:T(8,128)(2,1)S(1)} %get-tuple-element.31), channel_id=1, source_target_pairs={{0,1},{2,3},{4,5},{6,7},{8,9},{10,11},{12,13},{14,15},{16,17},{18,... | collective-permute-start | bytes 24584 | tf_op jit(solution)/shard_map/ppermute | solution.py:527
  10.3 4.8 %collective-permute-start.8 = (bf16[128,384]{1,0:T(8,128)(2,1)S(1)}, bf16[128,384]{1,0:T(8,128)(2,1)S(1)}, u32[]{:S(2)}, u32[]{:S(2)}) collective-permute-start(bf16[128,384]{1,0:T(8,128)(2,1)S(1)} %get-tuple-element.47), channel_id=1, source_target_pairs={{16,0},{0,16},{17,1},{1,17},{18,2},{2,18},{19,3},{3,19},{20,4},{4,... | collective-permute-start | bytes 294920 | tf_op jit(solution)/shard_map/ppermute | solution.py:580
  11.9 3.7 %collective-permute-start.4 = (bf16[8,512]{1,0:T(8,128)(2,1)S(1)}, bf16[8,512]{1,0:T(8,128)(2,1)S(1)}, u32[]{:S(2)}, u32[]{:S(2)}) collective-permute-start(bf16[8,512]{1,0:T(8,128)(2,1)S(1)} %get-tuple-element.40), channel_id=1, source_target_pairs={{0,2},{1,3},{4,6},{5,7},{8,10},{9,11},{12,14},{13,15},{16,18},{17,... | collective-permute-start | bytes 24584 | tf_op jit(solution)/shard_map/ppermute | solution.py:527
  12.8 3.7 %collective-permute-start.5 = (bf16[8,512]{1,0:T(8,128)(2,1)S(1)}, bf16[8,512]{1,0:T(8,128)(2,1)S(1)}, u32[]{:S(2)}, u32[]{:S(2)}) collective-permute-start(bf16[8,512]{1,0:T(8,128)(2,1)S(1)} %get-tuple-element.41), channel_id=1, source_target_pairs={{1,2},{3,4},{5,6},{7,8},{9,10},{11,12},{13,14},{17,18},{19,20},{21... | collective-permute-start | bytes 24584 | tf_op jit(solution)/shard_map/ppermute | solution.py:527
  13.3 3.1 %collective-permute-start.6 = (bf16[8,512]{1,0:T(8,128)(2,1)S(1)}, bf16[8,512]{1,0:T(8,128)(2,1)S(1)}, u32[]{:S(2)}, u32[]{:S(2)}) collective-permute-start(bf16[8,512]{1,0:T(8,128)(2,1)S(1)} %get-tuple-element.42), channel_id=1, source_target_pairs={{2,4},{3,5},{6,8},{7,9},{10,12},{11,13},{0,1},{14,15},{18,20},{19,... | collective-permute-start | bytes 24584 | tf_op jit(solution)/shard_map/ppermute | solution.py:527
  14.0 2.4 %collective-permute-start.7 = (bf16[8,512]{1,0:T(8,128)(2,1)S(1)}, bf16[8,512]{1,0:T(8,128)(2,1)S(1)}, u32[]{:S(2)}, u32[]{:S(2)}) collective-permute-start(bf16[8,512]{1,0:T(8,128)(2,1)S(1)} %get-tuple-element.43), channel_id=1, source_target_pairs={{0,1},{2,3},{4,5},{6,7},{8,9},{10,11},{12,13},{14,15},{16,17},{18,... | collective-permute-start | bytes 24584 | tf_op jit(solution)/shard_map/ppermute | solution.py:527

commit v14 on v12

--- a/solution.py
+++ b/solution.py
@@ -366,13 +366,13 @@
     flux = flux_order(flux_ref[...], order_ref[...])
     hot_ref[...] = hot
     flux_out_ref[...] = flux
-    factors = lax.dot_general(hot, flux, (((0,), (0,)), ((), ())), preferred_element_type=F32)
-    factor_ref[...] = rotated(factors[FACES * elems :])
     states = [state_ref[t] for t in range(insts)]
     spatial = local_terms(
         states, diag_ref, wide_ref, prod_ref, pool_ref[...], hot, flux, spread_ref[...],
         lift_ref[...], insts, elems,
     )
+    factors = lax.dot_general(hot, flux, (((0,), (0,)), ((), ())), preferred_element_type=F32)
+    factor_ref[...] = rotated(factors[FACES * elems :])
     for t in range(insts):
         spatial_ref[t] = spatial[t]
         rest_ref[t] = couple(entry_ref, states, t, 0, insts) - forcing_ref[t].astype(F32)

time: 17.8 us -> 17.8 us (level)
  no operation moved by 1% of the time
where the time goes in v14:
time: 17.8 us; the launch traced here: 17.5 us
  starting transfers between devices  9.62 us (54%)
  Pallas kernels  4.67 us (26%)
  waiting for transfers between devices  1.55 us (9%)
  between operations  1.49 us (8%)
  local copies, waits for them, and re-layouts  0.19 us (1%)
    ppermute x8, starting transfers between devices, exchange(): lax.ppermute(outgoing[swap], ('inst', 'dom'), routes[swap])  8.06 us
    ppermute x1, starting transfers between devices, on_device(): lax.ppermute(message, 'inst', [((i + rank) % ranks, i) for i in range(ran...  1.56 us
    ppermute x8, waiting for transfers between devices, exchange(): lax.ppermute(outgoing[swap], ('inst', 'dom'), routes[swap])  1.4 us
    pallas_call x1, Pallas kernels, on_device(): pl.pallas_call(functools.partial(base_kernel, slots * capacity), out_shap...  1.15 us
    pallas_call x1, Pallas kernels, on_device(): pl.pallas_call(functools.partial(last_kernel, parts), out_shape=[like(ini...  1.14 us
    pallas_call x1, Pallas kernels, on_device(): pl.pallas_call(last_base_kernel, out_shape=wide_shape, in_specs=[vmem] *...  0.92 us
    pallas_call x1, Pallas kernels, on_device(): pl.pallas_call(functools.partial(step_kernel, parts), out_shape=[wide_sha...  0.81 us
  transfers between devices with their start and end apart: 9, of which 3 were waited for; matrix products, arithmetic and copies ran while one was open for 0% of the time, Pallas kernels for 13%

profile of v14, /device:TPU:0, one launch (start us, length us, event | category | flops | bytes accessed | tf_op | source)
XLA Modules:
  0.0 17.5 jit_solution(17189849947987359419)
XLA Ops:
  0.6 0.0 copy-start.4
  0.6 0.0 copy-start.5
  0.7 0.0 copy-start.6
  0.7 0.2 %tables.1 = (bf16[128,640]{1,0:T(8,128)(2,1)S(1)}, bf16[400,640]{1,0:T(8,128)(2,1)S(1)}) custom-call(), custom_call_target="tpu_custom_call" | custom-call | flops 10000000000 | bytes 1000000 | tf_op jit(solution)/shard_map/tables/pallas_call | solution.py:521
  1.6 0.1 copy-done.5
  1.6 0.1 copy-done.6
  1.7 0.0 copy-start.3
  1.7 0.0 copy-start.7
  1.8 0.0 copy-start.8
  1.8 0.3 %first_traces.1 = (f32[8,320]{1,0:T(8,128)S(1)}, bf16[96,512]{1,0:T(8,128)(2,1)S(1)}, bf16[8,512]{1,0:T(8,128)(2,1)S(1)}, bf16[8,512]{1,0:T(8,128)(2,1)S(1)}, bf...) custom-call(s32[1]{0:T(128)} %bitcast.place_ref, f32[1]{0:T(128)S(6)} %copy.13.freq_ref, ...), custom_call_target="tpu_custom_call" | custom-call | flops 10000000000 | bytes 1000000 | tf_op jit(solution)/shard_map/first_traces/pallas_call | solution.py:533
  2.1 0.5 %collective-permute-start = (bf16[8,512]{1,0:T(8,128)(2,1)S(1)}, bf16[8,512]{1,0:T(8,128)(2,1)S(1)}, u32[]{:S(2)}, u32[]{:S(2)}) collective-permute-start(bf16[8,512]{1,0:T(8,128)(2,1)S(1)} %get-tuple-element.27), channel_id=1, source_target_pairs={{2,4},{3,5},{6,8},{7,9},{10,12},{11,13},{0,1},{14,15},{18,20},{19,... | collective-permute-start | bytes 24584 | tf_op jit(solution)/shard_map/ppermute | solution.py:511
  2.6 2.6 %collective-permute-start.1 = (bf16[8,512]{1,0:T(8,128)(2,1)S(1)}, bf16[8,512]{1,0:T(8,128)(2,1)S(1)}, u32[]{:S(2)}, u32[]{:S(2)}) collective-permute-start(bf16[8,512]{1,0:T(8,128)(2,1)S(1)} %get-tuple-element.28), channel_id=1, source_target_pairs={{1,2},{3,4},{5,6},{7,8},{9,10},{11,12},{13,14},{17,18},{19,20},{21... | collective-permute-start | bytes 24584 | tf_op jit(solution)/shard_map/ppermute | solution.py:511
  5.2 1.5 %collective-permute-start.2 = (bf16[8,512]{1,0:T(8,128)(2,1)S(1)}, bf16[8,512]{1,0:T(8,128)(2,1)S(1)}, u32[]{:S(2)}, u32[]{:S(2)}) collective-permute-start(bf16[8,512]{1,0:T(8,128)(2,1)S(1)} %get-tuple-element.29), channel_id=1, source_target_pairs={{0,2},{1,3},{4,6},{5,7},{8,10},{9,11},{12,14},{13,15},{16,18},{17,... | collective-permute-start | bytes 24584 | tf_op jit(solution)/shard_map/ppermute | solution.py:511
  6.7 1.2 %collective-permute-start.3 = (bf16[8,512]{1,0:T(8,128)(2,1)S(1)}, bf16[8,512]{1,0:T(8,128)(2,1)S(1)}, u32[]{:S(2)}, u32[]{:S(2)}) collective-permute-start(bf16[8,512]{1,0:T(8,128)(2,1)S(1)} %get-tuple-element.30), channel_id=1, source_target_pairs={{0,1},{2,3},{4,5},{6,7},{8,9},{10,11},{12,13},{14,15},{16,17},{18,... | collective-permute-start | bytes 24584 | tf_op jit(solution)/shard_map/ppermute | solution.py:511
  7.9 1.1 %own_terms.1 = (f32[4,16,320]{2,1,0:T(8,128)S(1)}, f32[4,16,320]{2,1,0:T(8,128)S(1)}, bf16[96,640]{1,0:T(8,128)(2,1)S(1)}, bf16[96,128]{1,0:T(8,128)(2,1)S(1)}, f32[32,1024]{1,0:T(8,128)S(1)}) custom-call(bf16[4,16,320]{2,1,0:T(8,128)(2,1)S(1)} %copy-done.2, bf16[16,320,320]{2,1,0:T(8,128)(2,1)S(1)} %copy-done, bf16[4,16,320]{2,1,0:T(8,128)(2,1)S(1)} %copy-done.3, ...), custom_call_target="tpu_custom_call" | custom-call | flops 13107200 | bytes 3276800 | tf_op jit(solution)/shard_map/own_terms/pallas_call | solution.py:543
  9.1 0.0 collective-permute-done.refs_0_
  9.1 0.0 collective-permute-done.1.refs_1_
  9.1 0.0 collective-permute-done.2.refs_2_
  9.1 0.0 collective-permute-done.3.refs_3_
  9.1 0.8 %first_step.1 = (f32[4,16,320]{2,1,0:T(8,128)S(1)}, bf16[128,384]{1,0:T(8,128)(2,1)S(1)}, bf16[96,512]{1,0:T(8,128)(2,1)S(1)}, bf16[8,512]{1,0:T(8,128)(2,1)S(1)...) custom-call(s32[1]{0:T(128)} %bitcast.place_ref, ...), custom_call_target="tpu_custom_call" | custom-call | tf_op jit(solution)/shard_map/first_step/pallas_call | solution.py:554
  9.9 1.6 %collective-permute-start.8 = (bf16[128,384]{1,0:T(8,128)(2,1)S(1)}, bf16[128,384]{1,0:T(8,128)(2,1)S(1)}, u32[]{:S(2)}, u32[]{:S(2)}) collective-permute-start(bf16[128,384]{1,0:T(8,128)(2,1)S(1)} %get-tuple-element.45), channel_id=1, source_target_pairs={{16,0},{0,16},{17,1},{1,17},{18,2},{2,18},{19,3},{3,19},{20,4},{4,... | collective-permute-start | bytes 294920 | tf_op jit(solution)/shard_map/ppermute | solution.py:563
  11.5 1.2 %collective-permute-start.4 = (bf16[8,512]{1,0:T(8,128)(2,1)S(1)}, bf16[8,512]{1,0:T(8,128)(2,1)S(1)}, u32[]{:S(2)}, u32[]{:S(2)}) collective-permute-start(bf16[8,512]{1,0:T(8,128)(2,1)S(1)} %get-tuple-element.38), channel_id=1, source_target_pairs={{0,2},{1,3},{4,6},{5,7},{8,10},{9,11},{12,14},{13,15},{16,18},{17,... | collective-permute-start | bytes 24584 | tf_op jit(solution)/shard_map/ppermute | solution.py:511
  12.7 0.5 %collective-permute-start.5 = (bf16[8,512]{1,0:T(8,128)(2,1)S(1)}, bf16[8,512]{1,0:T(8,128)(2,1)S(1)}, u32[]{:S(2)}, u32[]{:S(2)}) collective-permute-start(bf16[8,512]{1,0:T(8,128)(2,1)S(1)} %get-tuple-element.39), channel_id=1, source_target_pairs={{1,2},{3,4},{5,6},{7,8},{9,10},{11,12},{13,14},{17,18},{19,20},{21... | collective-permute-start | bytes 24584 | tf_op jit(solution)/shard_map/ppermute | solution.py:511
  13.3 0.4 %collective-permute-start.6 = (bf16[8,512]{1,0:T(8,128)(2,1)S(1)}, bf16[8,512]{1,0:T(8,128)(2,1)S(1)}, u32[]{:S(2)}, u32[]{:S(2)}) collective-permute-start(bf16[8,512]{1,0:T(8,128)(2,1)S(1)} %get-tuple-element.40), channel_id=1, source_target_pairs={{2,4},{3,5},{6,8},{7,9},{10,12},{11,13},{0,1},{14,15},{18,20},{19,... | collective-permute-start | bytes 24584 | tf_op jit(solution)/shard_map/ppermute | solution.py:511
  13.6 0.1 collective-permute-start.7
  13.8 0.9 %last_own_terms.1.base_ref = f32[4,16,320]{2,1,0:T(8,128)S(1)} custom-call(f32[4,16,320]{2,1,0:T(8,128)S(1)} %get-tuple-element.42.state_ref.partial_ref, bf16[96,512]{1,0:T(8,128)(2,1)S(1)} %get-tuple-element.43.pool_ref, bf16[16,320,320]{2,1,0:T(8,128)(2,1)S(1)} %copy-done, bf16[4,16,320]{2,1,0:T(8,128)(2,1)S(1)} %copy-done.3, ...), custom_call_target="tpu_custom_call" | custom-call | flops 13107200 | bytes 3276800 | tf_op jit(solution)/shard_map/last_own_terms/pallas_call | solution.py:567
  14.7 0.2 collective-permute-done.8.refs_0_
  14.9 0.1 message_terms.1
  15.0 0.2 collective-permute-done.4.refs_0_
  15.2 1.2 %collective-permute-done.5.refs_1_ = bf16[8,512]{1,0:T(8,128)(2,1)S(1)} collective-permute-done((bf16[8,512]{1,0:T(8,128)(2,1)S(1)}, bf16[8,512]{1,0:T(8,128)(2,1)S(1)}, u32[]{:S(2)}, u32[]{:S(2)}) %collective-permute-start.5) | collective-permute-done | bytes 8224 | tf_op jit(solution)/shard_map/ppermute | solution.py:511
  16.4 0.0 collective-permute-done.6.refs_2_
  16.4 1.1 %last_step.1 = (bf16[4,16,320]{2,1,0:T(8,128)(2,1)}, f32[4,16,320]{2,1,0:T(8,128)}) custom-call(s32[1]{0:T(128)} %bitcast.place_ref, bf16[8,512]{1,0:T(8,128)(2,1)S(1)} %collective-permute-done.4.refs_0_, bf16[8,512]{1,0:T(8,128)(2,1)S(1)} %collective-permute-done.5.refs_1_, bf16[8,512]{1,0:T(8,128)(2,1)S(1)} %collective-permute-done.6.refs_2_, ...), custom_call_target="tpu_custom_call" | custom-call | tf_op jit(solution)/shard_map/last_step/pallas_call | solution.py:585
  (13 shorter events, 0.0 us)
Async XLA Ops:
  0.6 0.9 %copy-start.4 = (bf16[320,256]{1,0:T(8,128)(2,1)S(1)}, bf16[320,256]{1,0:T(8,128)(2,1)}, u32[]{:S(2)}) copy-start(bf16[320,256]{1,0:T(8,128)(2,1)} %constant.12.clone.refs_0_.refs_4_) | copy-start | bytes 491524
  0.6 1.0 %copy-start.5 = (bf16[320,256]{1,0:T(8,128)(2,1)S(1)}, bf16[320,256]{1,0:T(8,128)(2,1)}, u32[]{:S(2)}) copy-start(bf16[320,256]{1,0:T(8,128)(2,1)} %constant.13.clone.refs_1_.refs_5_) | copy-start | bytes 491524
  0.7 1.1 %copy-start.6 = (bf16[320,256]{1,0:T(8,128)(2,1)S(1)}, bf16[320,256]{1,0:T(8,128)(2,1)}, u32[]{:S(2)}) copy-start(bf16[320,256]{1,0:T(8,128)(2,1)} %constant.14.clone.refs_2_.refs_6_) | copy-start | bytes 491524
  0.7 1.0 %copy-start.2 = (bf16[4,16,320]{2,1,0:T(8,128)(2,1)S(1)}, bf16[4,16,320]{2,1,0:T(8,128)(2,1)}, u32[]{:S(2)}) copy-start(bf16[4,16,320]{2,1,0:T(8,128)(2,1)} %first_ref.1) | copy-start | bytes 122884
  0.7 1.0 %copy-start.9 = (s32[1,4,8]{2,1,0:T(4,128)S(1)}, s32[1,4,8]{2,1,0:T(4,128)}, u32[]{:S(2)}) copy-start(s32[1,4,8]{2,1,0:T(4,128)} %refs_13_.1) | copy-start | bytes 388
  1.7 6.2 %copy-start = (bf16[16,320,320]{2,1,0:T(8,128)(2,1)S(1)}, bf16[16,320,320]{2,1,0:T(8,128)(2,1)}, u32[]{:S(2)}) copy-start(bf16[16,320,320]{2,1,0:T(8,128)(2,1)} %diag_ref.3) | copy-start | bytes 9830404
  1.7 6.2 %copy-start.1 = (bf16[768,320]{1,0:T(8,128)(2,1)S(1)}, bf16[768,320]{1,0:T(8,128)(2,1)}, u32[]{:S(2)}) copy-start(bf16[768,320]{1,0:T(8,128)(2,1)} %constant.15.clone.lift_ref.refs_12_.refs_8_) | copy-start | bytes 1474564
  1.7 6.2 %copy-start.3 = (bf16[4,16,320]{2,1,0:T(8,128)(2,1)S(1)}, bf16[4,16,320]{2,1,0:T(8,128)(2,1)}, u32[]{:S(2)}) copy-start(bf16[4,16,320]{2,1,0:T(8,128)(2,1)} %forcing_ref.3) | copy-start | bytes 122884
  1.7 6.2 %copy-start.7 = (bf16[16,2400]{1,0:T(8,128)(2,1)S(1)}, bf16[16,2400]{1,0:T(8,128)(2,1)}, u32[]{:S(2)}) copy-start(bf16[16,2400]{1,0:T(8,128)(2,1)} %flux_ref.1) | copy-start | bytes 230404
  1.8 6.2 %copy-start.8 = (s32[16,6]{0,1:T(8,128)S(1)}, s32[16,6]{0,1:T(8,128)}, u32[]{:S(2)}) copy-start(s32[16,6]{0,1:T(8,128)} %param.16) | copy-start | bytes 1156
  2.1 7.0 %collective-permute-start = (bf16[8,512]{1,0:T(8,128)(2,1)S(1)}, bf16[8,512]{1,0:T(8,128)(2,1)S(1)}, u32[]{:S(2)}, u32[]{:S(2)}) collective-permute-start(bf16[8,512]{1,0:T(8,128)(2,1)S(1)} %get-tuple-element.27), channel_id=1, source_target_pairs={{2,4},{3,5},{6,8},{7,9},{10,12},{11,13},{0,1},{14,15},{18,20},{19,... | collective-permute-start | bytes 24584 | tf_op jit(solution)/shard_map/ppermute | solution.py:511
  2.6 6.5 %collective-permute-start.1 = (bf16[8,512]{1,0:T(8,128)(2,1)S(1)}, bf16[8,512]{1,0:T(8,128)(2,1)S(1)}, u32[]{:S(2)}, u32[]{:S(2)}) collective-permute-start(bf16[8,512]{1,0:T(8,128)(2,1)S(1)} %get-tuple-element.28), channel_id=1, source_target_pairs={{1,2},{3,4},{5,6},{7,8},{9,10},{11,12},{13,14},{17,18},{19,20},{21... | collective-permute-start | bytes 24584 | tf_op jit(solution)/shard_map/ppermute | solution.py:511
  5.2 3.9 %collective-permute-start.2 = (bf16[8,512]{1,0:T(8,128)(2,1)S(1)}, bf16[8,512]{1,0:T(8,128)(2,1)S(1)}, u32[]{:S(2)}, u32[]{:S(2)}) collective-permute-start(bf16[8,512]{1,0:T(8,128)(2,1)S(1)} %get-tuple-element.29), channel_id=1, source_target_pairs={{0,2},{1,3},{4,6},{5,7},{8,10},{9,11},{12,14},{13,15},{16,18},{17,... | collective-permute-start | bytes 24584 | tf_op jit(solution)/shard_map/ppermute | solution.py:511
  6.7 2.4 %collective-permute-start.3 = (bf16[8,512]{1,0:T(8,128)(2,1)S(1)}, bf16[8,512]{1,0:T(8,128)(2,1)S(1)}, u32[]{:S(2)}, u32[]{:S(2)}) collective-permute-start(bf16[8,512]{1,0:T(8,128)(2,1)S(1)} %get-tuple-element.30), channel_id=1, source_target_pairs={{0,1},{2,3},{4,5},{6,7},{8,9},{10,11},{12,13},{14,15},{16,17},{18,... | collective-permute-start | bytes 24584 | tf_op jit(solution)/shard_map/ppermute | solution.py:511
  9.9 4.9 %collective-permute-start.8 = (bf16[128,384]{1,0:T(8,128)(2,1)S(1)}, bf16[128,384]{1,0:T(8,128)(2,1)S(1)}, u32[]{:S(2)}, u32[]{:S(2)}) collective-permute-start(bf16[128,384]{1,0:T(8,128)(2,1)S(1)} %get-tuple-element.45), channel_id=1, source_target_pairs={{16,0},{0,16},{17,1},{1,17},{18,2},{2,18},{19,3},{3,19},{20,4},{4,... | collective-permute-start | bytes 294920 | tf_op jit(solution)/shard_map/ppermute | solution.py:563
  11.5 3.7 %collective-permute-start.4 = (bf16[8,512]{1,0:T(8,128)(2,1)S(1)}, bf16[8,512]{1,0:T(8,128)(2,1)S(1)}, u32[]{:S(2)}, u32[]{:S(2)}) collective-permute-start(bf16[8,512]{1,0:T(8,128)(2,1)S(1)} %get-tuple-element.38), channel_id=1, source_target_pairs={{0,2},{1,3},{4,6},{5,7},{8,10},{9,11},{12,14},{13,15},{16,18},{17,... | collective-permute-start | bytes 24584 | tf_op jit(solution)/shard_map/ppermute | solution.py:511
  12.7 3.7 %collective-permute-start.5 = (bf16[8,512]{1,0:T(8,128)(2,1)S(1)}, bf16[8,512]{1,0:T(8,128)(2,1)S(1)}, u32[]{:S(2)}, u32[]{:S(2)}) collective-permute-start(bf16[8,512]{1,0:T(8,128)(2,1)S(1)} %get-tuple-element.39), channel_id=1, source_target_pairs={{1,2},{3,4},{5,6},{7,8},{9,10},{11,12},{13,14},{17,18},{19,20},{21... | collective-permute-start | bytes 24584 | tf_op jit(solution)/shard_map/ppermute | solution.py:511
  13.3 3.1 %collective-permute-start.6 = (bf16[8,512]{1,0:T(8,128)(2,1)S(1)}, bf16[8,512]{1,0:T(8,128)(2,1)S(1)}, u32[]{:S(2)}, u32[]{:S(2)}) collective-permute-start(bf16[8,512]{1,0:T(8,128)(2,1)S(1)} %get-tuple-element.40), channel_id=1, source_target_pairs={{2,4},{3,5},{6,8},{7,9},{10,12},{11,13},{0,1},{14,15},{18,20},{19,... | collective-permute-start | bytes 24584 | tf_op jit(solution)/shard_map/ppermute | solution.py:511
  13.6 2.7 %collective-permute-start.7 = (bf16[8,512]{1,0:T(8,128)(2,1)S(1)}, bf16[8,512]{1,0:T(8,128)(2,1)S(1)}, u32[]{:S(2)}, u32[]{:S(2)}) collective-permute-start(bf16[8,512]{1,0:T(8,128)(2,1)S(1)} %get-tuple-element.41), channel_id=1, source_target_pairs={{0,1},{2,3},{4,5},{6,7},{8,9},{10,11},{12,13},{14,15},{16,17},{18,... | collective-permute-start | bytes 24584 | tf_op jit(solution)/shard_map/ppermute | solution.py:511
